TPU v7x, 32 devices: a whole 2x2x4 slice. The times are simulated.
32 devices in a mesh: expert: 8 (over z, y), tensor: 4 (over x, core).
Axes of the slice: x: 2, y: 2, z: 4, core: 2. Of those that a mesh axis runs over, the one named last changes fastest.
Arguments:
- tokens_in: bfloat16 [2048, 2048], P('expert'), may hold values from -6 to 6
- out_grad: bfloat16 [2048, 2048], P('expert'), may hold values from -6 to 6
- w_qkv: float32 [3, 2048, 2048], P(None, 'expert', 'tensor'), may hold values from -0.125 to 0.125
- w_attn_out: float32 [2048, 2048], P('tensor', 'expert'), may hold values from -3 to 3
- attn_gain: float32 [2048], P('expert'), may hold values from 0.5 to 2
- ffn_gain: float32 [2048], P('expert'), may hold values from 0.5 to 2
- qk_gain: float32 [2, 16, 128], P(None, 'tensor', 'expert'), may hold values from 0.6 to 1.6
- w_router: float32 [2048, 16], P('expert'), may hold values from -0.0625 to 0.0625
- w_gate: float32 [16, 2048, 1024], P('expert', None, 'tensor'), may hold values from -0.125 to 0.125
- w_up: float32 [16, 2048, 1024], P('expert', None, 'tensor'), may hold values from -0.125 to 0.125
- w_down: float32 [16, 1024, 2048], P('expert', 'tensor'), may hold values from -2.5 to 2.5
- routes: int32 [2048, 8], P('expert'), may hold values from 0 to 15, all different within a row; in each aligned block of 256 rows (0 to 255, 256 to 511, ...) at most 192 rows name the same one
- segments: int32 [2048], replicated, may hold values from 0 to 2, as said below
Outputs:
- block_out: bfloat16 [2048, 2048], P('expert')
- tokens_grad: bfloat16 [2048, 2048], P('expert')
- grad_w_qkv: float32 [3, 2048, 2048], P(None, 'expert', 'tensor')
- grad_w_attn_out: float32 [2048, 2048], P('tensor', 'expert')
- grad_attn_gain: float32 [2048], P('expert')
- grad_ffn_gain: float32 [2048], P('expert')
- grad_qk_gain: float32 [2, 16, 128], P(None, 'tensor', 'expert')
- grad_w_router: float32 [2048, 16], P('expert')
- grad_w_gate: float32 [16, 2048, 1024], P('expert', None, 'tensor')
- grad_w_up: float32 [16, 2048, 1024], P('expert', None, 'tensor')
- grad_w_down: float32 [16, 1024, 2048], P('expert', 'tensor')
Inputs may be any that keep to these rules, and one draw needn't show every extreme that they name: `routes`: each row names 8 different experts; among the 256 rows of one device no expert is named more than 192 times, and in every draw some device's rows name some expert exactly 192 times. `segments`: document numbers never fall; every sequence of 2048 tokens holds exactly three documents, the first beginning at its first token, the second within its first 128 tokens and the third within its last 128 tokens.
All inputs are finite; a program needn't handle non-finite values.
Results may differ from a plain program's by a relative error of at most 0.03.
Values may be sent and summed in bfloat16 or wider, within the bound.
A program may use at most 256 MiB of HBM per device.

v0:
```python
import jax
import jax.numpy as jnp
from jax import lax
from jax.sharding import PartitionSpec as P

HEAD = 128
WINDOW = 1024
SEQ = 2048


EPS = 1e-05
THETA = 10000.0


def from_behind(value, axis, steps):
    count = lax.axis_size(axis)
    initial, last = (max(0, -steps), min(count, count - steps))
    return lax.ppermute(value, axis, [(source, source + steps) for source in range(initial, last)])


def angles(position, head_size):
    half_size = head_size // 2
    frequency = THETA ** (-(jnp.arange(half_size, dtype=jnp.float32) * 2.0 / head_size))
    phase_angle = position.astype(jnp.float32)[:, None] * frequency[None, :]
    return (jnp.cos(phase_angle)[:, None, :], jnp.sin(phase_angle)[:, None, :])


def rotate(rotated_in, cosine_table, sine_table):
    half_size = rotated_in.shape[-1] // 2
    first_half = rotated_in[..., :half_size]
    second_half = rotated_in[..., half_size:]
    return jnp.concatenate(
        [
            first_half * cosine_table - second_half * sine_table,
            second_half * cosine_table + first_half * sine_table,
        ],
        axis=-1,
    )


def slot_layout(block_routes, experts, capacity):
    flat_routes = block_routes.reshape(-1)
    onehot = (flat_routes[:, None] == jnp.arange(experts, dtype=jnp.int32)[None, :]).astype(
        jnp.int32
    )
    before = jnp.cumsum(onehot, axis=0) - onehot
    rank_within = jnp.sum(before * onehot, axis=1)
    slot_index = flat_routes * capacity + rank_within
    slot_table = (
        jnp.zeros((experts * capacity,), jnp.int32)
        .at[slot_index]
        .set(jnp.arange(flat_routes.shape[0], dtype=jnp.int32) + 1)
    )
    return (slot_index, slot_table)


def shards(
    tokens_in,
    out_grad,
    w_qkv,
    w_attn_out,
    attn_gain,
    ffn_gain,
    qk_gain,
    w_router,
    w_gate,
    w_up,
    w_down,
    routes,
    segments,
):
    row_count, model_width = tokens_in.shape
    experts = w_router.shape[1]
    per_token = routes.shape[1]
    local_experts = w_gate.shape[0]
    heads_here = qk_gain.shape[1]
    local_width = heads_here * HEAD
    groups = lax.axis_size("expert")
    device = lax.axis_index("expert")
    capacity = row_count * per_token * 3 // (2 * experts)
    hop_count = WINDOW // row_count
    buffer_shape = (groups, local_experts, capacity, model_width)
    score_scale = HEAD ** (-0.5)

    def fetch_weights():
        return (
            lax.all_gather(w_qkv.astype(jnp.bfloat16), "expert", axis=1, tiled=True),
            lax.all_gather(w_attn_out.astype(jnp.bfloat16), "expert", axis=1, tiled=True),
            lax.all_gather(w_router.astype(jnp.bfloat16), "expert", axis=0, tiled=True),
            lax.all_gather(attn_gain.astype(jnp.bfloat16), "expert", axis=0, tiled=True),
            lax.all_gather(ffn_gain.astype(jnp.bfloat16), "expert", axis=0, tiled=True),
            lax.all_gather(qk_gain.astype(jnp.bfloat16), "expert", axis=2, tiled=True),
        )

    def prepare(pieces):
        return (
            pieces[0],
            pieces[1],
            pieces[2],
            pieces[3].astype(jnp.float32),
            pieces[4].astype(jnp.float32),
            pieces[5].astype(jnp.float32).reshape(2, local_width),
        )

    qkv_low, out_low, router_low, gain_one_f, gain_two_f, qk_gains = prepare(fetch_weights())
    tokens_f = tokens_in.astype(jnp.float32)
    scale_one = lax.rsqrt(jnp.mean(tokens_f * tokens_f, axis=-1, keepdims=True) + EPS)
    hidden_one = (tokens_f * scale_one * gain_one_f).astype(jnp.bfloat16)
    projected = jnp.einsum("td,jde->jte", hidden_one, qkv_low, preferred_element_type=jnp.float32)
    query_raw = projected[0]
    key_raw = projected[1]
    query_sq, key_sq = lax.psum(
        (jnp.sum(query_raw * query_raw, axis=-1), jnp.sum(key_raw * key_raw, axis=-1)), "tensor"
    )
    query_scale = lax.rsqrt(query_sq / model_width + EPS)[:, None]
    key_scale = lax.rsqrt(key_sq / model_width + EPS)[:, None]
    normed_query = query_raw * query_scale
    normed_key = key_raw * key_scale
    global_rows = device * row_count + jnp.arange(row_count, dtype=jnp.int32)
    cosine_table, sine_table = angles(global_rows % SEQ, HEAD)
    query_low = rotate(
        (normed_query * qk_gains[0]).reshape(row_count, heads_here, HEAD), cosine_table, sine_table
    ).astype(jnp.bfloat16)
    key_low = rotate(
        (normed_key * qk_gains[1]).reshape(row_count, heads_here, HEAD), cosine_table, sine_table
    ).astype(jnp.bfloat16)
    value_low = projected[2].astype(jnp.bfloat16).reshape(row_count, heads_here, HEAD)
    own_pair = jnp.stack([key_low, value_low])
    earlier = []
    for steps_back in range(hop_count, 0, -1):
        earlier.append(from_behind(own_pair, "expert", steps_back))
    context = jnp.concatenate(earlier + [own_pair], axis=1)
    key_rows = (device - hop_count) * row_count + jnp.arange(
        (hop_count + 1) * row_count, dtype=jnp.int32
    )
    segment_keys = segments[jnp.maximum(key_rows, 0)]
    segment_query = segments[global_rows]
    distance = global_rows[:, None] - key_rows[None, :]
    allowed = (
        (key_rows[None, :] >= 0)
        & (segment_query[:, None] == segment_keys[None, :])
        & (distance >= 0)
        & (distance < WINDOW)
    )

    def score_block():
        raw_scores = (
            jnp.einsum("qhd,khd->hqk", query_low, context[0], preferred_element_type=jnp.float32)
            * score_scale
        )
        return jnp.where(allowed[None], raw_scores, -1e30)

    scores = score_block()
    largest = jnp.max(scores, axis=-1, keepdims=True)
    exp_scores = jnp.exp(scores - largest)
    exp_total = jnp.sum(exp_scores, axis=-1, keepdims=True)
    log_total = largest + jnp.log(exp_total)
    attn_probs = (exp_scores / exp_total).astype(jnp.bfloat16)
    attended = (
        jnp.einsum("hqk,khd->qhd", attn_probs, context[1], preferred_element_type=jnp.float32)
        .reshape(row_count, local_width)
        .astype(jnp.bfloat16)
    )
    attention_out = lax.psum(
        jnp.dot(attended, out_low, preferred_element_type=jnp.float32).astype(jnp.bfloat16),
        "tensor",
    ).astype(jnp.float32)
    residual = tokens_f + attention_out
    scale_two = lax.rsqrt(jnp.mean(residual * residual, axis=-1, keepdims=True) + EPS)
    normed_two = residual * scale_two
    hidden_two = (normed_two * gain_two_f).astype(jnp.bfloat16)
    logits = jnp.dot(hidden_two, router_low, preferred_element_type=jnp.float32)
    logit_exp = jnp.exp(logits - jnp.max(logits, axis=-1, keepdims=True))
    router_probs = logit_exp / jnp.sum(logit_exp, axis=-1, keepdims=True)
    chosen = routes[:, :, None] == jnp.arange(experts, dtype=jnp.int32)[None, None, :]
    gate_probs = jnp.sum(jnp.where(chosen, router_probs[:, None, :], 0.0), axis=-1)
    slot_index, slot_table = slot_layout(routes, experts, capacity)
    present = (slot_table > 0)[:, None]
    assigned = jnp.maximum(slot_table - 1, 0)
    row_of_slot = assigned // per_token
    gate_low = w_gate.astype(jnp.bfloat16)
    up_low = w_up.astype(jnp.bfloat16)
    down_low = w_down.astype(jnp.bfloat16)

    def send_rows():
        buffer_rows = jnp.where(
            present, hidden_two[row_of_slot], jnp.zeros((), jnp.bfloat16)
        ).reshape(buffer_shape)
        return lax.all_to_all(buffer_rows, "expert", split_axis=0, concat_axis=0, tiled=True)

    def expert_front(arrived):
        gate_pre = jnp.einsum(
            "secd,edh->sech", arrived, gate_low, preferred_element_type=jnp.float32
        )
        up_pre = jnp.einsum("secd,edh->sech", arrived, up_low, preferred_element_type=jnp.float32)
        return (gate_pre, up_pre)

    received = send_rows()
    gate_pre, up_pre = expert_front(received)
    activated = (gate_pre * jax.nn.sigmoid(gate_pre) * up_pre).astype(jnp.bfloat16)
    partial_value = jnp.einsum(
        "sech,ehd->secd", activated, down_low, preferred_element_type=jnp.float32
    ).astype(jnp.bfloat16)
    returned = lax.all_to_all(
        partial_value, "expert", split_axis=0, concat_axis=0, tiled=True
    ).reshape(experts * capacity, model_width)
    expert_rows = returned[slot_index].reshape(row_count, per_token, model_width)
    expert_part = jnp.einsum(
        "tk,tkd->td", gate_probs, expert_rows, preferred_element_type=jnp.float32
    )
    block_out = residual + lax.psum(expert_part.astype(jnp.bfloat16), "tensor").astype(jnp.float32)
    qkv_low, out_low, router_low, gain_one_f, gain_two_f, qk_gains = prepare(fetch_weights())
    grad_out = out_grad.astype(jnp.float32)
    grad_gate_part = jnp.einsum(
        "td,tkd->tk", grad_out, expert_rows, preferred_element_type=jnp.float32
    )
    slot_grads = (
        (gate_probs[:, :, None] * grad_out[:, None, :])
        .astype(jnp.bfloat16)
        .reshape(row_count * per_token, model_width)
    )
    grad_buffer = jnp.where(present, slot_grads[assigned], jnp.zeros((), jnp.bfloat16)).reshape(
        buffer_shape
    )
    grad_received = lax.all_to_all(grad_buffer, "expert", split_axis=0, concat_axis=0, tiled=True)
    received = send_rows()
    gate_pre, up_pre = expert_front(received)
    sigmoid_gate = jax.nn.sigmoid(gate_pre)
    swish_gate = gate_pre * sigmoid_gate
    activated = (swish_gate * up_pre).astype(jnp.bfloat16)
    grad_act = jnp.einsum(
        "secd,ehd->sech", grad_received, down_low, preferred_element_type=jnp.float32
    )
    grad_down = jnp.einsum(
        "sech,secd->ehd", activated, grad_received, preferred_element_type=jnp.float32
    )
    grad_gate_pre = (
        grad_act * up_pre * sigmoid_gate * (1.0 + gate_pre * (1.0 - sigmoid_gate))
    ).astype(jnp.bfloat16)
    grad_up_pre = (grad_act * swish_gate).astype(jnp.bfloat16)
    grad_gate_w = jnp.einsum(
        "secd,sech->edh", received, grad_gate_pre, preferred_element_type=jnp.float32
    )
    grad_up_w = jnp.einsum(
        "secd,sech->edh", received, grad_up_pre, preferred_element_type=jnp.float32
    )
    grad_rows = (
        jnp.einsum("sech,edh->secd", grad_gate_pre, gate_low, preferred_element_type=jnp.float32)
        + jnp.einsum("sech,edh->secd", grad_up_pre, up_low, preferred_element_type=jnp.float32)
    ).astype(jnp.bfloat16)
    grad_back = lax.all_to_all(
        grad_rows, "expert", split_axis=0, concat_axis=0, tiled=True
    ).reshape(experts * capacity, model_width)
    grad_hidden_part = jnp.sum(
        grad_back[slot_index].reshape(row_count, per_token, model_width), axis=1, dtype=jnp.float32
    )
    grad_hidden_sum, grad_gates = (
        lax.psum(grad_hidden_part.astype(jnp.bfloat16), "tensor").astype(jnp.float32),
        lax.psum(grad_gate_part.astype(jnp.bfloat16), "tensor").astype(jnp.float32),
    )
    grad_probs = jnp.sum(jnp.where(chosen, grad_gates[:, :, None], 0.0), axis=1)
    grad_logits = (
        router_probs * (grad_probs - jnp.sum(router_probs * grad_probs, axis=-1, keepdims=True))
    ).astype(jnp.bfloat16)
    grad_hidden_two = grad_hidden_sum + jnp.dot(
        grad_logits, router_low.T, preferred_element_type=jnp.float32
    )
    grad_router = jnp.dot(hidden_two.T, grad_logits, preferred_element_type=jnp.float32)
    grad_gain_two = jnp.sum(grad_hidden_two * normed_two, axis=0)
    scaled_two = grad_hidden_two * gain_two_f
    grad_residual = (
        grad_out
        + scale_two * scaled_two
        - residual
        * (scale_two * scale_two * scale_two)
        * jnp.mean(scaled_two * residual, axis=-1, keepdims=True)
    )
    grad_attn = grad_residual.astype(jnp.bfloat16)
    grad_out_w = jnp.dot(attended.T, grad_attn, preferred_element_type=jnp.float32)
    grad_attended = (
        jnp.dot(grad_attn, out_low.T, preferred_element_type=jnp.float32)
        .astype(jnp.bfloat16)
        .reshape(row_count, heads_here, HEAD)
    )
    attn_weights = jnp.where(allowed[None], jnp.exp(score_block() - log_total), 0.0)
    grad_weights = jnp.einsum(
        "qhd,khd->hqk", grad_attended, context[1], preferred_element_type=jnp.float32
    )
    inner_sum = jnp.sum(attn_weights * grad_weights, axis=-1, keepdims=True)
    grad_scores = (attn_weights * (grad_weights - inner_sum) * score_scale).astype(jnp.bfloat16)
    grad_query = jnp.einsum(
        "hqk,khd->qhd", grad_scores, context[0], preferred_element_type=jnp.float32
    )
    grad_keys = jnp.einsum(
        "hqk,qhd->khd", grad_scores, query_low, preferred_element_type=jnp.float32
    )
    grad_values = jnp.einsum(
        "hqk,qhd->khd",
        attn_weights.astype(jnp.bfloat16),
        grad_attended,
        preferred_element_type=jnp.float32,
    )
    grad_pair = jnp.stack([grad_keys, grad_values]).reshape(
        2, hop_count + 1, row_count, heads_here, HEAD
    )
    own_grad = grad_pair[:, hop_count]
    for steps_back in range(1, hop_count + 1):
        own_grad = own_grad + from_behind(
            grad_pair[:, hop_count - steps_back].astype(jnp.bfloat16), "expert", -steps_back
        ).astype(jnp.float32)
    grad_query_norm = rotate(grad_query, cosine_table, -sine_table).reshape(row_count, local_width)
    grad_key_norm = rotate(own_grad[0], cosine_table, -sine_table).reshape(row_count, local_width)
    grad_gain_query = jnp.sum(grad_query_norm * normed_query, axis=0)
    grad_gain_key = jnp.sum(grad_key_norm * normed_key, axis=0)
    scaled_query = grad_query_norm * qk_gains[0]
    scaled_key = grad_key_norm * qk_gains[1]
    query_inner, key_inner = lax.psum(
        (jnp.sum(scaled_query * query_raw, axis=-1), jnp.sum(scaled_key * key_raw, axis=-1)),
        "tensor",
    )
    grad_query_raw = (
        query_scale * scaled_query
        - query_raw * (query_scale * query_scale * query_scale) * query_inner[:, None] / model_width
    ).astype(jnp.bfloat16)
    grad_key_raw = (
        key_scale * scaled_key
        - key_raw * (key_scale * key_scale * key_scale) * key_inner[:, None] / model_width
    ).astype(jnp.bfloat16)
    grad_value_raw = own_grad[1].reshape(row_count, local_width).astype(jnp.bfloat16)
    grad_proj = jnp.stack([grad_query_raw, grad_key_raw, grad_value_raw])
    grad_qkv = jnp.einsum("td,jte->jde", hidden_one, grad_proj, preferred_element_type=jnp.float32)
    grad_hidden_one = lax.psum(
        jnp.einsum("jte,jde->td", grad_proj, qkv_low, preferred_element_type=jnp.float32).astype(
            jnp.bfloat16
        ),
        "tensor",
    ).astype(jnp.float32)
    grad_gain_one = jnp.sum(grad_hidden_one * tokens_f * scale_one, axis=0)
    scaled_one = grad_hidden_one * gain_one_f
    grad_tokens = (
        grad_residual
        + scale_one * scaled_one
        - tokens_f
        * (scale_one * scale_one * scale_one)
        * jnp.mean(scaled_one * tokens_f, axis=-1, keepdims=True)
    )
    grad_qk = jnp.stack([grad_gain_query, grad_gain_key]).reshape(2, heads_here, HEAD)
    reduced = (
        lax.psum_scatter(
            grad_qkv.astype(jnp.bfloat16), "expert", scatter_dimension=1, tiled=True
        ).astype(jnp.float32),
        lax.psum_scatter(
            grad_out_w.astype(jnp.bfloat16), "expert", scatter_dimension=1, tiled=True
        ).astype(jnp.float32),
        lax.psum_scatter(
            grad_router.astype(jnp.bfloat16), "expert", scatter_dimension=0, tiled=True
        ).astype(jnp.float32),
        lax.psum_scatter(
            grad_gain_one.astype(jnp.bfloat16), "expert", scatter_dimension=0, tiled=True
        ).astype(jnp.float32),
        lax.psum_scatter(
            grad_gain_two.astype(jnp.bfloat16), "expert", scatter_dimension=0, tiled=True
        ).astype(jnp.float32),
        lax.psum_scatter(
            grad_qk.astype(jnp.bfloat16), "expert", scatter_dimension=2, tiled=True
        ).astype(jnp.float32),
    )
    return (
        block_out.astype(jnp.bfloat16),
        grad_tokens.astype(jnp.bfloat16),
        reduced[0],
        reduced[1],
        reduced[3],
        reduced[4],
        reduced[5],
        reduced[2],
        grad_gate_w,
        grad_up_w,
        grad_down,
    )


def solution(mesh):
    placed = (
        P("expert", None),
        P("expert", None),
        P(None, "expert", "tensor"),
        P("tensor", "expert"),
        P("expert"),
        P("expert"),
        P(None, "tensor", "expert"),
        P("expert", None),
        P("expert", None, "tensor"),
        P("expert", None, "tensor"),
        P("expert", "tensor", None),
        P("expert", None),
        P(),
    )
    return jax.shard_map(
        shards,
        mesh=mesh,
        in_specs=placed,
        out_specs=(
            P("expert", None),
            P("expert", None),
            P(None, "expert", "tensor"),
            P("tensor", "expert"),
            P("expert"),
            P("expert"),
            P(None, "tensor", "expert"),
            P("expert", None),
            P("expert", None, "tensor"),
            P("expert", None, "tensor"),
            P("expert", "tensor", None),
        ),
        check_vma=False,
    )
```

profile of v0, /device:TPU:0, one launch (start us, length us, event | category | flops | bytes accessed | tf_op | source)
XLA Modules:
  0.0 2116.8 jit_solution(13573714360899573489)
XLA Ops:
  12.2 22.5 %all-gather = bf16[8,1,256]{2,1,0:T(2,128)(2,1)S(1)} all-gather(bf16[1,1,256]{2,1,0:T(2,128)(2,1)S(1)} %reshape.694), channel_id=1, replica_groups=mesh['expert'=8,'tensor'=4] {'expert'}, dimensions={0}, use_global_device_ids=true | all-gather | bytes 4608 | tf_op jit(solution)/shard_map/all_gather | solution.py:90
  43.5 31.0 %all_gather.26 = bf16[2,4,128]{1,0,2:T(2,128)(2,1)S(1)} all-gather(bf16[2,4,16]{1,0,2:T(2,128)(2,1)S(1)} %copy.184), channel_id=1, replica_groups=mesh['expert'=8,'tensor'=4] {'expert'}, dimensions={2}, use_global_device_ids=true | all-gather | bytes 2304 | tf_op jit(solution)/shard_map/all_gather | solution.py:92
  82.3 30.9 %all-gather.5.cloned.1.call-done = bf16[3,2048,512]{2,1,0:T(8,128)(2,1)} async-done(((bf16[3,256,512]{2,1,0:T(8,128)(2,1)}), bf16[3,2048,512]{2,1,0:T(8,128)(2,1)}) %all-gather.5.cloned.1.call-update) | async-done | bytes 6291472 | tf_op jit(solution)/shard_map/all_gather | solution.py:87
  139.6 65.3 %all-gather.1 = bf16[8,1,256]{2,1,0:T(2,128)(2,1)S(1)} all-gather(bf16[1,1,256]{2,1,0:T(2,128)(2,1)S(1)} %reshape.696), channel_id=1, replica_groups=mesh['expert'=8,'tensor'=4] {'expert'}, dimensions={0}, use_global_device_ids=true | all-gather | bytes 4608 | tf_op jit(solution)/shard_map/all_gather | solution.py:91
  222.6 51.2 %all-reduce.10.cloned.1.call-done = bf16[256,2048]{1,0:T(8,128)(2,1)} async-done(((bf16[256,2048]{1,0:T(8,128)(2,1)}), bf16[256,2048]{1,0:T(8,128)(2,1)}) %all-reduce.10.cloned.1.call-update) | async-done | bytes 1048592 | tf_op jit(solution)/shard_map/psum | solution.py:164
  277.8 15.9 gather_fusion.2
  300.2 278.9 %all_to_all.21 = bf16[8,2,192,2048]{3,2,1,0:T(8,128)(2,1)} all-to-all(bf16[8,2,192,2048]{3,2,1,0:T(8,128)(2,1)S(1)} %broadcast_select_fusion.1), channel_id=1, replica_groups=mesh['expert'=8,'tensor'=4] {'expert'}, dimensions={0} | all-to-all | bytes 25165824 | tf_op jit(solution)/shard_map/all_to_all | solution.py:189
  588.9 12.3 fusion.36
  610.2 10.7 copy.195
  627.9 290.4 %all_gather.29 = bf16[2048,16]{0,1:T(8,128)(2,1)S(1)} all-gather(bf16[256,16]{0,1:T(8,128)(2,1)S(1)} %convert_element_type.282), channel_id=1, replica_groups=mesh['expert'=8,'tensor'=4] {'expert'}, dimensions={0}, use_global_device_ids=true | all-gather | bytes 73728 | tf_op jit(solution)/shard_map/all_gather | solution.py:89
  918.8 22.5 %gather_fusion.3 = bf16[2048,2048]{1,0:T(8,128)(2,1)} fusion(bf16[3072,2048]{1,0:T(8,128)(2,1)} %bitcast.29, s32[2048]{0:T(1024)S(1)} %broadcast_clamp_fusion), kind=kCustom, calls=%fused_computation.3 | custom fusion | bytes 16785408 | tf_op jit(solution)/shard_map/gather | solution.py:207
  960.5 28.3 %gather_fusion.4 = bf16[3072,2048]{1,0:T(8,128)(2,1)} fusion(bf16[2048,2048]{1,0:T(8,128)(2,1)} %fusion.1, s32[3072]{0:T(1024)S(1)} %get-tuple-element.123), kind=kCustom, calls=%fused_computation.4 | custom fusion | bytes 25178112 | tf_op jit(solution)/shard_map/gather | solution.py:222
  995.2 277.2 %all_to_all.22 = bf16[8,2,192,2048]{3,2,1,0:T(8,128)(2,1)} all-to-all(bf16[8,2,192,2048]{3,2,1,0:T(8,128)(2,1)S(1)} %broadcast_select_fusion), channel_id=1, replica_groups=mesh['expert'=8,'tensor'=4] {'expert'}, dimensions={0} | all-to-all | bytes 25165824 | tf_op jit(solution)/shard_map/all_to_all | solution.py:225
  1272.3 13.5 fusion.35
  1285.8 12.9 fusion.74
  1298.8 16.6 fusion.2
  1315.4 10.7 copy.198
  1332.0 271.7 %all-to-all-done.3 = bf16[8,2,192,2048]{3,2,1,0:T(8,128)(2,1)} async-done(((bf16[8,2,192,2048]{3,2,1,0:T(8,128)(2,1)}), bf16[8,2,192,2048]{3,2,1,0:T(8,128)(2,1)}, u32[]{:S(2)}, u32[]{:S(2)}) %all-to-all-start.3) | async-done | bytes 12582944 | tf_op jit(solution)/shard_map/all_to_all | solution.py:251
  1603.7 22.5 %gather_fusion.5 = bf16[2048,2048]{1,0:T(8,128)(2,1)} fusion(bf16[3072,2048]{1,0:T(8,128)(2,1)} %bitcast.39, s32[2048]{0:T(1024)S(1)} %broadcast_clamp_fusion), kind=kCustom, calls=%fused_computation.5 | custom fusion | bytes 16785408 | tf_op jit(solution)/shard_map/gather | solution.py:255
  1626.2 11.2 bitcast_reduce_fusion
  1638.8 33.1 %all-reduce.12.cloned.1.call-done = bf16[256,2048]{1,0:T(8,128)(2,1)} async-done(((bf16[256,2048]{1,0:T(8,128)(2,1)}), bf16[256,2048]{1,0:T(8,128)(2,1)}) %all-reduce.12.cloned.1.call-update) | async-done | bytes 1048592 | tf_op jit(solution)/shard_map/psum | solution.py:258
  1690.4 16.1 fusion.26
  1726.0 11.5 fusion.84
  1739.7 26.3 %collective-permute-done.7 = bf16[2,256,4,128]{3,1,2,0:T(8,128)(2,1)} collective-permute-done((bf16[2,256,4,128]{3,1,2,0:T(8,128)(2,1)}, bf16[2,256,4,128]{3,1,2,0:T(8,128)(2,1)}, u32[]{:S(2)}, u32[]{:S(2)}) %collective-permute-start.7) | collective-permute-done | bytes 524320 | tf_op jit(solution)/shard_map/ppermute | solution.py:18
  1806.4 10.5 fusion.29
  1816.9 12.0 convolution_bitcast_fusion
  1828.9 12.3 convolution_bitcast_fusion.1
  1841.2 19.1 reduce-scatter.13.cloned.1.call-done
  1861.7 52.2 %all-reduce.14.cloned.1.call-done = (bf16[256,2048]{1,0:T(8,128)(2,1)}, bf16[256,2048]{1,0:T(8,128)(2,1)}) async-done(((bf16[256,2048]{1,0:T(8,128)(2,1)}, bf16[256,2048]{1,0:T(8,128)(2,1)}), (bf16[256,2048]{1,0:T(8,128)(2,1)}, bf16[256,2048]{1,0:T(8,128)(2,1)})) %all-reduce.14.cloned.1.call-update) | async-done | bytes 2097168 | tf_op jit(solution)/shard_map/psum | solution.py:211
  1915.8 22.0 %all-reduce.4 = (bf16[2048]{0:T(1024)(128)(2,1)S(1)}, bf16[2048]{0:T(1024)(128)(2,1)S(1)}) all-reduce(bf16[2048]{0:T(1024)(128)(2,1)S(1)} %get-tuple-element.79, bf16[2048]{0:T(1024)(128)(2,1)S(1)} %get-tuple-element.77), channel_id=4, replica_groups=mesh['expert'=8,'tensor'=4] {'expert'}, use_global_device_ids=true, to_apply=%region_33.34.clone | all-reduce | flops 4096 | bytes 16384
  1943.8 42.3 %reduce-scatter.9.cloned.1.call-done = bf16[512,256]{1,0:T(8,128)(2,1)} async-done(((bf16[512,2048]{1,0:T(8,128)(2,1)}), bf16[512,256]{1,0:T(8,128)(2,1)}) %reduce-scatter.9.cloned.1.call-update) | async-done | bytes 262160 | tf_op jit(solution)/shard_map/reduce_scatter | solution.py:352
  1987.8 119.7 %reduce-scatter.7.cloned.1.call-done = bf16[3,256,512]{1,2,0:T(8,128)(2,1)} async-done(((bf16[3,2048,512]{1,2,0:T(8,128)(2,1)}), bf16[3,256,512]{1,2,0:T(8,128)(2,1)}) %reduce-scatter.7.cloned.1.call-update) | async-done | bytes 786448 | tf_op jit(solution)/shard_map/reduce_scatter | solution.py:349
  (296 shorter events, 227.7 us)
Async XLA Ops:
  7.2 106.0 %all-gather.5.cloned.1.call-start = ((), (), s32[]{:S(2)}) async-start(), calls=%async_computation.8 | async-start | bytes 7077888 | tf_op jit(solution)/shard_map/all_gather | solution.py:87
  9.8 201.2 %all-gather.7.cloned.1.call-start = ((), (), s32[]{:S(2)}) async-start(), calls=%async_computation.9 | async-start | bytes 2359296 | tf_op jit(solution)/shard_map/all_gather | solution.py:88
  10.6 263.2 %all-reduce.10.cloned.1.call-start = ((), (), s32[]{:S(2)}) async-start(), calls=%async_computation.10 | async-start | bytes 2097152 | tf_op jit(solution)/shard_map/psum | solution.py:164
  12.1 101.2 %copy-start.44 = (f32[256]{0:T(256)}, f32[256]{0:T(256)S(1)}, u32[]{:S(2)}) copy-start(f32[256]{0:T(256)S(1)} %get-tuple-element.129) | copy-start | bytes 3076
  34.7 78.6 %copy-start.37 = (f32[8,1,256]{2,1,0:T(1,128)}, f32[8,1,256]{2,1,0:T(1,128)S(1)}, u32[]{:S(2)}) copy-start(f32[8,1,256]{2,1,0:T(1,128)S(1)} %convert_element_type.334) | copy-start | bytes 24580
  82.3 123.1 %copy-start.15 = (pred[256,1280]{1,0:T(8,128)(4,1)}, pred[256,1280]{1,0:T(8,128)(4,1)S(1)}, u32[]{:S(2)}) copy-start(pred[256,1280]{1,0:T(8,128)(4,1)S(1)} %fusion.83) | copy-start | bytes 983044
  127.9 77.6 %copy-start.24 = (bf16[256,4,64]{2,0,1:T(8,128)(2,1)}, bf16[256,4,64]{2,0,1:T(8,128)(2,1)S(1)}, u32[]{:S(2)}) copy-start(bf16[256,4,64]{2,0,1:T(8,128)(2,1)S(1)} %get-tuple-element.113) | copy-start | bytes 393220
  127.9 77.6 %copy-start.26 = (bf16[256,4,64]{2,0,1:T(8,128)(2,1)}, bf16[256,4,64]{2,0,1:T(8,128)(2,1)S(1)}, u32[]{:S(2)}) copy-start(bf16[256,4,64]{2,0,1:T(8,128)(2,1)S(1)} %get-tuple-element.114) | copy-start | bytes 393220
  128.1 76.8 %collective-permute-start = (bf16[2,256,4,128]{3,1,2,0:T(8,128)(2,1)S(1)}, bf16[2,256,4,128]{3,1,2,0:T(8,128)(2,1)S(1)}, u32[]{:S(2)}, u32[]{:S(2)}) collective-permute-start(bf16[2,256,4,128]{3,1,2,0:T(8,128)(2,1)S(1)} %pad_maximum_fusion.2), channel_id=1, source_target_pairs={{0,16},{4,20},{8,24},{12,28},{1,17},{5,21},{9,25},{13,29},{2,18},{... | collective-permute-start | bytes 1572872 | tf_op jit(solution)/shard_map/ppermute | solution.py:18
  131.7 73.4 %collective-permute-start.3 = (bf16[2,256,4,128]{3,1,2,0:T(8,128)(2,1)S(1)}, bf16[2,256,4,128]{3,1,2,0:T(8,128)(2,1)S(1)}, u32[]{:S(2)}, u32[]{:S(2)}) collective-permute-start(bf16[2,256,4,128]{3,1,2,0:T(8,128)(2,1)S(1)} %pad_maximum_fusion.2), channel_id=1, source_target_pairs={{0,4},{4,8},{8,12},{12,16},{16,20},{20,24},{24,28},{1,5},{5,9},{9,... | collective-permute-start | bytes 1572872 | tf_op jit(solution)/shard_map/ppermute | solution.py:18
  134.4 70.6 %collective-permute-start.2 = (bf16[2,256,4,128]{3,1,2,0:T(8,128)(2,1)S(1)}, bf16[2,256,4,128]{3,1,2,0:T(8,128)(2,1)S(1)}, u32[]{:S(2)}, u32[]{:S(2)}) collective-permute-start(bf16[2,256,4,128]{3,1,2,0:T(8,128)(2,1)S(1)} %pad_maximum_fusion.2), channel_id=1, source_target_pairs={{0,8},{4,12},{8,16},{12,20},{16,24},{20,28},{1,9},{5,13},{9,17},{1... | collective-permute-start | bytes 1572872 | tf_op jit(solution)/shard_map/ppermute | solution.py:18
  137.4 67.6 %collective-permute-start.1 = (bf16[2,256,4,128]{3,1,2,0:T(8,128)(2,1)S(1)}, bf16[2,256,4,128]{3,1,2,0:T(8,128)(2,1)S(1)}, u32[]{:S(2)}, u32[]{:S(2)}) collective-permute-start(bf16[2,256,4,128]{3,1,2,0:T(8,128)(2,1)S(1)} %pad_maximum_fusion.2), channel_id=1, source_target_pairs={{0,12},{4,16},{8,20},{12,24},{16,28},{1,13},{5,17},{9,21},{13,25},... | collective-permute-start | bytes 1572872 | tf_op jit(solution)/shard_map/ppermute | solution.py:18
  204.9 71.2 %copy-start.34 = (f32[8,1,256]{2,1,0:T(1,128)}, f32[8,1,256]{2,1,0:T(1,128)S(1)}, u32[]{:S(2)}) copy-start(f32[8,1,256]{2,1,0:T(1,128)S(1)} %convert_element_type.335) | copy-start | bytes 24580
  211.0 64.5 %copy-start.22 = (bf16[4,128,256]{2,1,0:T(8,128)(2,1)}, bf16[4,128,256]{2,1,0:T(8,128)(2,1)S(1)}, u32[]{:S(2)}) copy-start(bf16[4,128,256]{2,1,0:T(8,128)(2,1)S(1)} %fusion.87) | copy-start | bytes 786436
  300.1 279.0 %copy-start.12 = (f32[2,2048,256]{2,1,0:T(8,128)S(1)}, f32[2,2048,256]{2,1,0:T(8,128)}, u32[]{:S(2)}) copy-start(f32[2,2048,256]{2,1,0:T(8,128)} %param.21) | copy-start | bytes 12582916
  620.9 297.8 %all-to-all-start.1 = ((bf16[8,2,192,2048]{3,2,1,0:T(8,128)(2,1)}), bf16[8,2,192,2048]{3,2,1,0:T(8,128)(2,1)}, u32[]{:S(2)}, u32[]{:S(2)}) async-start(bf16[8,2,192,2048]{3,2,1,0:T(8,128)(2,1)} %copy.195), calls=%async_computation.1 | async-start | bytes 25165824 | tf_op jit(solution)/shard_map/all_to_all | solution.py:204
  1326.1 277.6 %all-to-all-start.3 = ((bf16[8,2,192,2048]{3,2,1,0:T(8,128)(2,1)}), bf16[8,2,192,2048]{3,2,1,0:T(8,128)(2,1)}, u32[]{:S(2)}, u32[]{:S(2)}) async-start(bf16[8,2,192,2048]{3,2,1,0:T(8,128)(2,1)} %copy.198), calls=%async_computation.3 | async-start | bytes 25165824 | tf_op jit(solution)/shard_map/all_to_all | solution.py:251
  1331.6 340.4 %all-reduce.12.cloned.1.call-start = ((), (), s32[]{:S(2)}) async-start(), calls=%async_computation.11 | async-start | bytes 2097152 | tf_op jit(solution)/shard_map/psum | solution.py:258
  1626.2 45.8 %copy-start.6 = (bf16[256,2048]{1,0:T(8,128)(2,1)S(1)}, bf16[256,2048]{1,0:T(8,128)(2,1)}, u32[]{:S(2)}) copy-start(bf16[256,2048]{1,0:T(8,128)(2,1)} %all-reduce.10.cloned.1.call-done) | copy-start | bytes 3145732
  1626.2 45.8 %copy-start.35 = (f32[8,1,256]{2,1,0:T(1,128)S(1)}, f32[8,1,256]{2,1,0:T(1,128)}, u32[]{:S(2)}) copy-start(f32[8,1,256]{2,1,0:T(1,128)} %copy-done.34) | copy-start | bytes 24580
  1626.2 45.8 %copy-start.51 = (f32[256]{0:T(256)S(1)}, f32[256]{0:T(256)}, u32[]{:S(2)}) copy-start(f32[256]{0:T(256)} %copy-done.50) | copy-start | bytes 3076
  1637.4 167.7 %reduce-scatter.11.cloned.1.call-start = ((), (), s32[]{:S(2)}) async-start(), calls=%async_computation.14 | async-start | bytes 73728 | tf_op jit(solution)/shard_map/reduce_scatter | solution.py:355
  1638.6 221.7 %reduce-scatter.13.cloned.1.call-start = ((), (), s32[]{:S(2)}) async-start(), calls=%async_computation.15 | async-start | bytes 36864
  1713.1 26.6 %collective-permute-start.4 = (bf16[2,256,4,128]{3,1,2,0:T(8,128)(2,1)}, bf16[2,256,4,128]{3,1,2,0:T(8,128)(2,1)}, u32[]{:S(2)}, u32[]{:S(2)}) collective-permute-start(bf16[2,256,4,128]{3,1,2,0:T(8,128)(2,1)} %get-tuple-element.99), channel_id=1, source_target_pairs={{4,0},{8,4},{12,8},{16,12},{20,16},{24,20},{28,24},{5,1},{9,5},{13... | collective-permute-start | bytes 1572872 | tf_op jit(solution)/shard_map/ppermute | solution.py:18
  1714.4 51.6 %collective-permute-start.7 = (bf16[2,256,4,128]{3,1,2,0:T(8,128)(2,1)}, bf16[2,256,4,128]{3,1,2,0:T(8,128)(2,1)}, u32[]{:S(2)}, u32[]{:S(2)}) collective-permute-start(bf16[2,256,4,128]{3,1,2,0:T(8,128)(2,1)} %get-tuple-element.100), channel_id=1, source_target_pairs={{16,0},{20,4},{24,8},{28,12},{17,1},{21,5},{25,9},{29,13},{18,2},{... | collective-permute-start | bytes 1572872 | tf_op jit(solution)/shard_map/ppermute | solution.py:18
  1715.7 50.3 %collective-permute-start.6 = (bf16[2,256,4,128]{3,1,2,0:T(8,128)(2,1)}, bf16[2,256,4,128]{3,1,2,0:T(8,128)(2,1)}, u32[]{:S(2)}, u32[]{:S(2)}) collective-permute-start(bf16[2,256,4,128]{3,1,2,0:T(8,128)(2,1)} %get-tuple-element.101), channel_id=1, source_target_pairs={{12,0},{16,4},{20,8},{24,12},{28,16},{13,1},{17,5},{21,9},{25,13},... | collective-permute-start | bytes 1572872 | tf_op jit(solution)/shard_map/ppermute | solution.py:18
  1717.0 49.0 %collective-permute-start.5 = (bf16[2,256,4,128]{3,1,2,0:T(8,128)(2,1)S(1)}, bf16[2,256,4,128]{3,1,2,0:T(8,128)(2,1)}, u32[]{:S(2)}, u32[]{:S(2)}) collective-permute-start(bf16[2,256,4,128]{3,1,2,0:T(8,128)(2,1)S(1)} %get-tuple-element.102), channel_id=1, source_target_pairs={{8,0},{12,4},{16,8},{20,12},{24,16},{28,20},{9,1},{13,5},{17,9},{2... | collective-permute-start | bytes 1572872 | tf_op jit(solution)/shard_map/ppermute | solution.py:18
  1788.8 125.1 %all-reduce.14.cloned.1.call-start = ((), (), s32[]{:S(2)}) async-start(), calls=%async_computation.16 | async-start | bytes 4194304 | tf_op jit(solution)/shard_map/psum | solution.py:211
  1794.5 191.5 %reduce-scatter.9.cloned.1.call-start = ((), (), s32[]{:S(2)}) async-start(), calls=%async_computation.13 | async-start | bytes 2359296 | tf_op jit(solution)/shard_map/reduce_scatter | solution.py:352
  1798.3 309.2 %reduce-scatter.7.cloned.1.call-start = ((), (), s32[]{:S(2)}) async-start(), calls=%async_computation.12 | async-start | bytes 7077888 | tf_op jit(solution)/shard_map/reduce_scatter | solution.py:349
  1828.9 110.2 %copy-start.54 = (f32[256]{0:T(256)S(1)}, f32[256]{0:T(256)}, u32[]{:S(2)}) copy-start(f32[256]{0:T(256)} %get-tuple-element.128) | copy-start | bytes 3076
  1939.1 170.9 %copy-start.1 = (s32[2048]{0:T(1024)S(1)}, s32[2048]{0:T(1024)}, u32[]{:S(2)}) copy-start(s32[2048]{0:T(1024)} %param.25) | copy-start | bytes 24580
  (47 other events, 479.8 us)
Sparse Core Ops, SparseCore 0:
  10.8 102.3 all-gather.4
  115.9 68.8 all-gather.6
  214.5 59.2 all-reduce.9
  1637.5 34.3 all-reduce.11
  1674.9 54.6 reduce-scatter.10
  1788.9 71.3 reduce-scatter.12
  1863.3 50.5 all-reduce.13
  1917.9 68.1 reduce-scatter.8
  1990.1 117.3 reduce-scatter.6
where the time goes:
time: 2120 us
  blocking collectives  1000 us (47%)
  waiting for transfers between devices  649 us (31%)
  matrix products  190 us (9%)
  local copies, waits for them, and re-layouts  158 us (7%)
  other arithmetic  70.1 us (3%)
  starting transfers between devices  28.8 us (1%)
    all_gather x1, blocking collectives, fetch_weights(): lax.all_gather(w_router.astype(jnp.bfloat16), 'expert', axis=0, tiled=True)  290 us
    all_to_all x1, blocking collectives, send_rows(): lax.all_to_all(buffer_rows, 'expert', split_axis=0, concat_axis=0, tiled=...  279 us
    all_to_all x1, blocking collectives, shards(): lax.all_to_all(grad_buffer, 'expert', split_axis=0, concat_axis=0, tiled=...  277 us
    all_to_all x1, waiting for transfers between devices, shards(): lax.all_to_all(grad_rows, 'expert', split_axis=0, concat_axis=0, tiled=True)  272 us
    reduce_scatter x1, waiting for transfers between devices, shards(): lax.psum_scatter(grad_qkv.astype(jnp.bfloat16), 'expert', scatter_dimensi...  120 us
    all_gather x1, blocking collectives, fetch_weights(): lax.all_gather(ffn_gain.astype(jnp.bfloat16), 'expert', axis=0, tiled=True)  65.3 us
    psum x1, waiting for transfers between devices, shards(): lax.psum(expert_part.astype(jnp.bfloat16), 'tensor').astype(jnp.float32)  52.2 us
    psum x1, waiting for transfers between devices, shards(): lax.psum(jnp.dot(attended, out_low, preferred_element_type=jnp.float32).a...  51.2 us
  transfers between devices with their start and end apart: 19, of which 10 were waited for; matrix products, arithmetic and copies ran while one was open for 8% of the time, Pallas kernels for 0%

commit v1 on v0

--- a/solution.py
+++ b/solution.py
@@ -1,6 +1,8 @@
 import jax
 import jax.numpy as jnp
 from jax import lax
+from jax.experimental import pallas as pl
+from jax.experimental.pallas import tpu as pltpu
 from jax.sharding import PartitionSpec as P
 
 HEAD = 128
@@ -380,6 +382,1014 @@
     )
 
 
+MESH_ID = pl.DeviceIdType.MESH
+HBM = pl.BlockSpec(memory_space=pl.ANY)
+VMEM = pl.BlockSpec(memory_space=pltpu.VMEM)
+NZ, NY, NX, NC = 4, 2, 2, 2
+GROUPS = NZ * NY
+
+
+def place():
+    e = lax.axis_index("expert")
+    t = lax.axis_index("tensor")
+    return lax.div(e, NY), lax.rem(e, NY), lax.div(t, NC), lax.rem(t, NC)
+
+
+def device(z, y, x, c):
+    return (z * NY + y, x * NC + c)
+
+
+def run_if(condition, body):
+    if condition is None:
+        body()
+    else:
+        pl.when(condition)(body)
+
+
+def greet(partners):
+    barrier = pltpu.get_barrier_semaphore()
+    for target, condition in partners:
+        run_if(
+            condition,
+            lambda target=target: pl.semaphore_signal(
+                barrier, inc=1, device_id=target, device_id_type=MESH_ID
+            ),
+        )
+    count = sum(1 for _, condition in partners if condition is None)
+    for _, condition in partners:
+        if condition is not None:
+            count = count + condition.astype(jnp.int32)
+    pl.semaphore_wait(barrier, count)
+
+
+def remote(source, target_ref, send_sem, recv_sem, target):
+    return pltpu.make_async_remote_copy(
+        src_ref=source,
+        dst_ref=target_ref,
+        send_sem=send_sem,
+        recv_sem=recv_sem,
+        device_id=target,
+        device_id_type=MESH_ID,
+    )
+
+
+def block_rows(block, rows):
+    return pl.ds(pl.multiple_of(block * rows, rows), rows)
+
+
+class LineGather:
+    def __init__(self, streams, sources, views, send_sem, recv_sem):
+        self.z, self.y, self.x, self.c = place()
+        self.streams, self.sources, self.views = streams, sources, views
+        self.send_sem, self.recv_sem = send_sem, recv_sem
+        self.has_up, self.has_down = self.z < NZ - 1, self.z > 0
+        self.pending = []
+
+    def partners(self):
+        z, y, x, c = self.z, self.y, self.x, self.c
+        return [
+            (device(z + 1, y, x, c), z < NZ - 1),
+            (device(z - 1, y, x, c), z > 0),
+            (device(z, 1 - y, x, c), None),
+        ]
+
+    def exists(self, rel):
+        rel = rel % 7
+        if rel == 0:
+            return None
+        return self.z >= rel if rel < 4 else self.z + (rel - 3) < NZ
+
+    def block(self, rel):
+        y = self.y if rel < 7 else 1 - self.y
+        rel = rel % 7
+        z = self.z if rel == 0 else (self.z - rel if rel < 4 else self.z + (rel - 3))
+        return z * NY + y
+
+    def send(self, stream, rel, way):
+        z, y, x, c = self.z, self.y, self.x, self.c
+        block = self.block(rel)
+        there = self.views[stream](block)
+        source = self.sources[stream] if rel == 0 else there
+        if way == 0:
+            target, landing = device(z + 1, y, x, c), (1 if rel == 0 else rel + 1)
+        elif way == 1:
+            target, landing = device(z - 1, y, x, c), (4 if rel == 0 else rel + 1)
+        else:
+            target, landing = device(z, 1 - y, x, c), 7 + rel
+        return remote(
+            source,
+            there,
+            self.send_sem.at[stream, rel, way],
+            self.recv_sem.at[stream, landing],
+            target,
+        )
+
+    def start(self, stream, rel):
+        if rel < 4:
+            run = self.has_up
+            run_if(run, lambda: self.send(stream, rel, 0).start())
+            self.pending.append((stream, rel, 0, run))
+        if rel == 0 or rel >= 4:
+            run = self.has_down
+            run_if(run, lambda: self.send(stream, rel, 1).start())
+            self.pending.append((stream, rel, 1, run))
+        self.send(stream, rel, 2).start()
+        self.pending.append((stream, rel, 2, None))
+
+    def arrive(self, stream, rel):
+        there = self.views[stream](self.block(rel))
+        remote(
+            there,
+            there,
+            self.send_sem.at[stream, 0, 0],
+            self.recv_sem.at[stream, rel],
+            device(self.z, 1 - self.y, self.x, self.c),
+        ).wait_recv()
+
+    def order(self):
+        return [7, 1, 4, 8, 11, 2, 5, 9, 12, 3, 6, 10, 13]
+
+    def run(self, hook=None):
+        for stream in self.streams:
+            self.start(stream, 0)
+        for rel in self.order():
+            def step(rel=rel):
+                marks = len(self.pending)
+                for stream in self.streams:
+                    self.arrive(stream, rel)
+                    if rel < 7:
+                        self.start(stream, rel)
+                    if hook is not None:
+                        hook(stream, rel)
+                if rel < 7:
+                    late = self.pending[marks:]
+                    del self.pending[marks:]
+                    self.finish_later(late, rel)
+            run_if(self.exists(rel), step)
+
+    def finish_later(self, late, rel):
+        self.late = getattr(self, "late", []) + [(rel, late)]
+
+    def finish(self):
+        for stream, rel, way, run in self.pending:
+            run_if(run, lambda s=stream, r=rel, w=way: self.send(s, r, w).wait_send())
+        for rel, late in getattr(self, "late", []):
+            def body(late=late):
+                for stream, rel, way, run in late:
+                    run_if(run, lambda s=stream, r=rel, w=way: self.send(s, r, w).wait_send())
+            run_if(self.exists(rel), body)
+
+
+def comm_params(collective_id, megabytes=56):
+    return pltpu.CompilerParams(
+        collective_id=collective_id,
+        has_side_effects=True,
+        vmem_limit_bytes=megabytes * 1024 * 1024,
+    )
+
+
+def weight_gather(qkv_low, out_low, smalls, collective_id):
+    parts, rows, width = qkv_low.shape
+    depth, columns = out_low.shape
+
+    def kernel(qkv, out, small, qkv_all, out_all, small_all, send_sem, recv_sem, local_sem):
+        views = [
+            lambda b: qkv_all.at[:, block_rows(b, rows), :],
+            lambda b: out_all.at[:, block_rows(b, columns)],
+            lambda b: small_all.at[b],
+        ]
+        line = LineGather([2, 0, 1], [qkv, out, small], views, send_sem, recv_sem)
+        greet(line.partners())
+        own = line.block(0)
+        keep = [
+            pltpu.make_async_copy(source, view(own), local_sem.at[i])
+            for i, (source, view) in enumerate(zip([qkv, out, small], views))
+        ]
+        for copy in keep:
+            copy.start()
+        line.run()
+        line.finish()
+        for copy in keep:
+            copy.wait()
+
+    return pl.pallas_call(
+        kernel,
+        out_shape=(
+            jax.ShapeDtypeStruct((parts, rows * GROUPS, width), jnp.bfloat16),
+            jax.ShapeDtypeStruct((depth, columns * GROUPS), jnp.bfloat16),
+            jax.ShapeDtypeStruct((GROUPS,) + smalls.shape, jnp.float32),
+        ),
+        in_specs=[HBM] * 3,
+        out_specs=(HBM, HBM, HBM),
+        scratch_shapes=[
+            pltpu.SemaphoreType.DMA((3, 7, 3)),
+            pltpu.SemaphoreType.DMA((3, 14)),
+            pltpu.SemaphoreType.DMA((3,)),
+        ],
+        compiler_params=comm_params(collective_id),
+        name="weight_gather",
+    )(qkv_low, out_low, smalls)
+
+
+def token_gather(block, collective_id):
+    rows, width = block.shape
+    a_cols, c_cols = width * 3 // 16, width // 8
+
+    def kernel(own_ref, all_ref, send_sem, recv_sem, x_send, x_recv, core_send, core_recv, local_sem):
+        z, y, x, c = place()
+
+        def a_at(xx, cc):
+            return pl.ds(pl.multiple_of(xx * (2 * a_cols) + cc * a_cols, 128), a_cols)
+
+        def c_at(cc):
+            return pl.ds(pl.multiple_of(4 * a_cols + cc * c_cols, 128), c_cols)
+
+        def view(b, columns):
+            return all_ref.at[block_rows(b, rows), columns]
+
+        sources = [own_ref.at[:, a_at(x, c)], own_ref.at[:, c_at(c)]]
+        views = [lambda b: view(b, a_at(x, c)), lambda b: view(b, c_at(c))]
+        line = LineGather([0, 1], sources, views, send_sem, recv_sem)
+        across, twin = device(z, y, 1 - x, c), device(z, y, x, 1 - c)
+        greet(line.partners() + [(across, None), (twin, None)])
+        keep = pltpu.make_async_copy(own_ref, all_ref.at[block_rows(line.block(0), rows), :], local_sem)
+        keep.start()
+
+        def to_twin(rel, stream, landing=False):
+            b = line.block(rel)
+            columns = [a_at(x, c), c_at(c), a_at(1 - x, c)][stream]
+            other = [a_at(x, 1 - c), c_at(1 - c), a_at(1 - x, 1 - c)][stream]
+            piece = view(b, other if landing else columns)
+            return remote(piece, piece, core_send.at[rel, stream], core_recv.at[rel, stream], twin)
+
+        def to_across(rel, landing=False):
+            b = line.block(rel)
+            piece = view(b, a_at(1 - x if landing else x, c))
+            return remote(piece, piece, x_send.at[rel], x_recv.at[rel], across)
+
+        def hook(stream, rel):
+            if stream == 0:
+                to_across(rel).start()
+            to_twin(rel, stream).start()
+
+        line.run(hook)
+        for rel in line.order():
+            def relay(rel=rel):
+                to_across(rel, True).wait_recv()
+                to_twin(rel, 2).start()
+            run_if(line.exists(rel), relay)
+        for rel in line.order():
+            def end(rel=rel):
+                to_across(rel).wait_send()
+                for stream in range(3):
+                    to_twin(rel, stream, True).wait_recv()
+                    to_twin(rel, stream).wait_send()
+            run_if(line.exists(rel), end)
+        line.finish()
+        keep.wait()
+
+    return pl.pallas_call(
+        kernel,
+        out_shape=jax.ShapeDtypeStruct((rows * GROUPS, width), block.dtype),
+        in_specs=[HBM],
+        out_specs=HBM,
+        scratch_shapes=[
+            pltpu.SemaphoreType.DMA((2, 7, 3)),
+            pltpu.SemaphoreType.DMA((2, 14)),
+            pltpu.SemaphoreType.DMA((14,)),
+            pltpu.SemaphoreType.DMA((14,)),
+            pltpu.SemaphoreType.DMA((14, 3)),
+            pltpu.SemaphoreType.DMA((14, 3)),
+            pltpu.SemaphoreType.DMA,
+        ],
+        compiler_params=comm_params(collective_id),
+        name="token_gather",
+    )(block)
+
+
+def add_into(rows, step, store):
+    def body(i, carry):
+        store(pl.ds(pl.multiple_of(i * step, step), step))
+        return carry
+
+    lax.fori_loop(0, rows // step, body, 0)
+
+
+def tensor_sum(part, collective_id):
+    rows, width = part.shape
+    half, quarter = width // 2, width // 4
+
+    def kernel(part_ref, out_ref, core_buf, x_buf, send_sem, recv_sem):
+        z, y, x, c = place()
+        across, twin = device(z, y, 1 - x, c), device(z, y, x, 1 - c)
+        greet([(across, None), (twin, None)])
+
+        def half_of(cc):
+            return pl.ds(pl.multiple_of(cc * half, half), half)
+
+        def quarter_of(xx, cc):
+            return pl.ds(pl.multiple_of(cc * half + xx * quarter, quarter), quarter)
+
+        first = remote(part_ref.at[:, half_of(1 - c)], core_buf, send_sem.at[0], recv_sem.at[0], twin)
+        first.start()
+        first.wait_recv()
+        base = pl.multiple_of(c * half, half)
+
+        def add_core(r):
+            core_buf[r, :] = (
+                core_buf[r, :].astype(jnp.float32) + part_ref[r, pl.ds(base, half)].astype(jnp.float32)
+            ).astype(jnp.bfloat16)
+
+        add_into(rows, 32, add_core)
+        second = remote(
+            core_buf.at[:, pl.ds(pl.multiple_of((1 - x) * quarter, quarter), quarter)],
+            x_buf, send_sem.at[1], recv_sem.at[1], across,
+        )
+        second.start()
+        second.wait_recv()
+        mine = pl.multiple_of(x * quarter, quarter)
+        out_at = pl.multiple_of(c * half + x * quarter, quarter)
+
+        def add_x(r):
+            out_ref[r, pl.ds(out_at, quarter)] = (
+                core_buf[r, pl.ds(mine, quarter)].astype(jnp.float32) + x_buf[r, :].astype(jnp.float32)
+            ).astype(jnp.bfloat16)
+
+        add_into(rows, 32, add_x)
+        own = out_ref.at[:, quarter_of(x, c)]
+        third = remote(own, own, send_sem.at[2], recv_sem.at[2], across)
+        third.start()
+        fourth = remote(own, own, send_sem.at[3], recv_sem.at[3], twin)
+        fourth.start()
+        from_x = out_ref.at[:, quarter_of(1 - x, c)]
+        remote(from_x, from_x, send_sem.at[2], recv_sem.at[2], across).wait_recv()
+        fifth = remote(from_x, from_x, send_sem.at[4], recv_sem.at[4], twin)
+        fifth.start()
+        for index, column in ((3, quarter_of(x, 1 - c)), (4, quarter_of(1 - x, 1 - c))):
+            landing = out_ref.at[:, column]
+            remote(landing, landing, send_sem.at[index], recv_sem.at[index], twin).wait_recv()
+        for copy in (first, second, third, fourth, fifth):
+            copy.wait_send()
+
+    return pl.pallas_call(
+        kernel,
+        out_shape=jax.ShapeDtypeStruct((rows, width), jnp.bfloat16),
+        in_specs=[VMEM],
+        out_specs=VMEM,
+        scratch_shapes=[
+            pltpu.VMEM((rows, half), jnp.bfloat16),
+            pltpu.VMEM((rows, quarter), jnp.bfloat16),
+            pltpu.SemaphoreType.DMA((5,)),
+            pltpu.SemaphoreType.DMA((5,)),
+        ],
+        compiler_params=comm_params(collective_id, 16),
+        name="tensor_sum",
+    )(part)
+
+
+Z_ORDER = (3, 0, 2, 1)
+
+
+def accumulate(into, addend, step=64):
+    rows = into.shape[0]
+    step = min(step, rows)
+
+    def body(i, carry):
+        r = pl.ds(pl.multiple_of(i * step, step), step)
+        total = into[r, :].astype(jnp.float32) + addend[r, :].astype(jnp.float32)
+        into[r, :] = total.astype(into.dtype)
+        return carry
+
+    lax.fori_loop(0, rows // step, body, 0)
+
+
+class LineReduce:
+    def __init__(self, streams, own, y_buf, lo_buf, hi_buf, send_sem, recv_sem):
+        self.z, self.y, self.x, self.c = place()
+        self.streams = streams
+        self.own, self.y_buf, self.lo_buf, self.hi_buf = own, y_buf, lo_buf, hi_buf
+        self.send_sem, self.recv_sem = send_sem, recv_sem
+
+    def partners(self):
+        z, y, x, c = self.z, self.y, self.x, self.c
+        return [
+            (device(z + 1, y, x, c), z < NZ - 1),
+            (device(z - 1, y, x, c), z > 0),
+            (device(z, 1 - y, x, c), None),
+        ]
+
+    def copy(self, s, zz, way):
+        z, y, x, c = self.z, self.y, self.x, self.c
+        if way == 0:
+            source, landing, target = self.own(s, zz, 1 - y), self.y_buf, device(z, 1 - y, x, c)
+        elif way == 1:
+            source, landing, target = self.y_buf(s, zz), self.lo_buf, device(z + 1, y, x, c)
+        else:
+            source, landing, target = self.y_buf(s, zz), self.hi_buf, device(z - 1, y, x, c)
+        return remote(
+            source, landing(s, zz), self.send_sem.at[s, zz, way], self.recv_sem.at[s, zz, way], target
+        )
+
+    def to_y(self, s, zz):
+        self.copy(s, zz, 0).start()
+
+    def take(self, s, zz, way):
+        self.copy(s, zz, way).wait_recv()
+        accumulate(self.y_buf(s, zz), (self.lo_buf if way == 1 else self.hi_buf)(s, zz))
+
+    def along_z(self, s, zz):
+        z = self.z
+        self.copy(s, zz, 0).wait_recv()
+        accumulate(self.y_buf(s, zz), self.own(s, zz, self.y))
+
+        def upward():
+            run_if(z > 0, lambda: self.take(s, zz, 1))
+            self.copy(s, zz, 1).start()
+
+        def downward():
+            run_if(z < NZ - 1, lambda: self.take(s, zz, 2))
+            self.copy(s, zz, 2).start()
+
+        run_if(z < zz, upward)
+        run_if(z > zz, downward)
+
+    def home(self, done):
+        for zz in range(NZ):
+            def land(zz=zz):
+                for s in self.streams:
+                    if zz > 0:
+                        self.take(s, zz, 1)
+                    if zz < NZ - 1:
+                        self.take(s, zz, 2)
+                    done(s, self.y_buf(s, zz))
+            run_if(self.z == zz, land)
+
+    def finish(self):
+        for zz in range(NZ):
+            for s in self.streams:
+                self.copy(s, zz, 0).wait_send()
+                run_if(self.z < zz, lambda s=s, zz=zz: self.copy(s, zz, 1).wait_send())
+                run_if(self.z > zz, lambda s=s, zz=zz: self.copy(s, zz, 2).wait_send())
+
+
+def weight_reduce(qkv, out, smalls, collective_id):
+    parts, depth, width = qkv.shape
+    rows = depth // GROUPS
+    out_rows, columns = out.shape[0], out.shape[1] // GROUPS
+
+    def kernel(qkv_ref, out_ref, small_ref, qkv_sum, out_sum, small_sum,
+               qkv_buf, out_buf, small_buf, send_sem, recv_sem):
+        def own(s, zz, yy):
+            b = zz * NY + yy
+            if s < parts:
+                return qkv_ref.at[s, block_rows(b, rows), :]
+            if s == parts:
+                return out_ref.at[:, block_rows(b, columns)]
+            return small_ref.at[b]
+
+        def slot(kind):
+            def view(s, zz):
+                if s < parts:
+                    return qkv_buf.at[kind, zz, s]
+                if s == parts:
+                    return out_buf.at[kind, zz]
+                return small_buf.at[kind, zz]
+            return view
+
+        streams = list(range(parts + 2))
+        line = LineReduce(streams, own, slot(0), slot(1), slot(2), send_sem, recv_sem)
+        greet(line.partners())
+        work = [(s, zz) for s in [parts + 1, parts] + list(range(parts)) for zz in Z_ORDER]
+        for s, zz in work:
+            line.to_y(s, zz)
+        for s, zz in work:
+            line.along_z(s, zz)
+
+        def done(s, total):
+            target = qkv_sum.at[s] if s < parts else (out_sum if s == parts else small_sum)
+            step = min(64, target.shape[0])
+
+            def body(i, carry):
+                r = pl.ds(pl.multiple_of(i * step, step), step)
+                target[r, :] = total[r, :].astype(jnp.float32)
+                return carry
+
+            lax.fori_loop(0, target.shape[0] // step, body, 0)
+
+        line.home(done)
+        line.finish()
+
+    return pl.pallas_call(
+        kernel,
+        out_shape=(
+            jax.ShapeDtypeStruct((parts, rows, width), jnp.float32),
+            jax.ShapeDtypeStruct((out_rows, columns), jnp.float32),
+            jax.ShapeDtypeStruct(smalls.shape[1:], jnp.float32),
+        ),
+        in_specs=[VMEM] * 3,
+        out_specs=(VMEM,) * 3,
+        scratch_shapes=[
+            pltpu.VMEM((3, NZ, parts, rows, width), jnp.bfloat16),
+            pltpu.VMEM((3, NZ, out_rows, columns), jnp.bfloat16),
+            pltpu.VMEM((3, NZ) + smalls.shape[1:], jnp.float32),
+            pltpu.SemaphoreType.DMA((parts + 2, NZ, 3)),
+            pltpu.SemaphoreType.DMA((parts + 2, NZ, 3)),
+        ],
+        compiler_params=comm_params(collective_id),
+        name="weight_reduce",
+    )(qkv, out, smalls)
+
+
+def token_reduce(part, collective_id, pairs=None):
+    tokens, width = part.shape
+    rows = tokens // GROUPS
+    half, quarter = width // 2, width // 4
+
+    def kernel(part_ref, out_ref, core_buf, x_buf, y_buf, lo_buf, hi_buf,
+               core_send, core_recv, x_send, x_recv, send_sem, recv_sem):
+        z, y, x, c = place()
+        across, twin = device(z, y, 1 - x, c), device(z, y, x, 1 - c)
+
+        line = LineReduce(
+            [0], lambda s, zz, yy: x_buf.at[zz * NY + yy], lambda s, zz: y_buf.at[zz],
+            lambda s, zz: lo_buf.at[zz], lambda s, zz: hi_buf.at[zz], send_sem, recv_sem,
+        )
+        greet(line.partners() + [(across, None), (twin, None)])
+        order = [(zz, flip) for zz in Z_ORDER for flip in (1, 0)]
+
+        def number(zz, flip):
+            return zz * NY + (1 - y if flip else y)
+
+        def to_twin(zz, flip):
+            b = number(zz, flip)
+            return remote(
+                part_ref.at[block_rows(b, rows), pl.ds(pl.multiple_of((1 - c) * half, half), half)],
+                core_buf.at[b], core_send.at[zz, flip], core_recv.at[zz, flip], twin,
+            )
+
+        def to_across(zz, flip):
+            b = number(zz, flip)
+            return remote(
+                core_buf.at[b, :, pl.ds(pl.multiple_of((1 - x) * quarter, quarter), quarter)],
+                x_buf.at[b], x_send.at[zz, flip], x_recv.at[zz, flip], across,
+            )
+
+        def add_core(zz, flip):
+            b = number(zz, flip)
+
+            def store(r):
+                at = pl.ds(pl.multiple_of(b * rows + r.start, 16), r.size)
+                core_buf[b, r, :] = (
+                    core_buf[b, r, :].astype(jnp.float32)
+                    + part_ref[at, pl.ds(pl.multiple_of(c * half, half), half)].astype(jnp.float32)
+                ).astype(jnp.bfloat16)
+
+            add_into(rows, 32, store)
+
+        def add_across(zz, flip):
+            b = number(zz, flip)
+
+            def store(r):
+                x_buf[b, r, :] = (
+                    x_buf[b, r, :].astype(jnp.float32)
+                    + core_buf[b, r, pl.ds(pl.multiple_of(x * quarter, quarter), quarter)].astype(jnp.float32)
+                ).astype(jnp.bfloat16)
+
+            add_into(rows, 64, store)
+
+        def stage_twin(i):
+            to_twin(*order[i]).wait_recv()
+            add_core(*order[i])
+            to_across(*order[i]).start()
+
+        def stage_across(i):
+            zz, flip = order[i]
+            to_across(zz, flip).wait_recv()
+            add_across(zz, flip)
+            if flip:
+                line.to_y(0, zz)
+
+        def stage_y(zz):
+            line.along_z(0, zz)
+
+        for zz, flip in order:
+            to_twin(zz, flip).start()
+        count = len(order)
+        for i in range(count + 4):
+            if i < count:
+                stage_twin(i)
+            if 0 <= i - 1 < count:
+                stage_across(i - 1)
+            if i >= 3 and (i - 3) % 2 == 0 and (i - 3) // 2 < NZ:
+                stage_y(Z_ORDER[(i - 3) // 2])
+
+        def done(s, total):
+            def store(r):
+                out_ref[r, :] = total[r, :]
+
+            add_into(rows, 64, store)
+
+        line.home(done)
+        for zz, flip in order:
+            to_twin(zz, flip).wait_send()
+            to_across(zz, flip).wait_send()
+        line.finish()
+
+    return pl.pallas_call(
+        kernel,
+        out_shape=jax.ShapeDtypeStruct((rows, quarter), jnp.bfloat16),
+        in_specs=[VMEM],
+        out_specs=VMEM,
+        scratch_shapes=[
+            pltpu.VMEM((GROUPS, rows, half), jnp.bfloat16),
+            pltpu.VMEM((GROUPS, rows, quarter), jnp.bfloat16),
+            pltpu.VMEM((NZ, rows, quarter), jnp.bfloat16),
+            pltpu.VMEM((NZ, rows, quarter), jnp.bfloat16),
+            pltpu.VMEM((NZ, rows, quarter), jnp.bfloat16),
+            pltpu.SemaphoreType.DMA((NZ, 2)),
+            pltpu.SemaphoreType.DMA((NZ, 2)),
+            pltpu.SemaphoreType.DMA((NZ, 2)),
+            pltpu.SemaphoreType.DMA((NZ, 2)),
+            pltpu.SemaphoreType.DMA((1, NZ, 3)),
+            pltpu.SemaphoreType.DMA((1, NZ, 3)),
+        ],
+        compiler_params=comm_params(collective_id),
+        name="token_reduce",
+    )(part)
+
+
+def gate_exchange(part, collective_id):
+    groups = part.shape[0]
+    tensors = NX * NC
+
+    def kernel(part_ref, out_ref, landing, total, send_t, recv_t, send_e, recv_e):
+        e = lax.axis_index("expert")
+        t = lax.axis_index("tensor")
+        mates = [(e, lax.rem(t + k, tensors)) for k in range(1, tensors)]
+        peers = [(lax.rem(e + k, groups), t) for k in range(1, groups)]
+        greet([(target, None) for target in mates + peers])
+        near = [
+            remote(part_ref, landing.at[k], send_t.at[k], recv_t.at[k], mates[k])
+            for k in range(tensors - 1)
+        ]
+        for copy in near:
+            copy.start()
+        for copy in near:
+            copy.wait_recv()
+        value = part_ref[...]
+        for k in range(tensors - 1):
+            value = value + landing[k]
+        total[...] = value
+        far = [
+            remote(
+                total.at[lax.rem(e + k, groups)], out_ref.at[e], send_e.at[k - 1], recv_e.at[k - 1],
+                peers[k - 1],
+            )
+            for k in range(1, groups)
+        ]
+        for copy in far:
+            copy.start()
+        out_ref[e] = total[e]
+        for k in range(1, groups):
+            source = out_ref.at[lax.rem(e + groups - k, groups)]
+            remote(source, source, send_e.at[k - 1], recv_e.at[k - 1], peers[k - 1]).wait_recv()
+        for copy in near + far:
+            copy.wait_send()
+
+    return pl.pallas_call(
+        kernel,
+        out_shape=jax.ShapeDtypeStruct(part.shape, jnp.float32),
+        in_specs=[VMEM],
+        out_specs=VMEM,
+        scratch_shapes=[
+            pltpu.VMEM((tensors - 1,) + part.shape, jnp.float32),
+            pltpu.VMEM(part.shape, jnp.float32),
+            pltpu.SemaphoreType.DMA((tensors - 1,)),
+            pltpu.SemaphoreType.DMA((tensors - 1,)),
+            pltpu.SemaphoreType.DMA((groups - 1,)),
+            pltpu.SemaphoreType.DMA((groups - 1,)),
+        ],
+        compiler_params=comm_params(collective_id, 16),
+        name="gate_exchange",
+    )(part)
+
+
+def fast_shards(
+    tokens_in,
+    out_grad,
+    w_qkv,
+    w_attn_out,
+    attn_gain,
+    ffn_gain,
+    qk_gain,
+    w_router,
+    w_gate,
+    w_up,
+    w_down,
+    routes,
+    segments,
+):
+    row_count, model_width = tokens_in.shape
+    experts = w_router.shape[1]
+    local_experts = w_gate.shape[0]
+    heads_here = qk_gain.shape[1]
+    local_width = heads_here * HEAD
+    groups = lax.axis_size("expert")
+    device_index = lax.axis_index("expert")
+    tensor_index = lax.axis_index("tensor")
+    quarter = model_width // lax.axis_size("tensor")
+    hop_count = WINDOW // row_count
+    score_scale = HEAD ** (-0.5)
+    low = jnp.bfloat16
+
+    chosen = jnp.any(
+        routes[:, :, None] == jnp.arange(experts, dtype=jnp.int32)[None, None, :], axis=1
+    ).astype(jnp.float32)
+    qk_row = qk_gain.reshape(1, -1)
+    smalls = jnp.concatenate(
+        [
+            attn_gain[None, :],
+            ffn_gain[None, :],
+            jnp.pad(qk_row, ((0, 0), (0, row_count - qk_row.shape[1]))),
+            jnp.zeros((5, row_count), jnp.float32),
+            w_router.T,
+            chosen.T,
+        ],
+        axis=0,
+    )
+    qkv_low, out_low, small_all = weight_gather(
+        w_qkv.astype(low), w_attn_out.astype(low), smalls, 0
+    )
+
+    def rounded(v):
+        return v.astype(low).astype(jnp.float32)
+
+    gain_one_f = rounded(small_all[:, 0]).reshape(model_width)
+    gain_two_f = rounded(small_all[:, 1]).reshape(model_width)
+    qk_gains = (
+        rounded(small_all[:, 2, : qk_row.shape[1]])
+        .reshape(groups, 2, heads_here, HEAD // groups)
+        .transpose(1, 2, 0, 3)
+        .reshape(2, local_width)
+    )
+    router_t = small_all[:, 8 : 8 + experts].transpose(1, 0, 2).reshape(experts, model_width).astype(low)
+    chosen_all = small_all[:, 8 + experts : 8 + 2 * experts].transpose(0, 2, 1).reshape(
+        groups * row_count, experts
+    )
+    grad_out_all = token_gather(out_grad, 1)
+
+    tokens_f = tokens_in.astype(jnp.float32)
+    scale_one = lax.rsqrt(jnp.mean(tokens_f * tokens_f, axis=-1, keepdims=True) + EPS)
+    hidden_one = (tokens_f * scale_one * gain_one_f).astype(low)
+    projected = jnp.einsum("td,jde->jte", hidden_one, qkv_low, preferred_element_type=jnp.float32)
+    query_raw = projected[0]
+    key_raw = projected[1]
+    query_sq, key_sq = lax.psum(
+        (jnp.sum(query_raw * query_raw, axis=-1), jnp.sum(key_raw * key_raw, axis=-1)), "tensor"
+    )
+    query_scale = lax.rsqrt(query_sq / model_width + EPS)[:, None]
+    key_scale = lax.rsqrt(key_sq / model_width + EPS)[:, None]
+    normed_query = query_raw * query_scale
+    normed_key = key_raw * key_scale
+    global_rows = device_index * row_count + jnp.arange(row_count, dtype=jnp.int32)
+    cosine_table, sine_table = angles(global_rows % SEQ, HEAD)
+    query_low = rotate(
+        (normed_query * qk_gains[0]).reshape(row_count, heads_here, HEAD), cosine_table, sine_table
+    ).astype(low)
+    key_low = rotate(
+        (normed_key * qk_gains[1]).reshape(row_count, heads_here, HEAD), cosine_table, sine_table
+    ).astype(low)
+    value_low = projected[2].astype(low).reshape(row_count, heads_here, HEAD)
+    own_pair = jnp.stack([key_low, value_low])
+    earlier = []
+    for steps_back in range(hop_count, 0, -1):
+        earlier.append(from_behind(own_pair, "expert", steps_back))
+    context = jnp.concatenate(earlier + [own_pair], axis=1)
+    key_rows = (device_index - hop_count) * row_count + jnp.arange(
+        (hop_count + 1) * row_count, dtype=jnp.int32
+    )
+    segment_keys = segments[jnp.maximum(key_rows, 0)]
+    segment_query = segments[global_rows]
+    distance = global_rows[:, None] - key_rows[None, :]
+    allowed = (
+        (key_rows[None, :] >= 0)
+        & (segment_query[:, None] == segment_keys[None, :])
+        & (distance >= 0)
+        & (distance < WINDOW)
+    )
+
+    def score_block():
+        raw_scores = (
+            jnp.einsum("qhd,khd->hqk", query_low, context[0], preferred_element_type=jnp.float32)
+            * score_scale
+        )
+        return jnp.where(allowed[None], raw_scores, -1e30)
+
+    scores = score_block()
+    largest = jnp.max(scores, axis=-1, keepdims=True)
+    exp_scores = jnp.exp(scores - largest)
+    exp_total = jnp.sum(exp_scores, axis=-1, keepdims=True)
+    log_total = largest + jnp.log(exp_total)
+    attn_probs = (exp_scores / exp_total).astype(low)
+    attended = (
+        jnp.einsum("hqk,khd->qhd", attn_probs, context[1], preferred_element_type=jnp.float32)
+        .reshape(row_count, local_width)
+        .astype(low)
+    )
+    attention_out = tensor_sum(
+        jnp.dot(attended, out_low, preferred_element_type=jnp.float32).astype(low), 2
+    ).astype(jnp.float32)
+    residual = tokens_f + attention_out
+    scale_two = lax.rsqrt(jnp.mean(residual * residual, axis=-1, keepdims=True) + EPS)
+    normed_two = residual * scale_two
+    hidden_two = (normed_two * gain_two_f).astype(low)
+
+    hidden_all = token_gather(hidden_two, 3)
+    contract_last = (((1,), (1,)), ((), ()))
+
+    def router(rows):
+        logits = lax.dot_general(rows, router_t, contract_last, preferred_element_type=jnp.float32)
+        logit_exp = jnp.exp(logits - jnp.max(logits, axis=-1, keepdims=True))
+        return logit_exp / jnp.sum(logit_exp, axis=-1, keepdims=True)
+
+    gates_here = lax.dynamic_slice_in_dim(
+        router(hidden_all) * chosen_all, device_index * local_experts, local_experts, axis=1
+    ).T[:, :, None]
+    gate_low = w_gate.astype(low)
+    up_low = w_up.astype(low)
+    down_low = w_down.astype(low)
+    gate_pre = jnp.einsum("td,edh->eth", hidden_all, gate_low, preferred_element_type=jnp.float32)
+    up_pre = jnp.einsum("td,edh->eth", hidden_all, up_low, preferred_element_type=jnp.float32)
+    sigmoid_gate = jax.nn.sigmoid(gate_pre)
+    swish_gate = gate_pre * sigmoid_gate
+    activated = swish_gate * up_pre
+    gated = (activated * gates_here).astype(low)
+    expert_part = jnp.einsum(
+        "eth,ehd->td", gated, down_low, preferred_element_type=jnp.float32
+    ).astype(low)
+    grad_gated = jnp.einsum(
+        "td,ehd->eth", grad_out_all, down_low, preferred_element_type=jnp.float32
+    )
+    grad_gates_here = jnp.sum(activated * grad_gated, axis=-1)
+    grad_act = grad_gated * gates_here
+    grad_gate_pre = (
+        grad_act * up_pre * sigmoid_gate * (1.0 + gate_pre * (1.0 - sigmoid_gate))
+    ).astype(low)
+    grad_up_pre = (grad_act * swish_gate).astype(low)
+    grad_rows = (
+        jnp.einsum("eth,edh->td", grad_gate_pre, gate_low, preferred_element_type=jnp.float32)
+        + jnp.einsum("eth,edh->td", grad_up_pre, up_low, preferred_element_type=jnp.float32)
+    ).astype(low)
+    grad_gate_sum = gate_exchange(
+        jnp.pad(
+            grad_gates_here.reshape(local_experts, groups, row_count).transpose(1, 0, 2),
+            ((0, 0), (0, 8 - local_experts), (0, 0)),
+        ),
+        4,
+    )
+    grad_probs = (
+        grad_gate_sum[:, :local_experts].reshape(experts, row_count).T * chosen
+    )
+    grad_hidden_quarter = token_reduce(grad_rows, 5)
+    expert_quarter = token_reduce(expert_part, 6)
+    grad_down = jnp.einsum(
+        "eth,td->ehd", gated, grad_out_all, preferred_element_type=jnp.float32
+    )
+    grad_gate_w = jnp.einsum(
+        "td,eth->edh", hidden_all, grad_gate_pre, preferred_element_type=jnp.float32
+    )
+    grad_up_w = jnp.einsum(
+        "td,eth->edh", hidden_all, grad_up_pre, preferred_element_type=jnp.float32
+    )
+    column_order = [0, 2, 1, 3]
+
+    def spread(piece):
+        all_pieces = lax.all_gather(piece, "tensor", axis=0)
+        return jnp.concatenate([all_pieces[i] for i in column_order], axis=1)
+
+    def quarter_slot(t):
+        return (t % 2) * 2 + t // 2
+
+    grad_hidden_sum = spread(grad_hidden_quarter).astype(jnp.float32)
+    block_out = residual + spread(expert_quarter).astype(jnp.float32)
+    router_probs = router(hidden_two)
+    grad_logits = (
+        router_probs * (grad_probs - jnp.sum(router_probs * grad_probs, axis=-1, keepdims=True))
+    ).astype(low)
+    grad_out = out_grad.astype(jnp.float32)
+    grad_hidden_two = grad_hidden_sum + jnp.dot(
+        grad_logits, router_t, preferred_element_type=jnp.float32
+    )
+    grad_router_t = lax.dot_general(
+        grad_logits, hidden_two, (((0,), (0,)), ((), ())), preferred_element_type=jnp.float32
+    )
+    grad_gain_two = jnp.sum(grad_hidden_two * normed_two, axis=0)
+    scaled_two = grad_hidden_two * gain_two_f
+    grad_residual = (
+        grad_out
+        + scale_two * scaled_two
+        - residual
+        * (scale_two * scale_two * scale_two)
+        * jnp.mean(scaled_two * residual, axis=-1, keepdims=True)
+    )
+    grad_attn = grad_residual.astype(low)
+    grad_out_w = jnp.dot(attended.T, grad_attn, preferred_element_type=jnp.float32)
+    grad_attended = (
+        lax.dot_general(grad_attn, out_low, contract_last, preferred_element_type=jnp.float32)
+        .astype(low)
+        .reshape(row_count, heads_here, HEAD)
+    )
+    attn_weights = jnp.where(allowed[None], jnp.exp(score_block() - log_total), 0.0)
+    grad_weights = jnp.einsum(
+        "qhd,khd->hqk", grad_attended, context[1], preferred_element_type=jnp.float32
+    )
+    inner_sum = jnp.sum(attn_weights * grad_weights, axis=-1, keepdims=True)
+    grad_scores = (attn_weights * (grad_weights - inner_sum) * score_scale).astype(low)
+    grad_query = jnp.einsum(
+        "hqk,khd->qhd", grad_scores, context[0], preferred_element_type=jnp.float32
+    )
+    grad_keys = jnp.einsum(
+        "hqk,qhd->khd", grad_scores, query_low, preferred_element_type=jnp.float32
+    )
+    grad_values = jnp.einsum(
+        "hqk,qhd->khd", attn_weights.astype(low), grad_attended, preferred_element_type=jnp.float32
+    )
+    grad_pair = jnp.stack([grad_keys, grad_values]).reshape(
+        2, hop_count + 1, row_count, heads_here, HEAD
+    )
+    own_grad = grad_pair[:, hop_count]
+    for steps_back in range(1, hop_count + 1):
+        own_grad = own_grad + from_behind(
+            grad_pair[:, hop_count - steps_back].astype(low), "expert", -steps_back
+        ).astype(jnp.float32)
+    grad_query_norm = rotate(grad_query, cosine_table, -sine_table).reshape(row_count, local_width)
+    grad_key_norm = rotate(own_grad[0], cosine_table, -sine_table).reshape(row_count, local_width)
+    grad_gain_query = jnp.sum(grad_query_norm * normed_query, axis=0)
+    grad_gain_key = jnp.sum(grad_key_norm * normed_key, axis=0)
+    scaled_query = grad_query_norm * qk_gains[0]
+    scaled_key = grad_key_norm * qk_gains[1]
+    query_inner, key_inner = lax.psum(
+        (jnp.sum(scaled_query * query_raw, axis=-1), jnp.sum(scaled_key * key_raw, axis=-1)),
+        "tensor",
+    )
+    grad_query_raw = (
+        query_scale * scaled_query
+        - query_raw * (query_scale * query_scale * query_scale) * query_inner[:, None] / model_width
+    ).astype(low)
+    grad_key_raw = (
+        key_scale * scaled_key
+        - key_raw * (key_scale * key_scale * key_scale) * key_inner[:, None] / model_width
+    ).astype(low)
+    grad_value_raw = own_grad[1].reshape(row_count, local_width).astype(low)
+    grad_proj = jnp.stack([grad_query_raw, grad_key_raw, grad_value_raw])
+    grad_qkv = jnp.einsum("td,jte->jde", hidden_one, grad_proj, preferred_element_type=jnp.float32)
+    grad_hidden_one = tensor_sum(
+        jnp.einsum("jte,jde->td", grad_proj, qkv_low, preferred_element_type=jnp.float32).astype(low),
+        7,
+    ).astype(jnp.float32)
+    grad_gain_one = jnp.sum(grad_hidden_one * tokens_f * scale_one, axis=0)
+    scaled_one = grad_hidden_one * gain_one_f
+    grad_tokens = (
+        grad_residual
+        + scale_one * scaled_one
+        - tokens_f
+        * (scale_one * scale_one * scale_one)
+        * jnp.mean(scaled_one * tokens_f, axis=-1, keepdims=True)
+    )
+    grad_qk = (
+        jnp.stack([grad_gain_query, grad_gain_key])
+        .reshape(2, heads_here, groups, HEAD // groups)
+        .transpose(2, 0, 1, 3)
+        .reshape(groups, 1, qk_row.shape[1])
+    )
+    small_grads = jnp.concatenate(
+        [
+            grad_gain_one.reshape(groups, 1, row_count),
+            grad_gain_two.reshape(groups, 1, row_count),
+            jnp.pad(grad_qk, ((0, 0), (0, 0), (0, row_count - qk_row.shape[1]))),
+            jnp.zeros((groups, 5, row_count), jnp.float32),
+            grad_router_t.reshape(experts, groups, row_count).transpose(1, 0, 2),
+        ],
+        axis=1,
+    )
+    qkv_sum, out_sum, small_sum = weight_reduce(
+        grad_qkv.astype(low), grad_out_w.astype(low), small_grads, 8
+    )
+    return (
+        block_out.astype(low),
+        grad_tokens.astype(low),
+        qkv_sum,
+        out_sum,
+        small_sum[0],
+        small_sum[1],
+        small_sum[2, : qk_row.shape[1]].reshape(qk_gain.shape),
+        small_sum[8 : 8 + experts].T,
+        grad_gate_w,
+        grad_up_w,
+        grad_down,
+    )
+
+
 def solution(mesh):
     placed = (
         P("expert", None),
@@ -396,8 +1406,9 @@
         P("expert", None),
         P(),
     )
+    compact = (mesh.shape["expert"], mesh.shape["tensor"]) == (GROUPS, NX * NC)
     return jax.shard_map(
-        shards,
+        fast_shards if compact else shards,
         mesh=mesh,
         in_specs=placed,
         out_specs=(

time: 2120 us -> 917 us (0.43)
  blocking collectives: 1000 us -> 11.6 us
  waiting for transfers between devices: 649 us -> 43.3 us
  Pallas kernels: 0 us -> 553 us
  local copies, waits for them, and re-layouts: 158 us -> 59.1 us
  other arithmetic: 70.1 us -> 39.5 us
  matrix products: 190 us -> 161 us
    all_to_all x2 -> x0, blocking collectives: 556 us -> none  [the longest x1 279 us: send_rows(): lax.all_to_all(buffer_rows, 'expert', split_axis=0, concat_axis=0, tiled=...]
    pallas_call x0 -> x9, Pallas kernels: none -> 553 us  [the longest x2 133 us: token_reduce(): pl.pallas_call(kernel, out_shape=jax.ShapeDtypeStruct((rows, quarter), jn...]
    all_gather x4 -> x0, blocking collectives: 409 us -> none  [the longest x1 290 us: fetch_weights(): lax.all_gather(w_router.astype(jnp.bfloat16), 'expert', axis=0, tiled=True)]
    all_to_all x2 -> x0, waiting for transfers between devices: 272 us -> none  [the longest x1 272 us: shards(): lax.all_to_all(grad_rows, 'expert', split_axis=0, concat_axis=0, tiled=True)]
    reduce_scatter x3 -> x0, waiting for transfers between devices: 162 us -> none  [the longest x1 120 us: shards(): lax.psum_scatter(grad_qkv.astype(jnp.bfloat16), 'expert', scatter_dimensi...]
    psum x3 -> x0, waiting for transfers between devices: 137 us -> none  [the longest x1 52.2 us: shards(): lax.psum(expert_part.astype(jnp.bfloat16), 'tensor').astype(jnp.float32)]
    gather x6 -> x2, local copies, waits for them, and re-layouts: 98.1 us -> 8.8 us  [the longest x1 7.08 us: fast_shards(): segment_keys = segments[jnp.maximum(key_rows, 0)]]
    dot_general x25 -> x24, matrix products: 189 us -> 159 us  [the longest x1 15.5 us: fast_shards(): jnp.einsum('hqk,qhd->khd', grad_scores, query_low, preferred_element_type...]
  transfers between devices with their start and end apart: 19 -> 10, of which waited for: 10 -> 3; matrix products, arithmetic and copies ran while one was open for 8% -> 7% of each run, Pallas kernels for 0% -> 16%
where the time goes in v1:
time: 917 us; the launch traced here: 902 us
  Pallas kernels  553 us (60%)
  matrix products  161 us (18%)
  local copies, waits for them, and re-layouts  59.1 us (6%)
  waiting for transfers between devices  43.3 us (5%)
  other arithmetic  39.5 us (4%)
  starting transfers between devices  18.6 us (2%)
  between operations  15.5 us (2%)
  blocking collectives  11.6 us (1%)
    pallas_call x2, Pallas kernels, token_reduce(): pl.pallas_call(kernel, out_shape=jax.ShapeDtypeStruct((rows, quarter), jn...  133 us
    pallas_call x2, Pallas kernels, token_gather(): pl.pallas_call(kernel, out_shape=jax.ShapeDtypeStruct((rows * GROUPS, wid...  126 us
    pallas_call x1, Pallas kernels, weight_reduce(): pl.pallas_call(kernel, out_shape=(jax.ShapeDtypeStruct((parts, rows, widt...  125 us
    pallas_call x1, Pallas kernels, weight_gather(): pl.pallas_call(kernel, out_shape=(jax.ShapeDtypeStruct((parts, rows * GRO...  119 us
    pallas_call x2, Pallas kernels, tensor_sum(): pl.pallas_call(kernel, out_shape=jax.ShapeDtypeStruct((rows, width), jnp....  37.5 us
    ppermute x8, waiting for transfers between devices, from_behind(): lax.ppermute(value, axis, [(source, source + steps) for source in range(i...  33.2 us
    unnamed x120, local copies, waits for them, and re-layouts  23.7 us
    ppermute x8, starting transfers between devices, from_behind(): lax.ppermute(value, axis, [(source, source + steps) for source in range(i...  18.4 us
  transfers between devices with their start and end apart: 10, of which 3 were waited for; matrix products, arithmetic and copies ran while one was open for 7% of the time, Pallas kernels for 16%

profile of v1, /device:TPU:0, one launch (start us, length us, event | category | flops | bytes accessed | tf_op | source)
XLA Modules:
  0.0 901.7 jit_solution(3007905326568932964)
XLA Ops:
  15.5 118.7 %weight_gather.1 = (bf16[3,2048,512]{2,1,0:T(8,128)(2,1)}, bf16[512,2048]{1,0:T(8,128)(2,1)}, f32[8,40,256]{2,1,0:T(8,128)}) custom-call(bf16[3,256,512]{2,1,0:T(8,128)(2,1)} %convert_element_type.236.qkv, bf16[512,256]{1,0:T(8,128)(2,1)} %convert_element_type.237.out, f32[40,256]{1,0:T(8,128)} %concatenate.42.small), custom_call_target="tpu_custom_call" | custom-call | tf_op jit(solution)/shard_map/weight_gather/pallas_call | solution.py:575
  136.8 4.8 convolution_bitcast_fusion.2
  144.9 5.6 all-reduce.4
  157.4 6.4 collective-permute-start.1
  167.7 7.1 gather_fusion.1
  174.8 74.6 %token_gather.3 = bf16[2048,2048]{1,0:T(8,128)(2,1)} custom-call(bf16[256,2048]{1,0:T(8,128)(2,1)} %own_ref.1), custom_call_target="tpu_custom_call" | custom-call | tf_op jit(solution)/shard_map/token_gather/pallas_call | solution.py:651
  249.5 9.5 %fusion.4 = f32[2,256,2048]{2,1,0:T(8,128)} fusion(bf16[2048,2048]{1,0:T(8,128)(2,1)} %token_gather.3, f32[2,256,2048]{2,1,0:T(8,128)S(1)} %copy-done.54), kind=kOutput, calls=%fused_computation.8 | convolution fusion | flops 4296015872 | bytes 16777216 | tf_op jit(solution)/shard_map/td,ehd->eth/dot_general | solution.py:1230
  273.1 18.6 %tensor_sum.2 = bf16[256,2048]{1,0:T(8,128)(2,1)S(1)} custom-call(bf16[256,2048]{1,0:T(8,128)(2,1)S(1)} %convolution_convert_fusion.1.part_ref), custom_call_target="tpu_custom_call" | custom-call | tf_op jit(solution)/shard_map/tensor_sum/pallas_call | solution.py:734
  294.2 51.1 %token_gather.2 = bf16[2048,2048]{1,0:T(8,128)(2,1)} custom-call(bf16[256,2048]{1,0:T(8,128)(2,1)} %multiply_convert_fusion.3.own_ref), custom_call_target="tpu_custom_call" | custom-call | tf_op jit(solution)/shard_map/token_gather/pallas_call | solution.py:651
  346.8 5.8 fusion.138
  352.7 8.6 fusion.12
  362.2 11.7 %fusion.21 = (bf16[2,2048,256]{1,2,0:T(8,128)(2,1)S(1)}, f32[2,2048]{1,0:T(2,128)S(1)}, bf16[2,2048,256]{1,2,0:T(8,128)(2,1)}, bf16[2,2048,256]{1,2,0:T(8,128)(2,1)}) fusion(f32[2048,2,256]{0,2,1:T(8,128)} %fusion.12, f32[2,256,2048]{2,1,0:T(8,128)} %fusion.4, f32[2,2048]{1,0:T(2,128)S(1)} %fusion.114, f32[2,2048,256]{2,1,0:T(8,128)} %param.22, ...), kind=kOutput, calls=%fused_computation.41 | convolution fusion | flops 4315934720 | bytes 27295744 | tf_op jit(solution)/shard_map/td,edh->eth/dot_general | solution.py:1222
  374.0 6.1 fusion.36
  380.0 8.5 fusion.89
  388.6 13.9 %gate_exchange.1 = f32[8,8,256]{2,1,0:T(8,128)S(1)} custom-call(f32[8,8,256]{2,1,0:T(8,128)S(1)} %pad.13.part_ref), custom_call_target="tpu_custom_call" | custom-call | tf_op jit(solution)/shard_map/gate_exchange/pallas_call | solution.py:1059
  407.7 10.5 %fusion.39 = f32[2,2048,256]{1,2,0:T(8,128)} fusion(bf16[2,2048,256]{1,2,0:T(8,128)(2,1)} %get-tuple-element.74, bf16[2048,2048]{1,0:T(8,128)(2,1)} %token_gather.2), kind=kOutput, calls=%fused_computation.57 | convolution fusion | flops 4294967296 | bytes 14680064 | tf_op jit(solution)/shard_map/td,eth->edh/dot_general | solution.py:1261
  418.2 5.3 copy.115
  423.5 5.3 copy.114
  428.9 15.5 %fusion.1.part_ref = bf16[2048,2048]{1,0:T(8,128)(2,1)} fusion(f32[2048,2048,1]{1,0,2:T(8,128)} %fusion.89, bf16[2,2048,256]{1,2,0:T(8,128)(2,1)} %get-tuple-element.74, f32[2,2048,256]{2,1,0:T(8,128)} %param.22), kind=kOutput, calls=%fused_computation.4 | convolution fusion | flops 4304404480 | bytes 31457280 | tf_op jit(solution)/shard_map/eth,edh->td/dot_general | solution.py:1241
  444.3 63.0 %token_reduce.3 = bf16[256,512]{1,0:T(8,128)(2,1)} custom-call(bf16[2048,2048]{1,0:T(8,128)(2,1)} %fusion.1.part_ref), custom_call_target="tpu_custom_call" | custom-call | tf_op jit(solution)/shard_map/token_reduce/pallas_call | solution.py:998
  507.6 10.6 %bitcast_convert_fusion.part_ref = bf16[2048,2048]{1,0:T(8,128)(2,1)} fusion(bf16[2,2048,256]{1,2,0:T(8,128)(2,1)} %get-tuple-element.75, f32[2,256,2048]{2,1,0:T(8,128)} %param.23), kind=kOutput, calls=%fused_computation.5 | convolution fusion | flops 4300210176 | bytes 14680064 | tf_op jit(solution)/shard_map/eth,ehd->td/dot_general | solution.py:1227
  518.3 70.0 %token_reduce.2 = bf16[256,512]{1,0:T(8,128)(2,1)} custom-call(bf16[2048,2048]{1,0:T(8,128)(2,1)} %bitcast_convert_fusion.part_ref), custom_call_target="tpu_custom_call" | custom-call | tf_op jit(solution)/shard_map/token_reduce/pallas_call | solution.py:998
  588.9 10.5 %fusion.2 = f32[2,256,2048]{2,1,0:T(8,128)} fusion(bf16[2,2048,256]{1,2,0:T(8,128)(2,1)} %get-tuple-element.75, bf16[2048,2048]{1,0:T(8,128)(2,1)} %token_gather.3), kind=kOutput, calls=%fused_computation.6 | convolution fusion | flops 4294967296 | bytes 14680064 | tf_op jit(solution)/shard_map/eth,td->ehd/dot_general | solution.py:1255
  604.3 10.0 %all-gather.5.cloned.1.call-done = bf16[1024,512]{1,0:T(8,128)(2,1)} async-done(((bf16[256,512]{1,0:T(8,128)(2,1)}), bf16[1024,512]{1,0:T(8,128)(2,1)}) %all-gather.5.cloned.1.call-update) | async-done | bytes 1048592 | tf_op jit(solution)/shard_map/all_gather | solution.py:1267
  626.0 5.3 convolution_bitcast_fusion
  634.7 15.5 %fusion.33 = f32[1280,4,128]{0,2,1:T(8,128)} fusion(f32[4,256,1280]{2,1,0:T(8,128)} %fusion.79, f32[4,256,1280]{2,1,0:T(8,128)} %copy-done.2, f32[4,256]{1,0:T(4,128)S(1)} %copy-done.36, pred[256,1280]{1,0:T(8,128)(4,1)S(1)} %fusion.74, bf16[256,4,64]{2,0,1:T(8,128)(2,1)S(1)} %copy-done.22, bf16[256,4,64]{2,0,1:T(8,128)(2,1)S(1)} %copy-done.20), kind=kOutput, calls=%fused_computation.54 | convolution fusion | flops 347867392 | bytes 13701120 | tf_op jit(solution)/shard_map/hqk,qhd->khd/dot_general | solution.py:1311
  662.5 11.0 %fusion.75 = f32[256,4,128]{2,0,1:T(8,128)} fusion(f32[4,256,1280]{2,1,0:T(8,128)} %fusion.79, f32[4,256,1280]{2,1,0:T(8,128)} %copy-done.2, f32[4,256]{1,0:T(4,128)S(1)} %copy-done.36, pred[256,1280]{1,0:T(8,128)(4,1)S(1)} %fusion.74, bf16[2,1280,4,128]{3,1,2,0:T(8,128)(2,1)} %copy-done.14), kind=kOutput, calls=%fused_computation.100 | convolution fusion | flops 347343104 | bytes 23470080 | tf_op jit(solution)/shard_map/hqk,khd->qhd/dot_general | solution.py:1308
  676.7 8.0 collective-permute-done.4
  684.7 25.2 %collective-permute-done.7 = bf16[2,256,4,128]{3,1,2,0:T(8,128)(2,1)} collective-permute-done((bf16[2,256,4,128]{3,1,2,0:T(8,128)(2,1)}, bf16[2,256,4,128]{3,1,2,0:T(8,128)(2,1)}, u32[]{:S(2)}, u32[]{:S(2)}) %collective-permute-start.7) | collective-permute-done | bytes 524320 | tf_op jit(solution)/shard_map/ppermute | solution.py:20
  722.1 5.9 all-reduce.3
  739.0 18.9 %tensor_sum.3 = bf16[256,2048]{1,0:T(8,128)(2,1)S(1)} custom-call(bf16[256,2048]{1,0:T(8,128)(2,1)S(1)} %fusion.61.part_ref), custom_call_target="tpu_custom_call" | custom-call | tf_op jit(solution)/shard_map/tensor_sum/pallas_call | solution.py:734
  760.3 124.6 %weight_reduce.1 = (f32[3,256,512]{2,1,0:T(8,128)}, f32[512,256]{1,0:T(8,128)}, f32[24,256]{1,0:T(8,128)}) custom-call(bf16[3,2048,512]{2,1,0:T(8,128)(2,1)} %convert_bitcast_fusion.qkv_ref, bf16[512,2048]{1,0:T(8,128)(2,1)} %convolution_convert_fusion.out_ref, f32[8,24,256]{2,1,0:T(8,128)} %concatenate.52.small_ref), custom_call_target="tpu_custom_call" | custom-call | tf_op jit(solution)/shard_map/weight_reduce/pallas_call | solution.py:882
  (241 shorter events, 119.9 us)
Async XLA Ops:
  7.2 158.8 %copy-start = (s32[2048]{0:T(1024)S(1)}, s32[2048]{0:T(1024)}, u32[]{:S(2)}) copy-start(s32[2048]{0:T(1024)} %param.25) | copy-start | bytes 24580
  7.2 128.6 %copy-start.4 = (bf16[256,2048]{1,0:T(8,128)(2,1)S(1)}, bf16[256,2048]{1,0:T(8,128)(2,1)}, u32[]{:S(2)}) copy-start(bf16[256,2048]{1,0:T(8,128)(2,1)} %param.13) | copy-start | bytes 3145732
  7.2 592.2 %all-gather.7.cloned.1.call-start = ((), (), s32[]{:S(2)}) async-start(), calls=%async_computation.1 | async-start | bytes 1310720 | tf_op jit(solution)/shard_map/all_gather | solution.py:1267
  151.8 115.2 %copy-start.19 = (bf16[256,4,64]{2,0,1:T(8,128)(2,1)}, bf16[256,4,64]{2,0,1:T(8,128)(2,1)S(1)}, u32[]{:S(2)}) copy-start(bf16[256,4,64]{2,0,1:T(8,128)(2,1)S(1)} %get-tuple-element.98) | copy-start | bytes 393220
  151.8 115.2 %copy-start.21 = (bf16[256,4,64]{2,0,1:T(8,128)(2,1)}, bf16[256,4,64]{2,0,1:T(8,128)(2,1)S(1)}, u32[]{:S(2)}) copy-start(bf16[256,4,64]{2,0,1:T(8,128)(2,1)S(1)} %get-tuple-element.99) | copy-start | bytes 393220
  152.8 113.9 %collective-permute-start.3 = (bf16[2,256,4,128]{3,1,2,0:T(8,128)(2,1)}, bf16[2,256,4,128]{3,1,2,0:T(8,128)(2,1)S(1)}, u32[]{:S(2)}, u32[]{:S(2)}) collective-permute-start(bf16[2,256,4,128]{3,1,2,0:T(8,128)(2,1)} %pad_maximum_fusion.2), channel_id=1, source_target_pairs={{0,4},{4,8},{8,12},{12,16},{16,20},{20,24},{24,28},{1,5},{5,9},{9,... | collective-permute-start | bytes 1572872 | tf_op jit(solution)/shard_map/ppermute | solution.py:20
  155.2 110.3 %collective-permute-start.2 = (bf16[2,256,4,128]{3,1,2,0:T(8,128)(2,1)}, bf16[2,256,4,128]{3,1,2,0:T(8,128)(2,1)}, u32[]{:S(2)}, u32[]{:S(2)}) collective-permute-start(bf16[2,256,4,128]{3,1,2,0:T(8,128)(2,1)} %pad_maximum_fusion.2), channel_id=1, source_target_pairs={{0,8},{4,12},{8,16},{12,20},{16,24},{20,28},{1,9},{5,13},{9,17},{1... | collective-permute-start | bytes 1572872 | tf_op jit(solution)/shard_map/ppermute | solution.py:20
  157.4 107.0 %collective-permute-start.1 = (bf16[2,256,4,128]{3,1,2,0:T(8,128)(2,1)}, bf16[2,256,4,128]{3,1,2,0:T(8,128)(2,1)}, u32[]{:S(2)}, u32[]{:S(2)}) collective-permute-start(bf16[2,256,4,128]{3,1,2,0:T(8,128)(2,1)} %pad_maximum_fusion.2), channel_id=1, source_target_pairs={{0,12},{4,16},{8,20},{12,24},{16,28},{1,13},{5,17},{9,21},{13,25},... | collective-permute-start | bytes 1572872 | tf_op jit(solution)/shard_map/ppermute | solution.py:20
  163.8 99.5 %collective-permute-start = (bf16[2,256,4,128]{3,1,2,0:T(8,128)(2,1)}, bf16[2,256,4,128]{3,1,2,0:T(8,128)(2,1)}, u32[]{:S(2)}, u32[]{:S(2)}) collective-permute-start(bf16[2,256,4,128]{3,1,2,0:T(8,128)(2,1)} %pad_maximum_fusion.2), channel_id=1, source_target_pairs={{0,16},{4,20},{8,24},{12,28},{1,17},{5,21},{9,25},{13,29},{2,18},{... | collective-permute-start | bytes 1572872 | tf_op jit(solution)/shard_map/ppermute | solution.py:20
  174.8 74.7 %copy-start.54 = (f32[2,256,2048]{2,1,0:T(8,128)S(1)}, f32[2,256,2048]{2,1,0:T(8,128)}, u32[]{:S(2)}) copy-start(f32[2,256,2048]{2,1,0:T(8,128)} %param.23) | copy-start | bytes 12582916
  272.3 19.3 %copy-start.23 = (bf16[4,128,256]{2,1,0:T(8,128)(2,1)}, bf16[4,128,256]{2,1,0:T(8,128)(2,1)S(1)}, u32[]{:S(2)}) copy-start(bf16[4,128,256]{2,1,0:T(8,128)(2,1)S(1)} %fusion.78) | copy-start | bytes 786436
  292.7 52.6 %copy-start.40 = (f32[256]{0:T(256)}, f32[256]{0:T(256)S(1)}, u32[]{:S(2)}) copy-start(f32[256]{0:T(256)S(1)} %get-tuple-element.122) | copy-start | bytes 3076
  294.2 51.1 %copy-start.8 = (bf16[256,2048]{1,0:T(8,128)(2,1)S(1)}, bf16[256,2048]{1,0:T(8,128)(2,1)}, u32[]{:S(2)}) copy-start(bf16[256,2048]{1,0:T(8,128)(2,1)} %multiply_convert_fusion.3.own_ref) | copy-start | bytes 3145732
  380.0 25.2 %copy-start.31 = (pred[256,16]{0,1:T(8,128)(4,1)S(1)}, pred[256,16]{0,1:T(8,128)(4,1)}, u32[]{:S(2)}) copy-start(pred[256,16]{0,1:T(8,128)(4,1)} %copy-done.30) | copy-start | bytes 12292
  507.4 106.9 %all-gather.5.cloned.1.call-start = ((), (), s32[]{:S(2)}) async-start(), calls=%async_computation | async-start | bytes 1310720 | tf_op jit(solution)/shard_map/all_gather | solution.py:1267
  518.3 70.0 %copy-start.38 = (f32[4,256]{1,0:T(4,128)S(1)}, f32[4,256]{1,0:T(4,128)}, u32[]{:S(2)}) copy-start(f32[4,256]{1,0:T(4,128)} %copy-done.37) | copy-start | bytes 12292
  588.9 11.8 %copy-start.33 = (bf16[256,16]{0,1:T(8,128)(2,1)S(1)}, bf16[256,16]{0,1:T(8,128)(2,1)}, u32[]{:S(2)}) copy-start(bf16[256,16]{0,1:T(8,128)(2,1)} %copy-done.32) | copy-start | bytes 24580
  657.2 27.5 %collective-permute-start.4 = (bf16[2,256,4,128]{3,1,2,0:T(8,128)(2,1)}, bf16[2,256,4,128]{3,1,2,0:T(8,128)(2,1)}, u32[]{:S(2)}, u32[]{:S(2)}) collective-permute-start(bf16[2,256,4,128]{3,1,2,0:T(8,128)(2,1)} %get-tuple-element.76), channel_id=1, source_target_pairs={{4,0},{8,4},{12,8},{16,12},{20,16},{24,20},{28,24},{5,1},{9,5},{13... | collective-permute-start | bytes 1572872 | tf_op jit(solution)/shard_map/ppermute | solution.py:20
  658.4 51.4 %collective-permute-start.7 = (bf16[2,256,4,128]{3,1,2,0:T(8,128)(2,1)}, bf16[2,256,4,128]{3,1,2,0:T(8,128)(2,1)}, u32[]{:S(2)}, u32[]{:S(2)}) collective-permute-start(bf16[2,256,4,128]{3,1,2,0:T(8,128)(2,1)} %get-tuple-element.77), channel_id=1, source_target_pairs={{16,0},{20,4},{24,8},{28,12},{17,1},{21,5},{25,9},{29,13},{18,2},{... | collective-permute-start | bytes 1572872 | tf_op jit(solution)/shard_map/ppermute | solution.py:20
  659.7 50.1 %collective-permute-start.6 = (bf16[2,256,4,128]{3,1,2,0:T(8,128)(2,1)}, bf16[2,256,4,128]{3,1,2,0:T(8,128)(2,1)}, u32[]{:S(2)}, u32[]{:S(2)}) collective-permute-start(bf16[2,256,4,128]{3,1,2,0:T(8,128)(2,1)} %get-tuple-element.78), channel_id=1, source_target_pairs={{12,0},{16,4},{20,8},{24,12},{28,16},{13,1},{17,5},{21,9},{25,13},... | collective-permute-start | bytes 1572872 | tf_op jit(solution)/shard_map/ppermute | solution.py:20
  661.0 12.5 %copy-start.6 = (f32[256,2048]{1,0:T(8,128)S(1)}, f32[256,2048]{1,0:T(8,128)}, u32[]{:S(2)}) copy-start(f32[256,2048]{1,0:T(8,128)} %copy-done.5) | copy-start | bytes 6291460
  661.1 48.8 %collective-permute-start.5 = (bf16[2,256,4,128]{3,1,2,0:T(8,128)(2,1)}, bf16[2,256,4,128]{3,1,2,0:T(8,128)(2,1)}, u32[]{:S(2)}, u32[]{:S(2)}) collective-permute-start(bf16[2,256,4,128]{3,1,2,0:T(8,128)(2,1)} %get-tuple-element.79), channel_id=1, source_target_pairs={{8,0},{12,4},{16,8},{20,12},{24,16},{28,20},{9,1},{13,5},{17,9},{2... | collective-permute-start | bytes 1572872 | tf_op jit(solution)/shard_map/ppermute | solution.py:20
  673.5 36.3 %copy-start.7 = (f32[1280,4,128]{2,0,1:T(8,128)S(1)}, f32[1280,4,128]{2,0,1:T(8,128)}, u32[]{:S(2)}) copy-start(f32[1280,4,128]{2,0,1:T(8,128)} %copy.104) | copy-start | bytes 7864324
  676.7 35.4 %copy-start.18 = (f32[256,64]{1,0:T(8,128)S(1)}, f32[256,64]{1,0:T(8,128)}, u32[]{:S(2)}) copy-start(f32[256,64]{1,0:T(8,128)} %copy-done.17) | copy-start | bytes 196612
  676.7 35.4 %copy-start.24 = (f32[256,64]{1,0:T(8,128)S(1)}, f32[256,64]{1,0:T(8,128)}, u32[]{:S(2)}) copy-start(f32[256,64]{1,0:T(8,128)} %get-tuple-element.112) | copy-start | bytes 196612
  716.4 11.6 %copy-start.42 = (f32[256]{0:T(256)S(1)}, f32[256]{0:T(256)}, u32[]{:S(2)}) copy-start(f32[256]{0:T(256)} %copy-done.41) | copy-start | bytes 3076
  716.4 11.6 %copy-start.44 = (f32[256]{0:T(256)S(1)}, f32[256]{0:T(256)}, u32[]{:S(2)}) copy-start(f32[256]{0:T(256)} %copy-done.43) | copy-start | bytes 3076
  716.4 11.6 %copy-start.48 = (f32[256]{0:T(256)S(1)}, f32[256]{0:T(256)}, u32[]{:S(2)}) copy-start(f32[256]{0:T(256)} %get-tuple-element.119) | copy-start | bytes 3076
  716.5 11.6 %copy-start.49 = (f32[256]{0:T(256)S(1)}, f32[256]{0:T(256)}, u32[]{:S(2)}) copy-start(f32[256]{0:T(256)} %get-tuple-element.131) | copy-start | bytes 3076
  739.0 19.9 %copy-start.25 = (f32[2,8,8,256]{3,2,0,1:T(8,128)S(1)}, f32[2,8,8,256]{3,2,0,1:T(8,128)}, u32[]{:S(2)}) copy-start(f32[2,8,8,256]{3,2,0,1:T(8,128)} %copy.141) | copy-start | bytes 393220
  739.0 20.0 %copy-start.47 = (f32[2048]{0:T(1024)S(1)}, f32[2048]{0:T(1024)}, u32[]{:S(2)}) copy-start(f32[2048]{0:T(1024)} %get-tuple-element.56) | copy-start | bytes 24580
  760.3 128.6 %copy-start.50 = (f32[256]{0:T(256)S(1)}, f32[256]{0:T(256)}, u32[]{:S(2)}) copy-start(f32[256]{0:T(256)} %get-tuple-element.115) | copy-start | bytes 3076
  (33 other events, 130.8 us)
Sparse Core Ops, SparseCore 0:
  507.5 24.4 all-gather.6
  589.0 25.2 all-gather.4

commit v2 on v1

--- a/solution.py
+++ b/solution.py
@@ -540,6 +540,10 @@
             run_if(self.exists(rel), body)
 
 
+def cost(microseconds):
+    return pl.CostEstimate(flops=0, bytes_accessed=int(microseconds * 3.0e6), transcendentals=0)
+
+
 def comm_params(collective_id, megabytes=56):
     return pltpu.CompilerParams(
         collective_id=collective_id,
@@ -587,6 +591,7 @@
             pltpu.SemaphoreType.DMA((3,)),
         ],
         compiler_params=comm_params(collective_id),
+        cost_estimate=cost(100),
         name="weight_gather",
     )(qkv_low, out_low, smalls)
 
@@ -663,6 +668,7 @@
             pltpu.SemaphoreType.DMA,
         ],
         compiler_params=comm_params(collective_id),
+        cost_estimate=cost(45),
         name="token_gather",
     )(block)
 
@@ -675,61 +681,54 @@
     lax.fori_loop(0, rows // step, body, 0)
 
 
+def group_sum(part_ref, out_ref, core_buf, x_buf, send_sem, recv_sem, meanwhile=None):
+    rows, width = part_ref.shape
+    half, quarter = width // 2, width // 4
+    z, y, x, c = place()
+    across, twin = device(z, y, 1 - x, c), device(z, y, x, 1 - c)
+
+    def half_of(cc):
+        return pl.ds(pl.multiple_of(cc * half, half), half)
+
+    def quarter_of(xx, cc):
+        return pl.ds(pl.multiple_of(cc * half + xx * quarter, quarter), quarter)
+
+    first = remote(part_ref.at[:, half_of(1 - c)], core_buf, send_sem.at[0], recv_sem.at[0], twin)
+    first.start()
+    if meanwhile is not None:
+        meanwhile()
+    first.wait_recv()
+    add_to(core_buf, core_buf, part_ref.at[:, half_of(c)], 32)
+    second = remote(
+        core_buf.at[:, pl.ds(pl.multiple_of((1 - x) * quarter, quarter), quarter)],
+        x_buf, send_sem.at[1], recv_sem.at[1], across,
+    )
+    second.start()
+    second.wait_recv()
+    own = out_ref.at[:, quarter_of(x, c)]
+    add_to(own, x_buf, core_buf.at[:, pl.ds(pl.multiple_of(x * quarter, quarter), quarter)], 32)
+    third = remote(own, own, send_sem.at[2], recv_sem.at[2], across)
+    third.start()
+    fourth = remote(own, own, send_sem.at[3], recv_sem.at[3], twin)
+    fourth.start()
+    from_x = out_ref.at[:, quarter_of(1 - x, c)]
+    remote(from_x, from_x, send_sem.at[2], recv_sem.at[2], across).wait_recv()
+    fifth = remote(from_x, from_x, send_sem.at[4], recv_sem.at[4], twin)
+    fifth.start()
+    for index, column in ((3, quarter_of(x, 1 - c)), (4, quarter_of(1 - x, 1 - c))):
+        landing = out_ref.at[:, column]
+        remote(landing, landing, send_sem.at[index], recv_sem.at[index], twin).wait_recv()
+    for copy in (first, second, third, fourth, fifth):
+        copy.wait_send()
+
+
 def tensor_sum(part, collective_id):
     rows, width = part.shape
-    half, quarter = width // 2, width // 4
 
     def kernel(part_ref, out_ref, core_buf, x_buf, send_sem, recv_sem):
         z, y, x, c = place()
-        across, twin = device(z, y, 1 - x, c), device(z, y, x, 1 - c)
-        greet([(across, None), (twin, None)])
-
-        def half_of(cc):
-            return pl.ds(pl.multiple_of(cc * half, half), half)
-
-        def quarter_of(xx, cc):
-            return pl.ds(pl.multiple_of(cc * half + xx * quarter, quarter), quarter)
-
-        first = remote(part_ref.at[:, half_of(1 - c)], core_buf, send_sem.at[0], recv_sem.at[0], twin)
-        first.start()
-        first.wait_recv()
-        base = pl.multiple_of(c * half, half)
-
-        def add_core(r):
-            core_buf[r, :] = (
-                core_buf[r, :].astype(jnp.float32) + part_ref[r, pl.ds(base, half)].astype(jnp.float32)
-            ).astype(jnp.bfloat16)
-
-        add_into(rows, 32, add_core)
-        second = remote(
-            core_buf.at[:, pl.ds(pl.multiple_of((1 - x) * quarter, quarter), quarter)],
-            x_buf, send_sem.at[1], recv_sem.at[1], across,
-        )
-        second.start()
-        second.wait_recv()
-        mine = pl.multiple_of(x * quarter, quarter)
-        out_at = pl.multiple_of(c * half + x * quarter, quarter)
-
-        def add_x(r):
-            out_ref[r, pl.ds(out_at, quarter)] = (
-                core_buf[r, pl.ds(mine, quarter)].astype(jnp.float32) + x_buf[r, :].astype(jnp.float32)
-            ).astype(jnp.bfloat16)
-
-        add_into(rows, 32, add_x)
-        own = out_ref.at[:, quarter_of(x, c)]
-        third = remote(own, own, send_sem.at[2], recv_sem.at[2], across)
-        third.start()
-        fourth = remote(own, own, send_sem.at[3], recv_sem.at[3], twin)
-        fourth.start()
-        from_x = out_ref.at[:, quarter_of(1 - x, c)]
-        remote(from_x, from_x, send_sem.at[2], recv_sem.at[2], across).wait_recv()
-        fifth = remote(from_x, from_x, send_sem.at[4], recv_sem.at[4], twin)
-        fifth.start()
-        for index, column in ((3, quarter_of(x, 1 - c)), (4, quarter_of(1 - x, 1 - c))):
-            landing = out_ref.at[:, column]
-            remote(landing, landing, send_sem.at[index], recv_sem.at[index], twin).wait_recv()
-        for copy in (first, second, third, fourth, fifth):
-            copy.wait_send()
+        greet([(device(z, y, 1 - x, c), None), (device(z, y, x, 1 - c), None)])
+        group_sum(part_ref, out_ref, core_buf, x_buf, send_sem, recv_sem)
 
     return pl.pallas_call(
         kernel,
@@ -737,12 +736,13 @@
         in_specs=[VMEM],
         out_specs=VMEM,
         scratch_shapes=[
-            pltpu.VMEM((rows, half), jnp.bfloat16),
-            pltpu.VMEM((rows, quarter), jnp.bfloat16),
+            pltpu.VMEM((rows, width // 2), jnp.bfloat16),
+            pltpu.VMEM((rows, width // 4), jnp.bfloat16),
             pltpu.SemaphoreType.DMA((5,)),
             pltpu.SemaphoreType.DMA((5,)),
         ],
         compiler_params=comm_params(collective_id, 16),
+        cost_estimate=cost(17),
         name="tensor_sum",
     )(part)
 
@@ -896,6 +896,7 @@
             pltpu.SemaphoreType.DMA((parts + 2, NZ, 3)),
         ],
         compiler_params=comm_params(collective_id),
+        cost_estimate=cost(120),
         name="weight_reduce",
     )(qkv, out, smalls)
 
@@ -1014,6 +1015,7 @@
             pltpu.SemaphoreType.DMA((1, NZ, 3)),
         ],
         compiler_params=comm_params(collective_id),
+        cost_estimate=cost(60),
         name="token_reduce",
     )(part)
 
@@ -1070,8 +1072,782 @@
             pltpu.SemaphoreType.DMA((groups - 1,)),
         ],
         compiler_params=comm_params(collective_id, 16),
+        cost_estimate=cost(10),
         name="gate_exchange",
     )(part)
+
+
+def dot(a, b, dims):
+    return lax.dot_general(a, b, ((dims[:1], dims[1:]), ((), ())), preferred_element_type=jnp.float32)
+
+
+def add_to(target, first, second, step=64):
+    rows = target.shape[0]
+
+    def body(i, carry):
+        r = pl.ds(pl.multiple_of(i * step, step), step)
+        total = first[r, :].astype(jnp.float32) + second[r, :].astype(jnp.float32)
+        target[r, :] = total.astype(target.dtype)
+        return carry
+
+    lax.fori_loop(0, rows // step, body, 0)
+
+
+def expert_layer(hidden_all, grad_out_all, gate_up, down, router_t, chosen_all, collective_id):
+    tokens, width = hidden_all.shape
+    rows = tokens // GROUPS
+    units = down.shape[0]
+    local = 2
+    hidden = units // local
+    experts = router_t.shape[0]
+    half, part, piece = width // 2, width // 4, width // 8
+    tensors = NX * NC
+    steps = GROUPS + 4
+    low = jnp.bfloat16
+    wide = width // 4
+
+    def kernel(
+        h_in, dy_in, gu_ref, down_ref, router_ref, chosen_ref,
+        y_out, dh_out, gates_out, gate_w, up_w, down_w,
+        h, dy, gated, dgu, dx, y_stage, gu_stage, d_stage,
+        core_buf, px_buf, py_buf, qy_buf, qx_buf, z_sum, lo_buf, hi_buf, gate_part, gate_land,
+        in_sem, y_sem, gu_sem, d_sem, core_s, core_r, px_s, px_r, py_s, py_r, qy_s, qy_r, qx_s, qx_r,
+        z_s, z_r, near_s, near_r, far_s, far_r, end_s, end_r,
+    ):
+        z, y, x, c = place()
+        e, t = lax.axis_index("expert"), lax.axis_index("tensor")
+        across, twin, beside = device(z, y, 1 - x, c), device(z, y, x, 1 - c), device(z, 1 - y, x, c)
+        mates = [(e, lax.rem(t + k, tensors)) for k in range(1, tensors)]
+        peers = [(lax.rem(e + k, GROUPS), t) for k in range(1, GROUPS)]
+        greet([(target, None) for target in mates + peers])
+
+        def zz_of(j):
+            return jnp.where(j == 0, 3, jnp.where(j == 1, 0, jnp.where(j == 2, 2, 1)))
+
+        def block_of(i):
+            own = lax.rem(i, 2)
+            return zz_of(lax.div(i, 2)) * NY + jnp.where(own == 1, y, 1 - y)
+
+        def load(i):
+            r = block_rows(block_of(i), rows)
+            return (
+                pltpu.make_async_copy(h_in.at[r, :], h.at[r, :], in_sem.at[0, i]),
+                pltpu.make_async_copy(dy_in.at[r, :], dy.at[r, :], in_sem.at[1, i]),
+            )
+
+        def start_load(i, carry):
+            for copy in load(i):
+                copy.start()
+            return carry
+
+        lax.fori_loop(0, GROUPS, start_load, 0)
+
+        def to_twin(i):
+            b = block_of(i)
+            return remote(
+                dx.at[block_rows(b, rows), pl.ds(pl.multiple_of((1 - c) * half, half), half)],
+                core_buf.at[b], core_s.at[i], core_r.at[i], twin,
+            )
+
+        def p_across(i):
+            b = block_of(i)
+            return remote(
+                core_buf.at[b, :, pl.ds(pl.multiple_of((1 - x) * piece, piece), piece)],
+                px_buf.at[b], px_s.at[i], px_r.at[i], across,
+            )
+
+        def p_beside(j):
+            return remote(px_buf.at[block_of(2 * j)], py_buf.at[j], py_s.at[j], py_r.at[j], beside)
+
+        def q_beside(j):
+            return remote(
+                core_buf.at[block_of(2 * j), :, pl.ds(part, part)], qy_buf.at[j], qy_s.at[j], qy_r.at[j], beside
+            )
+
+        def q_across(j):
+            return remote(
+                qy_buf.at[j, :, pl.ds(pl.multiple_of((1 - x) * piece, piece), piece)],
+                qx_buf.at[j], qx_s.at[j], qx_r.at[j], across,
+            )
+
+        def up(j, s):
+            return remote(z_sum.at[s, j], lo_buf.at[s, j], z_s.at[0, s, j], z_r.at[0, s, j], device(z + 1, y, x, c))
+
+        def down_z(j, s):
+            return remote(z_sum.at[s, j], hi_buf.at[s, j], z_s.at[1, s, j], z_r.at[1, s, j], device(z - 1, y, x, c))
+
+        def take_twin(i):
+            to_twin(i).wait_recv()
+            b = block_of(i)
+            mine = core_buf.at[b]
+            add_to(mine, mine, dx.at[block_rows(b, rows), pl.ds(pl.multiple_of(c * half, half), half)], 32)
+            p_across(i).start()
+            pl.when(lax.rem(i, 2) == 0)(lambda: q_beside(lax.div(i, 2)).start())
+
+        def take_p_across(i):
+            p_across(i).wait_recv()
+            b = block_of(i)
+            add_to(
+                px_buf.at[b], px_buf.at[b],
+                core_buf.at[b, :, pl.ds(pl.multiple_of(x * piece, piece), piece)],
+            )
+
+        def take_q_beside(j):
+            q_beside(j).wait_recv()
+            add_to(qy_buf.at[j], qy_buf.at[j], core_buf.at[block_of(2 * j + 1), :, pl.ds(part, part)])
+            q_across(j).start()
+
+        def take_q_across(j):
+            q_across(j).wait_recv()
+            add_to(
+                z_sum.at[1, j], qx_buf.at[j], qy_buf.at[j, :, pl.ds(pl.multiple_of(x * piece, piece), piece)]
+            )
+
+        def take_p_beside(j):
+            p_beside(j).wait_recv()
+            add_to(z_sum.at[0, j], py_buf.at[j], px_buf.at[block_of(2 * j + 1)])
+
+        def hop(j, k):
+            zz = zz_of(j)
+
+            def upward():
+                for s in range(2):
+                    if k > 0:
+                        up(j, s).wait_recv()
+                        add_to(z_sum.at[s, j], z_sum.at[s, j], lo_buf.at[s, j])
+                    up(j, s).start()
+
+            def downward():
+                for s in range(2):
+                    if k > 0:
+                        down_z(j, s).wait_recv()
+                        add_to(z_sum.at[s, j], z_sum.at[s, j], hi_buf.at[s, j])
+                    down_z(j, s).start()
+
+            pl.when((z < zz) & (z == k))(upward)
+            pl.when((z > zz) & (NZ - 1 - z == k))(downward)
+
+        def front(i):
+            for copy in load(i):
+                copy.wait()
+            b = block_of(i)
+            r = block_rows(b, rows)
+            rows_h, rows_dy = h[r, :], dy[r, :]
+            logits = dot(rows_h, router_ref[...], (1, 1))
+            shifted = jnp.exp(logits - jnp.max(logits, axis=-1, keepdims=True))
+            probs = shifted / jnp.sum(shifted, axis=-1, keepdims=True) * chosen_ref[r, :]
+            lane = lax.broadcasted_iota(jnp.int32, probs.shape, 1)
+            line = lax.broadcasted_iota(jnp.int32, (rows, 128), 1)
+            found = jnp.zeros((rows, 128), jnp.float32)
+            for expert in range(local):
+                at, up_at = pl.ds(expert * hidden, hidden), pl.ds((local + expert) * hidden, hidden)
+                gate = jnp.sum(jnp.where(lane == e * local + expert, probs, 0.0), axis=-1, keepdims=True)
+                pre = dot(rows_h, gu_ref[:, at], (1, 0))
+                scale = dot(rows_h, gu_ref[:, up_at], (1, 0))
+                back = dot(rows_dy, down_ref[at, :], (1, 1))
+                sigmoid = jax.nn.sigmoid(pre)
+                swish = pre * sigmoid
+                active = swish * scale
+                gated[r, at] = (active * gate).astype(low)
+                found = jnp.where(line == expert, jnp.sum(active * back, axis=-1, keepdims=True), found)
+                back = back * gate
+                dgu[r, at] = (back * scale * sigmoid * (1.0 + pre * (1.0 - sigmoid))).astype(low)
+                dgu[r, up_at] = (back * swish).astype(low)
+            gate_part[b] = jnp.transpose(found)[:8, :]
+
+        def y_copy(i):
+            return pltpu.make_async_copy(
+                y_stage.at[lax.rem(i, 2)], y_out.at[block_rows(block_of(i), rows), :], y_sem.at[lax.rem(i, 2)]
+            )
+
+        def rear(i):
+            r = block_rows(block_of(i), rows)
+            slot = lax.rem(i, 2)
+
+            def columns(k, carry):
+                at = pl.ds(pl.multiple_of(k * wide, wide), wide)
+                dx[r, at] = dot(dgu[r, :], gu_ref[at, :], (1, 1)).astype(low)
+                return carry
+
+            lax.fori_loop(0, width // wide, columns, 0)
+            to_twin(i).start()
+            pl.when(i >= 2)(lambda: y_copy(i - 2).wait())
+
+            def y_columns(k, carry):
+                at = pl.ds(pl.multiple_of(k * wide, wide), wide)
+                y_stage[slot, :, at] = dot(gated[r, :], down_ref[:, at], (1, 0)).astype(low)
+                return carry
+
+            lax.fori_loop(0, width // wide, y_columns, 0)
+            y_copy(i).start()
+
+        tiles = width // piece // 4
+        d_width = width // 4
+
+        def gu_copies(n):
+            slot = lax.rem(n, 2)
+            at = pl.ds(pl.multiple_of(n * piece, piece), piece)
+            return [
+                pltpu.make_async_copy(
+                    gu_stage.at[slot, :, pl.ds(k * hidden, hidden)],
+                    (gate_w if k < local else up_w).at[k % local, at, :],
+                    gu_sem.at[slot, k],
+                )
+                for k in range(2 * local)
+            ]
+
+        def d_copies(n):
+            slot = lax.rem(n, 2)
+            at = pl.ds(pl.multiple_of(n * d_width, d_width), d_width)
+            return [
+                pltpu.make_async_copy(
+                    d_stage.at[slot, pl.ds(k * hidden, hidden), :], down_w.at[k, :, at], d_sem.at[slot, k]
+                )
+                for k in range(local)
+            ]
+
+        def each(copies, what):
+            for copy in copies:
+                getattr(copy, what)()
+
+        def weight_grads(q):
+            def tile(k, carry):
+                n = q * tiles + k
+                pl.when(n >= 2)(lambda: each(gu_copies(n - 2), "wait"))
+                at = pl.ds(pl.multiple_of(n * piece, piece), piece)
+                gu_stage[lax.rem(n, 2)] = dot(h[:, at], dgu[...], (0, 0))
+                each(gu_copies(n), "start")
+                return carry
+
+            lax.fori_loop(0, tiles, tile, 0)
+            pl.when(q >= 2)(lambda: each(d_copies(q - 2), "wait"))
+            at = pl.ds(pl.multiple_of(q * d_width, d_width), d_width)
+            d_stage[lax.rem(q, 2)] = dot(gated[...], dy[:, at], (0, 0))
+            each(d_copies(q), "start")
+
+        near = [
+            remote(gate_part, gate_land.at[k], near_s.at[k], near_r.at[k], mates[k])
+            for k in range(tensors - 1)
+        ]
+
+        def far(k):
+            return remote(
+                gate_land.at[tensors - 1, lax.rem(e + k, GROUPS)], gates_out.at[e],
+                far_s.at[k - 1], far_r.at[k - 1], peers[k - 1],
+            )
+
+        def sum_near():
+            for copy in near:
+                copy.wait_recv()
+            total = gate_part[...]
+            for k in range(tensors - 1):
+                total = total + gate_land[k]
+            gate_land[tensors - 1] = total
+            for k in range(1, GROUPS):
+                far(k).start()
+            gates_out[e] = gate_land[tensors - 1, e]
+
+        def step(i, carry):
+            j_even, j_odd = lax.div(i, 2) - 1, lax.div(i - 1, 2) - 1
+            even = lax.rem(i, 2) == 0
+            pl.when(i < GROUPS)(lambda: front(i))
+            pl.when((i >= 1) & (i <= GROUPS))(lambda: take_twin(i - 1))
+            pl.when(even & (i >= 2) & (i <= GROUPS))(lambda: take_q_beside(j_even))
+
+            def late():
+                take_p_across(i - 2)
+                take_q_across(j_odd)
+
+            pl.when((lax.rem(i, 2) == 1) & (i >= 3) & (i <= GROUPS + 1))(late)
+            pl.when(i == GROUPS)(lambda: each(near, "start"))
+            pl.when(i == GROUPS + 1)(sum_near)
+            pl.when(i < GROUPS)(lambda: rear(i))
+            pl.when(i >= GROUPS)(lambda: weight_grads(i - GROUPS))
+
+            def pass_p():
+                take_p_across(i - 2)
+                p_beside(j_even).start()
+
+            pl.when(even & (i >= 2) & (i <= GROUPS))(pass_p)
+
+            def join():
+                take_p_beside(j_odd)
+                hop(j_odd, 0)
+
+            pl.when((lax.rem(i, 2) == 1) & (i >= 3) & (i <= GROUPS + 1))(join)
+            pl.when(even & (i >= 4) & (i <= GROUPS + 2))(lambda: hop(j_even - 1, 1))
+            pl.when((lax.rem(i, 2) == 1) & (i >= 5) & (i <= GROUPS + 3))(lambda: hop(j_odd - 1, 2))
+            return carry
+
+        lax.fori_loop(0, steps, step, 0)
+
+        def columns_of(s, xx, cc):
+            return pl.ds(pl.multiple_of(cc * half + s * part + xx * piece, piece), piece)
+
+        mine = jnp.where(z == 3, 0, jnp.where(z == 0, 1, jnp.where(z == 2, 2, 3)))
+        for s in range(2):
+            def below(s=s):
+                up(mine, s).wait_recv()
+                add_to(z_sum.at[s, mine], z_sum.at[s, mine], lo_buf.at[s, mine])
+
+            def above(s=s):
+                down_z(mine, s).wait_recv()
+                add_to(z_sum.at[s, mine], z_sum.at[s, mine], hi_buf.at[s, mine])
+
+            pl.when(z > 0)(below)
+            pl.when(z < NZ - 1)(above)
+            own = dh_out.at[:, columns_of(s, x, c)]
+
+            def keep(k, carry, s=s, own=own):
+                r = pl.ds(pl.multiple_of(k * 64, 64), 64)
+                own[r, :] = z_sum[s, mine, r, :]
+                return carry
+
+            lax.fori_loop(0, rows // 64, keep, 0)
+            remote(own, own, end_s.at[0, s], end_r.at[0, s], across).start()
+            remote(own, own, end_s.at[1, s], end_r.at[1, s], twin).start()
+        for s in range(2):
+            there = dh_out.at[:, columns_of(s, 1 - x, c)]
+            remote(there, there, end_s.at[0, s], end_r.at[0, s], across).wait_recv()
+            remote(there, there, end_s.at[2, s], end_r.at[2, s], twin).start()
+        for s in range(2):
+            for k, xx in ((1, x), (2, 1 - x)):
+                there = dh_out.at[:, columns_of(s, xx, 1 - c)]
+                remote(there, there, end_s.at[k, s], end_r.at[k, s], twin).wait_recv()
+            for k, target in ((0, across), (1, twin), (2, twin)):
+                there = dh_out.at[:, columns_of(s, 1 - x if k == 2 else x, c)]
+                remote(there, there, end_s.at[k, s], end_r.at[k, s], target).wait_send()
+        for k in range(1, GROUPS):
+            there = gates_out.at[lax.rem(e + GROUPS - k, GROUPS)]
+            remote(there, there, far_s.at[k - 1], far_r.at[k - 1], peers[k - 1]).wait_recv()
+            far(k).wait_send()
+        each(near, "wait_send")
+
+        def drain(i, carry):
+            to_twin(i).wait_send()
+            p_across(i).wait_send()
+            return carry
+
+        lax.fori_loop(0, GROUPS, drain, 0)
+
+        def drain_pair(j, carry):
+            p_beside(j).wait_send()
+            q_beside(j).wait_send()
+            q_across(j).wait_send()
+            for s in range(2):
+                pl.when(z < zz_of(j))(lambda s=s: up(j, s).wait_send())
+                pl.when(z > zz_of(j))(lambda s=s: down_z(j, s).wait_send())
+            return carry
+
+        lax.fori_loop(0, NZ, drain_pair, 0)
+        for k in range(2):
+            y_copy(GROUPS - 2 + k).wait()
+            each(gu_copies(4 * tiles - 2 + k), "wait")
+            each(d_copies(2 + k), "wait")
+
+    shape = jax.ShapeDtypeStruct
+    dma = pltpu.SemaphoreType.DMA
+    f32 = jnp.float32
+    return pl.pallas_call(
+        kernel,
+        out_shape=(
+            shape((tokens, width), low),
+            shape((rows, width), low),
+            shape((GROUPS, 8, rows), f32),
+            shape((local, width, hidden), f32),
+            shape((local, width, hidden), f32),
+            shape((local, hidden, width), f32),
+        ),
+        in_specs=[HBM, HBM, VMEM, VMEM, VMEM, VMEM],
+        out_specs=(HBM, VMEM, VMEM, HBM, HBM, HBM),
+        scratch_shapes=[
+            pltpu.VMEM((tokens, width), low),
+            pltpu.VMEM((tokens, width), low),
+            pltpu.VMEM((tokens, units), low),
+            pltpu.VMEM((tokens, 2 * units), low),
+            pltpu.VMEM((tokens, width), low),
+            pltpu.VMEM((2, rows, width), low),
+            pltpu.VMEM((2, piece, 2 * units), f32),
+            pltpu.VMEM((2, units, width // 4), f32),
+            pltpu.VMEM((GROUPS, rows, half), low),
+            pltpu.VMEM((GROUPS, rows, piece), low),
+            pltpu.VMEM((NZ, rows, piece), low),
+            pltpu.VMEM((NZ, rows, part), low),
+            pltpu.VMEM((NZ, rows, piece), low),
+            pltpu.VMEM((2, NZ, rows, piece), low),
+            pltpu.VMEM((2, NZ, rows, piece), low),
+            pltpu.VMEM((2, NZ, rows, piece), low),
+            pltpu.VMEM((GROUPS, 8, rows), f32),
+            pltpu.VMEM((tensors, GROUPS, 8, rows), f32),
+            dma((2, GROUPS)), dma((2,)), dma((2, 2 * local)), dma((2, local)),
+            dma((GROUPS,)), dma((GROUPS,)), dma((GROUPS,)), dma((GROUPS,)),
+            dma((NZ,)), dma((NZ,)), dma((NZ,)), dma((NZ,)), dma((NZ,)), dma((NZ,)),
+            dma((2, 2, NZ)), dma((2, 2, NZ)),
+            dma((tensors - 1,)), dma((tensors - 1,)), dma((GROUPS - 1,)), dma((GROUPS - 1,)),
+            dma((3, 2)), dma((3, 2)),
+        ],
+        compiler_params=comm_params(collective_id, 62),
+        cost_estimate=cost(80),
+        name="expert_layer",
+    )(hidden_all, grad_out_all, gate_up, down, router_t, chosen_all)
+
+
+def exchange_rows(value, part_ref, land_ref, send_sem, recv_sem, mates):
+    rows = value.shape[0]
+    line = lax.broadcasted_iota(jnp.int32, (rows, 128), 1)
+    part_ref[...] = jnp.transpose(jnp.where(line == 0, value, 0.0))[:8, :]
+    for k, mate in enumerate(mates):
+        remote(part_ref, land_ref.at[k], send_sem.at[k], recv_sem.at[k], mate).start()
+
+
+def exchanged_rows(part_ref, land_ref, send_sem, recv_sem, mates):
+    total = part_ref[...]
+    for k, mate in enumerate(mates):
+        remote(part_ref, land_ref.at[k], send_sem.at[k], recv_sem.at[k], mate).wait_recv()
+    for k in range(len(mates)):
+        total = total + land_ref[k]
+    rows = part_ref.shape[1]
+    tall = jnp.concatenate([total, jnp.zeros((120, rows), jnp.float32)], axis=0)
+    return jnp.transpose(tall)[:, :1]
+
+
+def drain_rows(part_ref, land_ref, send_sem, recv_sem, mates):
+    for k, mate in enumerate(mates):
+        remote(part_ref, land_ref.at[k], send_sem.at[k], recv_sem.at[k], mate).wait_send()
+
+
+def turn(value, cosine, sine):
+    return value * cosine + pltpu.roll(value, HEAD // 2, 1) * sine
+
+
+def project(tokens, w_qkv, smalls, cosine, sine, collective_id):
+    rows, width = tokens.shape
+    parts, depth, columns = w_qkv.shape
+    heads = columns // HEAD
+    tensors = NX * NC
+    back = WINDOW // rows
+    low, f32 = jnp.bfloat16, jnp.float32
+    QUERY, KEY, VALUE, SMALL = 0, 1, 2, 3
+
+    def kernel(
+        tok_ref, w_ref, small_ref, cos_ref, sin_ref,
+        w_all, small_all, h1_ref, raw_ref, scale_ref, q_ref, context,
+        own_w, weights, total, part_k, land_k, part_q, land_q,
+        send_sem, recv_sem, out_sem, small_sem, ks_s, ks_r, qs_s, qs_r, c_s, c_r,
+    ):
+        z, y, x, c = place()
+        e, t = lax.axis_index("expert"), lax.axis_index("tensor")
+        mates = [(e, lax.rem(t + k, tensors)) for k in range(1, tensors)]
+        beside, above = device(z, 1 - y, x, c), device(z + 1, y, x, c)
+        views = [
+            lambda b: weights.at[QUERY, block_rows(b, depth), :],
+            lambda b: weights.at[KEY, block_rows(b, depth), :],
+            lambda b: weights.at[VALUE, block_rows(b, depth), :],
+            lambda b: small_all.at[b],
+        ]
+        line = LineGather(
+            [SMALL, VALUE, KEY, QUERY], [own_w.at[0], own_w.at[1], own_w.at[2], small_ref], views,
+            send_sem, recv_sem,
+        )
+        greet(line.partners() + [(mate, None) for mate in mates])
+        line.start(SMALL, 0)
+        for part in (VALUE, KEY, QUERY):
+            def cast(i, carry, part=part):
+                r = pl.ds(pl.multiple_of(i * 32, 32), 32)
+                own_w[part, r, :] = w_ref[part, r, :].astype(low)
+                return carry
+
+            lax.fori_loop(0, depth // 32, cast, 0)
+            if part != QUERY:
+                line.start(part, 0)
+
+        def square(i, carry):
+            r = pl.ds(pl.multiple_of(i * 32, 32), 32)
+            value = tok_ref[r, :].astype(f32)
+            scale_ref[r, 0:1] = lax.rsqrt(jnp.mean(value * value, axis=-1, keepdims=True) + EPS)
+            return carry
+
+        lax.fori_loop(0, rows // 32, square, 0)
+        total[...] = jnp.zeros_like(total)
+        own_small = pltpu.make_async_copy(small_ref, small_all.at[line.block(0)], small_sem)
+        own_small.start()
+
+        def use(stream, rel):
+            b = line.block(rel)
+            at = pl.ds(pl.multiple_of(b * depth, depth), depth)
+            if stream == SMALL:
+                gain = small_ref[0:1, :] if rel == 0 else small_all[b, 0:1, :]
+                h1_ref[:, at] = (tok_ref[:, at].astype(f32) * scale_ref[:, 0:1] * gain).astype(low)
+                return
+            block = own_w[stream] if rel == 0 else weights[stream, block_rows(b, depth), :]
+            total[stream] += dot(h1_ref[:, at], block, (1, 0))
+
+        def event(stream, rel):
+            def body():
+                line.arrive(stream, rel)
+                if rel < 7:
+                    marks = len(line.pending)
+                    line.start(stream, rel)
+                    late = line.pending[marks:]
+                    del line.pending[marks:]
+                    line.finish_later(late, rel)
+                use(stream, rel)
+            run_if(line.exists(rel), body)
+
+        use(SMALL, 0)
+        use(VALUE, 0)
+        own_small.wait()
+        use(KEY, 0)
+        early, late = [7, 1, 4, 8, 11, 2, 5], [9, 12, 3, 6, 10, 13]
+        for rel in early:
+            event(SMALL, rel)
+            event(VALUE, rel)
+        line.start(QUERY, 0)
+        for rel in late:
+            event(SMALL, rel)
+            event(VALUE, rel)
+
+        def context_copy(which, k):
+            if k == 2:
+                source, target = 0, above
+            elif k == 4:
+                source, target = 2, above
+            else:
+                source, target = jnp.where(y == 0, k - 1, k + 1), beside
+            return remote(
+                context.at[source, which], context.at[k, which], c_s.at[which, k], c_r.at[which, k], target
+            )
+
+        sends = {2: z < NZ - 1, 4: (z >= 1) & (z < NZ - 1), 1: (y == 0) | (z >= 1), 3: z >= 1 + y}
+        takes = {2: z >= 1, 4: z >= 2, 1: (y == 1) | (z >= 1), 3: z >= 2 - y}
+
+        def context_send(which, k):
+            run_if(sends[k], lambda: context_copy(which, k).start())
+
+        def context_take(which, k):
+            run_if(takes[k], lambda: context_copy(which, k).wait_recv())
+
+        for k in range(1, back + 1):
+            def clear(k=k):
+                context[k] = jnp.zeros_like(context[k])
+            run_if(jnp.logical_not(takes[k]), clear)
+
+        context[0, 1] = total[VALUE].astype(low)
+        context_send(1, 2)
+        run_if(y == 0, lambda: context_copy(1, 1).start())
+        for rel in early:
+            event(KEY, rel)
+        for rel in late:
+            event(KEY, rel)
+        key_raw = total[KEY]
+        raw_ref[1] = key_raw
+        exchange_rows(jnp.sum(key_raw * key_raw, axis=-1, keepdims=True), part_k, land_k, ks_s, ks_r, mates)
+        use(QUERY, 0)
+        for rel in early[:3]:
+            event(QUERY, rel)
+
+        key_scale = lax.rsqrt(exchanged_rows(part_k, land_k, ks_s, ks_r, mates) / width + EPS)
+        scale_ref[:, 2:3] = key_scale
+        slices = HEAD // GROUPS
+        gains = []
+        for which in range(2):
+            per_head = []
+            for head in range(heads):
+                start = (which * heads + head) * slices
+                per_head.append(
+                    jnp.concatenate([small_all[b, 2:3, start : start + slices] for b in range(GROUPS)], axis=1)
+                )
+            gains.append(per_head)
+
+        def rotated(which, scale, store):
+            for head in range(heads):
+                at = pl.ds(head * HEAD, HEAD)
+                value = total[which, :, at] * scale * gains[which][head]
+                store(at, turn(value, cos_ref[...], sin_ref[...]).astype(low))
+
+        def store_key(at, value):
+            context[0, 0, :, at] = value
+
+        rotated(KEY, key_scale, store_key)
+        context_send(0, 2)
+        run_if(y == 0, lambda: context_copy(0, 1).start())
+
+        def relay_two(which):
+            context_take(which, 2)
+            context_send(which, 4)
+            run_if((y == 1) & (z >= 1), lambda: context_copy(which, 1).start())
+            run_if((y == 0) & sends[3], lambda: context_copy(which, 3).start())
+
+        def relay_four(which):
+            context_take(which, 4)
+            run_if((y == 1) & sends[3], lambda: context_copy(which, 3).start())
+
+        relay_two(1)
+        for rel in early[3:]:
+            event(QUERY, rel)
+        relay_four(1)
+        for rel in late[:4]:
+            event(QUERY, rel)
+        relay_two(0)
+        for rel in late[4:]:
+            event(QUERY, rel)
+        query_raw = total[QUERY]
+        raw_ref[0] = query_raw
+        exchange_rows(jnp.sum(query_raw * query_raw, axis=-1, keepdims=True), part_q, land_q, qs_s, qs_r, mates)
+        for part in range(parts):
+            weights[part, block_rows(line.block(0), depth), :] = own_w[part]
+        keep = pltpu.make_async_copy(weights, w_all, out_sem)
+        keep.start()
+        relay_four(0)
+        query_scale = lax.rsqrt(exchanged_rows(part_q, land_q, qs_s, qs_r, mates) / width + EPS)
+        scale_ref[:, 1:2] = query_scale
+
+        def store_query(at, value):
+            q_ref[:, at] = value
+
+        rotated(QUERY, query_scale, store_query)
+        for which in (1, 0):
+            for k in (1, 3):
+                context_take(which, k)
+        line.finish()
+        for which in range(2):
+            for k in range(1, back + 1):
+                run_if(sends[k], lambda which=which, k=k: context_copy(which, k).wait_send())
+        drain_rows(part_k, land_k, ks_s, ks_r, mates)
+        drain_rows(part_q, land_q, qs_s, qs_r, mates)
+        keep.wait()
+
+    shape, dma = jax.ShapeDtypeStruct, pltpu.SemaphoreType.DMA
+    return pl.pallas_call(
+        kernel,
+        out_shape=(
+            shape((parts, depth * GROUPS, columns), low),
+            shape((GROUPS,) + smalls.shape, f32),
+            shape((rows, width), low),
+            shape((2, rows, columns), f32),
+            shape((rows, 128), f32),
+            shape((rows, columns), low),
+            shape((back + 1, 2, rows, columns), low),
+        ),
+        in_specs=[VMEM] * 5,
+        out_specs=(HBM,) + (VMEM,) * 6,
+        scratch_shapes=[
+            pltpu.VMEM((parts, depth, columns), low),
+            pltpu.VMEM((parts, depth * GROUPS, columns), low),
+            pltpu.VMEM((parts, rows, columns), f32),
+            pltpu.VMEM((8, rows), f32),
+            pltpu.VMEM((tensors - 1, 8, rows), f32),
+            pltpu.VMEM((8, rows), f32),
+            pltpu.VMEM((tensors - 1, 8, rows), f32),
+            dma((4, 7, 3)), dma((4, 14)), dma, dma,
+            dma((tensors - 1,)), dma((tensors - 1,)), dma((tensors - 1,)), dma((tensors - 1,)),
+            dma((2, back + 1)), dma((2, back + 1)),
+        ],
+        compiler_params=comm_params(collective_id, 48),
+        cost_estimate=cost(100),
+        name="project",
+    )(tokens, w_qkv, smalls, cosine, sine)
+
+
+def attend(query, context, segment_query, segment_keys, tokens, out_low, gain, collective_id):
+    rows, columns = query.shape
+    width = tokens.shape[1]
+    blocks = context.shape[0]
+    heads = columns // HEAD
+    half, quarter = width // 2, width // 4
+    low, f32 = jnp.bfloat16, jnp.float32
+
+    def kernel(
+        q_ref, context_ref, sq_ref, sk_ref, tok_ref, out_ref, gain_ref,
+        o_ref, lse_ref, x1_ref, h2_ref, scale_ref,
+        part, full, core_buf, x_buf, send_sem, recv_sem,
+    ):
+        z, y, x, c = place()
+        across, twin = device(z, y, 1 - x, c), device(z, y, x, 1 - c)
+        greet([(across, None), (twin, None)])
+        row = lax.broadcasted_iota(jnp.int32, (rows, rows), 0)
+        column = lax.broadcasted_iota(jnp.int32, (rows, rows), 1)
+        allowed = []
+        for k in range(blocks):
+            distance = row - column + k * rows
+            allowed.append(
+                (sq_ref[...] == sk_ref[k : k + 1, :]) & (distance >= 0) & (distance < WINDOW)
+            )
+        line = lax.broadcasted_iota(jnp.int32, (rows, 128), 1)
+        lse = jnp.zeros((rows, 128), f32)
+        for head in range(heads):
+            at = pl.ds(head * HEAD, HEAD)
+            scores = [
+                jnp.where(
+                    allowed[k], dot(q_ref[:, at], context_ref[k, 0, :, at], (1, 1)) * HEAD ** (-0.5), -1e30
+                )
+                for k in range(blocks)
+            ]
+            largest = scores[0]
+            for k in range(1, blocks):
+                largest = jnp.maximum(largest, scores[k])
+            largest = jnp.max(largest, axis=-1, keepdims=True)
+            weights = [jnp.exp(s - largest) for s in scores]
+            amount = weights[0]
+            for k in range(1, blocks):
+                amount = amount + weights[k]
+            amount = jnp.sum(amount, axis=-1, keepdims=True)
+            inverse = 1.0 / amount
+            value = jnp.zeros((rows, HEAD), f32)
+            for k in range(blocks):
+                value = value + dot((weights[k] * inverse).astype(low), context_ref[k, 1, :, at], (1, 0))
+            o_ref[:, at] = value.astype(low)
+            lse = jnp.where(line == head, largest + jnp.log(amount), lse)
+        lse_ref[...] = lse
+
+        def half_of(cc):
+            return pl.ds(pl.multiple_of(cc * half, half), half)
+
+        def fill(cc):
+            def body(k, carry):
+                at = pl.ds(pl.multiple_of(cc * half + k * quarter, quarter), quarter)
+                part[:, at] = dot(o_ref[...], out_ref[:, at], (1, 0)).astype(low)
+                return carry
+
+            lax.fori_loop(0, 2, body, 0)
+
+        fill(1 - c)
+        group_sum(part, full, core_buf, x_buf, send_sem, recv_sem, lambda: fill(c))
+
+        def norm(i, carry):
+            r = pl.ds(pl.multiple_of(i * 32, 32), 32)
+            value = tok_ref[r, :].astype(f32) + full[r, :].astype(f32)
+            scale = lax.rsqrt(jnp.mean(value * value, axis=-1, keepdims=True) + EPS)
+            x1_ref[r, :] = value
+            scale_ref[r, :] = jnp.broadcast_to(scale, (32, 128))
+            h2_ref[r, :] = (value * scale * gain_ref[...]).astype(low)
+            return carry
+
+        lax.fori_loop(0, rows // 32, norm, 0)
+
+    shape, dma = jax.ShapeDtypeStruct, pltpu.SemaphoreType.DMA
+    return pl.pallas_call(
+        kernel,
+        out_shape=(
+            shape((rows, columns), low),
+            shape((rows, 128), f32),
+            shape((rows, width), f32),
+            shape((rows, width), low),
+            shape((rows, 128), f32),
+        ),
+        in_specs=[VMEM] * 7,
+        out_specs=(VMEM,) * 5,
+        scratch_shapes=[
+            pltpu.VMEM((rows, width), low),
+            pltpu.VMEM((rows, width), low),
+            pltpu.VMEM((rows, half), low),
+            pltpu.VMEM((rows, quarter), low),
+            dma((5,)), dma((5,)),
+        ],
+        compiler_params=comm_params(collective_id, 40),
+        cost_estimate=cost(40),
+        name="attend",
+    )(query, context, segment_query, segment_keys, tokens, out_low, gain)
 
 
 def fast_shards(
@@ -1106,28 +1882,37 @@
         routes[:, :, None] == jnp.arange(experts, dtype=jnp.int32)[None, None, :], axis=1
     ).astype(jnp.float32)
     qk_row = qk_gain.reshape(1, -1)
+
+    def rounded(v):
+        return lax.reduce_precision(v, 8, 7)
+
     smalls = jnp.concatenate(
         [
-            attn_gain[None, :],
-            ffn_gain[None, :],
-            jnp.pad(qk_row, ((0, 0), (0, row_count - qk_row.shape[1]))),
+            rounded(attn_gain)[None, :],
+            rounded(ffn_gain)[None, :],
+            jnp.pad(rounded(qk_row), ((0, 0), (0, row_count - qk_row.shape[1]))),
             jnp.zeros((5, row_count), jnp.float32),
             w_router.T,
             chosen.T,
         ],
         axis=0,
     )
-    qkv_low, out_low, small_all = weight_gather(
-        w_qkv.astype(low), w_attn_out.astype(low), smalls, 0
-    )
-
-    def rounded(v):
-        return v.astype(low).astype(jnp.float32)
-
-    gain_one_f = rounded(small_all[:, 0]).reshape(model_width)
-    gain_two_f = rounded(small_all[:, 1]).reshape(model_width)
+    global_rows = device_index * row_count + jnp.arange(row_count, dtype=jnp.int32)
+    cosine_table, sine_table = angles(global_rows % SEQ, HEAD)
+    wide_cosine = jnp.concatenate([cosine_table[:, 0], cosine_table[:, 0]], axis=1)
+    wide_sine = jnp.concatenate([-sine_table[:, 0], sine_table[:, 0]], axis=1)
+    grad_out_piece = lax.dynamic_slice_in_dim(out_grad, tensor_index * quarter, quarter, axis=1)
+    grad_out_rows = lax.all_gather(grad_out_piece, "expert", axis=0, tiled=True)
+    out_low = lax.all_gather(w_attn_out.astype(low), "expert", axis=1, tiled=True)
+    qkv_low, small_all, hidden_one, raw, scales, query_low, context_blocks = project(
+        tokens_in, w_qkv, smalls, wide_cosine, wide_sine, 0
+    )
+    grad_out_rows, query_low = lax.optimization_barrier((grad_out_rows, query_low))
+    grad_out_all = lax.all_gather(grad_out_rows, "tensor", axis=1, tiled=True)
+    gain_one_f = small_all[:, 0].reshape(model_width)
+    gain_two_f = small_all[:, 1].reshape(model_width)
     qk_gains = (
-        rounded(small_all[:, 2, : qk_row.shape[1]])
+        small_all[:, 2, : qk_row.shape[1]]
         .reshape(groups, 2, heads_here, HEAD // groups)
         .transpose(1, 2, 0, 3)
         .reshape(2, local_width)
@@ -1136,47 +1921,35 @@
     chosen_all = small_all[:, 8 + experts : 8 + 2 * experts].transpose(0, 2, 1).reshape(
         groups * row_count, experts
     )
-    grad_out_all = token_gather(out_grad, 1)
-
+    segment_window = lax.dynamic_slice_in_dim(
+        jnp.concatenate([jnp.full((WINDOW,), -1, jnp.int32), segments]),
+        device_index * row_count, (hop_count + 1) * row_count,
+    )
+    segment_query = segment_window[WINDOW:]
+    segment_keys = segment_window.reshape(hop_count + 1, row_count)[::-1]
+    attended, log_sums, residual, hidden_two, scale_two_wide = attend(
+        query_low, context_blocks, segment_query[:, None], segment_keys, tokens_in, out_low,
+        gain_two_f[None, :], 2,
+    )
+    scale_one, query_scale, key_scale = scales[:, 0:1], scales[:, 1:2], scales[:, 2:3]
+    scale_two = scale_two_wide[:, :1]
     tokens_f = tokens_in.astype(jnp.float32)
-    scale_one = lax.rsqrt(jnp.mean(tokens_f * tokens_f, axis=-1, keepdims=True) + EPS)
-    hidden_one = (tokens_f * scale_one * gain_one_f).astype(low)
-    projected = jnp.einsum("td,jde->jte", hidden_one, qkv_low, preferred_element_type=jnp.float32)
-    query_raw = projected[0]
-    key_raw = projected[1]
-    query_sq, key_sq = lax.psum(
-        (jnp.sum(query_raw * query_raw, axis=-1), jnp.sum(key_raw * key_raw, axis=-1)), "tensor"
-    )
-    query_scale = lax.rsqrt(query_sq / model_width + EPS)[:, None]
-    key_scale = lax.rsqrt(key_sq / model_width + EPS)[:, None]
+    query_raw, key_raw = raw[0], raw[1]
     normed_query = query_raw * query_scale
     normed_key = key_raw * key_scale
-    global_rows = device_index * row_count + jnp.arange(row_count, dtype=jnp.int32)
-    cosine_table, sine_table = angles(global_rows % SEQ, HEAD)
-    query_low = rotate(
-        (normed_query * qk_gains[0]).reshape(row_count, heads_here, HEAD), cosine_table, sine_table
-    ).astype(low)
-    key_low = rotate(
-        (normed_key * qk_gains[1]).reshape(row_count, heads_here, HEAD), cosine_table, sine_table
-    ).astype(low)
-    value_low = projected[2].astype(low).reshape(row_count, heads_here, HEAD)
-    own_pair = jnp.stack([key_low, value_low])
-    earlier = []
-    for steps_back in range(hop_count, 0, -1):
-        earlier.append(from_behind(own_pair, "expert", steps_back))
-    context = jnp.concatenate(earlier + [own_pair], axis=1)
+    normed_two = residual * scale_two
+    query_low = query_low.reshape(row_count, heads_here, HEAD)
+    context = (
+        context_blocks[::-1].transpose(1, 0, 2, 3).reshape(2, -1, heads_here, HEAD)
+    )
     key_rows = (device_index - hop_count) * row_count + jnp.arange(
         (hop_count + 1) * row_count, dtype=jnp.int32
     )
-    segment_keys = segments[jnp.maximum(key_rows, 0)]
-    segment_query = segments[global_rows]
     distance = global_rows[:, None] - key_rows[None, :]
     allowed = (
-        (key_rows[None, :] >= 0)
-        & (segment_query[:, None] == segment_keys[None, :])
-        & (distance >= 0)
-        & (distance < WINDOW)
-    )
+        (segment_query[:, None] == segment_window[None, :]) & (distance >= 0) & (distance < WINDOW)
+    )
+    log_total = log_sums[:, :heads_here].T[:, :, None]
 
     def score_block():
         raw_scores = (
@@ -1185,25 +1958,6 @@
         )
         return jnp.where(allowed[None], raw_scores, -1e30)
 
-    scores = score_block()
-    largest = jnp.max(scores, axis=-1, keepdims=True)
-    exp_scores = jnp.exp(scores - largest)
-    exp_total = jnp.sum(exp_scores, axis=-1, keepdims=True)
-    log_total = largest + jnp.log(exp_total)
-    attn_probs = (exp_scores / exp_total).astype(low)
-    attended = (
-        jnp.einsum("hqk,khd->qhd", attn_probs, context[1], preferred_element_type=jnp.float32)
-        .reshape(row_count, local_width)
-        .astype(low)
-    )
-    attention_out = tensor_sum(
-        jnp.dot(attended, out_low, preferred_element_type=jnp.float32).astype(low), 2
-    ).astype(jnp.float32)
-    residual = tokens_f + attention_out
-    scale_two = lax.rsqrt(jnp.mean(residual * residual, axis=-1, keepdims=True) + EPS)
-    normed_two = residual * scale_two
-    hidden_two = (normed_two * gain_two_f).astype(low)
-
     hidden_all = token_gather(hidden_two, 3)
     contract_last = (((1,), (1,)), ((), ()))
 
@@ -1212,66 +1966,22 @@
         logit_exp = jnp.exp(logits - jnp.max(logits, axis=-1, keepdims=True))
         return logit_exp / jnp.sum(logit_exp, axis=-1, keepdims=True)
 
-    gates_here = lax.dynamic_slice_in_dim(
-        router(hidden_all) * chosen_all, device_index * local_experts, local_experts, axis=1
-    ).T[:, :, None]
-    gate_low = w_gate.astype(low)
-    up_low = w_up.astype(low)
-    down_low = w_down.astype(low)
-    gate_pre = jnp.einsum("td,edh->eth", hidden_all, gate_low, preferred_element_type=jnp.float32)
-    up_pre = jnp.einsum("td,edh->eth", hidden_all, up_low, preferred_element_type=jnp.float32)
-    sigmoid_gate = jax.nn.sigmoid(gate_pre)
-    swish_gate = gate_pre * sigmoid_gate
-    activated = swish_gate * up_pre
-    gated = (activated * gates_here).astype(low)
-    expert_part = jnp.einsum(
-        "eth,ehd->td", gated, down_low, preferred_element_type=jnp.float32
+    gate_up = jnp.concatenate(
+        [w[i] for w in (w_gate, w_up) for i in range(local_experts)], axis=1
     ).astype(low)
-    grad_gated = jnp.einsum(
-        "td,ehd->eth", grad_out_all, down_low, preferred_element_type=jnp.float32
-    )
-    grad_gates_here = jnp.sum(activated * grad_gated, axis=-1)
-    grad_act = grad_gated * gates_here
-    grad_gate_pre = (
-        grad_act * up_pre * sigmoid_gate * (1.0 + gate_pre * (1.0 - sigmoid_gate))
-    ).astype(low)
-    grad_up_pre = (grad_act * swish_gate).astype(low)
-    grad_rows = (
-        jnp.einsum("eth,edh->td", grad_gate_pre, gate_low, preferred_element_type=jnp.float32)
-        + jnp.einsum("eth,edh->td", grad_up_pre, up_low, preferred_element_type=jnp.float32)
-    ).astype(low)
-    grad_gate_sum = gate_exchange(
-        jnp.pad(
-            grad_gates_here.reshape(local_experts, groups, row_count).transpose(1, 0, 2),
-            ((0, 0), (0, 8 - local_experts), (0, 0)),
-        ),
-        4,
-    )
+    down_low = w_down.reshape(-1, model_width).astype(low)
+    expert_part, grad_hidden_sum, grad_gate_sum, grad_gate_w, grad_up_w, grad_down = expert_layer(
+        hidden_all, grad_out_all, gate_up, down_low, router_t, chosen_all, 5
+    )
+    expert_quarter = token_reduce(expert_part, 6)
     grad_probs = (
         grad_gate_sum[:, :local_experts].reshape(experts, row_count).T * chosen
     )
-    grad_hidden_quarter = token_reduce(grad_rows, 5)
-    expert_quarter = token_reduce(expert_part, 6)
-    grad_down = jnp.einsum(
-        "eth,td->ehd", gated, grad_out_all, preferred_element_type=jnp.float32
-    )
-    grad_gate_w = jnp.einsum(
-        "td,eth->edh", hidden_all, grad_gate_pre, preferred_element_type=jnp.float32
-    )
-    grad_up_w = jnp.einsum(
-        "td,eth->edh", hidden_all, grad_up_pre, preferred_element_type=jnp.float32
-    )
-    column_order = [0, 2, 1, 3]
-
-    def spread(piece):
-        all_pieces = lax.all_gather(piece, "tensor", axis=0)
-        return jnp.concatenate([all_pieces[i] for i in column_order], axis=1)
-
-    def quarter_slot(t):
-        return (t % 2) * 2 + t // 2
-
-    grad_hidden_sum = spread(grad_hidden_quarter).astype(jnp.float32)
-    block_out = residual + spread(expert_quarter).astype(jnp.float32)
+    grad_hidden_sum = grad_hidden_sum.astype(jnp.float32)
+    expert_pieces = lax.all_gather(expert_quarter, "tensor", axis=0)
+    block_out = residual + jnp.concatenate(
+        [expert_pieces[i] for i in (0, 2, 1, 3)], axis=1
+    ).astype(jnp.float32)
     router_probs = router(hidden_two)
     grad_logits = (
         router_probs * (grad_probs - jnp.sum(router_probs * grad_probs, axis=-1, keepdims=True))

time: 917 us -> 776 us (0.85)
  matrix products: 161 us -> 52.4 us
  local copies, waits for them, and re-layouts: 59.1 us -> 74.6 us
  starting transfers between devices: 18.6 us -> 5.7 us
  Pallas kernels: 553 us -> 541 us
    pallas_call x2 -> x3, Pallas kernels: 133 us -> 263 us  [the longest x1 132 us: project(): pl.pallas_call(kernel, out_shape=(shape((parts, depth * GROUPS, columns),...]
    dot_general x12 -> x0, matrix products: 98.8 us -> none  [the longest x1 15.5 us: fast_shards(): jnp.einsum('eth,edh->td', grad_up_pre, up_low, preferred_element_type=jnp...]
    pallas_call x2 -> x1, Pallas kernels: 126 us -> 55 us  [token_gather(): pl.pallas_call(kernel, out_shape=jax.ShapeDtypeStruct((rows * GROUPS, wid...]
    pallas_call x2 -> x1, Pallas kernels: 133 us -> 62.8 us  [token_reduce(): pl.pallas_call(kernel, out_shape=jax.ShapeDtypeStruct((rows, quarter), jn...]
    pallas_call x2 -> x1, Pallas kernels: 37.5 us -> 18.4 us  [tensor_sum(): pl.pallas_call(kernel, out_shape=jax.ShapeDtypeStruct((rows, width), jnp....]
    pallas_call x1, Pallas kernels: 125 us -> 142 us  [weight_reduce(): pl.pallas_call(kernel, out_shape=(jax.ShapeDtypeStruct((parts, rows, widt...]
    ppermute x8 -> x4, starting transfers between devices: 18.4 us -> 5.33 us  [from_behind(): lax.ppermute(value, axis, [(source, source + steps) for source in range(i...]
    squeeze x2 -> x4, local copies, waits for them, and re-layouts: 0.39 us -> 13.2 us  [the longest x2 7.04 us: fast_shards(): context[0]]
  transfers between devices with their start and end apart: 10 -> 8, of which waited for: 3 -> 2; matrix products, arithmetic and copies ran while one was open for 7% -> 9% of each run, Pallas kernels for 16% -> 29%
where the time goes in v2:
time: 776 us; the launch traced here: 766 us
  Pallas kernels  541 us (70%)
  local copies, waits for them, and re-layouts  74.6 us (10%)
  matrix products  52.4 us (7%)
  other arithmetic  35.9 us (5%)
  waiting for transfers between devices  35.3 us (5%)
  between operations  14.7 us (2%)
    pallas_call x1, Pallas kernels, weight_reduce(): pl.pallas_call(kernel, out_shape=(jax.ShapeDtypeStruct((parts, rows, widt...  142 us
    pallas_call x1, Pallas kernels, project(): pl.pallas_call(kernel, out_shape=(shape((parts, depth * GROUPS, columns),...  132 us
    pallas_call x1, Pallas kernels, expert_layer(): pl.pallas_call(kernel, out_shape=(shape((tokens, width), low), shape((row...  93.9 us
    pallas_call x1, Pallas kernels, token_reduce(): pl.pallas_call(kernel, out_shape=jax.ShapeDtypeStruct((rows, quarter), jn...  62.8 us
    pallas_call x1, Pallas kernels, token_gather(): pl.pallas_call(kernel, out_shape=jax.ShapeDtypeStruct((rows * GROUPS, wid...  55 us
    pallas_call x1, Pallas kernels, attend(): pl.pallas_call(kernel, out_shape=(shape((rows, columns), low), shape((row...  36.9 us
    unnamed x98, local copies, waits for them, and re-layouts  23.1 us
    ppermute x4, waiting for transfers between devices, from_behind(): lax.ppermute(value, axis, [(source, source + steps) for source in range(i...  22.7 us
  transfers between devices with their start and end apart: 8, of which 2 were waited for; matrix products, arithmetic and copies ran while one was open for 9% of the time, Pallas kernels for 29%

profile of v2, /device:TPU:0, one launch (start us, length us, event | category | flops | bytes accessed | tf_op | source)
XLA Modules:
  0.0 765.9 jit_solution(16033279605920383058)
XLA Ops:
  17.1 132.5 %project.1 = (bf16[3,2048,512]{2,1,0:T(8,128)(2,1)}, f32[8,40,256]{2,1,0:T(8,128)S(1)}, bf16[256,2048]{1,0:T(8,128)(2,1)S(1)}, f32[2,256,512]{2,1,0:T(8,128)S(1)...) custom-call(bf16[256,2048]{1,0:T(8,128)(2,1)S(1)} %copy-done, ...), custom_call_target="tpu_custom_call" | custom-call | bytes 300000000 | tf_op jit(solution)/shard_map/project/pallas_call | solution.py:1721
  154.0 3.9 convert.30
  167.4 3.6 squeeze.65
  171.0 3.5 copy.108
  174.5 3.7 squeeze.66
  180.6 2.4 slice_bitcast_fusion.1
  190.8 36.9 %attend.1 = (bf16[256,512]{1,0:T(8,128)(2,1)S(1)}, f32[256,128]{1,0:T(8,128)S(1)}, f32[256,2048]{1,0:T(8,128)S(1)}, bf16[256,2048]{1,0:T(8,128)(2,1)S(1)}, f32[256,128]{1,0:T(8,128)S(1)}) custom-call(bf16[256,512]{1,0:T(8,128)(2,1)S(1)} %get-tuple-element.35.q_ref, bf16[5,2,256,512]{3,2,1,0:T(8,128)(2,1)S(1)} %copy-done.1, s32[256,1]{1,0:T(8,128)S(1)} %copy.100.sq_ref, ...), custom_call_target="tpu_custom_call" | custom-call | bytes 120000000 | tf_op jit(solution)/shard_map/attend/pallas_call | solution.py:1829
  230.0 55.0 %token_gather.1.h_in = bf16[2048,2048]{1,0:T(8,128)(2,1)} custom-call(bf16[256,2048]{1,0:T(8,128)(2,1)} %copy-done.2), custom_call_target="tpu_custom_call" | custom-call | bytes 135000000 | tf_op jit(solution)/shard_map/token_gather/pallas_call | solution.py:656
  286.2 93.9 %expert_layer.1 = (bf16[2048,2048]{1,0:T(8,128)(2,1)}, bf16[256,2048]{1,0:T(8,128)(2,1)}, f32[8,8,256]{2,1,0:T(8,128)}, f32[2,2048,256]{2,1,0:T(8,128)}, f32[2,2...) custom-call(bf16[2048,2048]{1,0:T(8,128)(2,1)} %token_gather.1.h_in, bf16[2048,2048]{1,0:T(8,128)(2,1)} %all-gather.10.cloned.1.call-done.dy_in, ...), custom_call_target="tpu_custom_call" | custom-call | bytes 240000000 | tf_op jit(solution)/shard_map/expert_layer/pallas_call | solution.py:1451
  380.1 62.8 %token_reduce.1 = bf16[256,512]{1,0:T(8,128)(2,1)} custom-call(bf16[2048,2048]{1,0:T(8,128)(2,1)} %get-tuple-element.41.part_ref), custom_call_target="tpu_custom_call" | custom-call | bytes 180000000 | tf_op jit(solution)/shard_map/token_reduce/pallas_call | solution.py:999
  443.0 5.5 exponential_select_fusion
  450.3 4.7 multiply_reduce_fusion.1
  455.0 12.5 %all-gather.12.cloned.1.call-done = bf16[1024,512]{1,0:T(8,128)(2,1)} async-done(((bf16[256,512]{1,0:T(8,128)(2,1)}), bf16[1024,512]{1,0:T(8,128)(2,1)}) %all-gather.12.cloned.1.call-update) | async-done | bytes 1048592 | tf_op jit(solution)/shard_map/all_gather | solution.py:1981
  469.3 3.9 multiply_subtract_fusion
  473.2 2.5 convolution_convert_fusion.1
  475.9 3.2 fusion.22
  479.1 4.5 convolution_bitcast_fusion
  483.6 9.9 %convolution_bitcast_fusion.1 = f32[1280,4,128]{0,2,1:T(8,128)} fusion(bf16[256,4,128]{0,2,1:T(8,128)(2,1)S(1)} %bitcast.152, f32[4,256,1280]{2,1,0:T(8,128)} %exponential_select_fusion, f32[4,256,1280]{2,1,0:T(8,128)} %fusion.22), kind=kOutput, calls=%fused_computation.12 | convolution fusion | flops 342100224 | bytes 13369344 | tf_op jit(solution)/shard_map/hqk,qhd->khd/dot_general | solution.py:2021
  493.6 3.2 copy.115
  496.8 3.2 copy.118
  500.0 3.2 copy.117
  503.2 3.2 copy.119
  506.4 2.8 fusion.1
  516.0 8.5 %fusion.26 = f32[256,4,128]{0,2,1:T(8,128)S(1)} fusion(bf16[1280,4,128]{0,2,1:T(8,128)(2,1)S(1)} %copy-done.23, f32[4,256,1280]{2,1,0:T(8,128)} %exponential_select_fusion, f32[4,256,1280]{2,1,0:T(8,128)} %fusion.22), kind=kOutput, calls=%fused_computation.44 | convolution fusion | flops 342100224 | bytes 12320768 | tf_op jit(solution)/shard_map/hqk,khd->qhd/dot_general | solution.py:2018
  524.5 3.8 convolution_convert_fusion.out_ref
  528.3 22.7 %collective-permute-done.3 = bf16[2,256,4,128]{1,3,2,0:T(8,128)(2,1)} collective-permute-done((bf16[2,256,4,128]{1,3,2,0:T(8,128)(2,1)}, bf16[2,256,4,128]{1,3,2,0:T(8,128)(2,1)}, u32[]{:S(2)}, u32[]{:S(2)}) %collective-permute-start.3) | collective-permute-done | bytes 524320 | tf_op jit(solution)/shard_map/ppermute | solution.py:20
  559.9 5.8 all-reduce.3
  567.3 4.6 fusion.13.part_ref
  571.9 18.4 %tensor_sum.1 = bf16[256,2048]{1,0:T(8,128)(2,1)S(1)} custom-call(bf16[256,2048]{1,0:T(8,128)(2,1)S(1)} %fusion.13.part_ref), custom_call_target="tpu_custom_call" | custom-call | bytes 51000000 | tf_op jit(solution)/shard_map/tensor_sum/pallas_call | solution.py:733
  590.3 4.5 convert_bitcast_fusion.qkv_ref
  597.2 142.1 %weight_reduce.1 = (f32[3,256,512]{2,1,0:T(8,128)}, f32[512,256]{1,0:T(8,128)}, f32[24,256]{1,0:T(8,128)}) custom-call(bf16[3,2048,512]{2,1,0:T(8,128)(2,1)} %convert_bitcast_fusion.qkv_ref, bf16[512,2048]{1,0:T(8,128)(2,1)} %convolution_convert_fusion.out_ref, f32[8,24,256]{2,1,0:T(8,128)} %concatenate.38.small_ref), custom_call_target="tpu_custom_call" | custom-call | bytes 360000000 | tf_op jit(solution)/shard_map/weight_reduce/pallas_call | solution.py:882
  743.4 3.4 fusion.17
  (199 shorter events, 77.0 us)
Async XLA Ops:
  7.2 9.9 %copy-start = (bf16[256,2048]{1,0:T(8,128)(2,1)S(1)}, bf16[256,2048]{1,0:T(8,128)(2,1)}, u32[]{:S(2)}) copy-start(bf16[256,2048]{1,0:T(8,128)(2,1)} %tok_ref.3) | copy-start | bytes 3145732
  7.2 9.9 %copy-start.11 = (f32[3,256,512]{2,1,0:T(8,128)S(1)}, f32[3,256,512]{2,1,0:T(8,128)}, u32[]{:S(2)}) copy-start(f32[3,256,512]{2,1,0:T(8,128)} %w_ref.1) | copy-start | bytes 4718596
  7.2 144.4 %all-gather.6.cloned.1.call-start = ((), (), s32[]{:S(2)}) async-start(), calls=%async_computation | async-start | bytes 2359296 | tf_op jit(solution)/shard_map/all_gather | solution.py:1905
  9.1 178.3 %all-gather.8.cloned.1.call-start = ((), (), s32[]{:S(2)}) async-start(), calls=%async_computation.1 | async-start | bytes 2359296 | tf_op jit(solution)/shard_map/all_gather | solution.py:1906
  10.9 275.2 %all-gather.10.cloned.1.call-start = ((), (), s32[]{:S(2)}) async-start(), calls=%async_computation.2 | async-start | bytes 10485760 | tf_op jit(solution)/shard_map/all_gather | solution.py:1911
  17.1 136.5 %copy-start.36 = (s32[2048]{0:T(1024)S(1)}, s32[2048]{0:T(1024)}, u32[]{:S(2)}) copy-start(s32[2048]{0:T(1024)} %param.25) | copy-start | bytes 24580
  151.6 315.8 %all-gather.12.cloned.1.call-start = ((), (), s32[]{:S(2)}) async-start(), calls=%async_computation.3 | async-start | bytes 1310720 | tf_op jit(solution)/shard_map/all_gather | solution.py:1981
  162.4 122.6 %copy-start.25 = (bf16[8,2,8,256]{3,2,0,1:T(8,128)(2,1)}, bf16[8,2,8,256]{3,2,0,1:T(8,128)(2,1)S(1)}, u32[]{:S(2)}) copy-start(bf16[8,2,8,256]{3,2,0,1:T(8,128)(2,1)S(1)} %copy.137) | copy-start | bytes 196612
  229.9 55.1 %copy-start.3 = (bf16[256,2048]{1,0:T(8,128)(2,1)S(1)}, bf16[256,2048]{1,0:T(8,128)(2,1)}, u32[]{:S(2)}) copy-start(bf16[256,2048]{1,0:T(8,128)(2,1)} %copy-done.2) | copy-start | bytes 3145732
  380.1 62.8 %copy-start.29 = (pred[256,1280]{1,0:T(8,128)(4,1)S(1)}, pred[256,1280]{1,0:T(8,128)(4,1)}, u32[]{:S(2)}) copy-start(pred[256,1280]{1,0:T(8,128)(4,1)} %fusion.25) | copy-start | bytes 983044
  380.1 62.8 %copy-start.31 = (bf16[256,512]{0,1:T(8,128)(2,1)S(1)}, bf16[256,512]{0,1:T(8,128)(2,1)}, u32[]{:S(2)}) copy-start(bf16[256,512]{0,1:T(8,128)(2,1)} %copy.134) | copy-start | bytes 786436
  442.9 6.4 copy-start.34
  442.9 6.4 copy-start.4
  442.9 7.3 copy-start.26
  450.3 18.6 %copy-start.8 = (f32[256,2048]{1,0:T(8,128)S(1)}, f32[256,2048]{1,0:T(8,128)}, u32[]{:S(2)}) copy-start(f32[256,2048]{1,0:T(8,128)} %copy-done.7) | copy-start | bytes 6291460
  479.1 4.5 copy-start.32
  509.3 6.7 copy-start.23
  510.6 40.4 %collective-permute-start.3 = (bf16[2,256,4,128]{1,3,2,0:T(8,128)(2,1)}, bf16[2,256,4,128]{1,3,2,0:T(8,128)(2,1)}, u32[]{:S(2)}, u32[]{:S(2)}) collective-permute-start(bf16[2,256,4,128]{1,3,2,0:T(8,128)(2,1)} %get-tuple-element.76), channel_id=1, source_target_pairs={{16,0},{20,4},{24,8},{28,12},{17,1},{21,5},{25,9},{29,13},{18,2},{... | collective-permute-start | bytes 1572872 | tf_op jit(solution)/shard_map/ppermute | solution.py:20
  511.9 39.1 %collective-permute-start.2 = (bf16[2,256,4,128]{1,3,2,0:T(8,128)(2,1)}, bf16[2,256,4,128]{1,3,2,0:T(8,128)(2,1)}, u32[]{:S(2)}, u32[]{:S(2)}) collective-permute-start(bf16[2,256,4,128]{1,3,2,0:T(8,128)(2,1)} %get-tuple-element.77), channel_id=1, source_target_pairs={{12,0},{16,4},{20,8},{24,12},{28,16},{13,1},{17,5},{21,9},{25,13},... | collective-permute-start | bytes 1572872 | tf_op jit(solution)/shard_map/ppermute | solution.py:20
  513.2 37.8 %collective-permute-start.1 = (bf16[2,256,4,128]{1,3,2,0:T(8,128)(2,1)}, bf16[2,256,4,128]{1,3,2,0:T(8,128)(2,1)}, u32[]{:S(2)}, u32[]{:S(2)}) collective-permute-start(bf16[2,256,4,128]{1,3,2,0:T(8,128)(2,1)} %get-tuple-element.78), channel_id=1, source_target_pairs={{8,0},{12,4},{16,8},{20,12},{24,16},{28,20},{9,1},{13,5},{17,9},{2... | collective-permute-start | bytes 1572872 | tf_op jit(solution)/shard_map/ppermute | solution.py:20
  514.5 36.6 %collective-permute-start = (bf16[2,256,4,128]{1,3,2,0:T(8,128)(2,1)}, bf16[2,256,4,128]{1,3,2,0:T(8,128)(2,1)}, u32[]{:S(2)}, u32[]{:S(2)}) collective-permute-start(bf16[2,256,4,128]{1,3,2,0:T(8,128)(2,1)} %get-tuple-element.75), channel_id=1, source_target_pairs={{4,0},{8,4},{12,8},{16,12},{20,16},{24,20},{28,24},{5,1},{9,5},{13... | collective-permute-start | bytes 1572872 | tf_op jit(solution)/shard_map/ppermute | solution.py:20
  524.5 26.6 %copy-start.14 = (f32[1,5,256,4,128]{2,4,3,0,1:T(8,128)S(1)}, f32[1,5,256,4,128]{2,4,3,0,1:T(8,128)}, u32[]{:S(2)}) copy-start(f32[1,5,256,4,128]{2,4,3,0,1:T(8,128)} %copy.118) | copy-start | bytes 7864324
  528.3 25.0 %copy-start.30 = (f32[256,64]{0,1:T(8,128)S(1)}, f32[256,64]{0,1:T(8,128)}, u32[]{:S(2)}) copy-start(f32[256,64]{0,1:T(8,128)} %copy.110) | copy-start | bytes 196612
  556.4 9.2 %copy-start.40 = (f32[256]{0:T(256)S(1)}, f32[256]{0:T(256)}, u32[]{:S(2)}) copy-start(f32[256]{0:T(256)} %get-tuple-element.67) | copy-start | bytes 3076
  556.4 9.2 %copy-start.41 = (f32[256]{0:T(256)S(1)}, f32[256]{0:T(256)}, u32[]{:S(2)}) copy-start(f32[256]{0:T(256)} %get-tuple-element.68) | copy-start | bytes 3076
  556.4 9.2 %copy-start.42 = (f32[256]{0:T(256)S(1)}, f32[256]{0:T(256)}, u32[]{:S(2)}) copy-start(f32[256]{0:T(256)} %get-tuple-element.69) | copy-start | bytes 3076
  556.4 9.2 %copy-start.43 = (f32[256]{0:T(256)S(1)}, f32[256]{0:T(256)}, u32[]{:S(2)}) copy-start(f32[256]{0:T(256)} %get-tuple-element.70) | copy-start | bytes 3076
  571.9 18.4 %copy-start.13 = (bf16[256,2048]{1,0:T(8,128)(2,1)S(1)}, bf16[256,2048]{1,0:T(8,128)(2,1)}, u32[]{:S(2)}) copy-start(bf16[256,2048]{1,0:T(8,128)(2,1)} %copy-done.12) | copy-start | bytes 3145732
  590.3 4.8 copy-start.39
  590.3 5.5 copy-start.27
  590.3 5.5 copy-start.35
  597.2 146.2 %copy-start.45 = (f32[256]{0:T(256)S(1)}, f32[256]{0:T(256)}, u32[]{:S(2)}) copy-start(f32[256]{0:T(256)} %get-tuple-element.66) | copy-start | bytes 3076
  (22 other events, 57.7 us)
Sparse Core Ops, SparseCore 0:
  10.7 71.4 all-gather.5
  84.9 65.7 all-gather.7
  152.2 84.4 all-gather.9
  443.0 24.3 all-gather.11

commit v3 on v2

--- a/solution.py
+++ b/solution.py
@@ -681,7 +681,7 @@
     lax.fori_loop(0, rows // step, body, 0)
 
 
-def group_sum(part_ref, out_ref, core_buf, x_buf, send_sem, recv_sem, meanwhile=None):
+def group_stages(part_ref, out_ref, core_buf, x_buf, send_sem, recv_sem):
     rows, width = part_ref.shape
     half, quarter = width // 2, width // 4
     z, y, x, c = place()
@@ -693,33 +693,52 @@
     def quarter_of(xx, cc):
         return pl.ds(pl.multiple_of(cc * half + xx * quarter, quarter), quarter)
 
-    first = remote(part_ref.at[:, half_of(1 - c)], core_buf, send_sem.at[0], recv_sem.at[0], twin)
-    first.start()
+    own, from_x = out_ref.at[:, quarter_of(x, c)], out_ref.at[:, quarter_of(1 - x, c)]
+    to_x = core_buf.at[:, pl.ds(pl.multiple_of((1 - x) * quarter, quarter), quarter)]
+    sources = [part_ref.at[:, half_of(1 - c)], to_x, own, own, from_x]
+    landings = [core_buf, x_buf, own, own, from_x]
+    targets = [twin, across, across, twin, twin]
+
+    def copy(k):
+        return remote(sources[k], landings[k], send_sem.at[k], recv_sem.at[k], targets[k])
+
+    def arrive(k, landing):
+        remote(landing, landing, send_sem.at[k], recv_sem.at[k], targets[k]).wait_recv()
+
+    def begin():
+        copy(0).start()
+
+    def core_step():
+        copy(0).wait_recv()
+        add_to(core_buf, core_buf, part_ref.at[:, half_of(c)], 32)
+        copy(1).start()
+
+    def x_step():
+        copy(1).wait_recv()
+        add_to(own, x_buf, core_buf.at[:, pl.ds(pl.multiple_of(x * quarter, quarter), quarter)], 32)
+        copy(2).start()
+        copy(3).start()
+
+    def spread():
+        arrive(2, from_x)
+        copy(4).start()
+
+    def end():
+        arrive(3, out_ref.at[:, quarter_of(x, 1 - c)])
+        arrive(4, out_ref.at[:, quarter_of(1 - x, 1 - c)])
+        for k in range(5):
+            copy(k).wait_send()
+
+    return [begin, core_step, x_step, spread, end]
+
+
+def group_sum(part_ref, out_ref, core_buf, x_buf, send_sem, recv_sem, meanwhile=None):
+    stages = group_stages(part_ref, out_ref, core_buf, x_buf, send_sem, recv_sem)
+    stages[0]()
     if meanwhile is not None:
         meanwhile()
-    first.wait_recv()
-    add_to(core_buf, core_buf, part_ref.at[:, half_of(c)], 32)
-    second = remote(
-        core_buf.at[:, pl.ds(pl.multiple_of((1 - x) * quarter, quarter), quarter)],
-        x_buf, send_sem.at[1], recv_sem.at[1], across,
-    )
-    second.start()
-    second.wait_recv()
-    own = out_ref.at[:, quarter_of(x, c)]
-    add_to(own, x_buf, core_buf.at[:, pl.ds(pl.multiple_of(x * quarter, quarter), quarter)], 32)
-    third = remote(own, own, send_sem.at[2], recv_sem.at[2], across)
-    third.start()
-    fourth = remote(own, own, send_sem.at[3], recv_sem.at[3], twin)
-    fourth.start()
-    from_x = out_ref.at[:, quarter_of(1 - x, c)]
-    remote(from_x, from_x, send_sem.at[2], recv_sem.at[2], across).wait_recv()
-    fifth = remote(from_x, from_x, send_sem.at[4], recv_sem.at[4], twin)
-    fifth.start()
-    for index, column in ((3, quarter_of(x, 1 - c)), (4, quarter_of(1 - x, 1 - c))):
-        landing = out_ref.at[:, column]
-        remote(landing, landing, send_sem.at[index], recv_sem.at[index], twin).wait_recv()
-    for copy in (first, second, third, fourth, fifth):
-        copy.wait_send()
+    for stage in stages[1:]:
+        stage()
 
 
 def tensor_sum(part, collective_id):
@@ -1850,6 +1869,365 @@
     )(query, context, segment_query, segment_keys, tokens, out_low, gain)
 
 
+def attend_back(
+    grad_hidden, grad_probs, router_t, hidden_two, residual, scale_two, gain_two, out_grad,
+    query, context, segment_query, segment_keys, attended, log_sums, raw, scales, qk_gains,
+    cosine, sine, hidden_one, tokens, gain_one, qkv_low, out_low, collective_id,
+):
+    rows, width = tokens.shape
+    columns = query.shape[1]
+    heads = columns // HEAD
+    experts = router_t.shape[0]
+    blocks = context.shape[0]
+    depth = width // GROUPS
+    small_rows = 8 + experts
+    tensors = NX * NC
+    half, quarter = width // 2, width // 4
+    low, f32 = jnp.bfloat16, jnp.float32
+    QUERY, KEY, VALUE, OUT, SMALL = 0, 1, 2, 3, 4
+
+    def kernel(
+        dh_ref, gates_ref, router_ref, h2_ref, x1_ref, s2_ref, g2_ref, dy_ref,
+        q_ref, context_ref, sq_ref, sk_ref, o_ref, lse_ref, raw_ref, scale_ref, qkg_ref,
+        cos_ref, sin_ref, h1_ref, tok_ref, g1_ref, w_hbm, out_ref,
+        tok_grad, qkv_sum, out_sum, small_sum,
+        weights, dx1, da, do, dot_sums, dq, dkv, proj, send_kv, land_y, land_z,
+        part, full, core_buf, x_buf, small, line_sum,
+        main_buf, out_buf, small_buf, part_k, land_k, part_q, land_q,
+        w_sem, y_s, y_r, z_s, z_r, group_s, group_r, ks_s, ks_r, qs_s, qs_r, line_s, line_r,
+    ):
+        z, y, x, c = place()
+        e, t = lax.axis_index("expert"), lax.axis_index("tensor")
+        mates = [(e, lax.rem(t + k, tensors)) for k in range(1, tensors)]
+        beside, below = device(z, 1 - y, x, c), device(z - 1, y, x, c)
+        fetch = pltpu.make_async_copy(w_hbm, weights, w_sem)
+        fetch.start()
+
+        def own_part(s, b):
+            if s == SMALL:
+                return small[b]
+            at = pl.ds(pl.multiple_of(b * depth, depth), depth)
+            if s == OUT:
+                return dot(o_ref[...], da[:, at], (0, 0))
+            return dot(h1_ref[:, at], proj[s], (0, 0))
+
+        def slot(kind):
+            def view(s, zz):
+                if s == SMALL:
+                    return small_buf.at[kind, zz]
+                return out_buf.at[kind, zz] if s == OUT else main_buf.at[kind, zz, s]
+            return view
+
+        line = LineReduce([], lambda s, zz, yy: slot(3)(s, zz), slot(0), slot(1), slot(2), line_s, line_r)
+        greet(line.partners() + [(mate, None) for mate in mates])
+
+        grad_probs = gates_ref[...]
+        logits = dot(h2_ref[...], router_ref[...], (1, 1))
+        shifted = jnp.exp(logits - jnp.max(logits, axis=-1, keepdims=True))
+        probs = shifted / jnp.sum(shifted, axis=-1, keepdims=True)
+        grad_logits = probs * (grad_probs - jnp.sum(probs * grad_probs, axis=-1, keepdims=True))
+        tall = jnp.transpose(
+            jnp.concatenate([grad_logits, jnp.zeros((rows, 128 - experts), f32)], axis=1)
+        )
+        grad_logits = grad_logits.astype(low)
+        tall = tall.astype(low)
+        for b in range(GROUPS):
+            small[b] = jnp.zeros_like(small[b])
+            small[b, 8 : 8 + experts, :] = dot(tall, h2_ref[:, pl.ds(b * depth, depth)], (1, 0))[:experts]
+        dx1[...] = dot(grad_logits, router_ref[...], (1, 0))
+        line_sum[...] = jnp.zeros_like(line_sum)
+
+        def norm_two(i, carry):
+            r = pl.ds(pl.multiple_of(i * 32, 32), 32)
+            grad = dh_ref[r, :].astype(f32) + dx1[r, :]
+            value, scale = x1_ref[r, :], s2_ref[r, 0:1]
+            line_sum[0:1, :] += jnp.sum(grad * (value * scale), axis=0, keepdims=True)
+            grad = grad * g2_ref[...]
+            inner = jnp.mean(grad * value, axis=-1, keepdims=True)
+            result = dy_ref[r, :].astype(f32) + scale * grad - value * (scale * scale * scale) * inner
+            dx1[r, :] = result
+            da[r, :] = result.astype(low)
+            return carry
+
+        lax.fori_loop(0, rows // 32, norm_two, 0)
+
+        do[...] = dot(da[...], out_ref[...], (1, 1)).astype(low)
+        wide = lax.broadcasted_iota(jnp.int32, (rows, 128), 1)
+        sums = jnp.zeros((rows, 128), f32)
+        for head in range(heads):
+            at = pl.ds(head * HEAD, HEAD)
+            inner = jnp.sum(do[:, at].astype(f32) * o_ref[:, at].astype(f32), axis=-1, keepdims=True)
+            sums = jnp.where(wide == head, inner, sums)
+        dot_sums[...] = sums
+        dq[...] = jnp.zeros_like(dq)
+        row = lax.broadcasted_iota(jnp.int32, (rows, rows), 0)
+        column = lax.broadcasted_iota(jnp.int32, (rows, rows), 1)
+
+        def attention_block(k):
+            distance = row - column + k * rows
+            allowed = (sq_ref[...] == sk_ref[k : k + 1, :]) & (distance >= 0) & (distance < WINDOW)
+            for head in range(heads):
+                at = pl.ds(head * HEAD, HEAD)
+                queries, keys, values = q_ref[:, at], context_ref[k, 0, :, at], context_ref[k, 1, :, at]
+                scores = dot(queries, keys, (1, 1)) * HEAD ** (-0.5)
+                weight = jnp.where(allowed, jnp.exp(scores - lse_ref[:, head : head + 1]), 0.0)
+                grad_weight = dot(do[:, at], values, (1, 1))
+                grad_score = (
+                    weight * (grad_weight - dot_sums[:, head : head + 1]) * HEAD ** (-0.5)
+                ).astype(low)
+                dq[:, at] += dot(grad_score, keys, (1, 0))
+                dkv[k, 0, :, at] = dot(grad_score, queries, (0, 0))
+                dkv[k, 1, :, at] = dot(weight.astype(low), do[:, at], (0, 0))
+
+        exists = {0: None, 1: (y == 1) | (z >= 1), 2: z >= 1, 3: z >= 2 - y, 4: z >= 2}
+        comes = {1: (y == 0) | (z >= 1), 3: z >= 1 + y}
+
+        def kv_copy(which, k):
+            if k in (1, 3):
+                landing, target = land_y.at[k // 2, which], beside
+                return remote(send_kv.at[k - 1, which], landing, y_s.at[k // 2, which], y_r.at[k // 2, which], target)
+            landing = land_z.at[k // 2 - 1, which]
+            return remote(
+                send_kv.at[k - 1, which], landing, z_s.at[k // 2 - 1, which], z_r.at[k // 2 - 1, which], below
+            )
+
+        def kv_send(which, k):
+            send_kv[k - 1, which] = dkv[k, which].astype(low)
+            kv_copy(which, k).start()
+
+        def merge(into, which, landed):
+            add_to(dkv.at[into, which], dkv.at[into, which], landed, 32)
+
+        for k in (3, 1, 4, 2, 0):
+            def one(k=k):
+                attention_block(k)
+                if k in (1, 3):
+                    kv_send(1, k)
+                    kv_send(0, k)
+            run_if(exists[k], one)
+
+        def take_three(which):
+            def land():
+                kv_copy(which, 3).wait_recv()
+                pl.when(y == 1)(lambda: merge(4, which, land_y.at[1, which]))
+                pl.when(y == 0)(lambda: merge(2, which, land_y.at[1, which]))
+            run_if(comes[3], land)
+            run_if(exists[4], lambda: kv_send(which, 4))
+
+        def take_one(which):
+            def land():
+                kv_copy(which, 1).wait_recv()
+                pl.when(y == 1)(lambda: merge(2, which, land_y.at[0, which]))
+                pl.when(y == 0)(lambda: merge(0, which, land_y.at[0, which]))
+            run_if(comes[1], land)
+
+        def take_four(which):
+            def land():
+                kv_copy(which, 4).wait_recv()
+                merge(2, which, land_z.at[1, which])
+            run_if((z >= 1) & (z < NZ - 1), land)
+            run_if(exists[2], lambda: kv_send(which, 2))
+
+        def take_two(which):
+            def land():
+                kv_copy(which, 2).wait_recv()
+                merge(0, which, land_z.at[0, which])
+            run_if(z < NZ - 1, land)
+
+        def unturn(which, grad_of):
+            inner = jnp.zeros((rows, 1), f32)
+            for head in range(heads):
+                at = pl.ds(head * HEAD, HEAD)
+                grad = turn(grad_of(at), cos_ref[...], -sin_ref[...])
+                value = raw_ref[which, :, at]
+                line_sum[1 + which : 2 + which, at] = jnp.sum(
+                    grad * (value * scale_ref[:, 1 + which : 2 + which]), axis=0, keepdims=True
+                )
+                grad = grad * qkg_ref[which : which + 1, at]
+                dkv[1 + which, 0, :, at] = grad
+                inner = inner + jnp.sum(grad * value, axis=-1, keepdims=True)
+            return inner
+
+        def denorm(which, inner):
+            scale = scale_ref[:, 1 + which : 2 + which]
+            rest = scale * scale * scale * inner / width
+            for head in range(heads):
+                at = pl.ds(head * HEAD, HEAD)
+                proj[which, :, at] = (
+                    scale * dkv[1 + which, 0, :, at] - raw_ref[which, :, at] * rest
+                ).astype(low)
+
+        def send_beside(s):
+            for zz in Z_ORDER:
+                buffer = slot(3)(s, zz)
+                buffer[...] = own_part(s, zz * NY + 1 - y).astype(buffer.dtype)
+                line.to_y(s, zz)
+
+        take_three(1)
+        take_three(0)
+        take_one(1)
+        take_one(0)
+        take_four(1)
+        take_four(0)
+        exchange_rows(unturn(QUERY, lambda at: dq[:, at]), part_q, land_q, qs_s, qs_r, mates)
+        take_two(1)
+        proj[VALUE] = dkv[0, 1].astype(low)
+        denorm(QUERY, exchanged_rows(part_q, land_q, qs_s, qs_r, mates))
+        send_beside(QUERY)
+        send_beside(VALUE)
+        take_two(0)
+        exchange_rows(unturn(KEY, lambda at: dkv[0, 0, :, at]), part_k, land_k, ks_s, ks_r, mates)
+        denorm(KEY, exchanged_rows(part_k, land_k, ks_s, ks_r, mates))
+        send_beside(KEY)
+        send_beside(OUT)
+        fetch.wait()
+
+        def half_of(cc):
+            def body(i, carry):
+                at = pl.ds(pl.multiple_of(cc * half + i * quarter, quarter), quarter)
+                value = dot(proj[0], weights[0, at, :], (1, 1))
+                for s in (1, 2):
+                    value = value + dot(proj[s], weights[s, at, :], (1, 1))
+                part[:, at] = value.astype(low)
+                return carry
+
+            lax.fori_loop(0, 2, body, 0)
+
+        stages = group_stages(part, full, core_buf, x_buf, group_s, group_r)
+        half_of(1 - c)
+        stages[0]()
+        half_of(c)
+        stages[1]()
+
+        def hop(s, zz, k):
+            def upward():
+                if k > 0:
+                    line.take(s, zz, 1)
+                line.copy(s, zz, 1).start()
+
+            def downward():
+                if k > 0:
+                    line.take(s, zz, 2)
+                line.copy(s, zz, 2).start()
+
+            if k < zz:
+                run_if((z < zz) & (z == k), upward)
+            if NZ - 1 - k > zz:
+                run_if((z > zz) & (NZ - 1 - z == k), downward)
+
+        def receive(s, zz):
+            line.copy(s, zz, 0).wait_recv()
+            buffer = slot(0)(s, zz)
+            buffer[...] = (buffer[...].astype(f32) + own_part(s, zz * NY + y)).astype(buffer.dtype)
+
+        units = []
+
+        def run_units(s):
+            for zz in Z_ORDER:
+                receive(s, zz)
+                hop(s, zz, 0)
+                units.append((s, zz))
+                for k in (1, 2):
+                    if len(units) > k:
+                        hop(*units[-1 - k], k)
+
+        def norm_one(i, carry):
+            r = pl.ds(pl.multiple_of(i * 32, 32), 32)
+            grad, value, scale = full[r, :].astype(f32), tok_ref[r, :].astype(f32), scale_ref[r, 0:1]
+            line_sum[3:4, :] += jnp.sum(grad * (value * scale), axis=0, keepdims=True)
+            grad = grad * g1_ref[...]
+            inner = jnp.mean(grad * value, axis=-1, keepdims=True)
+            tok_grad[r, :] = (
+                dx1[r, :] + scale * grad - value * (scale * scale * scale) * inner
+            ).astype(low)
+            return carry
+
+        run_units(QUERY)
+        stages[2]()
+        run_units(VALUE)
+        stages[3]()
+        stages[4]()
+        lax.fori_loop(0, rows // 32, norm_one, 0)
+        for b in range(GROUPS):
+            at = pl.ds(b * depth, depth)
+            small[b, 0:1, :] = line_sum[3:4, at]
+            small[b, 1:2, :] = line_sum[0:1, at]
+            for which in range(2):
+                for k in range(columns // depth):
+                    small[b, 2 + 2 * which + k : 3 + 2 * which + k, :] = line_sum[
+                        1 + which : 2 + which, pl.ds(k * depth, depth)
+                    ]
+        send_beside(SMALL)
+        run_units(KEY)
+        run_units(SMALL)
+        run_units(OUT)
+        hop(*units[-1], 1)
+        hop(*units[-2], 2)
+        hop(*units[-1], 2)
+
+        def done(s, total):
+            target = qkv_sum.at[s] if s < OUT else (out_sum if s == OUT else small_sum)
+            target[...] = total[...].astype(f32)
+
+        line.streams = [QUERY, VALUE, KEY, SMALL, OUT]
+        line.home(done)
+        line.finish()
+        for which in range(2):
+            for k in (1, 2, 3, 4):
+                run_if(exists[k], lambda which=which, k=k: kv_copy(which, k).wait_send())
+        drain_rows(part_k, land_k, ks_s, ks_r, mates)
+        drain_rows(part_q, land_q, qs_s, qs_r, mates)
+
+    shape, dma, vmem = jax.ShapeDtypeStruct, pltpu.SemaphoreType.DMA, pltpu.VMEM
+    return pl.pallas_call(
+        kernel,
+        out_shape=(
+            shape((rows, width), low),
+            shape((3, depth, columns), f32),
+            shape((columns, depth), f32),
+            shape((small_rows, depth), f32),
+        ),
+        in_specs=[VMEM] * 22 + [HBM, VMEM],
+        out_specs=(VMEM,) * 4,
+        scratch_shapes=[
+            vmem(qkv_low.shape, low),
+            vmem((rows, width), f32),
+            vmem((rows, width), low),
+            vmem((rows, columns), low),
+            vmem((rows, 128), f32),
+            vmem((rows, columns), f32),
+            vmem((blocks, 2, rows, columns), f32),
+            vmem((3, rows, columns), low),
+            vmem((blocks - 1, 2, rows, columns), low),
+            vmem((2, 2, rows, columns), low),
+            vmem((2, 2, rows, columns), low),
+            vmem((rows, width), low),
+            vmem((rows, width), low),
+            vmem((rows, half), low),
+            vmem((rows, quarter), low),
+            vmem((GROUPS, small_rows, depth), f32),
+            vmem((8, width), f32),
+            vmem((4, NZ, 3, depth, columns), low),
+            vmem((4, NZ, columns, depth), low),
+            vmem((4, NZ, small_rows, depth), f32),
+            vmem((8, rows), f32),
+            vmem((tensors - 1, 8, rows), f32),
+            vmem((8, rows), f32),
+            vmem((tensors - 1, 8, rows), f32),
+            dma, dma((2, 2)), dma((2, 2)), dma((2, 2)), dma((2, 2)), dma((5,)), dma((5,)),
+            dma((tensors - 1,)), dma((tensors - 1,)), dma((tensors - 1,)), dma((tensors - 1,)),
+            dma((5, NZ, 3)), dma((5, NZ, 3)),
+        ],
+        compiler_params=comm_params(collective_id, 62),
+        cost_estimate=cost(130),
+        name="attend_back",
+    )(
+        grad_hidden, grad_probs, router_t, hidden_two, residual, scale_two, gain_two, out_grad,
+        query, context, segment_query, segment_keys, attended, log_sums, raw, scales, qk_gains,
+        cosine, sine, hidden_one, tokens, gain_one, qkv_low, out_low,
+    )
+
+
 def fast_shards(
     tokens_in,
     out_grad,
@@ -1931,41 +2309,7 @@
         query_low, context_blocks, segment_query[:, None], segment_keys, tokens_in, out_low,
         gain_two_f[None, :], 2,
     )
-    scale_one, query_scale, key_scale = scales[:, 0:1], scales[:, 1:2], scales[:, 2:3]
-    scale_two = scale_two_wide[:, :1]
-    tokens_f = tokens_in.astype(jnp.float32)
-    query_raw, key_raw = raw[0], raw[1]
-    normed_query = query_raw * query_scale
-    normed_key = key_raw * key_scale
-    normed_two = residual * scale_two
-    query_low = query_low.reshape(row_count, heads_here, HEAD)
-    context = (
-        context_blocks[::-1].transpose(1, 0, 2, 3).reshape(2, -1, heads_here, HEAD)
-    )
-    key_rows = (device_index - hop_count) * row_count + jnp.arange(
-        (hop_count + 1) * row_count, dtype=jnp.int32
-    )
-    distance = global_rows[:, None] - key_rows[None, :]
-    allowed = (
-        (segment_query[:, None] == segment_window[None, :]) & (distance >= 0) & (distance < WINDOW)
-    )
-    log_total = log_sums[:, :heads_here].T[:, :, None]
-
-    def score_block():
-        raw_scores = (
-            jnp.einsum("qhd,khd->hqk", query_low, context[0], preferred_element_type=jnp.float32)
-            * score_scale
-        )
-        return jnp.where(allowed[None], raw_scores, -1e30)
-
     hidden_all = token_gather(hidden_two, 3)
-    contract_last = (((1,), (1,)), ((), ()))
-
-    def router(rows):
-        logits = lax.dot_general(rows, router_t, contract_last, preferred_element_type=jnp.float32)
-        logit_exp = jnp.exp(logits - jnp.max(logits, axis=-1, keepdims=True))
-        return logit_exp / jnp.sum(logit_exp, axis=-1, keepdims=True)
-
     gate_up = jnp.concatenate(
         [w[i] for w in (w_gate, w_up) for i in range(local_experts)], axis=1
     ).astype(low)
@@ -1974,125 +2318,28 @@
         hidden_all, grad_out_all, gate_up, down_low, router_t, chosen_all, 5
     )
     expert_quarter = token_reduce(expert_part, 6)
-    grad_probs = (
-        grad_gate_sum[:, :local_experts].reshape(experts, row_count).T * chosen
-    )
-    grad_hidden_sum = grad_hidden_sum.astype(jnp.float32)
     expert_pieces = lax.all_gather(expert_quarter, "tensor", axis=0)
     block_out = residual + jnp.concatenate(
         [expert_pieces[i] for i in (0, 2, 1, 3)], axis=1
     ).astype(jnp.float32)
-    router_probs = router(hidden_two)
-    grad_logits = (
-        router_probs * (grad_probs - jnp.sum(router_probs * grad_probs, axis=-1, keepdims=True))
-    ).astype(low)
-    grad_out = out_grad.astype(jnp.float32)
-    grad_hidden_two = grad_hidden_sum + jnp.dot(
-        grad_logits, router_t, preferred_element_type=jnp.float32
-    )
-    grad_router_t = lax.dot_general(
-        grad_logits, hidden_two, (((0,), (0,)), ((), ())), preferred_element_type=jnp.float32
-    )
-    grad_gain_two = jnp.sum(grad_hidden_two * normed_two, axis=0)
-    scaled_two = grad_hidden_two * gain_two_f
-    grad_residual = (
-        grad_out
-        + scale_two * scaled_two
-        - residual
-        * (scale_two * scale_two * scale_two)
-        * jnp.mean(scaled_two * residual, axis=-1, keepdims=True)
-    )
-    grad_attn = grad_residual.astype(low)
-    grad_out_w = jnp.dot(attended.T, grad_attn, preferred_element_type=jnp.float32)
-    grad_attended = (
-        lax.dot_general(grad_attn, out_low, contract_last, preferred_element_type=jnp.float32)
-        .astype(low)
-        .reshape(row_count, heads_here, HEAD)
-    )
-    attn_weights = jnp.where(allowed[None], jnp.exp(score_block() - log_total), 0.0)
-    grad_weights = jnp.einsum(
-        "qhd,khd->hqk", grad_attended, context[1], preferred_element_type=jnp.float32
-    )
-    inner_sum = jnp.sum(attn_weights * grad_weights, axis=-1, keepdims=True)
-    grad_scores = (attn_weights * (grad_weights - inner_sum) * score_scale).astype(low)
-    grad_query = jnp.einsum(
-        "hqk,khd->qhd", grad_scores, context[0], preferred_element_type=jnp.float32
-    )
-    grad_keys = jnp.einsum(
-        "hqk,qhd->khd", grad_scores, query_low, preferred_element_type=jnp.float32
-    )
-    grad_values = jnp.einsum(
-        "hqk,qhd->khd", attn_weights.astype(low), grad_attended, preferred_element_type=jnp.float32
-    )
-    grad_pair = jnp.stack([grad_keys, grad_values]).reshape(
-        2, hop_count + 1, row_count, heads_here, HEAD
-    )
-    own_grad = grad_pair[:, hop_count]
-    for steps_back in range(1, hop_count + 1):
-        own_grad = own_grad + from_behind(
-            grad_pair[:, hop_count - steps_back].astype(low), "expert", -steps_back
-        ).astype(jnp.float32)
-    grad_query_norm = rotate(grad_query, cosine_table, -sine_table).reshape(row_count, local_width)
-    grad_key_norm = rotate(own_grad[0], cosine_table, -sine_table).reshape(row_count, local_width)
-    grad_gain_query = jnp.sum(grad_query_norm * normed_query, axis=0)
-    grad_gain_key = jnp.sum(grad_key_norm * normed_key, axis=0)
-    scaled_query = grad_query_norm * qk_gains[0]
-    scaled_key = grad_key_norm * qk_gains[1]
-    query_inner, key_inner = lax.psum(
-        (jnp.sum(scaled_query * query_raw, axis=-1), jnp.sum(scaled_key * key_raw, axis=-1)),
-        "tensor",
-    )
-    grad_query_raw = (
-        query_scale * scaled_query
-        - query_raw * (query_scale * query_scale * query_scale) * query_inner[:, None] / model_width
-    ).astype(low)
-    grad_key_raw = (
-        key_scale * scaled_key
-        - key_raw * (key_scale * key_scale * key_scale) * key_inner[:, None] / model_width
-    ).astype(low)
-    grad_value_raw = own_grad[1].reshape(row_count, local_width).astype(low)
-    grad_proj = jnp.stack([grad_query_raw, grad_key_raw, grad_value_raw])
-    grad_qkv = jnp.einsum("td,jte->jde", hidden_one, grad_proj, preferred_element_type=jnp.float32)
-    grad_hidden_one = tensor_sum(
-        jnp.einsum("jte,jde->td", grad_proj, qkv_low, preferred_element_type=jnp.float32).astype(low),
-        7,
-    ).astype(jnp.float32)
-    grad_gain_one = jnp.sum(grad_hidden_one * tokens_f * scale_one, axis=0)
-    scaled_one = grad_hidden_one * gain_one_f
-    grad_tokens = (
-        grad_residual
-        + scale_one * scaled_one
-        - tokens_f
-        * (scale_one * scale_one * scale_one)
-        * jnp.mean(scaled_one * tokens_f, axis=-1, keepdims=True)
-    )
-    grad_qk = (
-        jnp.stack([grad_gain_query, grad_gain_key])
-        .reshape(2, heads_here, groups, HEAD // groups)
-        .transpose(2, 0, 1, 3)
-        .reshape(groups, 1, qk_row.shape[1])
-    )
-    small_grads = jnp.concatenate(
-        [
-            grad_gain_one.reshape(groups, 1, row_count),
-            grad_gain_two.reshape(groups, 1, row_count),
-            jnp.pad(grad_qk, ((0, 0), (0, 0), (0, row_count - qk_row.shape[1]))),
-            jnp.zeros((groups, 5, row_count), jnp.float32),
-            grad_router_t.reshape(experts, groups, row_count).transpose(1, 0, 2),
-        ],
-        axis=1,
-    )
-    qkv_sum, out_sum, small_sum = weight_reduce(
-        grad_qkv.astype(low), grad_out_w.astype(low), small_grads, 8
+    grad_probs = grad_gate_sum[:, :local_experts].reshape(experts, row_count).T * chosen
+    grad_tokens, qkv_sum, out_sum, small_sum = attend_back(
+        grad_hidden_sum, grad_probs, router_t, hidden_two, residual, scale_two_wide,
+        gain_two_f[None, :], out_grad, query_low, context_blocks, segment_query[:, None], segment_keys,
+        attended, log_sums, raw, scales, qk_gains, wide_cosine, wide_sine, hidden_one, tokens_in,
+        gain_one_f[None, :], qkv_low, out_low, 8,
     )
     return (
         block_out.astype(low),
-        grad_tokens.astype(low),
+        grad_tokens,
         qkv_sum,
         out_sum,
         small_sum[0],
         small_sum[1],
-        small_sum[2, : qk_row.shape[1]].reshape(qk_gain.shape),
+        lax.dynamic_slice_in_dim(
+            small_sum[2:6].reshape(2, heads_here, HEAD),
+            device_index * qk_gain.shape[2], qk_gain.shape[2], axis=2,
+        ),
         small_sum[8 : 8 + experts].T,
         grad_gate_w,
         grad_up_w,

time: 776 us -> 637 us (0.82)
  the two profiles are of different devices: /device:TPU:0 before, /device:TPU:12 now
where the time goes in v3:
time: 637 us; the launch traced here: 630 us
  Pallas kernels  556 us (87%)
  local copies, waits for them, and re-layouts  42 us (7%)
  other arithmetic  16.9 us (3%)
  between operations  14.5 us (2%)
    pallas_call x1, Pallas kernels, attend_back(): pl.pallas_call(kernel, out_shape=(shape((rows, width), low), shape((3, de...  163 us
    pallas_call x1, Pallas kernels, project(): pl.pallas_call(kernel, out_shape=(shape((parts, depth * GROUPS, columns),...  133 us
    pallas_call x1, Pallas kernels, expert_layer(): pl.pallas_call(kernel, out_shape=(shape((tokens, width), low), shape((row...  97.2 us
    pallas_call x1, Pallas kernels, token_reduce(): pl.pallas_call(kernel, out_shape=jax.ShapeDtypeStruct((rows, quarter), jn...  71.1 us
    pallas_call x1, Pallas kernels, token_gather(): pl.pallas_call(kernel, out_shape=jax.ShapeDtypeStruct((rows * GROUPS, wid...  54.4 us
    pallas_call x1, Pallas kernels, attend(): pl.pallas_call(kernel, out_shape=(shape((rows, columns), low), shape((row...  36.7 us
    unnamed x65, local copies, waits for them, and re-layouts  26.7 us
  transfers between devices with their start and end apart: 4, of which 0 were waited for; matrix products, arithmetic and copies ran while one was open for 4% of the time, Pallas kernels for 62%

profile of v3, /device:TPU:12, one launch (start us, length us, event | category | flops | bytes accessed | tf_op | source)
XLA Modules:
  0.0 629.6 jit_solution(3096706068528954361)
XLA Ops:
  7.2 1.7 constant_dynamic-slice_fusion.1
  9.0 1.8 convert_element_type.39
  15.2 1.3 copy-done.1
  16.5 1.4 copy-done.6
  17.9 132.8 %project.1 = (bf16[3,2048,512]{2,1,0:T(8,128)(2,1)}, f32[8,40,256]{2,1,0:T(8,128)S(1)}, bf16[256,2048]{1,0:T(8,128)(2,1)S(1)}, f32[2,256,512]{2,1,0:T(8,128)S(1)...) custom-call(bf16[256,2048]{1,0:T(8,128)(2,1)S(1)} %copy-done.1, ...), custom_call_target="tpu_custom_call" | custom-call | bytes 300000000 | tf_op jit(solution)/shard_map/project/pallas_call | solution.py:1740
  150.8 1.0 copy-done.11
  153.4 2.5 convert.20
  156.9 1.5 convert.21
  158.4 1.4 copy-done.21
  159.8 1.6 convert_element_type.40
  162.1 1.3 copy.54
  164.0 1.8 slice_bitcast_fusion.1
  165.9 2.3 pad_maximum_fusion.gu_ref
  168.7 1.2 copy-done.2
  169.9 1.6 copy-done.3
  171.5 36.7 %attend.1 = (bf16[256,512]{1,0:T(8,128)(2,1)S(1)}, f32[256,128]{1,0:T(8,128)S(1)}, f32[256,2048]{1,0:T(8,128)S(1)}, bf16[256,2048]{1,0:T(8,128)(2,1)S(1)}, f32[256,128]{1,0:T(8,128)S(1)}) custom-call(bf16[256,512]{1,0:T(8,128)(2,1)S(1)} %get-tuple-element.36.q_ref, bf16[5,2,256,512]{3,2,1,0:T(8,128)(2,1)S(1)} %copy-done, s32[256,1]{1,0:T(8,128)S(1)} %copy.52.sq_ref, ...), custom_call_target="tpu_custom_call" | custom-call | bytes 120000000 | tf_op jit(solution)/shard_map/attend/pallas_call | solution.py:1848
  208.3 1.3 copy-done.4
  211.9 54.4 %token_gather.1.h_in = bf16[2048,2048]{1,0:T(8,128)(2,1)} custom-call(bf16[256,2048]{1,0:T(8,128)(2,1)} %copy-done.5), custom_call_target="tpu_custom_call" | custom-call | bytes 135000000 | tf_op jit(solution)/shard_map/token_gather/pallas_call | solution.py:656
  266.3 97.2 %expert_layer.1 = (bf16[2048,2048]{1,0:T(8,128)(2,1)}, bf16[256,2048]{1,0:T(8,128)(2,1)}, f32[8,8,256]{2,1,0:T(8,128)}, f32[2,2048,256]{2,1,0:T(8,128)}, f32[2,2...) custom-call(bf16[2048,2048]{1,0:T(8,128)(2,1)} %token_gather.1.h_in, bf16[2048,2048]{1,0:T(8,128)(2,1)} %all-gather.10.cloned.1.call-done.dy_in, ...), custom_call_target="tpu_custom_call" | custom-call | bytes 240000000 | tf_op jit(solution)/shard_map/expert_layer/pallas_call | solution.py:1470
  363.6 71.1 %token_reduce.1 = bf16[256,512]{1,0:T(8,128)(2,1)} custom-call(bf16[2048,2048]{1,0:T(8,128)(2,1)} %get-tuple-element.42.part_ref), custom_call_target="tpu_custom_call" | custom-call | bytes 180000000 | tf_op jit(solution)/shard_map/token_reduce/pallas_call | solution.py:1018
  438.1 163.3 %attend_back.1 = (bf16[256,2048]{1,0:T(8,128)(2,1)}, f32[3,256,512]{2,1,0:T(8,128)}, f32[512,256]{1,0:T(8,128)}, f32[24,256]{1,0:T(8,128)}) custom-call(bf16[256,2048]{1,0:T(8,128)(2,1)} %get-tuple-element.43.dh_ref, f32[256,16]{1,0:T(8,128)} %bitcast_select_fusion.gates_ref, bf16[16,2048]{1,0:T(8,128)(2,1)} %bitcast.40, bf16[256,2048]{1,0:T(8,128)(2,1)} %copy-done.5, ...), custom_call_target="tpu_custom_call" | custom-call | bytes 390000000 | tf_op jit(solution)/shard_map/attend_back/pallas_call | solution.py:2182
  602.9 1.3 fusion.7
  604.2 1.3 slice_bitcast_fusion.5
  605.6 1.4 fusion.5
  607.0 2.9 add_convert_fusion
  609.9 1.0 copy.68
  610.9 1.1 copy.69
  613.2 2.1 copy.71
  615.3 1.6 copy-done.23
  616.9 2.1 copy.72
  619.0 1.6 copy-done.22
  620.6 2.0 copy.73
  (96 shorter events, 17.0 us)
Async XLA Ops:
  7.2 145.8 %copy-start.28 = (s32[2048]{0:T(1024)S(1)}, s32[2048]{0:T(1024)}, u32[]{:S(2)}) copy-start(s32[2048]{0:T(1024)} %param.25) | copy-start | bytes 24580
  7.2 145.6 %all-gather.6.cloned.1.call-start = ((), (), s32[]{:S(2)}) async-start(), calls=%async_computation | async-start | bytes 2359296 | tf_op jit(solution)/shard_map/all_gather | solution.py:2283
  8.9 159.3 %all-gather.8.cloned.1.call-start = ((), (), s32[]{:S(2)}) async-start(), calls=%async_computation.1 | async-start | bytes 2359296 | tf_op jit(solution)/shard_map/all_gather | solution.py:2284
  10.8 255.6 %all-gather.10.cloned.1.call-start = ((), (), s32[]{:S(2)}) async-start(), calls=%async_computation.2 | async-start | bytes 10485760 | tf_op jit(solution)/shard_map/all_gather | solution.py:2289
  15.2 140.8 %copy-start.7 = (f32[256,128]{1,0:T(8,128)}, f32[256,128]{1,0:T(8,128)S(1)}, u32[]{:S(2)}) copy-start(f32[256,128]{1,0:T(8,128)S(1)} %get-tuple-element.74.cos_ref) | copy-start | bytes 393220
  15.2 140.8 %copy-start.8 = (f32[256,128]{1,0:T(8,128)}, f32[256,128]{1,0:T(8,128)S(1)}, u32[]{:S(2)}) copy-start(f32[256,128]{1,0:T(8,128)S(1)} %get-tuple-element.75.sin_ref) | copy-start | bytes 393220
  15.2 1.3 copy-start.1
  16.5 1.4 copy-start.6
  150.8 1.0 copy-start.11
  151.8 1.0 copy-start.12
  152.7 3.2 copy-start.15
  152.7 10.7 %copy-start.14 = (f32[8,40,256]{2,1,0:T(8,128)}, f32[8,40,256]{2,1,0:T(8,128)S(1)}, u32[]{:S(2)}) copy-start(f32[8,40,256]{2,1,0:T(8,128)S(1)} %get-tuple-element.38) | copy-start | bytes 983044
  152.7 15.5 %copy-start.10 = (bf16[256,512]{1,0:T(8,128)(2,1)}, bf16[256,512]{1,0:T(8,128)(2,1)S(1)}, u32[]{:S(2)}) copy-start(bf16[256,512]{1,0:T(8,128)(2,1)S(1)} %get-tuple-element.36.q_ref) | copy-start | bytes 786436
  152.8 452.8 %all-gather.12.cloned.1.call-start = ((), (), s32[]{:S(2)}) async-start(), calls=%async_computation.3 | async-start | bytes 1310720 | tf_op jit(solution)/shard_map/all_gather | solution.py:2321
  153.1 15.1 %copy-start.18 = (s32[5,256]{1,0:T(8,128)}, s32[5,256]{1,0:T(8,128)S(1)}, u32[]{:S(2)}) copy-start(s32[5,256]{1,0:T(8,128)S(1)} %rev.3.sk_ref) | copy-start | bytes 15364
  153.4 14.8 %copy-start.9 = (s32[256,1]{1,0:T(8,128)}, s32[256,1]{1,0:T(8,128)S(1)}, u32[]{:S(2)}) copy-start(s32[256,1]{1,0:T(8,128)S(1)} %copy.52.sq_ref) | copy-start | bytes 3076
  153.4 3.5 copy-start.20
  156.9 2.9 copy-start.21
  164.0 4.2 copy-start.19
  165.9 2.9 copy-start
  168.7 1.2 copy-start.2
  169.9 1.6 copy-start.3
  208.3 1.3 copy-start.4
  209.6 1.0 copy-start.5
  210.6 0.7 copy-start.16
  211.9 54.5 %copy-start.13 = (bf16[256,512]{1,0:T(8,128)(2,1)}, bf16[256,512]{1,0:T(8,128)(2,1)S(1)}, u32[]{:S(2)}) copy-start(bf16[256,512]{1,0:T(8,128)(2,1)S(1)} %get-tuple-element.46.o_ref) | copy-start | bytes 786436
  601.4 8.5 %copy-start.26 = (bf16[256,2048]{1,0:T(8,128)(2,1)S(1)}, bf16[256,2048]{1,0:T(8,128)(2,1)}, u32[]{:S(2)}) copy-start(bf16[256,2048]{1,0:T(8,128)(2,1)} %get-tuple-element.90) | copy-start | bytes 3145732
  605.6 5.3 copy-start.25
  606.9 5.1 copy-start.27
  609.9 3.3 copy-start.24
  613.2 3.7 copy-start.23
  616.9 3.7 copy-start.22
  (1 other events, 0.7 us)
Sparse Core Ops, SparseCore 0:
  10.7 65.4 all-gather.5
  78.8 67.4 all-gather.7
  152.9 86.8 all-gather.9
  434.9 15.7 all-gather.11

commit v4 on v3

--- a/solution.py
+++ b/solution.py
@@ -1112,7 +1112,9 @@
     lax.fori_loop(0, rows // step, body, 0)
 
 
-def expert_layer(hidden_all, grad_out_all, gate_up, down, router_t, chosen_all, collective_id):
+def expert_layer(
+    hidden_all, grad_out_all, gate_up, down, router_t, chosen_all, residual, collective_id
+):
     tokens, width = hidden_all.shape
     rows = tokens // GROUPS
     units = down.shape[0]
@@ -1121,16 +1123,16 @@
     experts = router_t.shape[0]
     half, part, piece = width // 2, width // 4, width // 8
     tensors = NX * NC
-    steps = GROUPS + 4
+    steps = GROUPS + 5
     low = jnp.bfloat16
     wide = width // 4
 
     def kernel(
-        h_in, dy_in, gu_ref, down_ref, router_ref, chosen_ref,
-        y_out, dh_out, gates_out, gate_w, up_w, down_w,
-        h, dy, gated, dgu, dx, y_stage, gu_stage, d_stage,
+        h_in, dy_in, gu_ref, down_ref, router_ref, chosen_ref, x1_in,
+        block_out, dh_out, gates_out, gate_w, up_w, down_w,
+        h, dy, gated, dgu, dx, y_part, yc_buf, yx_buf, yy_buf, ylo_buf, yhi_buf, x1, gu_stage, d_stage,
         core_buf, px_buf, py_buf, qy_buf, qx_buf, z_sum, lo_buf, hi_buf, gate_part, gate_land,
-        in_sem, y_sem, gu_sem, d_sem, core_s, core_r, px_s, px_r, py_s, py_r, qy_s, qy_r, qx_s, qx_r,
+        in_sem, x1_sem, yc_s, yc_r, yx_s, yx_r, yy_s, yy_r, yz_s, yz_r, gu_sem, d_sem, core_s, core_r, px_s, px_r, py_s, py_r, qy_s, qy_r, qx_s, qx_r,
         z_s, z_r, near_s, near_r, far_s, far_r, end_s, end_r,
     ):
         z, y, x, c = place()
@@ -1160,11 +1162,15 @@
             return carry
 
         lax.fori_loop(0, GROUPS, start_load, 0)
+        x1_copy = pltpu.make_async_copy(
+            x1_in.at[:, pl.ds(pl.multiple_of(c * half + x * part, part), part)], x1, x1_sem
+        )
+        x1_copy.start()
 
         def to_twin(i):
             b = block_of(i)
             return remote(
-                dx.at[block_rows(b, rows), pl.ds(pl.multiple_of((1 - c) * half, half), half)],
+                dx.at[lax.rem(i, 2), :, pl.ds(pl.multiple_of((1 - c) * half, half), half)],
                 core_buf.at[b], core_s.at[i], core_r.at[i], twin,
             )
 
@@ -1199,7 +1205,7 @@
             to_twin(i).wait_recv()
             b = block_of(i)
             mine = core_buf.at[b]
-            add_to(mine, mine, dx.at[block_rows(b, rows), pl.ds(pl.multiple_of(c * half, half), half)], 32)
+            add_to(mine, mine, dx.at[lax.rem(i, 2), :, pl.ds(pl.multiple_of(c * half, half), half)], 32)
             p_across(i).start()
             pl.when(lax.rem(i, 2) == 0)(lambda: q_beside(lax.div(i, 2)).start())
 
@@ -1242,6 +1248,63 @@
                         down_z(j, s).wait_recv()
                         add_to(z_sum.at[s, j], z_sum.at[s, j], hi_buf.at[s, j])
                     down_z(j, s).start()
+
+            pl.when((z < zz) & (z == k))(upward)
+            pl.when((z > zz) & (NZ - 1 - z == k))(downward)
+
+        def y_twin(i):
+            return remote(
+                y_part.at[lax.rem(i, 2), :, pl.ds(pl.multiple_of((1 - c) * half, half), half)],
+                yc_buf.at[block_of(i)], yc_s.at[i], yc_r.at[i], twin,
+            )
+
+        def y_across(i):
+            b = block_of(i)
+            return remote(
+                yc_buf.at[b, :, pl.ds(pl.multiple_of((1 - x) * part, part), part)],
+                yx_buf.at[b], yx_s.at[i], yx_r.at[i], across,
+            )
+
+        def y_beside(j):
+            return remote(yx_buf.at[block_of(2 * j)], yy_buf.at[j], yy_s.at[j], yy_r.at[j], beside)
+
+        def y_up(j):
+            return remote(yy_buf.at[j], ylo_buf.at[j], yz_s.at[0, j], yz_r.at[0, j], device(z + 1, y, x, c))
+
+        def y_down(j):
+            return remote(yy_buf.at[j], yhi_buf.at[j], yz_s.at[1, j], yz_r.at[1, j], device(z - 1, y, x, c))
+
+        def take_y_twin(i):
+            y_twin(i).wait_recv()
+            mine = yc_buf.at[block_of(i)]
+            add_to(mine, mine, y_part.at[lax.rem(i, 2), :, pl.ds(pl.multiple_of(c * half, half), half)], 32)
+            y_across(i).start()
+
+        def take_y_across(i):
+            y_across(i).wait_recv()
+            b = block_of(i)
+            mine = yx_buf.at[b]
+            add_to(mine, mine, yc_buf.at[b, :, pl.ds(pl.multiple_of(x * part, part), part)])
+            pl.when(lax.rem(i, 2) == 0)(lambda: y_beside(lax.div(i, 2)).start())
+
+        def take_y_beside(j):
+            y_beside(j).wait_recv()
+            add_to(yy_buf.at[j], yy_buf.at[j], yx_buf.at[block_of(2 * j + 1)])
+
+        def y_hop(j, k):
+            zz = zz_of(j)
+
+            def upward():
+                if k > 0:
+                    y_up(j).wait_recv()
+                    add_to(yy_buf.at[j], yy_buf.at[j], ylo_buf.at[j])
+                y_up(j).start()
+
+            def downward():
+                if k > 0:
+                    y_down(j).wait_recv()
+                    add_to(yy_buf.at[j], yy_buf.at[j], yhi_buf.at[j])
+                y_down(j).start()
 
             pl.when((z < zz) & (z == k))(upward)
             pl.when((z > zz) & (NZ - 1 - z == k))(downward)
@@ -1254,7 +1317,7 @@
             rows_h, rows_dy = h[r, :], dy[r, :]
             logits = dot(rows_h, router_ref[...], (1, 1))
             shifted = jnp.exp(logits - jnp.max(logits, axis=-1, keepdims=True))
-            probs = shifted / jnp.sum(shifted, axis=-1, keepdims=True) * chosen_ref[r, :]
+            probs = shifted / jnp.sum(shifted, axis=-1, keepdims=True) * chosen_ref[r, :].astype(jnp.float32)
             lane = lax.broadcasted_iota(jnp.int32, probs.shape, 1)
             line = lax.broadcasted_iota(jnp.int32, (rows, 128), 1)
             found = jnp.zeros((rows, 128), jnp.float32)
@@ -1274,34 +1337,30 @@
                 dgu[r, up_at] = (back * swish).astype(low)
             gate_part[b] = jnp.transpose(found)[:8, :]
 
-        def y_copy(i):
-            return pltpu.make_async_copy(
-                y_stage.at[lax.rem(i, 2)], y_out.at[block_rows(block_of(i), rows), :], y_sem.at[lax.rem(i, 2)]
-            )
-
         def rear(i):
             r = block_rows(block_of(i), rows)
             slot = lax.rem(i, 2)
+            pl.when(i >= 2)(lambda: to_twin(i - 2).wait_send())
 
             def columns(k, carry):
                 at = pl.ds(pl.multiple_of(k * wide, wide), wide)
-                dx[r, at] = dot(dgu[r, :], gu_ref[at, :], (1, 1)).astype(low)
+                dx[slot, :, at] = dot(dgu[r, :], gu_ref[at, :], (1, 1)).astype(low)
                 return carry
 
             lax.fori_loop(0, width // wide, columns, 0)
             to_twin(i).start()
-            pl.when(i >= 2)(lambda: y_copy(i - 2).wait())
+            pl.when(i >= 2)(lambda: y_twin(i - 2).wait_send())
 
             def y_columns(k, carry):
                 at = pl.ds(pl.multiple_of(k * wide, wide), wide)
-                y_stage[slot, :, at] = dot(gated[r, :], down_ref[:, at], (1, 0)).astype(low)
+                y_part[slot, :, at] = dot(gated[r, :], down_ref[:, at], (1, 0)).astype(low)
                 return carry
 
             lax.fori_loop(0, width // wide, y_columns, 0)
-            y_copy(i).start()
+            y_twin(i).start()
 
         tiles = width // piece // 4
-        d_width = width // 4
+        d_width = width // 8
 
         def gu_copies(n):
             slot = lax.rem(n, 2)
@@ -1339,10 +1398,16 @@
                 return carry
 
             lax.fori_loop(0, tiles, tile, 0)
-            pl.when(q >= 2)(lambda: each(d_copies(q - 2), "wait"))
-            at = pl.ds(pl.multiple_of(q * d_width, d_width), d_width)
-            d_stage[lax.rem(q, 2)] = dot(gated[...], dy[:, at], (0, 0))
-            each(d_copies(q), "start")
+
+            def d_tile(k, carry):
+                n = q * 2 + k
+                pl.when(n >= 2)(lambda: each(d_copies(n - 2), "wait"))
+                at = pl.ds(pl.multiple_of(n * d_width, d_width), d_width)
+                d_stage[lax.rem(n, 2)] = dot(gated[...], dy[:, at], (0, 0))
+                each(d_copies(n), "start")
+                return carry
+
+            lax.fori_loop(0, 2, d_tile, 0)
 
         near = [
             remote(gate_part, gate_land.at[k], near_s.at[k], near_r.at[k], mates[k])
@@ -1371,6 +1436,7 @@
             even = lax.rem(i, 2) == 0
             pl.when(i < GROUPS)(lambda: front(i))
             pl.when((i >= 1) & (i <= GROUPS))(lambda: take_twin(i - 1))
+            pl.when((i >= 1) & (i <= GROUPS))(lambda: take_y_twin(i - 1))
             pl.when(even & (i >= 2) & (i <= GROUPS))(lambda: take_q_beside(j_even))
 
             def late():
@@ -1381,7 +1447,7 @@
             pl.when(i == GROUPS)(lambda: each(near, "start"))
             pl.when(i == GROUPS + 1)(sum_near)
             pl.when(i < GROUPS)(lambda: rear(i))
-            pl.when(i >= GROUPS)(lambda: weight_grads(i - GROUPS))
+            pl.when((i >= GROUPS) & (i < GROUPS + 4))(lambda: weight_grads(i - GROUPS))
 
             def pass_p():
                 take_p_across(i - 2)
@@ -1396,6 +1462,15 @@
             pl.when((lax.rem(i, 2) == 1) & (i >= 3) & (i <= GROUPS + 1))(join)
             pl.when(even & (i >= 4) & (i <= GROUPS + 2))(lambda: hop(j_even - 1, 1))
             pl.when((lax.rem(i, 2) == 1) & (i >= 5) & (i <= GROUPS + 3))(lambda: hop(j_odd - 1, 2))
+            pl.when((i >= 2) & (i <= GROUPS + 1))(lambda: take_y_across(i - 2))
+
+            def join_y():
+                take_y_beside(j_even - 1)
+                y_hop(j_even - 1, 0)
+
+            pl.when(even & (i >= 4) & (i <= GROUPS + 2))(join_y)
+            pl.when((lax.rem(i, 2) == 1) & (i >= 5) & (i <= GROUPS + 3))(lambda: y_hop(j_odd - 1, 1))
+            pl.when(even & (i >= 6) & (i <= GROUPS + 4))(lambda: y_hop(j_even - 2, 2))
             return carry
 
         lax.fori_loop(0, steps, step, 0)
@@ -1425,10 +1500,43 @@
             lax.fori_loop(0, rows // 64, keep, 0)
             remote(own, own, end_s.at[0, s], end_r.at[0, s], across).start()
             remote(own, own, end_s.at[1, s], end_r.at[1, s], twin).start()
+        def y_columns_of(xx, cc):
+            return pl.ds(pl.multiple_of(cc * half + xx * part, part), part)
+
+        def y_below():
+            y_up(mine).wait_recv()
+            add_to(yy_buf.at[mine], yy_buf.at[mine], ylo_buf.at[mine])
+
+        def y_above():
+            y_down(mine).wait_recv()
+            add_to(yy_buf.at[mine], yy_buf.at[mine], yhi_buf.at[mine])
+
+        pl.when(z > 0)(y_below)
+        pl.when(z < NZ - 1)(y_above)
+        x1_copy.wait()
+        y_own = block_out.at[:, y_columns_of(x, c)]
+
+        def finish(k, carry):
+            r = pl.ds(pl.multiple_of(k * 64, 64), 64)
+            y_own[r, :] = (x1[r, :] + yy_buf[mine, r, :].astype(jnp.float32)).astype(low)
+            return carry
+
+        lax.fori_loop(0, rows // 64, finish, 0)
+        remote(y_own, y_own, end_s.at[0, 2], end_r.at[0, 2], across).start()
+        remote(y_own, y_own, end_s.at[1, 2], end_r.at[1, 2], twin).start()
         for s in range(2):
             there = dh_out.at[:, columns_of(s, 1 - x, c)]
             remote(there, there, end_s.at[0, s], end_r.at[0, s], across).wait_recv()
             remote(there, there, end_s.at[2, s], end_r.at[2, s], twin).start()
+        there = block_out.at[:, y_columns_of(1 - x, c)]
+        remote(there, there, end_s.at[0, 2], end_r.at[0, 2], across).wait_recv()
+        remote(there, there, end_s.at[2, 2], end_r.at[2, 2], twin).start()
+        for k, xx in ((1, x), (2, 1 - x)):
+            there = block_out.at[:, y_columns_of(xx, 1 - c)]
+            remote(there, there, end_s.at[k, 2], end_r.at[k, 2], twin).wait_recv()
+        for k, target in ((0, across), (1, twin), (2, twin)):
+            there = block_out.at[:, y_columns_of(1 - x if k == 2 else x, c)]
+            remote(there, there, end_s.at[k, 2], end_r.at[k, 2], target).wait_send()
         for s in range(2):
             for k, xx in ((1, x), (2, 1 - x)):
                 there = dh_out.at[:, columns_of(s, xx, 1 - c)]
@@ -1443,8 +1551,10 @@
         each(near, "wait_send")
 
         def drain(i, carry):
-            to_twin(i).wait_send()
+            pl.when(i >= GROUPS - 2)(lambda: to_twin(i).wait_send())
+            pl.when(i >= GROUPS - 2)(lambda: y_twin(i).wait_send())
             p_across(i).wait_send()
+            y_across(i).wait_send()
             return carry
 
         lax.fori_loop(0, GROUPS, drain, 0)
@@ -1453,6 +1563,9 @@
             p_beside(j).wait_send()
             q_beside(j).wait_send()
             q_across(j).wait_send()
+            y_beside(j).wait_send()
+            pl.when(z < zz_of(j))(lambda: y_up(j).wait_send())
+            pl.when(z > zz_of(j))(lambda: y_down(j).wait_send())
             for s in range(2):
                 pl.when(z < zz_of(j))(lambda s=s: up(j, s).wait_send())
                 pl.when(z > zz_of(j))(lambda s=s: down_z(j, s).wait_send())
@@ -1460,9 +1573,8 @@
 
         lax.fori_loop(0, NZ, drain_pair, 0)
         for k in range(2):
-            y_copy(GROUPS - 2 + k).wait()
             each(gu_copies(4 * tiles - 2 + k), "wait")
-            each(d_copies(2 + k), "wait")
+            each(d_copies(6 + k), "wait")
 
     shape = jax.ShapeDtypeStruct
     dma = pltpu.SemaphoreType.DMA
@@ -1470,24 +1582,30 @@
     return pl.pallas_call(
         kernel,
         out_shape=(
-            shape((tokens, width), low),
+            shape((rows, width), low),
             shape((rows, width), low),
             shape((GROUPS, 8, rows), f32),
             shape((local, width, hidden), f32),
             shape((local, width, hidden), f32),
             shape((local, hidden, width), f32),
         ),
-        in_specs=[HBM, HBM, VMEM, VMEM, VMEM, VMEM],
-        out_specs=(HBM, VMEM, VMEM, HBM, HBM, HBM),
+        in_specs=[HBM, HBM, VMEM, VMEM, VMEM, VMEM, HBM],
+        out_specs=(VMEM, VMEM, VMEM, HBM, HBM, HBM),
         scratch_shapes=[
             pltpu.VMEM((tokens, width), low),
             pltpu.VMEM((tokens, width), low),
             pltpu.VMEM((tokens, units), low),
             pltpu.VMEM((tokens, 2 * units), low),
-            pltpu.VMEM((tokens, width), low),
             pltpu.VMEM((2, rows, width), low),
+            pltpu.VMEM((2, rows, width), low),
+            pltpu.VMEM((GROUPS, rows, half), low),
+            pltpu.VMEM((GROUPS, rows, part), low),
+            pltpu.VMEM((NZ, rows, part), low),
+            pltpu.VMEM((NZ, rows, part), low),
+            pltpu.VMEM((NZ, rows, part), low),
+            pltpu.VMEM((rows, part), f32),
             pltpu.VMEM((2, piece, 2 * units), f32),
-            pltpu.VMEM((2, units, width // 4), f32),
+            pltpu.VMEM((2, units, width // 8), f32),
             pltpu.VMEM((GROUPS, rows, half), low),
             pltpu.VMEM((GROUPS, rows, piece), low),
             pltpu.VMEM((NZ, rows, piece), low),
@@ -1498,17 +1616,18 @@
             pltpu.VMEM((2, NZ, rows, piece), low),
             pltpu.VMEM((GROUPS, 8, rows), f32),
             pltpu.VMEM((tensors, GROUPS, 8, rows), f32),
-            dma((2, GROUPS)), dma((2,)), dma((2, 2 * local)), dma((2, local)),
+            dma((2, GROUPS)), dma, dma((GROUPS,)), dma((GROUPS,)), dma((GROUPS,)), dma((GROUPS,)),
+            dma((NZ,)), dma((NZ,)), dma((2, NZ)), dma((2, NZ)), dma((2, 2 * local)), dma((2, local)),
             dma((GROUPS,)), dma((GROUPS,)), dma((GROUPS,)), dma((GROUPS,)),
             dma((NZ,)), dma((NZ,)), dma((NZ,)), dma((NZ,)), dma((NZ,)), dma((NZ,)),
             dma((2, 2, NZ)), dma((2, 2, NZ)),
             dma((tensors - 1,)), dma((tensors - 1,)), dma((GROUPS - 1,)), dma((GROUPS - 1,)),
-            dma((3, 2)), dma((3, 2)),
+            dma((3, 3)), dma((3, 3)),
         ],
         compiler_params=comm_params(collective_id, 62),
         cost_estimate=cost(80),
         name="expert_layer",
-    )(hidden_all, grad_out_all, gate_up, down, router_t, chosen_all)
+    )(hidden_all, grad_out_all, gate_up, down, router_t, chosen_all, residual)
 
 
 def exchange_rows(value, part_ref, land_ref, send_sem, recv_sem, mates):
@@ -1893,8 +2012,8 @@
         tok_grad, qkv_sum, out_sum, small_sum,
         weights, dx1, da, do, dot_sums, dq, dkv, proj, send_kv, land_y, land_z,
         part, full, core_buf, x_buf, small, line_sum,
-        main_buf, out_buf, small_buf, part_k, land_k, part_q, land_q,
-        w_sem, y_s, y_r, z_s, z_r, group_s, group_r, ks_s, ks_r, qs_s, qs_r, line_s, line_r,
+        main_buf, out_acc, out_lo, out_hi, out_land, small_buf, part_k, land_k, part_q, land_q,
+        w_sem, y_s, y_r, z_s, z_r, group_s, group_r, ks_s, ks_r, qs_s, qs_r, line_s, line_r, out_s, out_r, out_y_s, out_y_r,
     ):
         z, y, x, c = place()
         e, t = lax.axis_index("expert"), lax.axis_index("tensor")
@@ -1907,15 +2026,65 @@
             if s == SMALL:
                 return small[b]
             at = pl.ds(pl.multiple_of(b * depth, depth), depth)
-            if s == OUT:
-                return dot(o_ref[...], da[:, at], (0, 0))
             return dot(h1_ref[:, at], proj[s], (0, 0))
+
+        def out_copy(zz, yy, way):
+            landing = (out_lo if way == 0 else out_hi).at[zz, yy]
+            target = device(z + 1, y, x, c) if way == 0 else below
+            return remote(out_acc.at[zz, yy], landing, out_s.at[zz, yy, way], out_r.at[zz, yy, way], target)
+
+        def out_take(zz, yy, way):
+            out_copy(zz, yy, way).wait_recv()
+            total = out_acc.at[zz, yy]
+            add_to(total, total, (out_lo if way == 0 else out_hi).at[zz, yy])
+
+        def out_hop(k):
+            for zz in Z_ORDER:
+                for yy in range(NY):
+                    def upward(zz=zz, yy=yy):
+                        if k > 0:
+                            out_take(zz, yy, 0)
+                        out_copy(zz, yy, 0).start()
+
+                    def downward(zz=zz, yy=yy):
+                        if k > 0:
+                            out_take(zz, yy, 1)
+                        out_copy(zz, yy, 1).start()
+
+                    if k < zz:
+                        run_if((z < zz) & (z == k), upward)
+                    if NZ - 1 - k > zz:
+                        run_if((z > zz) & (NZ - 1 - z == k), downward)
+
+        def out_beside():
+            return remote(out_acc.at[z, 1 - y], out_land, out_y_s, out_y_r, beside)
+
+        def out_start():
+            for zz in range(NZ):
+                for yy in range(NY):
+                    at = pl.ds((zz * NY + yy) * depth, depth)
+                    out_acc[zz, yy] = dot(o_ref[...], da[:, at], (0, 0)).astype(low)
+
+        def out_home():
+            for yy in range(NY):
+                run_if(z > 0, lambda yy=yy: out_take(z, yy, 0))
+                run_if(z < NZ - 1, lambda yy=yy: out_take(z, yy, 1))
+            out_beside().start()
+
+        def out_end():
+            out_beside().wait_recv()
+            out_sum[...] = out_acc[z, y].astype(f32) + out_land[...].astype(f32)
+            out_beside().wait_send()
+            for zz in range(NZ):
+                for yy in range(NY):
+                    run_if(z < zz, lambda zz=zz, yy=yy: out_copy(zz, yy, 0).wait_send())
+                    run_if(z > zz, lambda zz=zz, yy=yy: out_copy(zz, yy, 1).wait_send())
 
         def slot(kind):
             def view(s, zz):
                 if s == SMALL:
                     return small_buf.at[kind, zz]
-                return out_buf.at[kind, zz] if s == OUT else main_buf.at[kind, zz, s]
+                return main_buf.at[kind, zz, s]
             return view
 
         line = LineReduce([], lambda s, zz, yy: slot(3)(s, zz), slot(0), slot(1), slot(2), line_s, line_r)
@@ -1951,6 +2120,9 @@
 
         lax.fori_loop(0, rows // 32, norm_two, 0)
 
+        out_start()
+        out_hop(0)
+
         do[...] = dot(da[...], out_ref[...], (1, 1)).astype(low)
         wide = lax.broadcasted_iota(jnp.int32, (rows, 128), 1)
         sums = jnp.zeros((rows, 128), f32)
@@ -2065,6 +2237,7 @@
 
         take_three(1)
         take_three(0)
+        out_hop(1)
         take_one(1)
         take_one(0)
         take_four(1)
@@ -2076,10 +2249,11 @@
         send_beside(QUERY)
         send_beside(VALUE)
         take_two(0)
+        out_hop(2)
         exchange_rows(unturn(KEY, lambda at: dkv[0, 0, :, at]), part_k, land_k, ks_s, ks_r, mates)
         denorm(KEY, exchanged_rows(part_k, land_k, ks_s, ks_r, mates))
         send_beside(KEY)
-        send_beside(OUT)
+        out_home()
         fetch.wait()
 
         def half_of(cc):
@@ -2160,16 +2334,16 @@
         send_beside(SMALL)
         run_units(KEY)
         run_units(SMALL)
-        run_units(OUT)
+        out_end()
         hop(*units[-1], 1)
         hop(*units[-2], 2)
         hop(*units[-1], 2)
 
         def done(s, total):
-            target = qkv_sum.at[s] if s < OUT else (out_sum if s == OUT else small_sum)
+            target = qkv_sum.at[s] if s < OUT else small_sum
             target[...] = total[...].astype(f32)
 
-        line.streams = [QUERY, VALUE, KEY, SMALL, OUT]
+        line.streams = [QUERY, VALUE, KEY, SMALL]
         line.home(done)
         line.finish()
         for which in range(2):
@@ -2208,7 +2382,10 @@
             vmem((GROUPS, small_rows, depth), f32),
             vmem((8, width), f32),
             vmem((4, NZ, 3, depth, columns), low),
-            vmem((4, NZ, columns, depth), low),
+            vmem((NZ, NY, columns, depth), low),
+            vmem((NZ, NY, columns, depth), low),
+            vmem((NZ, NY, columns, depth), low),
+            vmem((columns, depth), low),
             vmem((4, NZ, small_rows, depth), f32),
             vmem((8, rows), f32),
             vmem((tensors - 1, 8, rows), f32),
@@ -2216,7 +2393,7 @@
             vmem((tensors - 1, 8, rows), f32),
             dma, dma((2, 2)), dma((2, 2)), dma((2, 2)), dma((2, 2)), dma((5,)), dma((5,)),
             dma((tensors - 1,)), dma((tensors - 1,)), dma((tensors - 1,)), dma((tensors - 1,)),
-            dma((5, NZ, 3)), dma((5, NZ, 3)),
+            dma((5, NZ, 3)), dma((5, NZ, 3)), dma((NZ, NY, 2)), dma((NZ, NY, 2)), dma, dma,
         ],
         compiler_params=comm_params(collective_id, 62),
         cost_estimate=cost(130),
@@ -2314,14 +2491,9 @@
         [w[i] for w in (w_gate, w_up) for i in range(local_experts)], axis=1
     ).astype(low)
     down_low = w_down.reshape(-1, model_width).astype(low)
-    expert_part, grad_hidden_sum, grad_gate_sum, grad_gate_w, grad_up_w, grad_down = expert_layer(
-        hidden_all, grad_out_all, gate_up, down_low, router_t, chosen_all, 5
-    )
-    expert_quarter = token_reduce(expert_part, 6)
-    expert_pieces = lax.all_gather(expert_quarter, "tensor", axis=0)
-    block_out = residual + jnp.concatenate(
-        [expert_pieces[i] for i in (0, 2, 1, 3)], axis=1
-    ).astype(jnp.float32)
+    block_out, grad_hidden_sum, grad_gate_sum, grad_gate_w, grad_up_w, grad_down = expert_layer(
+        hidden_all, grad_out_all, gate_up, down_low, router_t, chosen_all.astype(low), residual, 5
+    )
     grad_probs = grad_gate_sum[:, :local_experts].reshape(experts, row_count).T * chosen
     grad_tokens, qkv_sum, out_sum, small_sum = attend_back(
         grad_hidden_sum, grad_probs, router_t, hidden_two, residual, scale_two_wide,
@@ -2330,7 +2502,7 @@
         gain_one_f[None, :], qkv_low, out_low, 8,
     )
     return (
-        block_out.astype(low),
+        block_out,
         grad_tokens,
         qkv_sum,
         out_sum,

time: 637 us -> 593 us (0.931)
  the two profiles are of different devices: /device:TPU:12 before, /device:TPU:0 now
where the time goes in v4:
time: 593 us; the launch traced here: 587 us
  Pallas kernels  516 us (87%)
  local copies, waits for them, and re-layouts  42.9 us (7%)
  between operations  14.5 us (2%)
  other arithmetic  14 us (2%)
    pallas_call x1, Pallas kernels, attend_back(): pl.pallas_call(kernel, out_shape=(shape((rows, width), low), shape((3, de...  155 us
    pallas_call x1, Pallas kernels, expert_layer(): pl.pallas_call(kernel, out_shape=(shape((rows, width), low), shape((rows,...  135 us
    pallas_call x1, Pallas kernels, project(): pl.pallas_call(kernel, out_shape=(shape((parts, depth * GROUPS, columns),...  132 us
    pallas_call x1, Pallas kernels, token_gather(): pl.pallas_call(kernel, out_shape=jax.ShapeDtypeStruct((rows * GROUPS, wid...  56.3 us
    pallas_call x1, Pallas kernels, attend(): pl.pallas_call(kernel, out_shape=(shape((rows, columns), low), shape((row...  36.8 us
    unnamed x63, local copies, waits for them, and re-layouts  30 us
  transfers between devices with their start and end apart: 3, of which 0 were waited for; matrix products, arithmetic and copies ran while one was open for 3% of the time, Pallas kernels for 38%

profile of v4, /device:TPU:0, one launch (start us, length us, event | category | flops | bytes accessed | tf_op | source)
XLA Modules:
  0.0 587.1 jit_solution(7802717092488192380)
XLA Ops:
  7.2 1.7 constant_dynamic-slice_fusion.1
  9.0 1.8 convert_element_type.38
  15.2 1.3 copy-done.1
  16.5 1.4 copy-done.6
  17.9 131.9 %project.1 = (bf16[3,2048,512]{2,1,0:T(8,128)(2,1)}, f32[8,40,256]{2,1,0:T(8,128)S(1)}, bf16[256,2048]{1,0:T(8,128)(2,1)S(1)}, f32[2,256,512]{2,1,0:T(8,128)S(1)...) custom-call(bf16[256,2048]{1,0:T(8,128)(2,1)S(1)} %copy-done.1, ...), custom_call_target="tpu_custom_call" | custom-call | bytes 300000000 | tf_op jit(solution)/shard_map/project/pallas_call | solution.py:1859
  149.9 1.0 copy-done.11
  150.9 1.0 copy-done.12
  153.1 2.5 convert.21
  156.6 1.5 convert.22
  158.1 1.4 copy-done.20
  159.5 1.6 convert_element_type.39
  162.6 1.0 copy.54
  164.2 1.8 slice_bitcast_fusion.1
  166.0 2.3 pad_maximum_fusion.gu_ref
  168.9 1.2 copy-done.2
  170.1 1.6 copy-done.3
  171.7 36.8 %attend.1 = (bf16[256,512]{1,0:T(8,128)(2,1)S(1)}, f32[256,128]{1,0:T(8,128)S(1)}, f32[256,2048]{1,0:T(8,128)S(1)}, bf16[256,2048]{1,0:T(8,128)(2,1)S(1)}, f32[256,128]{1,0:T(8,128)S(1)}) custom-call(bf16[256,512]{1,0:T(8,128)(2,1)S(1)} %get-tuple-element.36.q_ref, bf16[5,2,256,512]{3,2,1,0:T(8,128)(2,1)S(1)} %copy-done, s32[256,1]{1,0:T(8,128)S(1)} %copy.52.sq_ref, ...), custom_call_target="tpu_custom_call" | custom-call | bytes 120000000 | tf_op jit(solution)/shard_map/attend/pallas_call | solution.py:1967
  208.5 1.3 copy-done.4
  209.8 1.0 copy-done.5
  212.1 56.3 %token_gather.1.h_in = bf16[2048,2048]{1,0:T(8,128)(2,1)} custom-call(bf16[256,2048]{1,0:T(8,128)(2,1)} %copy-done.5), custom_call_target="tpu_custom_call" | custom-call | bytes 135000000 | tf_op jit(solution)/shard_map/token_gather/pallas_call | solution.py:656
  268.5 135.3 %expert_layer.1 = (bf16[256,2048]{1,0:T(8,128)(2,1)}, bf16[256,2048]{1,0:T(8,128)(2,1)}, f32[8,8,256]{2,1,0:T(8,128)}, f32[2,2048,256]{2,1,0:T(8,128)}, f32[2,20...) custom-call(bf16[2048,2048]{1,0:T(8,128)(2,1)} %token_gather.1.h_in, bf16[2048,2048]{1,0:T(8,128)(2,1)} %all-gather.8.cloned.1.call-done.dy_in, ...), custom_call_target="tpu_custom_call" | custom-call | bytes 240000000 | tf_op jit(solution)/shard_map/expert_layer/pallas_call | solution.py:1582
  405.4 155.2 %attend_back.1 = (bf16[256,2048]{1,0:T(8,128)(2,1)}, f32[3,256,512]{2,1,0:T(8,128)}, f32[512,256]{1,0:T(8,128)}, f32[24,256]{1,0:T(8,128)}) custom-call(bf16[256,2048]{1,0:T(8,128)(2,1)} %get-tuple-element.43.dh_ref, f32[256,16]{1,0:T(8,128)} %bitcast_select_fusion.gates_ref, bf16[16,2048]{1,0:T(8,128)(2,1)} %bitcast.40, bf16[256,2048]{1,0:T(8,128)(2,1)} %copy-done.5, ...), custom_call_target="tpu_custom_call" | custom-call | bytes 390000000 | tf_op jit(solution)/shard_map/attend_back/pallas_call | solution.py:2356
  560.7 1.4 fusion.5
  562.8 1.3 slice_bitcast_fusion.6
  564.8 1.0 copy.69
  565.8 3.0 copy.70
  568.7 1.1 copy.71
  570.7 2.1 copy.73
  572.8 1.6 copy-done.22
  574.4 2.1 copy.74
  576.5 1.6 copy-done.21
  578.1 2.0 copy.75
  (89 shorter events, 14.4 us)
Async XLA Ops:
  7.2 145.5 %copy-start.27 = (s32[2048]{0:T(1024)S(1)}, s32[2048]{0:T(1024)}, u32[]{:S(2)}) copy-start(s32[2048]{0:T(1024)} %param.25) | copy-start | bytes 24580
  7.2 145.3 %all-gather.4.cloned.1.call-start = ((), (), s32[]{:S(2)}) async-start(), calls=%async_computation | async-start | bytes 2359296 | tf_op jit(solution)/shard_map/all_gather | solution.py:2460
  8.9 159.4 %all-gather.6.cloned.1.call-start = ((), (), s32[]{:S(2)}) async-start(), calls=%async_computation.1 | async-start | bytes 2359296 | tf_op jit(solution)/shard_map/all_gather | solution.py:2461
  10.8 257.7 %all-gather.8.cloned.1.call-start = ((), (), s32[]{:S(2)}) async-start(), calls=%async_computation.2 | async-start | bytes 10485760 | tf_op jit(solution)/shard_map/all_gather | solution.py:2466
  15.2 140.4 %copy-start.7 = (f32[256,128]{1,0:T(8,128)}, f32[256,128]{1,0:T(8,128)S(1)}, u32[]{:S(2)}) copy-start(f32[256,128]{1,0:T(8,128)S(1)} %get-tuple-element.72.cos_ref) | copy-start | bytes 393220
  15.2 140.4 %copy-start.8 = (f32[256,128]{1,0:T(8,128)}, f32[256,128]{1,0:T(8,128)S(1)}, u32[]{:S(2)}) copy-start(f32[256,128]{1,0:T(8,128)S(1)} %get-tuple-element.73.sin_ref) | copy-start | bytes 393220
  15.2 1.3 copy-start.1
  16.5 1.4 copy-start.6
  149.9 1.0 copy-start.11
  150.9 1.0 copy-start.12
  151.8 0.7 copy-start.14
  152.5 15.9 %copy-start.10 = (bf16[256,512]{1,0:T(8,128)(2,1)}, bf16[256,512]{1,0:T(8,128)(2,1)S(1)}, u32[]{:S(2)}) copy-start(bf16[256,512]{1,0:T(8,128)(2,1)S(1)} %get-tuple-element.36.q_ref) | copy-start | bytes 786436
  152.8 15.6 %copy-start.17 = (s32[5,256]{1,0:T(8,128)}, s32[5,256]{1,0:T(8,128)S(1)}, u32[]{:S(2)}) copy-start(s32[5,256]{1,0:T(8,128)S(1)} %rev.3.sk_ref) | copy-start | bytes 15364
  153.0 15.3 %copy-start.9 = (s32[256,1]{1,0:T(8,128)}, s32[256,1]{1,0:T(8,128)S(1)}, u32[]{:S(2)}) copy-start(s32[256,1]{1,0:T(8,128)S(1)} %copy.52.sq_ref) | copy-start | bytes 3076
  153.0 3.5 copy-start.19
  156.5 2.9 copy-start.20
  164.2 4.2 copy-start.18
  166.0 2.9 copy-start
  168.9 1.2 copy-start.2
  170.1 1.6 copy-start.3
  208.5 1.3 copy-start.4
  209.8 1.0 copy-start.5
  210.8 0.7 copy-start.13
  211.5 0.6 copy-start.15
  212.1 56.3 %copy-start.16 = (f32[256,128]{1,0:T(8,128)}, f32[256,128]{1,0:T(8,128)S(1)}, u32[]{:S(2)}) copy-start(f32[256,128]{1,0:T(8,128)S(1)} %get-tuple-element.45.s2_ref) | copy-start | bytes 393220
  405.4 159.4 %copy-start.25 = (bf16[256,2048]{1,0:T(8,128)(2,1)S(1)}, bf16[256,2048]{1,0:T(8,128)(2,1)}, u32[]{:S(2)}) copy-start(bf16[256,2048]{1,0:T(8,128)(2,1)} %get-tuple-element.87) | copy-start | bytes 3145732
  560.6 8.1 %copy-start.24 = (f32[3,256,512]{2,1,0:T(8,128)S(1)}, f32[3,256,512]{2,1,0:T(8,128)}, u32[]{:S(2)}) copy-start(f32[3,256,512]{2,1,0:T(8,128)} %get-tuple-element.89) | copy-start | bytes 4718596
  560.6 9.2 %copy-start.26 = (f32[512,256]{1,0:T(8,128)S(1)}, f32[512,256]{1,0:T(8,128)}, u32[]{:S(2)}) copy-start(f32[512,256]{1,0:T(8,128)} %get-tuple-element.90) | copy-start | bytes 1572868
  564.8 5.9 %copy-start.23 = (f32[2,2048,256]{2,1,0:T(8,128)S(1)}, f32[2,2048,256]{2,1,0:T(8,128)}, u32[]{:S(2)}) copy-start(f32[2,2048,256]{2,1,0:T(8,128)} %get-tuple-element.95) | copy-start | bytes 12582916
  570.7 3.7 copy-start.22
  574.4 3.7 copy-start.21
Sparse Core Ops, SparseCore 0:
  10.7 71.1 all-gather.3
  84.6 63.8 all-gather.5
  152.6 95.4 all-gather.7

commit v5 on v4

--- a/solution.py
+++ b/solution.py
@@ -438,10 +438,11 @@
 
 
 class LineGather:
-    def __init__(self, streams, sources, views, send_sem, recv_sem):
+    def __init__(self, streams, sources, views, send_sem, recv_sem, y_first=()):
         self.z, self.y, self.x, self.c = place()
         self.streams, self.sources, self.views = streams, sources, views
         self.send_sem, self.recv_sem = send_sem, recv_sem
+        self.y_first = y_first
         self.has_up, self.has_down = self.z < NZ - 1, self.z > 0
         self.pending = []
 
@@ -470,10 +471,11 @@
         block = self.block(rel)
         there = self.views[stream](block)
         source = self.sources[stream] if rel == 0 else there
+        near = rel % 7 == 0
         if way == 0:
-            target, landing = device(z + 1, y, x, c), (1 if rel == 0 else rel + 1)
+            target, landing = device(z + 1, y, x, c), rel + 1
         elif way == 1:
-            target, landing = device(z - 1, y, x, c), (4 if rel == 0 else rel + 1)
+            target, landing = device(z - 1, y, x, c), rel + (4 if near else 1)
         else:
             target, landing = device(z, 1 - y, x, c), 7 + rel
         return remote(
@@ -484,17 +486,21 @@
             target,
         )
 
+    def forwards(self, stream, rel):
+        return rel < 7 or stream in self.y_first
+
     def start(self, stream, rel):
-        if rel < 4:
+        if rel % 7 < 4:
             run = self.has_up
             run_if(run, lambda: self.send(stream, rel, 0).start())
             self.pending.append((stream, rel, 0, run))
-        if rel == 0 or rel >= 4:
+        if rel % 7 == 0 or rel % 7 >= 4:
             run = self.has_down
             run_if(run, lambda: self.send(stream, rel, 1).start())
             self.pending.append((stream, rel, 1, run))
-        self.send(stream, rel, 2).start()
-        self.pending.append((stream, rel, 2, None))
+        if rel == 0 or stream not in self.y_first:
+            self.send(stream, rel, 2).start()
+            self.pending.append((stream, rel, 2, None))
 
     def arrive(self, stream, rel):
         there = self.views[stream](self.block(rel))
@@ -586,7 +592,7 @@
         in_specs=[HBM] * 3,
         out_specs=(HBM, HBM, HBM),
         scratch_shapes=[
-            pltpu.SemaphoreType.DMA((3, 7, 3)),
+            pltpu.SemaphoreType.DMA((3, 14, 3)),
             pltpu.SemaphoreType.DMA((3, 14)),
             pltpu.SemaphoreType.DMA((3,)),
         ],
@@ -659,7 +665,7 @@
         in_specs=[HBM],
         out_specs=HBM,
         scratch_shapes=[
-            pltpu.SemaphoreType.DMA((2, 7, 3)),
+            pltpu.SemaphoreType.DMA((2, 14, 3)),
             pltpu.SemaphoreType.DMA((2, 14)),
             pltpu.SemaphoreType.DMA((14,)),
             pltpu.SemaphoreType.DMA((14,)),
@@ -1113,26 +1119,27 @@
 
 
 def expert_layer(
-    hidden_all, grad_out_all, gate_up, down, router_t, chosen_all, residual, collective_id
+    hidden_two, grad_out_all, gate_up, down, router_t, chosen_all, residual, collective_id
 ):
-    tokens, width = hidden_all.shape
-    rows = tokens // GROUPS
+    rows, width = hidden_two.shape
+    tokens = rows * GROUPS
     units = down.shape[0]
     local = 2
     hidden = units // local
     experts = router_t.shape[0]
     half, part, piece = width // 2, width // 4, width // 8
     tensors = NX * NC
-    steps = GROUPS + 5
+    steps = GROUPS + 4
+    a_cols, c_cols = width * 3 // 16, width // 8
     low = jnp.bfloat16
     wide = width // 4
 
     def kernel(
-        h_in, dy_in, gu_ref, down_ref, router_ref, chosen_ref, x1_in,
+        own_in, dy_in, gu_ref, down_ref, router_ref, chosen_ref, x1_in,
         block_out, dh_out, gates_out, gate_w, up_w, down_w,
         h, dy, gated, dgu, dx, y_part, yc_buf, yx_buf, yy_buf, ylo_buf, yhi_buf, x1, gu_stage, d_stage,
         core_buf, px_buf, py_buf, qy_buf, qx_buf, z_sum, lo_buf, hi_buf, gate_part, gate_land,
-        in_sem, x1_sem, yc_s, yc_r, yx_s, yx_r, yy_s, yy_r, yz_s, yz_r, gu_sem, d_sem, core_s, core_r, px_s, px_r, py_s, py_r, qy_s, qy_r, qx_s, qx_r,
+        in_sem, own_sem, line_s, line_r, hx_s, hx_r, hc_s, hc_r, x1_sem, yc_s, yc_r, yx_s, yx_r, yy_s, yy_r, yz_s, yz_r, gu_sem, d_sem, core_s, core_r, px_s, px_r, py_s, py_r, qy_s, qy_r, qx_s, qx_r,
         z_s, z_r, near_s, near_r, far_s, far_r, end_s, end_r,
     ):
         z, y, x, c = place()
@@ -1142,23 +1149,82 @@
         peers = [(lax.rem(e + k, GROUPS), t) for k in range(1, GROUPS)]
         greet([(target, None) for target in mates + peers])
 
+        def pick(values, index):
+            result = values[-1]
+            for k in range(len(values) - 1):
+                result = jnp.where(index == k, values[k], result)
+            return result
+
         def zz_of(j):
-            return jnp.where(j == 0, 3, jnp.where(j == 1, 0, jnp.where(j == 2, 2, 1)))
+            return pick([z, pick([1, 0, 3, 2], z), pick([3, 3, 0, 0], z), pick([2, 2, 1, 1], z)], j)
+
+        def is_own(i):
+            return (i == 0) | ((i >= 2) & (lax.rem(i, 2) == 1))
 
         def block_of(i):
-            own = lax.rem(i, 2)
-            return zz_of(lax.div(i, 2)) * NY + jnp.where(own == 1, y, 1 - y)
+            return zz_of(lax.div(i, 2)) * NY + jnp.where(is_own(i), y, 1 - y)
+
+        def flip_block(j):
+            return zz_of(j) * NY + 1 - y
+
+        def own_block(j):
+            return zz_of(j) * NY + y
+
+        def a_at(xx, cc):
+            return pl.ds(pl.multiple_of(xx * (2 * a_cols) + cc * a_cols, 128), a_cols)
+
+        def c_at(cc):
+            return pl.ds(pl.multiple_of(4 * a_cols + cc * c_cols, 128), c_cols)
+
+        def h_view(b, columns):
+            return h.at[block_rows(b, rows), columns]
+
+        line = LineGather(
+            [0, 1], [own_in.at[:, a_at(x, c)], own_in.at[:, c_at(c)]],
+            [lambda b: h_view(b, a_at(x, c)), lambda b: h_view(b, c_at(c))], line_s, line_r,
+        )
+
+        def h_twin(b, stream, landing=False):
+            cc = 1 - c if landing else c
+            piece = h_view(b, [a_at(x, cc), c_at(cc), a_at(1 - x, cc)][stream])
+            return remote(piece, piece, hc_s.at[b, stream], hc_r.at[b, stream], twin)
+
+        def h_across(b, landing=False):
+            piece = h_view(b, a_at(1 - x if landing else x, c))
+            return remote(piece, piece, hx_s.at[b], hx_r.at[b], across)
+
+        def gather_event(rel):
+            def body():
+                b = line.block(rel)
+                marks = len(line.pending)
+                for stream in (0, 1):
+                    line.arrive(stream, rel)
+                    if rel < 7:
+                        line.start(stream, rel)
+                    if stream == 0:
+                        h_across(b).start()
+                    h_twin(b, stream).start()
+                late = line.pending[marks:]
+                del line.pending[marks:]
+                line.finish_later(late, rel)
+            run_if(line.exists(rel), body)
+
+        def relay(i):
+            b = block_of(i)
+            h_across(b, True).wait_recv()
+            h_twin(b, 2).start()
+
+        for stream in (0, 1):
+            line.start(stream, 0)
+        keep = pltpu.make_async_copy(own_in, h.at[block_rows(z * NY + y, rows), :], own_sem)
+        keep.start()
 
         def load(i):
             r = block_rows(block_of(i), rows)
-            return (
-                pltpu.make_async_copy(h_in.at[r, :], h.at[r, :], in_sem.at[0, i]),
-                pltpu.make_async_copy(dy_in.at[r, :], dy.at[r, :], in_sem.at[1, i]),
-            )
+            return pltpu.make_async_copy(dy_in.at[r, :], dy.at[r, :], in_sem.at[i])
 
         def start_load(i, carry):
-            for copy in load(i):
-                copy.start()
+            load(i).start()
             return carry
 
         lax.fori_loop(0, GROUPS, start_load, 0)
@@ -1182,11 +1248,11 @@
             )
 
         def p_beside(j):
-            return remote(px_buf.at[block_of(2 * j)], py_buf.at[j], py_s.at[j], py_r.at[j], beside)
+            return remote(px_buf.at[flip_block(j)], py_buf.at[j], py_s.at[j], py_r.at[j], beside)
 
         def q_beside(j):
             return remote(
-                core_buf.at[block_of(2 * j), :, pl.ds(part, part)], qy_buf.at[j], qy_s.at[j], qy_r.at[j], beside
+                core_buf.at[flip_block(j), :, pl.ds(part, part)], qy_buf.at[j], qy_s.at[j], qy_r.at[j], beside
             )
 
         def q_across(j):
@@ -1207,7 +1273,7 @@
             mine = core_buf.at[b]
             add_to(mine, mine, dx.at[lax.rem(i, 2), :, pl.ds(pl.multiple_of(c * half, half), half)], 32)
             p_across(i).start()
-            pl.when(lax.rem(i, 2) == 0)(lambda: q_beside(lax.div(i, 2)).start())
+            pl.when(jnp.logical_not(is_own(i)))(lambda: q_beside(lax.div(i, 2)).start())
 
         def take_p_across(i):
             p_across(i).wait_recv()
@@ -1219,18 +1285,18 @@
 
         def take_q_beside(j):
             q_beside(j).wait_recv()
-            add_to(qy_buf.at[j], qy_buf.at[j], core_buf.at[block_of(2 * j + 1), :, pl.ds(part, part)])
+            add_to(qy_buf.at[j], qy_buf.at[j], core_buf.at[own_block(j), :, pl.ds(part, part)])
             q_across(j).start()
 
         def take_q_across(j):
             q_across(j).wait_recv()
             add_to(
-                z_sum.at[1, j], qx_buf.at[j], qy_buf.at[j, :, pl.ds(pl.multiple_of(x * piece, piece), piece)]
+                z_sum.at[1, zz_of(j)], qx_buf.at[j], qy_buf.at[j, :, pl.ds(pl.multiple_of(x * piece, piece), piece)]
             )
 
         def take_p_beside(j):
             p_beside(j).wait_recv()
-            add_to(z_sum.at[0, j], py_buf.at[j], px_buf.at[block_of(2 * j + 1)])
+            add_to(z_sum.at[0, zz_of(j)], py_buf.at[j], px_buf.at[own_block(j)])
 
         def hop(j, k):
             zz = zz_of(j)
@@ -1238,16 +1304,16 @@
             def upward():
                 for s in range(2):
                     if k > 0:
-                        up(j, s).wait_recv()
-                        add_to(z_sum.at[s, j], z_sum.at[s, j], lo_buf.at[s, j])
-                    up(j, s).start()
+                        up(zz, s).wait_recv()
+                        add_to(z_sum.at[s, zz], z_sum.at[s, zz], lo_buf.at[s, zz])
+                    up(zz, s).start()
 
             def downward():
                 for s in range(2):
                     if k > 0:
-                        down_z(j, s).wait_recv()
-                        add_to(z_sum.at[s, j], z_sum.at[s, j], hi_buf.at[s, j])
-                    down_z(j, s).start()
+                        down_z(zz, s).wait_recv()
+                        add_to(z_sum.at[s, zz], z_sum.at[s, zz], hi_buf.at[s, zz])
+                    down_z(zz, s).start()
 
             pl.when((z < zz) & (z == k))(upward)
             pl.when((z > zz) & (NZ - 1 - z == k))(downward)
@@ -1266,7 +1332,7 @@
             )
 
         def y_beside(j):
-            return remote(yx_buf.at[block_of(2 * j)], yy_buf.at[j], yy_s.at[j], yy_r.at[j], beside)
+            return remote(yx_buf.at[flip_block(j)], yy_buf.at[zz_of(j)], yy_s.at[j], yy_r.at[j], beside)
 
         def y_up(j):
             return remote(yy_buf.at[j], ylo_buf.at[j], yz_s.at[0, j], yz_r.at[0, j], device(z + 1, y, x, c))
@@ -1285,34 +1351,40 @@
             b = block_of(i)
             mine = yx_buf.at[b]
             add_to(mine, mine, yc_buf.at[b, :, pl.ds(pl.multiple_of(x * part, part), part)])
-            pl.when(lax.rem(i, 2) == 0)(lambda: y_beside(lax.div(i, 2)).start())
+            pl.when(jnp.logical_not(is_own(i)))(lambda: y_beside(lax.div(i, 2)).start())
 
         def take_y_beside(j):
             y_beside(j).wait_recv()
-            add_to(yy_buf.at[j], yy_buf.at[j], yx_buf.at[block_of(2 * j + 1)])
+            add_to(yy_buf.at[zz_of(j)], yy_buf.at[zz_of(j)], yx_buf.at[own_block(j)])
 
         def y_hop(j, k):
             zz = zz_of(j)
 
             def upward():
                 if k > 0:
-                    y_up(j).wait_recv()
-                    add_to(yy_buf.at[j], yy_buf.at[j], ylo_buf.at[j])
-                y_up(j).start()
+                    y_up(zz).wait_recv()
+                    add_to(yy_buf.at[zz], yy_buf.at[zz], ylo_buf.at[zz])
+                y_up(zz).start()
 
             def downward():
                 if k > 0:
-                    y_down(j).wait_recv()
-                    add_to(yy_buf.at[j], yy_buf.at[j], yhi_buf.at[j])
-                y_down(j).start()
+                    y_down(zz).wait_recv()
+                    add_to(yy_buf.at[zz], yy_buf.at[zz], yhi_buf.at[zz])
+                y_down(zz).start()
 
             pl.when((z < zz) & (z == k))(upward)
             pl.when((z > zz) & (NZ - 1 - z == k))(downward)
 
         def front(i):
-            for copy in load(i):
-                copy.wait()
+            load(i).wait()
             b = block_of(i)
+            pl.when(i == 0)(keep.wait)
+
+            def landed():
+                for stream in range(3):
+                    h_twin(b, stream, True).wait_recv()
+
+            pl.when(i > 0)(landed)
             r = block_rows(b, rows)
             rows_h, rows_dy = h[r, :], dy[r, :]
             logits = dot(rows_h, router_ref[...], (1, 1))
@@ -1432,45 +1504,68 @@
             gates_out[e] = gate_land[tensors - 1, e]
 
         def step(i, carry):
+            def at(number, body):
+                pl.when(i == number)(body)
+
+            odd, even = lax.rem(i, 2) == 1, lax.rem(i, 2) == 0
             j_even, j_odd = lax.div(i, 2) - 1, lax.div(i - 1, 2) - 1
-            even = lax.rem(i, 2) == 0
             pl.when(i < GROUPS)(lambda: front(i))
-            pl.when((i >= 1) & (i <= GROUPS))(lambda: take_twin(i - 1))
-            pl.when((i >= 1) & (i <= GROUPS))(lambda: take_y_twin(i - 1))
-            pl.when(even & (i >= 2) & (i <= GROUPS))(lambda: take_q_beside(j_even))
+
+            def events(*rels):
+                for rel in rels:
+                    gather_event(rel)
+
+            at(1, lambda: events(2, 5, 8, 11))
+            at(2, lambda: events(3, 6))
+            at(3, lambda: events(10, 13))
+
+            def twins():
+                take_twin(i - 1)
+                take_y_twin(i - 1)
+
+            pl.when((i >= 1) & (i <= GROUPS))(twins)
+            pl.when(even & (i >= 4) & (i <= GROUPS))(lambda: take_q_beside(j_even))
+            at(3, lambda: take_q_beside(0))
+            at(4, lambda: take_q_across(0))
 
             def late():
                 take_p_across(i - 2)
-                take_q_across(j_odd)
-
-            pl.when((lax.rem(i, 2) == 1) & (i >= 3) & (i <= GROUPS + 1))(late)
-            pl.when(i == GROUPS)(lambda: each(near, "start"))
-            pl.when(i == GROUPS + 1)(sum_near)
+                pl.when(i > 3)(lambda: take_q_across(j_odd))
+                pl.when(i == 3)(lambda: p_beside(0).start())
+
+            pl.when(odd & (i >= 3) & (i <= GROUPS + 1))(late)
+            at(GROUPS, lambda: each(near, "start"))
+            at(GROUPS + 1, sum_near)
             pl.when(i < GROUPS)(lambda: rear(i))
-            pl.when((i >= GROUPS) & (i < GROUPS + 4))(lambda: weight_grads(i - GROUPS))
+            pl.when(i >= GROUPS)(lambda: weight_grads(i - GROUPS))
+            at(0, lambda: events(7, 1, 4))
+            at(2, lambda: events(9, 12))
+            pl.when(i < GROUPS - 1)(lambda: relay(i + 1))
 
             def pass_p():
                 take_p_across(i - 2)
-                p_beside(j_even).start()
+                pl.when(i > 2)(lambda: p_beside(j_even).start())
 
             pl.when(even & (i >= 2) & (i <= GROUPS))(pass_p)
+            at(4, lambda: take_p_beside(0))
 
             def join():
                 take_p_beside(j_odd)
                 hop(j_odd, 0)
 
-            pl.when((lax.rem(i, 2) == 1) & (i >= 3) & (i <= GROUPS + 1))(join)
-            pl.when(even & (i >= 4) & (i <= GROUPS + 2))(lambda: hop(j_even - 1, 1))
-            pl.when((lax.rem(i, 2) == 1) & (i >= 5) & (i <= GROUPS + 3))(lambda: hop(j_odd - 1, 2))
+            pl.when(odd & (i >= 5) & (i <= GROUPS + 1))(join)
+            pl.when((i == GROUPS) | (i == GROUPS + 2))(lambda: hop(j_even - 1, 1))
+            at(GROUPS + 1, lambda: hop(1, 2))
             pl.when((i >= 2) & (i <= GROUPS + 1))(lambda: take_y_across(i - 2))
+            at(5, lambda: take_y_beside(0))
 
             def join_y():
                 take_y_beside(j_even - 1)
                 y_hop(j_even - 1, 0)
 
-            pl.when(even & (i >= 4) & (i <= GROUPS + 2))(join_y)
-            pl.when((lax.rem(i, 2) == 1) & (i >= 5) & (i <= GROUPS + 3))(lambda: y_hop(j_odd - 1, 1))
-            pl.when(even & (i >= 6) & (i <= GROUPS + 4))(lambda: y_hop(j_even - 2, 2))
+            pl.when(even & (i >= 6) & (i <= GROUPS + 2))(join_y)
+            pl.when((i == GROUPS + 1) | (i == GROUPS + 3))(lambda: y_hop(j_odd - 1, 1))
+            at(GROUPS + 2, lambda: y_hop(1, 2))
             return carry
 
         lax.fori_loop(0, steps, step, 0)
@@ -1478,7 +1573,7 @@
         def columns_of(s, xx, cc):
             return pl.ds(pl.multiple_of(cc * half + s * part + xx * piece, piece), piece)
 
-        mine = jnp.where(z == 3, 0, jnp.where(z == 0, 1, jnp.where(z == 2, 2, 3)))
+        mine = z
         for s in range(2):
             def below(s=s):
                 up(mine, s).wait_recv()
@@ -1564,14 +1659,24 @@
             q_beside(j).wait_send()
             q_across(j).wait_send()
             y_beside(j).wait_send()
-            pl.when(z < zz_of(j))(lambda: y_up(j).wait_send())
-            pl.when(z > zz_of(j))(lambda: y_down(j).wait_send())
+            pl.when(z < j)(lambda: y_up(j).wait_send())
+            pl.when(z > j)(lambda: y_down(j).wait_send())
             for s in range(2):
-                pl.when(z < zz_of(j))(lambda s=s: up(j, s).wait_send())
-                pl.when(z > zz_of(j))(lambda s=s: down_z(j, s).wait_send())
+                pl.when(z < j)(lambda s=s: up(j, s).wait_send())
+                pl.when(z > j)(lambda s=s: down_z(j, s).wait_send())
             return carry
 
         lax.fori_loop(0, NZ, drain_pair, 0)
+
+        def drain_rows_of(i, carry):
+            b = block_of(i)
+            h_across(b).wait_send()
+            for stream in range(3):
+                h_twin(b, stream).wait_send()
+            return carry
+
+        lax.fori_loop(1, GROUPS, drain_rows_of, 0)
+        line.finish()
         for k in range(2):
             each(gu_copies(4 * tiles - 2 + k), "wait")
             each(d_copies(6 + k), "wait")
@@ -1616,7 +1721,8 @@
             pltpu.VMEM((2, NZ, rows, piece), low),
             pltpu.VMEM((GROUPS, 8, rows), f32),
             pltpu.VMEM((tensors, GROUPS, 8, rows), f32),
-            dma((2, GROUPS)), dma, dma((GROUPS,)), dma((GROUPS,)), dma((GROUPS,)), dma((GROUPS,)),
+            dma((GROUPS,)), dma, dma((2, 14, 3)), dma((2, 14)), dma((GROUPS,)), dma((GROUPS,)),
+            dma((GROUPS, 3)), dma((GROUPS, 3)), dma, dma((GROUPS,)), dma((GROUPS,)), dma((GROUPS,)), dma((GROUPS,)),
             dma((NZ,)), dma((NZ,)), dma((2, NZ)), dma((2, NZ)), dma((2, 2 * local)), dma((2, local)),
             dma((GROUPS,)), dma((GROUPS,)), dma((GROUPS,)), dma((GROUPS,)),
             dma((NZ,)), dma((NZ,)), dma((NZ,)), dma((NZ,)), dma((NZ,)), dma((NZ,)),
@@ -1627,7 +1733,7 @@
         compiler_params=comm_params(collective_id, 62),
         cost_estimate=cost(80),
         name="expert_layer",
-    )(hidden_all, grad_out_all, gate_up, down, router_t, chosen_all, residual)
+    )(hidden_two, grad_out_all, gate_up, down, router_t, chosen_all, residual)
 
 
 def exchange_rows(value, part_ref, land_ref, send_sem, recv_sem, mates):
@@ -1658,20 +1764,22 @@
     return value * cosine + pltpu.roll(value, HEAD // 2, 1) * sine
 
 
-def project(tokens, w_qkv, smalls, cosine, sine, collective_id):
+def project(tokens, w_qkv, w_out, out_grad, smalls, cosine, sine, collective_id):
     rows, width = tokens.shape
     parts, depth, columns = w_qkv.shape
     heads = columns // HEAD
     tensors = NX * NC
     back = WINDOW // rows
     low, f32 = jnp.bfloat16, jnp.float32
-    QUERY, KEY, VALUE, SMALL = 0, 1, 2, 3
+    QUERY, KEY, VALUE, SMALL, OUT, GRAD = 0, 1, 2, 3, 4, 5
+    out_rows, out_columns = w_out.shape
+    quarter = width // tensors
 
     def kernel(
-        tok_ref, w_ref, small_ref, cos_ref, sin_ref,
-        w_all, small_all, h1_ref, raw_ref, scale_ref, q_ref, context,
-        own_w, weights, total, part_k, land_k, part_q, land_q,
-        send_sem, recv_sem, out_sem, small_sem, ks_s, ks_r, qs_s, qs_r, c_s, c_r,
+        tok_ref, w_ref, out_ref, grad_in, small_ref, cos_ref, sin_ref,
+        w_all, out_all, grad_all, small_all, h1_ref, raw_ref, scale_ref, q_ref, context,
+        own_w, own_out, weights, total, part_k, land_k, part_q, land_q,
+        send_sem, recv_sem, out_sem, small_sem, kept, ks_s, ks_r, qs_s, qs_r, c_s, c_r, hx_s, hx_r, hc_s, hc_r,
     ):
         z, y, x, c = place()
         e, t = lax.axis_index("expert"), lax.axis_index("tensor")
@@ -1682,10 +1790,29 @@
             lambda b: weights.at[KEY, block_rows(b, depth), :],
             lambda b: weights.at[VALUE, block_rows(b, depth), :],
             lambda b: small_all.at[b],
+            lambda b: out_all.at[:, block_rows(b, out_columns)],
+            lambda b: grad_view(b, x, c),
         ]
+        across, twin = device(z, y, 1 - x, c), device(z, y, x, 1 - c)
+
+        def quarter_at(xx, cc):
+            return pl.ds(pl.multiple_of((xx * NC + cc) * quarter, quarter), quarter)
+
+        def grad_view(b, xx, cc):
+            return grad_all.at[block_rows(b, rows), quarter_at(xx, cc)]
+
+        def grad_across(b, landing=False):
+            piece = grad_view(b, 1 - x if landing else x, c)
+            return remote(piece, piece, hx_s.at[b], hx_r.at[b], across)
+
+        def grad_twin(b, relayed, landing=False):
+            piece = grad_view(b, 1 - x if relayed else x, 1 - c if landing else c)
+            return remote(piece, piece, hc_s.at[b, relayed], hc_r.at[b, relayed], twin)
+
         line = LineGather(
-            [SMALL, VALUE, KEY, QUERY], [own_w.at[0], own_w.at[1], own_w.at[2], small_ref], views,
-            send_sem, recv_sem,
+            [SMALL, VALUE, KEY, QUERY, OUT, GRAD],
+            [own_w.at[0], own_w.at[1], own_w.at[2], small_ref, own_out, grad_in.at[:, quarter_at(x, c)]],
+            views, send_sem, recv_sem, y_first=(OUT,),
         )
         greet(line.partners() + [(mate, None) for mate in mates])
         line.start(SMALL, 0)
@@ -1698,6 +1825,17 @@
             lax.fori_loop(0, depth // 32, cast, 0)
             if part != QUERY:
                 line.start(part, 0)
+
+        def cast_out(i, carry):
+            r = pl.ds(pl.multiple_of(i * 32, 32), 32)
+            own_out[r, :] = out_ref[r, :].astype(low)
+            return carry
+
+        lax.fori_loop(0, out_rows // 32, cast_out, 0)
+        keep_out = pltpu.make_async_copy(own_out, out_all.at[:, block_rows(line.block(0), out_columns)], kept.at[0])
+        keep_out.start()
+        keep_grad = pltpu.make_async_copy(grad_in, grad_all.at[block_rows(line.block(0), rows), :], kept.at[1])
+        keep_grad.start()
 
         def square(i, carry):
             r = pl.ds(pl.multiple_of(i * 32, 32), 32)
@@ -1723,13 +1861,18 @@
         def event(stream, rel):
             def body():
                 line.arrive(stream, rel)
-                if rel < 7:
+                if line.forwards(stream, rel):
                     marks = len(line.pending)
                     line.start(stream, rel)
                     late = line.pending[marks:]
                     del line.pending[marks:]
                     line.finish_later(late, rel)
-                use(stream, rel)
+                if stream == GRAD:
+                    b = line.block(rel)
+                    grad_across(b).start()
+                    grad_twin(b, 0).start()
+                elif stream != OUT:
+                    use(stream, rel)
             run_if(line.exists(rel), body)
 
         use(SMALL, 0)
@@ -1777,6 +1920,7 @@
             event(KEY, rel)
         for rel in late:
             event(KEY, rel)
+        line.start(OUT, 0)
         key_raw = total[KEY]
         raw_ref[1] = key_raw
         exchange_rows(jnp.sum(key_raw * key_raw, axis=-1, keepdims=True), part_k, land_k, ks_s, ks_r, mates)
@@ -1829,6 +1973,7 @@
         relay_two(0)
         for rel in late[4:]:
             event(QUERY, rel)
+        line.start(GRAD, 0)
         query_raw = total[QUERY]
         raw_ref[0] = query_raw
         exchange_rows(jnp.sum(query_raw * query_raw, axis=-1, keepdims=True), part_q, land_q, qs_s, qs_r, mates)
@@ -1844,10 +1989,32 @@
             q_ref[:, at] = value
 
         rotated(QUERY, query_scale, store_query)
+        for rel in early:
+            event(OUT, rel)
+            event(GRAD, rel)
         for which in (1, 0):
             for k in (1, 3):
                 context_take(which, k)
+        for rel in late:
+            event(OUT, rel)
+            event(GRAD, rel)
+        for rel in early + late:
+            def relay(rel=rel):
+                b = line.block(rel)
+                grad_across(b, True).wait_recv()
+                grad_twin(b, 1).start()
+            run_if(line.exists(rel), relay)
+        for rel in early + late:
+            def landed(rel=rel):
+                b = line.block(rel)
+                grad_across(b).wait_send()
+                for relayed in range(2):
+                    grad_twin(b, relayed, True).wait_recv()
+                    grad_twin(b, relayed).wait_send()
+            run_if(line.exists(rel), landed)
         line.finish()
+        keep_out.wait()
+        keep_grad.wait()
         for which in range(2):
             for k in range(1, back + 1):
                 run_if(sends[k], lambda which=which, k=k: context_copy(which, k).wait_send())
@@ -1860,6 +2027,8 @@
         kernel,
         out_shape=(
             shape((parts, depth * GROUPS, columns), low),
+            shape((out_rows, out_columns * GROUPS), low),
+            shape((rows * GROUPS, width), low),
             shape((GROUPS,) + smalls.shape, f32),
             shape((rows, width), low),
             shape((2, rows, columns), f32),
@@ -1867,24 +2036,26 @@
             shape((rows, columns), low),
             shape((back + 1, 2, rows, columns), low),
         ),
-        in_specs=[VMEM] * 5,
-        out_specs=(HBM,) + (VMEM,) * 6,
+        in_specs=[VMEM, VMEM, VMEM, HBM, VMEM, VMEM, VMEM],
+        out_specs=(HBM,) * 3 + (VMEM,) * 6,
         scratch_shapes=[
             pltpu.VMEM((parts, depth, columns), low),
+            pltpu.VMEM((out_rows, out_columns), low),
             pltpu.VMEM((parts, depth * GROUPS, columns), low),
             pltpu.VMEM((parts, rows, columns), f32),
             pltpu.VMEM((8, rows), f32),
             pltpu.VMEM((tensors - 1, 8, rows), f32),
             pltpu.VMEM((8, rows), f32),
             pltpu.VMEM((tensors - 1, 8, rows), f32),
-            dma((4, 7, 3)), dma((4, 14)), dma, dma,
+            dma((6, 14, 3)), dma((6, 14)), dma, dma, dma((2,)),
             dma((tensors - 1,)), dma((tensors - 1,)), dma((tensors - 1,)), dma((tensors - 1,)),
             dma((2, back + 1)), dma((2, back + 1)),
+            dma((GROUPS,)), dma((GROUPS,)), dma((GROUPS, 2)), dma((GROUPS, 2)),
         ],
         compiler_params=comm_params(collective_id, 48),
         cost_estimate=cost(100),
         name="project",
-    )(tokens, w_qkv, smalls, cosine, sine)
+    )(tokens, w_qkv, w_out, out_grad, smalls, cosine, sine)
 
 
 def attend(query, context, segment_query, segment_keys, tokens, out_low, gain, collective_id):
@@ -2456,14 +2627,9 @@
     cosine_table, sine_table = angles(global_rows % SEQ, HEAD)
     wide_cosine = jnp.concatenate([cosine_table[:, 0], cosine_table[:, 0]], axis=1)
     wide_sine = jnp.concatenate([-sine_table[:, 0], sine_table[:, 0]], axis=1)
-    grad_out_piece = lax.dynamic_slice_in_dim(out_grad, tensor_index * quarter, quarter, axis=1)
-    grad_out_rows = lax.all_gather(grad_out_piece, "expert", axis=0, tiled=True)
-    out_low = lax.all_gather(w_attn_out.astype(low), "expert", axis=1, tiled=True)
-    qkv_low, small_all, hidden_one, raw, scales, query_low, context_blocks = project(
-        tokens_in, w_qkv, smalls, wide_cosine, wide_sine, 0
-    )
-    grad_out_rows, query_low = lax.optimization_barrier((grad_out_rows, query_low))
-    grad_out_all = lax.all_gather(grad_out_rows, "tensor", axis=1, tiled=True)
+    (
+        qkv_low, out_low, grad_out_all, small_all, hidden_one, raw, scales, query_low, context_blocks
+    ) = project(tokens_in, w_qkv, w_attn_out, out_grad, smalls, wide_cosine, wide_sine, 0)
     gain_one_f = small_all[:, 0].reshape(model_width)
     gain_two_f = small_all[:, 1].reshape(model_width)
     qk_gains = (
@@ -2486,13 +2652,12 @@
         query_low, context_blocks, segment_query[:, None], segment_keys, tokens_in, out_low,
         gain_two_f[None, :], 2,
     )
-    hidden_all = token_gather(hidden_two, 3)
     gate_up = jnp.concatenate(
         [w[i] for w in (w_gate, w_up) for i in range(local_experts)], axis=1
     ).astype(low)
     down_low = w_down.reshape(-1, model_width).astype(low)
     block_out, grad_hidden_sum, grad_gate_sum, grad_gate_w, grad_up_w, grad_down = expert_layer(
-        hidden_all, grad_out_all, gate_up, down_low, router_t, chosen_all.astype(low), residual, 5
+        hidden_two, grad_out_all, gate_up, down_low, router_t, chosen_all.astype(low), residual, 5
     )
     grad_probs = grad_gate_sum[:, :local_experts].reshape(experts, row_count).T * chosen
     grad_tokens, qkv_sum, out_sum, small_sum = attend_back(

time: 593 us -> 571 us (0.963)
  between operations: 14.5 us -> 1.37 us
    pallas_call x1 -> x0, Pallas kernels: 56.3 us -> none  [token_gather(): pl.pallas_call(kernel, out_shape=jax.ShapeDtypeStruct((rows * GROUPS, wid...]
    pallas_call x1, Pallas kernels: 132 us -> 166 us  [project(): pl.pallas_call(kernel, out_shape=(shape((parts, depth * GROUPS, columns),...]
    pallas_call x1, Pallas kernels: 135 us -> 164 us  [expert_layer(): pl.pallas_call(kernel, out_shape=(shape((rows, width), low), shape((rows,...]
    pallas_call x1, Pallas kernels: 36.8 us -> 25.6 us  [attend(): pl.pallas_call(kernel, out_shape=(shape((rows, columns), low), shape((row...]
    unnamed x63 -> x61, local copies, waits for them, and re-layouts: 30 us -> 26.3 us
  transfers between devices with their start and end apart: 3 -> 0, of which waited for: 0 -> 0; matrix products, arithmetic and copies ran while one was open for 3% -> 0% of each run, Pallas kernels for 38% -> 0%
where the time goes in v5:
time: 571 us; the launch traced here: 563 us
  Pallas kernels  513 us (90%)
  local copies, waits for them, and re-layouts  37.4 us (7%)
  other arithmetic  11.3 us (2%)
    pallas_call x1, Pallas kernels, project(): pl.pallas_call(kernel, out_shape=(shape((parts, depth * GROUPS, columns),...  166 us
    pallas_call x1, Pallas kernels, expert_layer(): pl.pallas_call(kernel, out_shape=(shape((rows, width), low), shape((rows,...  164 us
    pallas_call x1, Pallas kernels, attend_back(): pl.pallas_call(kernel, out_shape=(shape((rows, width), low), shape((3, de...  157 us
    unnamed x61, local copies, waits for them, and re-layouts  26.3 us
    pallas_call x1, Pallas kernels, attend(): pl.pallas_call(kernel, out_shape=(shape((rows, columns), low), shape((row...  25.6 us

profile of v5, /device:TPU:0, one launch (start us, length us, event | category | flops | bytes accessed | tf_op | source)
XLA Modules:
  0.0 563.0 jit_solution(11927734298796588756)
XLA Ops:
  0.6 0.8 pad_dynamic-slice_fusion
  2.8 0.7 fusion
  4.3 0.8 pad_dynamic-slice_fusion.1
  5.2 0.7 concatenate.16.small_ref
  6.9 2.9 convert.21
  10.3 2.5 pad_maximum_fusion.gu_ref
  12.8 1.2 copy-done.20
  14.0 1.6 convert_element_type.35
  16.4 165.8 %project.1 = (bf16[3,2048,512]{2,1,0:T(8,128)(2,1)}, bf16[512,2048]{1,0:T(8,128)(2,1)}, bf16[2048,2048]{1,0:T(8,128)(2,1)}, f32[8,40,256]{2,1,0:T(8,128)S(1)}, b...) custom-call(bf16[256,2048]{1,0:T(8,128)(2,1)S(1)} %copy-done.1, ...), custom_call_target="tpu_custom_call" | custom-call | bytes 300000000 | tf_op jit(solution)/shard_map/project/pallas_call | solution.py:2026
  182.3 1.0 copy-done.10
  183.2 1.0 copy-done.11
  186.4 1.0 copy.54
  187.4 1.7 copy-done
  189.1 1.6 copy-done.2
  190.7 25.6 %attend.1 = (bf16[256,512]{1,0:T(8,128)(2,1)S(1)}, f32[256,128]{1,0:T(8,128)S(1)}, f32[256,2048]{1,0:T(8,128)S(1)}, bf16[256,2048]{1,0:T(8,128)(2,1)S(1)}, f32[256,128]{1,0:T(8,128)S(1)}) custom-call(bf16[256,512]{1,0:T(8,128)(2,1)S(1)} %get-tuple-element.35.q_ref, bf16[5,2,256,512]{3,2,1,0:T(8,128)(2,1)S(1)} %copy-done, s32[256,1]{1,0:T(8,128)S(1)} %copy.52.sq_ref, ...), custom_call_target="tpu_custom_call" | custom-call | bytes 120000000 | tf_op jit(solution)/shard_map/attend/pallas_call | solution.py:2138
  216.4 1.3 copy-done.3
  217.7 1.0 copy-done.5
  218.6 0.7 copy-done.13
  220.0 164.1 %expert_layer.1 = (bf16[256,2048]{1,0:T(8,128)(2,1)}, bf16[256,2048]{1,0:T(8,128)(2,1)}, f32[8,8,256]{2,1,0:T(8,128)}, f32[2,2048,256]{2,1,0:T(8,128)}, f32[2,20...) custom-call(bf16[256,2048]{1,0:T(8,128)(2,1)} %copy-done.5, bf16[2048,2048]{1,0:T(8,128)(2,1)} %get-tuple-element.40.dy_in, ...), custom_call_target="tpu_custom_call" | custom-call | bytes 240000000 | tf_op jit(solution)/shard_map/expert_layer/pallas_call | solution.py:1687
  384.1 0.8 slice.59
  385.7 157.3 %attend_back.1 = (bf16[256,2048]{1,0:T(8,128)(2,1)}, f32[3,256,512]{2,1,0:T(8,128)}, f32[512,256]{1,0:T(8,128)}, f32[24,256]{1,0:T(8,128)}) custom-call(bf16[256,2048]{1,0:T(8,128)(2,1)} %get-tuple-element.43.dh_ref, f32[256,16]{1,0:T(8,128)} %bitcast_select_fusion.gates_ref, bf16[16,2048]{1,0:T(8,128)(2,1)} %bitcast.40, bf16[256,2048]{1,0:T(8,128)(2,1)} %copy-done.5, ...), custom_call_target="tpu_custom_call" | custom-call | bytes 390000000 | tf_op jit(solution)/shard_map/attend_back/pallas_call | solution.py:2527
  543.1 1.4 fusion.5
  545.2 1.3 slice_bitcast_fusion.6
  547.2 1.0 copy.69
  548.2 3.0 copy.70
  551.2 1.1 copy.71
  552.3 0.8 copy.72
  553.1 2.1 copy.73
  555.2 1.6 copy-done.22
  556.8 2.1 copy.74
  558.9 1.6 copy-done.21
  560.5 2.0 copy.75
  (75 shorter events, 9.4 us)
Async XLA Ops:
  5.2 182.2 %copy-start.17 = (s32[5,256]{1,0:T(8,128)}, s32[5,256]{1,0:T(8,128)S(1)}, u32[]{:S(2)}) copy-start(s32[5,256]{1,0:T(8,128)S(1)} %rev.3.sk_ref) | copy-start | bytes 15364
  6.2 181.2 %copy-start.8 = (s32[256,1]{1,0:T(8,128)}, s32[256,1]{1,0:T(8,128)S(1)}, u32[]{:S(2)}) copy-start(s32[256,1]{1,0:T(8,128)S(1)} %copy.52.sq_ref) | copy-start | bytes 3076
  6.2 3.6 copy-start.19
  6.9 8.8 %copy-start.6 = (f32[256,128]{1,0:T(8,128)}, f32[256,128]{1,0:T(8,128)S(1)}, u32[]{:S(2)}) copy-start(f32[256,128]{1,0:T(8,128)S(1)} %get-tuple-element.72.cos_ref) | copy-start | bytes 393220
  6.9 8.8 %copy-start.7 = (f32[256,128]{1,0:T(8,128)}, f32[256,128]{1,0:T(8,128)S(1)}, u32[]{:S(2)}) copy-start(f32[256,128]{1,0:T(8,128)S(1)} %get-tuple-element.73.sin_ref) | copy-start | bytes 393220
  10.3 3.7 copy-start.20
  14.0 1.7 copy-start.1
  14.0 2.2 copy-start.4
  14.0 2.4 copy-start.12
  182.2 1.0 copy-start.10
  183.2 1.0 copy-start.11
  184.2 0.7 copy-start.14
  184.2 199.9 %copy-start.9 = (bf16[256,512]{1,0:T(8,128)(2,1)}, bf16[256,512]{1,0:T(8,128)(2,1)S(1)}, u32[]{:S(2)}) copy-start(bf16[256,512]{1,0:T(8,128)(2,1)S(1)} %get-tuple-element.35.q_ref) | copy-start | bytes 786436
  184.9 199.2 %copy-start.18 = (f32[8,1,256]{2,1,0:T(1,128)}, f32[8,1,256]{2,1,0:T(1,128)S(1)}, u32[]{:S(2)}) copy-start(f32[8,1,256]{2,1,0:T(1,128)S(1)} %get-tuple-element.64) | copy-start | bytes 24580
  187.4 1.7 copy-start
  189.1 1.6 copy-start.2
  216.3 1.3 copy-start.3
  217.7 1.0 copy-start.5
  218.6 0.7 copy-start.13
  219.4 0.6 copy-start.15
  220.0 164.1 %copy-start.16 = (f32[256,128]{1,0:T(8,128)}, f32[256,128]{1,0:T(8,128)S(1)}, u32[]{:S(2)}) copy-start(f32[256,128]{1,0:T(8,128)S(1)} %get-tuple-element.45.s2_ref) | copy-start | bytes 393220
  385.7 161.5 %copy-start.25 = (bf16[256,2048]{1,0:T(8,128)(2,1)S(1)}, bf16[256,2048]{1,0:T(8,128)(2,1)}, u32[]{:S(2)}) copy-start(bf16[256,2048]{1,0:T(8,128)(2,1)} %get-tuple-element.87) | copy-start | bytes 3145732
  543.1 8.1 %copy-start.24 = (f32[3,256,512]{2,1,0:T(8,128)S(1)}, f32[3,256,512]{2,1,0:T(8,128)}, u32[]{:S(2)}) copy-start(f32[3,256,512]{2,1,0:T(8,128)} %get-tuple-element.89) | copy-start | bytes 4718596
  543.1 9.2 %copy-start.26 = (f32[512,256]{1,0:T(8,128)S(1)}, f32[512,256]{1,0:T(8,128)}, u32[]{:S(2)}) copy-start(f32[512,256]{1,0:T(8,128)} %get-tuple-element.90) | copy-start | bytes 1572868
  547.2 5.9 %copy-start.23 = (f32[2,2048,256]{2,1,0:T(8,128)S(1)}, f32[2,2048,256]{2,1,0:T(8,128)}, u32[]{:S(2)}) copy-start(f32[2,2048,256]{2,1,0:T(8,128)} %get-tuple-element.95) | copy-start | bytes 12582916
  553.1 3.7 copy-start.22
  556.8 3.7 copy-start.21

commit v6 on v5

--- a/solution.py
+++ b/solution.py
@@ -1764,25 +1764,35 @@
     return value * cosine + pltpu.roll(value, HEAD // 2, 1) * sine
 
 
-def project(tokens, w_qkv, w_out, out_grad, smalls, cosine, sine, collective_id):
+def project(
+    tokens, w_qkv, w_out, out_grad, smalls, cosine, sine, w_gate, w_up, w_down, experts, collective_id
+):
     rows, width = tokens.shape
     parts, depth, columns = w_qkv.shape
     heads = columns // HEAD
     tensors = NX * NC
     back = WINDOW // rows
     low, f32 = jnp.bfloat16, jnp.float32
-    QUERY, KEY, VALUE, SMALL, OUT, GRAD = 0, 1, 2, 3, 4, 5
+    QUERY, KEY, VALUE, SMALL, OUT, GRAD, REST = 0, 1, 2, 3, 4, 5, 6
+    out_half = w_out.shape[0] // 2
     out_rows, out_columns = w_out.shape
     quarter = width // tensors
 
     def kernel(
-        tok_ref, w_ref, out_ref, grad_in, small_ref, cos_ref, sin_ref,
-        w_all, out_all, grad_all, small_all, h1_ref, raw_ref, scale_ref, q_ref, context,
-        own_w, own_out, weights, total, part_k, land_k, part_q, land_q,
-        send_sem, recv_sem, out_sem, small_sem, kept, ks_s, ks_r, qs_s, qs_r, c_s, c_r, hx_s, hx_r, hc_s, hc_r,
+        tok_ref, w_ref, out_ref, grad_in, small_ref, cos_ref, sin_ref, gate_in, up_in, down_in,
+        w_all, out_all, grad_all, h1_out, raw_out, gate_up, down_out, gain_ref, router_ref, chosen_ref, scale_ref, q_ref, context,
+        small_all, h1_ref, raw_ref, wide_in, wide_low, down_f, down_low, own_w, own_out, weights, total, part_k, land_k, part_q, land_q,
+        send_sem, recv_sem, out_sem, small_sem, kept, ks_s, ks_r, qs_s, qs_r, c_s, c_r, hx_s, hx_r, hc_s, hc_r, wide_s,
     ):
         z, y, x, c = place()
         e, t = lax.axis_index("expert"), lax.axis_index("tensor")
+        wide_loads = [
+            pltpu.make_async_copy(source.at[k], wide_in.at[2 * n + k], wide_s.at[2 * n + k])
+            for n, source in enumerate((gate_in, up_in))
+            for k in range(2)
+        ]
+        for copy in wide_loads:
+            copy.start()
         mates = [(e, lax.rem(t + k, tensors)) for k in range(1, tensors)]
         beside, above = device(z, 1 - y, x, c), device(z + 1, y, x, c)
         views = [
@@ -1790,8 +1800,9 @@
             lambda b: weights.at[KEY, block_rows(b, depth), :],
             lambda b: weights.at[VALUE, block_rows(b, depth), :],
             lambda b: small_all.at[b],
-            lambda b: out_all.at[:, block_rows(b, out_columns)],
+            lambda b: out_all.at[pl.ds(0, out_half), block_rows(b, out_columns)],
             lambda b: grad_view(b, x, c),
+            lambda b: out_all.at[pl.ds(out_half, out_half), block_rows(b, out_columns)],
         ]
         across, twin = device(z, y, 1 - x, c), device(z, y, x, 1 - c)
 
@@ -1810,8 +1821,11 @@
             return remote(piece, piece, hc_s.at[b, relayed], hc_r.at[b, relayed], twin)
 
         line = LineGather(
-            [SMALL, VALUE, KEY, QUERY, OUT, GRAD],
-            [own_w.at[0], own_w.at[1], own_w.at[2], small_ref, own_out, grad_in.at[:, quarter_at(x, c)]],
+            [SMALL, VALUE, KEY, QUERY, OUT, GRAD, REST],
+            [
+                own_w.at[0], own_w.at[1], own_w.at[2], small_ref, own_out.at[pl.ds(0, out_half)],
+                grad_in.at[:, quarter_at(x, c)], own_out.at[pl.ds(out_half, out_half)],
+            ],
             views, send_sem, recv_sem, y_first=(OUT,),
         )
         greet(line.partners() + [(mate, None) for mate in mates])
@@ -1871,22 +1885,77 @@
                     b = line.block(rel)
                     grad_across(b).start()
                     grad_twin(b, 0).start()
-                elif stream != OUT:
+                elif stream not in (OUT, REST):
                     use(stream, rel)
             run_if(line.exists(rel), body)
 
         use(SMALL, 0)
         use(VALUE, 0)
         own_small.wait()
+
+        units = down_in.shape[1]
+        for n, copy in enumerate(wide_loads):
+            copy.wait()
+
+            def round_wide(i, carry, n=n):
+                r = pl.ds(pl.multiple_of(i * 64, 64), 64)
+                wide_low[r, pl.ds(n * units, units)] = wide_in[n, r, :].astype(low)
+                return carry
+
+            lax.fori_loop(0, width // 64, round_wide, 0)
+        wide_out = pltpu.make_async_copy(wide_low, gate_up, wide_s.at[0])
+        wide_out.start()
+        down_loads = [
+            pltpu.make_async_copy(down_in.at[k], down_f.at[pl.ds(k * units, units), :], wide_s.at[1 + k])
+            for k in range(2)
+        ]
+        for copy in down_loads:
+            copy.start()
+
         use(KEY, 0)
-        early, late = [7, 1, 4, 8, 11, 2, 5], [9, 12, 3, 6, 10, 13]
-        for rel in early:
+        def events(*pairs):
+            for stream, rels in pairs:
+                for rel in rels:
+                    event(stream, rel)
+
+        for rel in (7, 1, 4, 2, 5):
             event(SMALL, rel)
             event(VALUE, rel)
+        for copy in down_loads:
+            copy.wait()
+
+        def round_down(i, carry):
+            r = pl.ds(pl.multiple_of(i * 32, 32), 32)
+            down_low[r, :] = down_f[r, :].astype(low)
+            return carry
+
+        lax.fori_loop(0, 2 * units // 32, round_down, 0)
+        down_copy = pltpu.make_async_copy(down_low, down_out, wide_s.at[3])
+        down_copy.start()
         line.start(QUERY, 0)
-        for rel in late:
+        for rel in (3, 6):
             event(SMALL, rel)
             event(VALUE, rel)
+        events((KEY, (7, 1, 4)))
+        for rel in (8, 11, 9, 12, 10, 13):
+            event(SMALL, rel)
+            event(VALUE, rel)
+
+        slices = HEAD // GROUPS
+        for b in range(GROUPS):
+            at = pl.ds(b * depth, depth)
+            gain_ref[0:2, at] = small_all[b, 0:2, :]
+            router_ref[:, at] = small_all[b, 8 : 8 + experts, :].astype(low)
+            tall = jnp.concatenate(
+                [small_all[b, 8 + experts : 8 + 2 * experts, :], jnp.zeros((128 - experts, depth), f32)], axis=0
+            )
+            chosen_ref[pl.ds(b * depth, depth), :] = jnp.transpose(tall)[:, :experts].astype(low)
+        for which in range(2):
+            for head in range(heads):
+                start = (which * heads + head) * slices
+                gain_ref[2 + which : 3 + which, pl.ds(head * HEAD, HEAD)] = jnp.concatenate(
+                    [small_all[b, 2:3, start : start + slices] for b in range(GROUPS)], axis=1
+                )
 
         def context_copy(which, k):
             if k == 2:
@@ -1916,35 +1985,22 @@
         context[0, 1] = total[VALUE].astype(low)
         context_send(1, 2)
         run_if(y == 0, lambda: context_copy(1, 1).start())
-        for rel in early:
-            event(KEY, rel)
-        for rel in late:
-            event(KEY, rel)
+        events((KEY, (2, 5, 3, 6)), (QUERY, (7, 1, 4)))
+        line.start(GRAD, 0)
         line.start(OUT, 0)
+        line.start(REST, 0)
+        events((KEY, (8, 11, 9, 12, 10, 13)))
         key_raw = total[KEY]
         raw_ref[1] = key_raw
         exchange_rows(jnp.sum(key_raw * key_raw, axis=-1, keepdims=True), part_k, land_k, ks_s, ks_r, mates)
         use(QUERY, 0)
-        for rel in early[:3]:
-            event(QUERY, rel)
-
+        events((QUERY, (2, 5)))
         key_scale = lax.rsqrt(exchanged_rows(part_k, land_k, ks_s, ks_r, mates) / width + EPS)
         scale_ref[:, 2:3] = key_scale
-        slices = HEAD // GROUPS
-        gains = []
-        for which in range(2):
-            per_head = []
-            for head in range(heads):
-                start = (which * heads + head) * slices
-                per_head.append(
-                    jnp.concatenate([small_all[b, 2:3, start : start + slices] for b in range(GROUPS)], axis=1)
-                )
-            gains.append(per_head)
-
         def rotated(which, scale, store):
             for head in range(heads):
                 at = pl.ds(head * HEAD, HEAD)
-                value = total[which, :, at] * scale * gains[which][head]
+                value = total[which, :, at] * scale * gain_ref[2 + which : 3 + which, at]
                 store(at, turn(value, cos_ref[...], sin_ref[...]).astype(low))
 
         def store_key(at, value):
@@ -1965,15 +2021,11 @@
             run_if((y == 1) & sends[3], lambda: context_copy(which, 3).start())
 
         relay_two(1)
-        for rel in early[3:]:
-            event(QUERY, rel)
+        events((QUERY, (3, 6)), (GRAD, (7, 1, 4)), (OUT, (7, 1, 4)), (REST, (7, 1, 4)))
         relay_four(1)
-        for rel in late[:4]:
-            event(QUERY, rel)
+        events((QUERY, (8, 11)), (GRAD, (2, 5)), (OUT, (8, 11, 2, 5)), (REST, (2, 5)))
         relay_two(0)
-        for rel in late[4:]:
-            event(QUERY, rel)
-        line.start(GRAD, 0)
+        events((QUERY, (9, 12, 10, 13)))
         query_raw = total[QUERY]
         raw_ref[0] = query_raw
         exchange_rows(jnp.sum(query_raw * query_raw, axis=-1, keepdims=True), part_q, land_q, qs_s, qs_r, mates)
@@ -1981,6 +2033,13 @@
             weights[part, block_rows(line.block(0), depth), :] = own_w[part]
         keep = pltpu.make_async_copy(weights, w_all, out_sem)
         keep.start()
+        keep_more = [
+            pltpu.make_async_copy(h1_ref, h1_out, kept.at[2]),
+            pltpu.make_async_copy(raw_ref, raw_out, kept.at[3]),
+        ]
+        for copy in keep_more:
+            copy.start()
+        events((GRAD, (3, 6)), (OUT, (9, 12, 3, 6)), (REST, (3, 6, 8, 11)))
         relay_four(0)
         query_scale = lax.rsqrt(exchanged_rows(part_q, land_q, qs_s, qs_r, mates) / width + EPS)
         scale_ref[:, 1:2] = query_scale
@@ -1989,22 +2048,17 @@
             q_ref[:, at] = value
 
         rotated(QUERY, query_scale, store_query)
-        for rel in early:
-            event(OUT, rel)
-            event(GRAD, rel)
+        events((GRAD, (8, 11, 9, 12)), (OUT, (10, 13)), (REST, (9, 12, 10, 13)), (GRAD, (10, 13)))
         for which in (1, 0):
             for k in (1, 3):
                 context_take(which, k)
-        for rel in late:
-            event(OUT, rel)
-            event(GRAD, rel)
-        for rel in early + late:
+        for rel in line.order():
             def relay(rel=rel):
                 b = line.block(rel)
                 grad_across(b, True).wait_recv()
                 grad_twin(b, 1).start()
             run_if(line.exists(rel), relay)
-        for rel in early + late:
+        for rel in line.order():
             def landed(rel=rel):
                 b = line.block(rel)
                 grad_across(b).wait_send()
@@ -2013,6 +2067,10 @@
                     grad_twin(b, relayed).wait_send()
             run_if(line.exists(rel), landed)
         line.finish()
+        for copy in keep_more:
+            copy.wait()
+        wide_out.wait()
+        down_copy.wait()
         keep_out.wait()
         keep_grad.wait()
         for which in range(2):
@@ -2029,16 +2087,27 @@
             shape((parts, depth * GROUPS, columns), low),
             shape((out_rows, out_columns * GROUPS), low),
             shape((rows * GROUPS, width), low),
-            shape((GROUPS,) + smalls.shape, f32),
             shape((rows, width), low),
             shape((2, rows, columns), f32),
+            shape((width, 4 * w_down.shape[1]), low),
+            shape((2 * w_down.shape[1], width), low),
+            shape((8, width), f32),
+            shape((experts, width), low),
+            shape((rows * GROUPS, experts), low),
             shape((rows, 128), f32),
             shape((rows, columns), low),
             shape((back + 1, 2, rows, columns), low),
         ),
-        in_specs=[VMEM, VMEM, VMEM, HBM, VMEM, VMEM, VMEM],
-        out_specs=(HBM,) * 3 + (VMEM,) * 6,
+        in_specs=[VMEM, VMEM, VMEM, HBM, VMEM, VMEM, VMEM, HBM, HBM, HBM],
+        out_specs=(HBM,) * 7 + (VMEM,) * 6,
         scratch_shapes=[
+            pltpu.VMEM((GROUPS,) + smalls.shape, f32),
+            pltpu.VMEM((rows, width), low),
+            pltpu.VMEM((2, rows, columns), f32),
+            pltpu.VMEM((4, width, w_down.shape[1]), f32),
+            pltpu.VMEM((width, 4 * w_down.shape[1]), low),
+            pltpu.VMEM((2 * w_down.shape[1], width), f32),
+            pltpu.VMEM((2 * w_down.shape[1], width), low),
             pltpu.VMEM((parts, depth, columns), low),
             pltpu.VMEM((out_rows, out_columns), low),
             pltpu.VMEM((parts, depth * GROUPS, columns), low),
@@ -2047,15 +2116,15 @@
             pltpu.VMEM((tensors - 1, 8, rows), f32),
             pltpu.VMEM((8, rows), f32),
             pltpu.VMEM((tensors - 1, 8, rows), f32),
-            dma((6, 14, 3)), dma((6, 14)), dma, dma, dma((2,)),
+            dma((7, 14, 3)), dma((7, 14)), dma, dma, dma((4,)),
             dma((tensors - 1,)), dma((tensors - 1,)), dma((tensors - 1,)), dma((tensors - 1,)),
             dma((2, back + 1)), dma((2, back + 1)),
-            dma((GROUPS,)), dma((GROUPS,)), dma((GROUPS, 2)), dma((GROUPS, 2)),
+            dma((GROUPS,)), dma((GROUPS,)), dma((GROUPS, 2)), dma((GROUPS, 2)), dma((4,)),
         ],
-        compiler_params=comm_params(collective_id, 48),
+        compiler_params=comm_params(collective_id, 56),
         cost_estimate=cost(100),
         name="project",
-    )(tokens, w_qkv, w_out, out_grad, smalls, cosine, sine)
+    )(tokens, w_qkv, w_out, out_grad, smalls, cosine, sine, w_gate, w_up, w_down)
 
 
 def attend(query, context, segment_query, segment_keys, tokens, out_low, gain, collective_id):
@@ -2129,7 +2198,7 @@
             scale = lax.rsqrt(jnp.mean(value * value, axis=-1, keepdims=True) + EPS)
             x1_ref[r, :] = value
             scale_ref[r, :] = jnp.broadcast_to(scale, (32, 128))
-            h2_ref[r, :] = (value * scale * gain_ref[...]).astype(low)
+            h2_ref[r, :] = (value * scale * gain_ref[1:2, :]).astype(low)
             return carry
 
         lax.fori_loop(0, rows // 32, norm, 0)
@@ -2160,9 +2229,9 @@
 
 
 def attend_back(
-    grad_hidden, grad_probs, router_t, hidden_two, residual, scale_two, gain_two, out_grad,
-    query, context, segment_query, segment_keys, attended, log_sums, raw, scales, qk_gains,
-    cosine, sine, hidden_one, tokens, gain_one, qkv_low, out_low, collective_id,
+    grad_hidden, grad_probs, router_t, hidden_two, residual, scale_two, gains, out_grad,
+    query, context, segment_query, segment_keys, attended, log_sums, raw, scales,
+    cosine, sine, hidden_one, tokens, qkv_low, out_low, collective_id,
 ):
     rows, width = tokens.shape
     columns = query.shape[1]
@@ -2177,11 +2246,11 @@
     QUERY, KEY, VALUE, OUT, SMALL = 0, 1, 2, 3, 4
 
     def kernel(
-        dh_ref, gates_ref, router_ref, h2_ref, x1_ref, s2_ref, g2_ref, dy_ref,
-        q_ref, context_ref, sq_ref, sk_ref, o_ref, lse_ref, raw_ref, scale_ref, qkg_ref,
-        cos_ref, sin_ref, h1_ref, tok_ref, g1_ref, w_hbm, out_ref,
+        dh_ref, gates_ref, router_ref, h2_ref, x1_ref, s2_ref, gain_ref, dy_ref,
+        q_ref, context_ref, sq_ref, sk_ref, o_ref, lse_ref, raw_ref, scale_ref,
+        cos_ref, sin_ref, h1_ref, tok_ref, w_hbm, out_ref,
         tok_grad, qkv_sum, out_sum, small_sum,
-        weights, dx1, da, do, dot_sums, dq, dkv, proj, send_kv, land_y, land_z,
+        weights, dx1, da, do, dot_sums, dq, dkv, scaled, proj, send_kv, land_y, land_z,
         part, full, core_buf, x_buf, small, line_sum,
         main_buf, out_acc, out_lo, out_hi, out_land, small_buf, part_k, land_k, part_q, land_q,
         w_sem, y_s, y_r, z_s, z_r, group_s, group_r, ks_s, ks_r, qs_s, qs_r, line_s, line_r, out_s, out_r, out_y_s, out_y_r,
@@ -2282,7 +2351,7 @@
             grad = dh_ref[r, :].astype(f32) + dx1[r, :]
             value, scale = x1_ref[r, :], s2_ref[r, 0:1]
             line_sum[0:1, :] += jnp.sum(grad * (value * scale), axis=0, keepdims=True)
-            grad = grad * g2_ref[...]
+            grad = grad * gain_ref[1:2, :]
             inner = jnp.mean(grad * value, axis=-1, keepdims=True)
             result = dy_ref[r, :].astype(f32) + scale * grad - value * (scale * scale * scale) * inner
             dx1[r, :] = result
@@ -2386,8 +2455,8 @@
                 line_sum[1 + which : 2 + which, at] = jnp.sum(
                     grad * (value * scale_ref[:, 1 + which : 2 + which]), axis=0, keepdims=True
                 )
-                grad = grad * qkg_ref[which : which + 1, at]
-                dkv[1 + which, 0, :, at] = grad
+                grad = grad * gain_ref[2 + which : 3 + which, at]
+                scaled[which, :, at] = grad
                 inner = inner + jnp.sum(grad * value, axis=-1, keepdims=True)
             return inner
 
@@ -2397,7 +2466,7 @@
             for head in range(heads):
                 at = pl.ds(head * HEAD, HEAD)
                 proj[which, :, at] = (
-                    scale * dkv[1 + which, 0, :, at] - raw_ref[which, :, at] * rest
+                    scale * scaled[which, :, at] - raw_ref[which, :, at] * rest
                 ).astype(low)
 
         def send_beside(s):
@@ -2406,18 +2475,18 @@
                 buffer[...] = own_part(s, zz * NY + 1 - y).astype(buffer.dtype)
                 line.to_y(s, zz)
 
+        exchange_rows(unturn(QUERY, lambda at: dq[:, at]), part_q, land_q, qs_s, qs_r, mates)
         take_three(1)
         take_three(0)
+        denorm(QUERY, exchanged_rows(part_q, land_q, qs_s, qs_r, mates))
+        send_beside(QUERY)
         out_hop(1)
         take_one(1)
         take_one(0)
         take_four(1)
         take_four(0)
-        exchange_rows(unturn(QUERY, lambda at: dq[:, at]), part_q, land_q, qs_s, qs_r, mates)
         take_two(1)
         proj[VALUE] = dkv[0, 1].astype(low)
-        denorm(QUERY, exchanged_rows(part_q, land_q, qs_s, qs_r, mates))
-        send_beside(QUERY)
         send_beside(VALUE)
         take_two(0)
         out_hop(2)
@@ -2480,7 +2549,7 @@
             r = pl.ds(pl.multiple_of(i * 32, 32), 32)
             grad, value, scale = full[r, :].astype(f32), tok_ref[r, :].astype(f32), scale_ref[r, 0:1]
             line_sum[3:4, :] += jnp.sum(grad * (value * scale), axis=0, keepdims=True)
-            grad = grad * g1_ref[...]
+            grad = grad * gain_ref[0:1, :]
             inner = jnp.mean(grad * value, axis=-1, keepdims=True)
             tok_grad[r, :] = (
                 dx1[r, :] + scale * grad - value * (scale * scale * scale) * inner
@@ -2532,7 +2601,7 @@
             shape((columns, depth), f32),
             shape((small_rows, depth), f32),
         ),
-        in_specs=[VMEM] * 22 + [HBM, VMEM],
+        in_specs=[VMEM] * 20 + [HBM, VMEM],
         out_specs=(VMEM,) * 4,
         scratch_shapes=[
             vmem(qkv_low.shape, low),
@@ -2542,6 +2611,7 @@
             vmem((rows, 128), f32),
             vmem((rows, columns), f32),
             vmem((blocks, 2, rows, columns), f32),
+            vmem((2, rows, columns), f32),
             vmem((3, rows, columns), low),
             vmem((blocks - 1, 2, rows, columns), low),
             vmem((2, 2, rows, columns), low),
@@ -2570,9 +2640,9 @@
         cost_estimate=cost(130),
         name="attend_back",
     )(
-        grad_hidden, grad_probs, router_t, hidden_two, residual, scale_two, gain_two, out_grad,
-        query, context, segment_query, segment_keys, attended, log_sums, raw, scales, qk_gains,
-        cosine, sine, hidden_one, tokens, gain_one, qkv_low, out_low,
+        grad_hidden, grad_probs, router_t, hidden_two, residual, scale_two, gains, out_grad,
+        query, context, segment_query, segment_keys, attended, log_sums, raw, scales,
+        cosine, sine, hidden_one, tokens, qkv_low, out_low,
     )
 
 
@@ -2628,19 +2698,11 @@
     wide_cosine = jnp.concatenate([cosine_table[:, 0], cosine_table[:, 0]], axis=1)
     wide_sine = jnp.concatenate([-sine_table[:, 0], sine_table[:, 0]], axis=1)
     (
-        qkv_low, out_low, grad_out_all, small_all, hidden_one, raw, scales, query_low, context_blocks
-    ) = project(tokens_in, w_qkv, w_attn_out, out_grad, smalls, wide_cosine, wide_sine, 0)
-    gain_one_f = small_all[:, 0].reshape(model_width)
-    gain_two_f = small_all[:, 1].reshape(model_width)
-    qk_gains = (
-        small_all[:, 2, : qk_row.shape[1]]
-        .reshape(groups, 2, heads_here, HEAD // groups)
-        .transpose(1, 2, 0, 3)
-        .reshape(2, local_width)
-    )
-    router_t = small_all[:, 8 : 8 + experts].transpose(1, 0, 2).reshape(experts, model_width).astype(low)
-    chosen_all = small_all[:, 8 + experts : 8 + 2 * experts].transpose(0, 2, 1).reshape(
-        groups * row_count, experts
+        qkv_low, out_low, grad_out_all, hidden_one, raw, gate_up, down_low, gains, router_t, chosen_all,
+        scales, query_low, context_blocks,
+    ) = project(
+        tokens_in, w_qkv, w_attn_out, out_grad, smalls, wide_cosine, wide_sine, w_gate, w_up, w_down,
+        experts, 0,
     )
     segment_window = lax.dynamic_slice_in_dim(
         jnp.concatenate([jnp.full((WINDOW,), -1, jnp.int32), segments]),
@@ -2650,21 +2712,16 @@
     segment_keys = segment_window.reshape(hop_count + 1, row_count)[::-1]
     attended, log_sums, residual, hidden_two, scale_two_wide = attend(
         query_low, context_blocks, segment_query[:, None], segment_keys, tokens_in, out_low,
-        gain_two_f[None, :], 2,
-    )
-    gate_up = jnp.concatenate(
-        [w[i] for w in (w_gate, w_up) for i in range(local_experts)], axis=1
-    ).astype(low)
-    down_low = w_down.reshape(-1, model_width).astype(low)
+        gains, 2,
+    )
     block_out, grad_hidden_sum, grad_gate_sum, grad_gate_w, grad_up_w, grad_down = expert_layer(
-        hidden_two, grad_out_all, gate_up, down_low, router_t, chosen_all.astype(low), residual, 5
+        hidden_two, grad_out_all, gate_up, down_low, router_t, chosen_all, residual, 5
     )
     grad_probs = grad_gate_sum[:, :local_experts].reshape(experts, row_count).T * chosen
     grad_tokens, qkv_sum, out_sum, small_sum = attend_back(
         grad_hidden_sum, grad_probs, router_t, hidden_two, residual, scale_two_wide,
-        gain_two_f[None, :], out_grad, query_low, context_blocks, segment_query[:, None], segment_keys,
-        attended, log_sums, raw, scales, qk_gains, wide_cosine, wide_sine, hidden_one, tokens_in,
-        gain_one_f[None, :], qkv_low, out_low, 8,
+        gains, out_grad, query_low, context_blocks, segment_query[:, None], segment_keys,
+        attended, log_sums, raw, scales, wide_cosine, wide_sine, hidden_one, tokens_in, qkv_low, out_low, 8,
     )
     return (
         block_out,

time: 571 us -> 541 us (0.947)
  Pallas kernels: 513 us -> 495 us
  other arithmetic: 11.3 us -> 4.85 us
    pallas_call x1, Pallas kernels: 166 us -> 133 us  [project(): pl.pallas_call(kernel, out_shape=(shape((parts, depth * GROUPS, columns),...]
    pallas_call x1, Pallas kernels: 164 us -> 179 us  [expert_layer(): pl.pallas_call(kernel, out_shape=(shape((rows, width), low), shape((rows,...]
    unnamed x61 -> x45, local copies, waits for them, and re-layouts: 26.3 us -> 24.7 us
where the time goes in v6:
time: 541 us; the launch traced here: 534 us
  Pallas kernels  495 us (91%)
  local copies, waits for them, and re-layouts  33 us (6%)
    pallas_call x1, Pallas kernels, expert_layer(): pl.pallas_call(kernel, out_shape=(shape((rows, width), low), shape((rows,...  179 us
    pallas_call x1, Pallas kernels, attend_back(): pl.pallas_call(kernel, out_shape=(shape((rows, width), low), shape((3, de...  158 us
    pallas_call x1, Pallas kernels, project(): pl.pallas_call(kernel, out_shape=(shape((parts, depth * GROUPS, columns),...  133 us
    pallas_call x1, Pallas kernels, attend(): pl.pallas_call(kernel, out_shape=(shape((rows, columns), low), shape((row...  25.9 us
    unnamed x45, local copies, waits for them, and re-layouts  24.7 us

profile of v6, /device:TPU:0, one launch (start us, length us, event | category | flops | bytes accessed | tf_op | source)
XLA Modules:
  0.0 534.3 jit_solution(16938206030627664873)
XLA Ops:
  1.2 0.8 pad_maximum_fusion
  2.1 0.7 fusion
  2.8 0.7 reduce_precision.22
  3.6 0.7 reduce_precision.20
  4.3 0.7 reduce_precision.21
  4.9 2.5 concatenate.12.small_ref
  7.5 133.0 %project.1 = (bf16[3,2048,512]{2,1,0:T(8,128)(2,1)}, bf16[512,2048]{1,0:T(8,128)(2,1)}, bf16[2048,2048]{1,0:T(8,128)(2,1)}, bf16[256,2048]{1,0:T(8,128)(2,1)}, f...) custom-call(bf16[256,2048]{1,0:T(8,128)(2,1)} %tok_ref.5, ...), custom_call_target="tpu_custom_call" | custom-call | bytes 300000000 | tf_op jit(solution)/shard_map/project/pallas_call | solution.py:2084
  140.9 1.7 copy-done
  142.7 1.6 copy-done.3
  144.3 0.9 copy-done.6
  145.2 0.8 copy-done.8
  146.0 25.9 %attend.1 = (bf16[256,512]{1,0:T(8,128)(2,1)S(1)}, f32[256,128]{1,0:T(8,128)S(1)}, f32[256,2048]{1,0:T(8,128)S(1)}, bf16[256,2048]{1,0:T(8,128)(2,1)S(1)}, f32[256,128]{1,0:T(8,128)S(1)}) custom-call(bf16[256,512]{1,0:T(8,128)(2,1)S(1)} %copy-done.6, bf16[5,2,256,512]{3,2,1,0:T(8,128)(2,1)S(1)} %copy-done, s32[256,1]{1,0:T(8,128)S(1)} %copy.43.sq_ref, ...), custom_call_target="tpu_custom_call" | custom-call | bytes 120000000 | tf_op jit(solution)/shard_map/attend/pallas_call | solution.py:2207
  171.9 1.3 copy-done.2
  173.3 1.0 copy-done.4
  174.2 0.7 copy-done.7
  176.2 178.6 %expert_layer.1 = (bf16[256,2048]{1,0:T(8,128)(2,1)}, bf16[256,2048]{1,0:T(8,128)(2,1)}, f32[8,8,256]{2,1,0:T(8,128)}, f32[2,2048,256]{2,1,0:T(8,128)}, f32[2,20...) custom-call(bf16[256,2048]{1,0:T(8,128)(2,1)} %copy-done.4, bf16[2048,2048]{1,0:T(8,128)(2,1)} %get-tuple-element.44.dy_in, ...), custom_call_target="tpu_custom_call" | custom-call | bytes 240000000 | tf_op jit(solution)/shard_map/expert_layer/pallas_call | solution.py:1687
  354.8 0.8 slice.19
  355.9 0.7 bitcast_select_fusion.gates_ref
  356.6 157.7 %attend_back.1 = (bf16[256,2048]{1,0:T(8,128)(2,1)}, f32[3,256,512]{2,1,0:T(8,128)}, f32[512,256]{1,0:T(8,128)}, f32[24,256]{1,0:T(8,128)}) custom-call(bf16[256,2048]{1,0:T(8,128)(2,1)} %get-tuple-element.51.dh_ref, f32[256,16]{1,0:T(8,128)} %bitcast_select_fusion.gates_ref, bf16[16,2048]{1,0:T(8,128)(2,1)} %get-tuple-element.47.router_ref, ...), custom_call_target="tpu_custom_call" | custom-call | bytes 390000000 | tf_op jit(solution)/shard_map/attend_back/pallas_call | solution.py:2596
  514.3 0.8 slice.22
  515.2 0.7 constant_dynamic-slice_fusion
  515.8 1.3 slice_bitcast_fusion
  517.2 1.3 fusion.4
  518.5 1.0 copy.54
  519.5 3.0 copy.55
  522.4 1.1 copy.56
  523.6 0.8 copy.57
  524.4 2.1 copy.58
  526.5 1.6 copy-done.13
  528.1 2.1 copy.59
  530.2 1.6 copy-done.12
  531.8 2.0 copy.60
  (45 shorter events, 2.6 us)
Async XLA Ops:
  7.5 133.0 %copy-start.18 = (s32[2048]{0:T(1024)S(1)}, s32[2048]{0:T(1024)}, u32[]{:S(2)}) copy-start(s32[2048]{0:T(1024)} %param.25) | copy-start | bytes 24580
  7.5 133.4 %copy-start.1 = (bf16[256,2048]{1,0:T(8,128)(2,1)S(1)}, bf16[256,2048]{1,0:T(8,128)(2,1)}, u32[]{:S(2)}) copy-start(bf16[256,2048]{1,0:T(8,128)(2,1)} %tok_ref.5) | copy-start | bytes 3145732
  140.8 214.1 %copy-start.5 = (s32[256,1]{1,0:T(8,128)}, s32[256,1]{1,0:T(8,128)S(1)}, u32[]{:S(2)}) copy-start(s32[256,1]{1,0:T(8,128)S(1)} %copy.43.sq_ref) | copy-start | bytes 3076
  140.9 1.7 copy-start
  142.7 1.6 copy-start.3
  144.3 0.9 copy-start.6
  145.2 0.8 copy-start.8
  146.0 208.8 %copy-start.11 = (s32[5,256]{1,0:T(8,128)}, s32[5,256]{1,0:T(8,128)S(1)}, u32[]{:S(2)}) copy-start(s32[5,256]{1,0:T(8,128)S(1)} %rev.3.sk_ref) | copy-start | bytes 15364
  171.9 1.3 copy-start.2
  173.3 1.0 copy-start.4
  174.2 0.7 copy-start.7
  174.9 0.7 copy-start.9
  175.6 0.7 copy-start.10
  356.6 161.9 %copy-start.16 = (bf16[256,2048]{1,0:T(8,128)(2,1)S(1)}, bf16[256,2048]{1,0:T(8,128)(2,1)}, u32[]{:S(2)}) copy-start(bf16[256,2048]{1,0:T(8,128)(2,1)} %get-tuple-element.85) | copy-start | bytes 3145732
  514.3 8.2 %copy-start.15 = (f32[3,256,512]{2,1,0:T(8,128)S(1)}, f32[3,256,512]{2,1,0:T(8,128)}, u32[]{:S(2)}) copy-start(f32[3,256,512]{2,1,0:T(8,128)} %get-tuple-element.87) | copy-start | bytes 4718596
  514.3 9.3 %copy-start.17 = (f32[512,256]{1,0:T(8,128)S(1)}, f32[512,256]{1,0:T(8,128)}, u32[]{:S(2)}) copy-start(f32[512,256]{1,0:T(8,128)} %get-tuple-element.88) | copy-start | bytes 1572868
  518.5 5.9 %copy-start.14 = (f32[2,2048,256]{2,1,0:T(8,128)S(1)}, f32[2,2048,256]{2,1,0:T(8,128)}, u32[]{:S(2)}) copy-start(f32[2,2048,256]{2,1,0:T(8,128)} %get-tuple-element.93) | copy-start | bytes 12582916
  524.4 3.7 copy-start.13
  528.1 3.7 copy-start.12

commit v7 on v6

--- a/solution.py
+++ b/solution.py
@@ -1130,16 +1130,18 @@
     half, part, piece = width // 2, width // 4, width // 8
     tensors = NX * NC
     steps = GROUPS + 4
-    a_cols, c_cols = width * 3 // 16, width // 8
+    a_cols, c_cols = width // 8, width // 4
     low = jnp.bfloat16
     wide = width // 4
 
     def kernel(
         own_in, dy_in, gu_ref, down_ref, router_ref, chosen_ref, x1_in,
         block_out, dh_out, gates_out, gate_w, up_w, down_w,
-        h, dy, gated, dgu, dx, y_part, yc_buf, yx_buf, yy_buf, ylo_buf, yhi_buf, x1, gu_stage, d_stage,
+        h, dy, gated, dgu, dx, y_part, yc_buf, ypx_buf, ypy_buf, yqy_buf, yqx_buf, yz_sum,
+        ylo_buf, yhi_buf, x1, gu_stage, d_stage,
         core_buf, px_buf, py_buf, qy_buf, qx_buf, z_sum, lo_buf, hi_buf, gate_part, gate_land,
-        in_sem, own_sem, line_s, line_r, hx_s, hx_r, hc_s, hc_r, x1_sem, yc_s, yc_r, yx_s, yx_r, yy_s, yy_r, yz_s, yz_r, gu_sem, d_sem, core_s, core_r, px_s, px_r, py_s, py_r, qy_s, qy_r, qx_s, qx_r,
+        in_sem, own_sem, line_s, line_r, hx_s, hx_r, hc_s, hc_r, x1_sem, yc_s, yc_r, ypx_s, ypx_r, ypy_s, ypy_r,
+        yqy_s, yqy_r, yqx_s, yqx_r, yz_s, yz_r, gu_sem, d_sem, core_s, core_r, px_s, px_r, py_s, py_r, qy_s, qy_r, qx_s, qx_r,
         z_s, z_r, near_s, near_r, far_s, far_r, end_s, end_r,
     ):
         z, y, x, c = place()
@@ -1228,10 +1230,15 @@
             return carry
 
         lax.fori_loop(0, GROUPS, start_load, 0)
-        x1_copy = pltpu.make_async_copy(
-            x1_in.at[:, pl.ds(pl.multiple_of(c * half + x * part, part), part)], x1, x1_sem
-        )
-        x1_copy.start()
+        x1_copies = [
+            pltpu.make_async_copy(
+                x1_in.at[:, pl.ds(pl.multiple_of(c * half + s * part + x * piece, piece), piece)],
+                x1.at[:, pl.ds(s * piece, piece)], x1_sem.at[s],
+            )
+            for s in range(2)
+        ]
+        for copy in x1_copies:
+            copy.start()
 
         def to_twin(i):
             b = block_of(i)
@@ -1324,53 +1331,85 @@
                 yc_buf.at[block_of(i)], yc_s.at[i], yc_r.at[i], twin,
             )
 
-        def y_across(i):
+        def yp_across(i):
             b = block_of(i)
             return remote(
-                yc_buf.at[b, :, pl.ds(pl.multiple_of((1 - x) * part, part), part)],
-                yx_buf.at[b], yx_s.at[i], yx_r.at[i], across,
+                yc_buf.at[b, :, pl.ds(pl.multiple_of((1 - x) * piece, piece), piece)],
+                ypx_buf.at[b], ypx_s.at[i], ypx_r.at[i], across,
             )
 
-        def y_beside(j):
-            return remote(yx_buf.at[flip_block(j)], yy_buf.at[zz_of(j)], yy_s.at[j], yy_r.at[j], beside)
-
-        def y_up(j):
-            return remote(yy_buf.at[j], ylo_buf.at[j], yz_s.at[0, j], yz_r.at[0, j], device(z + 1, y, x, c))
-
-        def y_down(j):
-            return remote(yy_buf.at[j], yhi_buf.at[j], yz_s.at[1, j], yz_r.at[1, j], device(z - 1, y, x, c))
+        def yp_beside(j):
+            return remote(ypx_buf.at[flip_block(j)], ypy_buf.at[j], ypy_s.at[j], ypy_r.at[j], beside)
+
+        def yq_beside(j):
+            return remote(
+                yc_buf.at[flip_block(j), :, pl.ds(part, part)], yqy_buf.at[j], yqy_s.at[j], yqy_r.at[j], beside
+            )
+
+        def yq_across(j):
+            return remote(
+                yqy_buf.at[j, :, pl.ds(pl.multiple_of((1 - x) * piece, piece), piece)],
+                yqx_buf.at[j], yqx_s.at[j], yqx_r.at[j], across,
+            )
+
+        def y_up(zz, s):
+            return remote(
+                yz_sum.at[s, zz], ylo_buf.at[s, zz], yz_s.at[0, s, zz], yz_r.at[0, s, zz], device(z + 1, y, x, c)
+            )
+
+        def y_down(zz, s):
+            return remote(
+                yz_sum.at[s, zz], yhi_buf.at[s, zz], yz_s.at[1, s, zz], yz_r.at[1, s, zz], device(z - 1, y, x, c)
+            )
 
         def take_y_twin(i):
             y_twin(i).wait_recv()
             mine = yc_buf.at[block_of(i)]
             add_to(mine, mine, y_part.at[lax.rem(i, 2), :, pl.ds(pl.multiple_of(c * half, half), half)], 32)
-            y_across(i).start()
-
-        def take_y_across(i):
-            y_across(i).wait_recv()
+            yp_across(i).start()
+            pl.when(jnp.logical_not(is_own(i)))(lambda: yq_beside(lax.div(i, 2)).start())
+
+        def take_yp_across(i):
+            yp_across(i).wait_recv()
             b = block_of(i)
-            mine = yx_buf.at[b]
-            add_to(mine, mine, yc_buf.at[b, :, pl.ds(pl.multiple_of(x * part, part), part)])
-            pl.when(jnp.logical_not(is_own(i)))(lambda: y_beside(lax.div(i, 2)).start())
-
-        def take_y_beside(j):
-            y_beside(j).wait_recv()
-            add_to(yy_buf.at[zz_of(j)], yy_buf.at[zz_of(j)], yx_buf.at[own_block(j)])
+            add_to(
+                ypx_buf.at[b], ypx_buf.at[b],
+                yc_buf.at[b, :, pl.ds(pl.multiple_of(x * piece, piece), piece)],
+            )
+            pl.when(jnp.logical_not(is_own(i)))(lambda: yp_beside(lax.div(i, 2)).start())
+
+        def take_yq_beside(j):
+            yq_beside(j).wait_recv()
+            add_to(yqy_buf.at[j], yqy_buf.at[j], yc_buf.at[own_block(j), :, pl.ds(part, part)])
+            yq_across(j).start()
+
+        def take_y_sums(j):
+            zz = zz_of(j)
+            yq_across(j).wait_recv()
+            add_to(
+                yz_sum.at[1, zz], yqx_buf.at[j], yqy_buf.at[j, :, pl.ds(pl.multiple_of(x * piece, piece), piece)]
+            )
+            yp_beside(j).wait_recv()
+            add_to(yz_sum.at[0, zz], ypy_buf.at[j], ypx_buf.at[own_block(j)])
+
+        def y_take(zz, s, copy, landed):
+            copy(zz, s).wait_recv()
+            add_to(yz_sum.at[s, zz], yz_sum.at[s, zz], landed.at[s, zz])
 
         def y_hop(j, k):
             zz = zz_of(j)
 
             def upward():
-                if k > 0:
-                    y_up(zz).wait_recv()
-                    add_to(yy_buf.at[zz], yy_buf.at[zz], ylo_buf.at[zz])
-                y_up(zz).start()
+                for s in range(2):
+                    if k > 0:
+                        y_take(zz, s, y_up, ylo_buf)
+                    y_up(zz, s).start()
 
             def downward():
-                if k > 0:
-                    y_down(zz).wait_recv()
-                    add_to(yy_buf.at[zz], yy_buf.at[zz], yhi_buf.at[zz])
-                y_down(zz).start()
+                for s in range(2):
+                    if k > 0:
+                        y_take(zz, s, y_down, yhi_buf)
+                    y_down(zz, s).start()
 
             pl.when((z < zz) & (z == k))(upward)
             pl.when((z > zz) & (NZ - 1 - z == k))(downward)
@@ -1431,12 +1470,13 @@
             lax.fori_loop(0, width // wide, y_columns, 0)
             y_twin(i).start()
 
-        tiles = width // piece // 4
+        tile_width = piece // 2
+        tiles = width // tile_width // 4
         d_width = width // 8
 
         def gu_copies(n):
             slot = lax.rem(n, 2)
-            at = pl.ds(pl.multiple_of(n * piece, piece), piece)
+            at = pl.ds(pl.multiple_of(n * tile_width, tile_width), tile_width)
             return [
                 pltpu.make_async_copy(
                     gu_stage.at[slot, :, pl.ds(k * hidden, hidden)],
@@ -1464,7 +1504,7 @@
             def tile(k, carry):
                 n = q * tiles + k
                 pl.when(n >= 2)(lambda: each(gu_copies(n - 2), "wait"))
-                at = pl.ds(pl.multiple_of(n * piece, piece), piece)
+                at = pl.ds(pl.multiple_of(n * tile_width, tile_width), tile_width)
                 gu_stage[lax.rem(n, 2)] = dot(h[:, at], dgu[...], (0, 0))
                 each(gu_copies(n), "start")
                 return carry
@@ -1519,11 +1559,7 @@
             at(2, lambda: events(3, 6))
             at(3, lambda: events(10, 13))
 
-            def twins():
-                take_twin(i - 1)
-                take_y_twin(i - 1)
-
-            pl.when((i >= 1) & (i <= GROUPS))(twins)
+            pl.when((i >= 1) & (i <= GROUPS))(lambda: take_twin(i - 1))
             pl.when(even & (i >= 4) & (i <= GROUPS))(lambda: take_q_beside(j_even))
             at(3, lambda: take_q_beside(0))
             at(4, lambda: take_q_across(0))
@@ -1556,11 +1592,14 @@
             pl.when(odd & (i >= 5) & (i <= GROUPS + 1))(join)
             pl.when((i == GROUPS) | (i == GROUPS + 2))(lambda: hop(j_even - 1, 1))
             at(GROUPS + 1, lambda: hop(1, 2))
-            pl.when((i >= 2) & (i <= GROUPS + 1))(lambda: take_y_across(i - 2))
-            at(5, lambda: take_y_beside(0))
+            pl.when((i >= 2) & (i <= GROUPS + 1))(lambda: take_yp_across(i - 2))
+            pl.when((i >= 1) & (i <= GROUPS))(lambda: take_y_twin(i - 1))
+            pl.when(even & (i >= 4) & (i <= GROUPS))(lambda: take_yq_beside(j_even))
+            at(3, lambda: take_yq_beside(0))
+            at(5, lambda: take_y_sums(0))
 
             def join_y():
-                take_y_beside(j_even - 1)
+                take_y_sums(j_even - 1)
                 y_hop(j_even - 1, 0)
 
             pl.when(even & (i >= 6) & (i <= GROUPS + 2))(join_y)
@@ -1595,50 +1634,39 @@
             lax.fori_loop(0, rows // 64, keep, 0)
             remote(own, own, end_s.at[0, s], end_r.at[0, s], across).start()
             remote(own, own, end_s.at[1, s], end_r.at[1, s], twin).start()
-        def y_columns_of(xx, cc):
-            return pl.ds(pl.multiple_of(cc * half + xx * part, part), part)
-
-        def y_below():
-            y_up(mine).wait_recv()
-            add_to(yy_buf.at[mine], yy_buf.at[mine], ylo_buf.at[mine])
-
-        def y_above():
-            y_down(mine).wait_recv()
-            add_to(yy_buf.at[mine], yy_buf.at[mine], yhi_buf.at[mine])
-
-        pl.when(z > 0)(y_below)
-        pl.when(z < NZ - 1)(y_above)
-        x1_copy.wait()
-        y_own = block_out.at[:, y_columns_of(x, c)]
-
-        def finish(k, carry):
-            r = pl.ds(pl.multiple_of(k * 64, 64), 64)
-            y_own[r, :] = (x1[r, :] + yy_buf[mine, r, :].astype(jnp.float32)).astype(low)
-            return carry
-
-        lax.fori_loop(0, rows // 64, finish, 0)
-        remote(y_own, y_own, end_s.at[0, 2], end_r.at[0, 2], across).start()
-        remote(y_own, y_own, end_s.at[1, 2], end_r.at[1, 2], twin).start()
+        for copy in x1_copies:
+            copy.wait()
+        for s in range(2):
+            pl.when(z > 0)(lambda s=s: y_take(z, s, y_up, ylo_buf))
+            pl.when(z < NZ - 1)(lambda s=s: y_take(z, s, y_down, yhi_buf))
+            y_own = block_out.at[:, columns_of(s, x, c)]
+
+            def finish(k, carry, s=s, y_own=y_own):
+                r = pl.ds(pl.multiple_of(k * 64, 64), 64)
+                y_own[r, :] = (
+                    x1[r, pl.ds(s * piece, piece)] + yz_sum[s, z, r, :].astype(jnp.float32)
+                ).astype(low)
+                return carry
+
+            lax.fori_loop(0, rows // 64, finish, 0)
+            remote(y_own, y_own, end_s.at[0, 2 + s], end_r.at[0, 2 + s], across).start()
+            remote(y_own, y_own, end_s.at[1, 2 + s], end_r.at[1, 2 + s], twin).start()
         for s in range(2):
             there = dh_out.at[:, columns_of(s, 1 - x, c)]
             remote(there, there, end_s.at[0, s], end_r.at[0, s], across).wait_recv()
             remote(there, there, end_s.at[2, s], end_r.at[2, s], twin).start()
-        there = block_out.at[:, y_columns_of(1 - x, c)]
-        remote(there, there, end_s.at[0, 2], end_r.at[0, 2], across).wait_recv()
-        remote(there, there, end_s.at[2, 2], end_r.at[2, 2], twin).start()
-        for k, xx in ((1, x), (2, 1 - x)):
-            there = block_out.at[:, y_columns_of(xx, 1 - c)]
-            remote(there, there, end_s.at[k, 2], end_r.at[k, 2], twin).wait_recv()
-        for k, target in ((0, across), (1, twin), (2, twin)):
-            there = block_out.at[:, y_columns_of(1 - x if k == 2 else x, c)]
-            remote(there, there, end_s.at[k, 2], end_r.at[k, 2], target).wait_send()
         for s in range(2):
-            for k, xx in ((1, x), (2, 1 - x)):
-                there = dh_out.at[:, columns_of(s, xx, 1 - c)]
-                remote(there, there, end_s.at[k, s], end_r.at[k, s], twin).wait_recv()
-            for k, target in ((0, across), (1, twin), (2, twin)):
-                there = dh_out.at[:, columns_of(s, 1 - x if k == 2 else x, c)]
-                remote(there, there, end_s.at[k, s], end_r.at[k, s], target).wait_send()
+            there = block_out.at[:, columns_of(s, 1 - x, c)]
+            remote(there, there, end_s.at[0, 2 + s], end_r.at[0, 2 + s], across).wait_recv()
+            remote(there, there, end_s.at[2, 2 + s], end_r.at[2, 2 + s], twin).start()
+        for n, result in ((0, dh_out), (2, block_out)):
+            for s in range(2):
+                for k, xx in ((1, x), (2, 1 - x)):
+                    there = result.at[:, columns_of(s, xx, 1 - c)]
+                    remote(there, there, end_s.at[k, n + s], end_r.at[k, n + s], twin).wait_recv()
+                for k, target in ((0, across), (1, twin), (2, twin)):
+                    there = result.at[:, columns_of(s, 1 - x if k == 2 else x, c)]
+                    remote(there, there, end_s.at[k, n + s], end_r.at[k, n + s], target).wait_send()
         for k in range(1, GROUPS):
             there = gates_out.at[lax.rem(e + GROUPS - k, GROUPS)]
             remote(there, there, far_s.at[k - 1], far_r.at[k - 1], peers[k - 1]).wait_recv()
@@ -1649,7 +1677,7 @@
             pl.when(i >= GROUPS - 2)(lambda: to_twin(i).wait_send())
             pl.when(i >= GROUPS - 2)(lambda: y_twin(i).wait_send())
             p_across(i).wait_send()
-            y_across(i).wait_send()
+            yp_across(i).wait_send()
             return carry
 
         lax.fori_loop(0, GROUPS, drain, 0)
@@ -1658,12 +1686,14 @@
             p_beside(j).wait_send()
             q_beside(j).wait_send()
             q_across(j).wait_send()
-            y_beside(j).wait_send()
-            pl.when(z < j)(lambda: y_up(j).wait_send())
-            pl.when(z > j)(lambda: y_down(j).wait_send())
+            yp_beside(j).wait_send()
+            yq_beside(j).wait_send()
+            yq_across(j).wait_send()
             for s in range(2):
                 pl.when(z < j)(lambda s=s: up(j, s).wait_send())
                 pl.when(z > j)(lambda s=s: down_z(j, s).wait_send())
+                pl.when(z < j)(lambda s=s: y_up(j, s).wait_send())
+                pl.when(z > j)(lambda s=s: y_down(j, s).wait_send())
             return carry
 
         lax.fori_loop(0, NZ, drain_pair, 0)
@@ -1704,12 +1734,15 @@
             pltpu.VMEM((2, rows, width), low),
             pltpu.VMEM((2, rows, width), low),
             pltpu.VMEM((GROUPS, rows, half), low),
-            pltpu.VMEM((GROUPS, rows, part), low),
+            pltpu.VMEM((GROUPS, rows, piece), low),
+            pltpu.VMEM((NZ, rows, piece), low),
             pltpu.VMEM((NZ, rows, part), low),
-            pltpu.VMEM((NZ, rows, part), low),
-            pltpu.VMEM((NZ, rows, part), low),
+            pltpu.VMEM((NZ, rows, piece), low),
+            pltpu.VMEM((2, NZ, rows, piece), low),
+            pltpu.VMEM((2, NZ, rows, piece), low),
+            pltpu.VMEM((2, NZ, rows, piece), low),
             pltpu.VMEM((rows, part), f32),
-            pltpu.VMEM((2, piece, 2 * units), f32),
+            pltpu.VMEM((2, piece // 2, 2 * units), f32),
             pltpu.VMEM((2, units, width // 8), f32),
             pltpu.VMEM((GROUPS, rows, half), low),
             pltpu.VMEM((GROUPS, rows, piece), low),
@@ -1722,13 +1755,14 @@
             pltpu.VMEM((GROUPS, 8, rows), f32),
             pltpu.VMEM((tensors, GROUPS, 8, rows), f32),
             dma((GROUPS,)), dma, dma((2, 14, 3)), dma((2, 14)), dma((GROUPS,)), dma((GROUPS,)),
-            dma((GROUPS, 3)), dma((GROUPS, 3)), dma, dma((GROUPS,)), dma((GROUPS,)), dma((GROUPS,)), dma((GROUPS,)),
-            dma((NZ,)), dma((NZ,)), dma((2, NZ)), dma((2, NZ)), dma((2, 2 * local)), dma((2, local)),
+            dma((GROUPS, 3)), dma((GROUPS, 3)), dma((2,)), dma((GROUPS,)), dma((GROUPS,)), dma((GROUPS,)), dma((GROUPS,)),
+            dma((NZ,)), dma((NZ,)), dma((NZ,)), dma((NZ,)), dma((NZ,)), dma((NZ,)),
+            dma((2, 2, NZ)), dma((2, 2, NZ)), dma((2, 2 * local)), dma((2, local)),
             dma((GROUPS,)), dma((GROUPS,)), dma((GROUPS,)), dma((GROUPS,)),
             dma((NZ,)), dma((NZ,)), dma((NZ,)), dma((NZ,)), dma((NZ,)), dma((NZ,)),
             dma((2, 2, NZ)), dma((2, 2, NZ)),
             dma((tensors - 1,)), dma((tensors - 1,)), dma((GROUPS - 1,)), dma((GROUPS - 1,)),
-            dma((3, 3)), dma((3, 3)),
+            dma((3, 4)), dma((3, 4)),
         ],
         compiler_params=comm_params(collective_id, 62),
         cost_estimate=cost(80),
@@ -2278,7 +2312,7 @@
             total = out_acc.at[zz, yy]
             add_to(total, total, (out_lo if way == 0 else out_hi).at[zz, yy])
 
-        def out_hop(k):
+        def out_hop(k, way):
             for zz in Z_ORDER:
                 for yy in range(NY):
                     def upward(zz=zz, yy=yy):
@@ -2291,9 +2325,9 @@
                             out_take(zz, yy, 1)
                         out_copy(zz, yy, 1).start()
 
-                    if k < zz:
+                    if k < zz and way == 0:
                         run_if((z < zz) & (z == k), upward)
-                    if NZ - 1 - k > zz:
+                    if NZ - 1 - k > zz and way == 1:
                         run_if((z > zz) & (NZ - 1 - z == k), downward)
 
         def out_beside():
@@ -2361,7 +2395,7 @@
         lax.fori_loop(0, rows // 32, norm_two, 0)
 
         out_start()
-        out_hop(0)
+        out_hop(0, 0)
 
         do[...] = dot(da[...], out_ref[...], (1, 1)).astype(low)
         wide = lax.broadcasted_iota(jnp.int32, (rows, 128), 1)
@@ -2480,20 +2514,21 @@
         take_three(0)
         denorm(QUERY, exchanged_rows(part_q, land_q, qs_s, qs_r, mates))
         send_beside(QUERY)
-        out_hop(1)
+        out_hop(1, 0)
         take_one(1)
         take_one(0)
         take_four(1)
         take_four(0)
+        out_hop(0, 1)
         take_two(1)
         proj[VALUE] = dkv[0, 1].astype(low)
         send_beside(VALUE)
         take_two(0)
-        out_hop(2)
+        out_hop(2, 0)
         exchange_rows(unturn(KEY, lambda at: dkv[0, 0, :, at]), part_k, land_k, ks_s, ks_r, mates)
         denorm(KEY, exchanged_rows(part_k, land_k, ks_s, ks_r, mates))
         send_beside(KEY)
-        out_home()
+        out_hop(1, 1)
         fetch.wait()
 
         def half_of(cc):
@@ -2557,8 +2592,10 @@
             return carry
 
         run_units(QUERY)
+        out_hop(2, 1)
         stages[2]()
         run_units(VALUE)
+        out_home()
         stages[3]()
         stages[4]()
         lax.fori_loop(0, rows // 32, norm_one, 0)

time: 541 us -> 517 us (0.956)
  Pallas kernels: 495 us -> 471 us
    pallas_call x1, Pallas kernels: 179 us -> 162 us  [expert_layer(): pl.pallas_call(kernel, out_shape=(shape((rows, width), low), shape((rows,...]
    pallas_call x1, Pallas kernels: 158 us -> 150 us  [attend_back(): pl.pallas_call(kernel, out_shape=(shape((rows, width), low), shape((3, de...]
where the time goes in v7:
time: 517 us; the launch traced here: 510 us
  Pallas kernels  471 us (91%)
  local copies, waits for them, and re-layouts  33 us (6%)
    pallas_call x1, Pallas kernels, expert_layer(): pl.pallas_call(kernel, out_shape=(shape((rows, width), low), shape((rows,...  162 us
    pallas_call x1, Pallas kernels, attend_back(): pl.pallas_call(kernel, out_shape=(shape((rows, width), low), shape((3, de...  150 us
    pallas_call x1, Pallas kernels, project(): pl.pallas_call(kernel, out_shape=(shape((parts, depth * GROUPS, columns),...  133 us
    pallas_call x1, Pallas kernels, attend(): pl.pallas_call(kernel, out_shape=(shape((rows, columns), low), shape((row...  25.9 us
    unnamed x45, local copies, waits for them, and re-layouts  24.7 us

profile of v7, /device:TPU:0, one launch (start us, length us, event | category | flops | bytes accessed | tf_op | source)
XLA Modules:
  0.0 509.8 jit_solution(283999052387235824)
XLA Ops:
  1.2 0.8 pad_maximum_fusion
  2.1 0.7 fusion
  2.8 0.7 reduce_precision.22
  3.6 0.7 reduce_precision.20
  4.3 0.7 reduce_precision.21
  4.9 2.5 concatenate.12.small_ref
  7.5 133.0 %project.1 = (bf16[3,2048,512]{2,1,0:T(8,128)(2,1)}, bf16[512,2048]{1,0:T(8,128)(2,1)}, bf16[2048,2048]{1,0:T(8,128)(2,1)}, bf16[256,2048]{1,0:T(8,128)(2,1)}, f...) custom-call(bf16[256,2048]{1,0:T(8,128)(2,1)} %tok_ref.5, ...), custom_call_target="tpu_custom_call" | custom-call | bytes 300000000 | tf_op jit(solution)/shard_map/project/pallas_call | solution.py:2118
  140.9 1.7 copy-done
  142.7 1.6 copy-done.3
  144.3 0.9 copy-done.6
  145.2 0.8 copy-done.8
  146.0 25.9 %attend.1 = (bf16[256,512]{1,0:T(8,128)(2,1)S(1)}, f32[256,128]{1,0:T(8,128)S(1)}, f32[256,2048]{1,0:T(8,128)S(1)}, bf16[256,2048]{1,0:T(8,128)(2,1)S(1)}, f32[256,128]{1,0:T(8,128)S(1)}) custom-call(bf16[256,512]{1,0:T(8,128)(2,1)S(1)} %copy-done.6, bf16[5,2,256,512]{3,2,1,0:T(8,128)(2,1)S(1)} %copy-done, s32[256,1]{1,0:T(8,128)S(1)} %copy.43.sq_ref, ...), custom_call_target="tpu_custom_call" | custom-call | bytes 120000000 | tf_op jit(solution)/shard_map/attend/pallas_call | solution.py:2241
  171.9 1.3 copy-done.2
  173.3 1.0 copy-done.4
  174.2 0.7 copy-done.7
  176.2 161.6 %expert_layer.1 = (bf16[256,2048]{1,0:T(8,128)(2,1)}, bf16[256,2048]{1,0:T(8,128)(2,1)}, f32[8,8,256]{2,1,0:T(8,128)}, f32[2,2048,256]{2,1,0:T(8,128)}, f32[2,20...) custom-call(bf16[256,2048]{1,0:T(8,128)(2,1)} %copy-done.4, bf16[2048,2048]{1,0:T(8,128)(2,1)} %get-tuple-element.44.dy_in, ...), custom_call_target="tpu_custom_call" | custom-call | bytes 240000000 | tf_op jit(solution)/shard_map/expert_layer/pallas_call | solution.py:1717
  337.9 0.8 slice.19
  339.0 0.7 bitcast_select_fusion.gates_ref
  339.7 150.1 %attend_back.1 = (bf16[256,2048]{1,0:T(8,128)(2,1)}, f32[3,256,512]{2,1,0:T(8,128)}, f32[512,256]{1,0:T(8,128)}, f32[24,256]{1,0:T(8,128)}) custom-call(bf16[256,2048]{1,0:T(8,128)(2,1)} %get-tuple-element.51.dh_ref, f32[256,16]{1,0:T(8,128)} %bitcast_select_fusion.gates_ref, bf16[16,2048]{1,0:T(8,128)(2,1)} %get-tuple-element.47.router_ref, ...), custom_call_target="tpu_custom_call" | custom-call | bytes 390000000 | tf_op jit(solution)/shard_map/attend_back/pallas_call | solution.py:2633
  489.8 0.8 slice.22
  490.7 0.7 constant_dynamic-slice_fusion
  491.3 1.3 slice_bitcast_fusion
  492.7 1.3 fusion.4
  494.0 1.0 copy.54
  495.0 3.0 copy.55
  498.0 1.1 copy.56
  499.1 0.8 copy.57
  499.9 2.1 copy.58
  502.0 1.6 copy-done.13
  503.6 2.1 copy.59
  505.7 1.6 copy-done.12
  507.3 2.0 copy.60
  (45 shorter events, 2.6 us)
Async XLA Ops:
  7.5 133.0 %copy-start.18 = (s32[2048]{0:T(1024)S(1)}, s32[2048]{0:T(1024)}, u32[]{:S(2)}) copy-start(s32[2048]{0:T(1024)} %param.25) | copy-start | bytes 24580
  7.5 133.4 %copy-start.1 = (bf16[256,2048]{1,0:T(8,128)(2,1)S(1)}, bf16[256,2048]{1,0:T(8,128)(2,1)}, u32[]{:S(2)}) copy-start(bf16[256,2048]{1,0:T(8,128)(2,1)} %tok_ref.5) | copy-start | bytes 3145732
  140.8 197.1 %copy-start.5 = (s32[256,1]{1,0:T(8,128)}, s32[256,1]{1,0:T(8,128)S(1)}, u32[]{:S(2)}) copy-start(s32[256,1]{1,0:T(8,128)S(1)} %copy.43.sq_ref) | copy-start | bytes 3076
  140.9 1.7 copy-start
  142.7 1.6 copy-start.3
  144.3 0.9 copy-start.6
  145.2 0.8 copy-start.8
  146.0 191.9 %copy-start.11 = (s32[5,256]{1,0:T(8,128)}, s32[5,256]{1,0:T(8,128)S(1)}, u32[]{:S(2)}) copy-start(s32[5,256]{1,0:T(8,128)S(1)} %rev.3.sk_ref) | copy-start | bytes 15364
  171.9 1.3 copy-start.2
  173.3 1.0 copy-start.4
  174.2 0.7 copy-start.7
  174.9 0.7 copy-start.9
  175.6 0.7 copy-start.10
  339.7 154.3 %copy-start.16 = (bf16[256,2048]{1,0:T(8,128)(2,1)S(1)}, bf16[256,2048]{1,0:T(8,128)(2,1)}, u32[]{:S(2)}) copy-start(bf16[256,2048]{1,0:T(8,128)(2,1)} %get-tuple-element.85) | copy-start | bytes 3145732
  489.8 8.2 %copy-start.15 = (f32[3,256,512]{2,1,0:T(8,128)S(1)}, f32[3,256,512]{2,1,0:T(8,128)}, u32[]{:S(2)}) copy-start(f32[3,256,512]{2,1,0:T(8,128)} %get-tuple-element.87) | copy-start | bytes 4718596
  489.8 9.3 %copy-start.17 = (f32[512,256]{1,0:T(8,128)S(1)}, f32[512,256]{1,0:T(8,128)}, u32[]{:S(2)}) copy-start(f32[512,256]{1,0:T(8,128)} %get-tuple-element.88) | copy-start | bytes 1572868
  494.0 5.9 %copy-start.14 = (f32[2,2048,256]{2,1,0:T(8,128)S(1)}, f32[2,2048,256]{2,1,0:T(8,128)}, u32[]{:S(2)}) copy-start(f32[2,2048,256]{2,1,0:T(8,128)} %get-tuple-element.93) | copy-start | bytes 12582916
  499.9 3.7 copy-start.13
  503.6 3.7 copy-start.12

commit v8 on v7

--- a/solution.py
+++ b/solution.py
@@ -383,7 +383,7 @@
 
 
 MESH_ID = pl.DeviceIdType.MESH
-HBM = pl.BlockSpec(memory_space=pl.ANY)
+HBM = pl.BlockSpec(memory_space=pltpu.HBM)
 VMEM = pl.BlockSpec(memory_space=pltpu.VMEM)
 NZ, NY, NX, NC = 4, 2, 2, 2
 GROUPS = NZ * NY
@@ -1119,7 +1119,7 @@
 
 
 def expert_layer(
-    hidden_two, grad_out_all, gate_up, down, router_t, chosen_all, residual, collective_id
+    hidden_two, grad_out_all, gate_up, down, router_t, chosen_all, residual, attended, collective_id
 ):
     rows, width = hidden_two.shape
     tokens = rows * GROUPS
@@ -1135,12 +1135,12 @@
     wide = width // 4
 
     def kernel(
-        own_in, dy_in, gu_ref, down_ref, router_ref, chosen_ref, x1_in,
-        block_out, dh_out, gates_out, gate_w, up_w, down_w,
+        own_in, dy_in, gu_ref, down_ref, router_ref, chosen_ref, x1_in, o_in,
+        block_out, dh_out, gates_out, gate_w, up_w, down_w, o_all,
         h, dy, gated, dgu, dx, y_part, yc_buf, ypx_buf, ypy_buf, yqy_buf, yqx_buf, yz_sum,
         ylo_buf, yhi_buf, x1, gu_stage, d_stage,
         core_buf, px_buf, py_buf, qy_buf, qx_buf, z_sum, lo_buf, hi_buf, gate_part, gate_land,
-        in_sem, own_sem, line_s, line_r, hx_s, hx_r, hc_s, hc_r, x1_sem, yc_s, yc_r, ypx_s, ypx_r, ypy_s, ypy_r,
+        in_sem, own_sem, o_sem, line_s, line_r, hx_s, hx_r, hc_s, hc_r, x1_sem, yc_s, yc_r, ypx_s, ypx_r, ypy_s, ypy_r,
         yqy_s, yqy_r, yqx_s, yqx_r, yz_s, yz_r, gu_sem, d_sem, core_s, core_r, px_s, px_r, py_s, py_r, qy_s, qy_r, qx_s, qx_r,
         z_s, z_r, near_s, near_r, far_s, far_r, end_s, end_r,
     ):
@@ -1182,8 +1182,13 @@
             return h.at[block_rows(b, rows), columns]
 
         line = LineGather(
-            [0, 1], [own_in.at[:, a_at(x, c)], own_in.at[:, c_at(c)]],
-            [lambda b: h_view(b, a_at(x, c)), lambda b: h_view(b, c_at(c))], line_s, line_r,
+            [0, 1, 2], [own_in.at[:, a_at(x, c)], own_in.at[:, c_at(c)], o_in],
+            [
+                lambda b: h_view(b, a_at(x, c)),
+                lambda b: h_view(b, c_at(c)),
+                lambda b: o_all.at[block_rows(b, rows), :],
+            ],
+            line_s, line_r,
         )
 
         def h_twin(b, stream, landing=False):
@@ -1211,6 +1216,17 @@
                 line.finish_later(late, rel)
             run_if(line.exists(rel), body)
 
+        def attended_event(rel):
+            def body():
+                marks = len(line.pending)
+                line.arrive(2, rel)
+                if rel < 7:
+                    line.start(2, rel)
+                late = line.pending[marks:]
+                del line.pending[marks:]
+                line.finish_later(late, rel)
+            run_if(line.exists(rel), body)
+
         def relay(i):
             b = block_of(i)
             h_across(b, True).wait_recv()
@@ -1220,6 +1236,8 @@
             line.start(stream, 0)
         keep = pltpu.make_async_copy(own_in, h.at[block_rows(z * NY + y, rows), :], own_sem)
         keep.start()
+        keep_o = pltpu.make_async_copy(o_in, o_all.at[block_rows(z * NY + y, rows), :], o_sem)
+        keep_o.start()
 
         def load(i):
             r = block_rows(block_of(i), rows)
@@ -1559,6 +1577,15 @@
             at(2, lambda: events(3, 6))
             at(3, lambda: events(10, 13))
 
+            def attended_events(*rels):
+                for rel in rels:
+                    attended_event(rel)
+
+            at(8, lambda: attended_events(1, 4))
+            at(9, lambda: attended_events(2, 5))
+            at(10, lambda: attended_events(3, 6))
+            at(11, lambda: attended_events(7, 8, 11))
+
             pl.when((i >= 1) & (i <= GROUPS))(lambda: take_twin(i - 1))
             pl.when(even & (i >= 4) & (i <= GROUPS))(lambda: take_q_beside(j_even))
             at(3, lambda: take_q_beside(0))
@@ -1576,6 +1603,7 @@
             pl.when(i >= GROUPS)(lambda: weight_grads(i - GROUPS))
             at(0, lambda: events(7, 1, 4))
             at(2, lambda: events(9, 12))
+            at(6, lambda: line.start(2, 0))
             pl.when(i < GROUPS - 1)(lambda: relay(i + 1))
 
             def pass_p():
@@ -1608,6 +1636,9 @@
             return carry
 
         lax.fori_loop(0, steps, step, 0)
+
+        for rel in (9, 12, 10, 13):
+            attended_event(rel)
 
         def columns_of(s, xx, cc):
             return pl.ds(pl.multiple_of(cc * half + s * part + xx * piece, piece), piece)
@@ -1707,6 +1738,7 @@
 
         lax.fori_loop(1, GROUPS, drain_rows_of, 0)
         line.finish()
+        keep_o.wait()
         for k in range(2):
             each(gu_copies(4 * tiles - 2 + k), "wait")
             each(d_copies(6 + k), "wait")
@@ -1723,9 +1755,10 @@
             shape((local, width, hidden), f32),
             shape((local, width, hidden), f32),
             shape((local, hidden, width), f32),
+            shape((tokens,) + attended.shape[1:], low),
         ),
-        in_specs=[HBM, HBM, VMEM, VMEM, VMEM, VMEM, HBM],
-        out_specs=(VMEM, VMEM, VMEM, HBM, HBM, HBM),
+        in_specs=[HBM, HBM, VMEM, VMEM, VMEM, VMEM, HBM, HBM],
+        out_specs=(VMEM, VMEM, VMEM, HBM, HBM, HBM, HBM),
         scratch_shapes=[
             pltpu.VMEM((tokens, width), low),
             pltpu.VMEM((tokens, width), low),
@@ -1754,7 +1787,7 @@
             pltpu.VMEM((2, NZ, rows, piece), low),
             pltpu.VMEM((GROUPS, 8, rows), f32),
             pltpu.VMEM((tensors, GROUPS, 8, rows), f32),
-            dma((GROUPS,)), dma, dma((2, 14, 3)), dma((2, 14)), dma((GROUPS,)), dma((GROUPS,)),
+            dma((GROUPS,)), dma, dma, dma((3, 14, 3)), dma((3, 14)), dma((GROUPS,)), dma((GROUPS,)),
             dma((GROUPS, 3)), dma((GROUPS, 3)), dma((2,)), dma((GROUPS,)), dma((GROUPS,)), dma((GROUPS,)), dma((GROUPS,)),
             dma((NZ,)), dma((NZ,)), dma((NZ,)), dma((NZ,)), dma((NZ,)), dma((NZ,)),
             dma((2, 2, NZ)), dma((2, 2, NZ)), dma((2, 2 * local)), dma((2, local)),
@@ -1767,7 +1800,7 @@
         compiler_params=comm_params(collective_id, 62),
         cost_estimate=cost(80),
         name="expert_layer",
-    )(hidden_two, grad_out_all, gate_up, down, router_t, chosen_all, residual)
+    )(hidden_two, grad_out_all, gate_up, down, router_t, chosen_all, residual, attended)
 
 
 def exchange_rows(value, part_ref, land_ref, send_sem, recv_sem, mates):
@@ -2155,7 +2188,7 @@
             dma((2, back + 1)), dma((2, back + 1)),
             dma((GROUPS,)), dma((GROUPS,)), dma((GROUPS, 2)), dma((GROUPS, 2)), dma((4,)),
         ],
-        compiler_params=comm_params(collective_id, 56),
+        compiler_params=comm_params(collective_id, 62),
         cost_estimate=cost(100),
         name="project",
     )(tokens, w_qkv, w_out, out_grad, smalls, cosine, sine, w_gate, w_up, w_down)
@@ -2170,12 +2203,16 @@
     low, f32 = jnp.bfloat16, jnp.float32
 
     def kernel(
-        q_ref, context_ref, sq_ref, sk_ref, tok_ref, out_ref, gain_ref,
-        o_ref, lse_ref, x1_ref, h2_ref, scale_ref,
-        part, full, core_buf, x_buf, send_sem, recv_sem,
+        q_ref, context_in, sq_ref, sk_ref, tok_ref, out_in, gain_ref,
+        o_ref, lse_ref, x1_out, h2_out, scale_ref,
+        context_ref, out_ref, x1_ref, h2_ref, copy_sem, part, full, core_buf, x_buf, send_sem, recv_sem,
     ):
         z, y, x, c = place()
         across, twin = device(z, y, 1 - x, c), device(z, y, x, 1 - c)
+        context_load = pltpu.make_async_copy(context_in, context_ref, copy_sem.at[0])
+        context_load.start()
+        out_load = pltpu.make_async_copy(out_in, out_ref, copy_sem.at[1])
+        out_load.start()
         greet([(across, None), (twin, None)])
         row = lax.broadcasted_iota(jnp.int32, (rows, rows), 0)
         column = lax.broadcasted_iota(jnp.int32, (rows, rows), 1)
@@ -2187,6 +2224,7 @@
             )
         line = lax.broadcasted_iota(jnp.int32, (rows, 128), 1)
         lse = jnp.zeros((rows, 128), f32)
+        context_load.wait()
         for head in range(heads):
             at = pl.ds(head * HEAD, HEAD)
             scores = [
@@ -2223,6 +2261,7 @@
 
             lax.fori_loop(0, 2, body, 0)
 
+        out_load.wait()
         fill(1 - c)
         group_sum(part, full, core_buf, x_buf, send_sem, recv_sem, lambda: fill(c))
 
@@ -2236,6 +2275,14 @@
             return carry
 
         lax.fori_loop(0, rows // 32, norm, 0)
+        keep = [
+            pltpu.make_async_copy(x1_ref, x1_out, copy_sem.at[2]),
+            pltpu.make_async_copy(h2_ref, h2_out, copy_sem.at[3]),
+        ]
+        for copy in keep:
+            copy.start()
+        for copy in keep:
+            copy.wait()
 
     shape, dma = jax.ShapeDtypeStruct, pltpu.SemaphoreType.DMA
     return pl.pallas_call(
@@ -2247,16 +2294,21 @@
             shape((rows, width), low),
             shape((rows, 128), f32),
         ),
-        in_specs=[VMEM] * 7,
-        out_specs=(VMEM,) * 5,
+        in_specs=[VMEM, HBM, VMEM, VMEM, VMEM, HBM, VMEM],
+        out_specs=(VMEM, VMEM, HBM, HBM, VMEM),
         scratch_shapes=[
+            pltpu.VMEM(context.shape, low),
+            pltpu.VMEM(out_low.shape, low),
+            pltpu.VMEM((rows, width), f32),
+            pltpu.VMEM((rows, width), low),
+            dma((4,)),
             pltpu.VMEM((rows, width), low),
             pltpu.VMEM((rows, width), low),
             pltpu.VMEM((rows, half), low),
             pltpu.VMEM((rows, quarter), low),
             dma((5,)), dma((5,)),
         ],
-        compiler_params=comm_params(collective_id, 40),
+        compiler_params=comm_params(collective_id, 62),
         cost_estimate=cost(40),
         name="attend",
     )(query, context, segment_query, segment_keys, tokens, out_low, gain)
@@ -2265,7 +2317,7 @@
 def attend_back(
     grad_hidden, grad_probs, router_t, hidden_two, residual, scale_two, gains, out_grad,
     query, context, segment_query, segment_keys, attended, log_sums, raw, scales,
-    cosine, sine, hidden_one, tokens, qkv_low, out_low, collective_id,
+    cosine, sine, hidden_one, tokens, attended_all, qkv_low, out_low, collective_id,
 ):
     rows, width = tokens.shape
     columns = query.shape[1]
@@ -2282,12 +2334,12 @@
     def kernel(
         dh_ref, gates_ref, router_ref, h2_ref, x1_ref, s2_ref, gain_ref, dy_ref,
         q_ref, context_ref, sq_ref, sk_ref, o_ref, lse_ref, raw_ref, scale_ref,
-        cos_ref, sin_ref, h1_ref, tok_ref, w_hbm, out_ref,
+        cos_ref, sin_ref, h1_ref, tok_ref, o_all, w_hbm, out_ref,
         tok_grad, qkv_sum, out_sum, small_sum,
         weights, dx1, da, do, dot_sums, dq, dkv, scaled, proj, send_kv, land_y, land_z,
         part, full, core_buf, x_buf, small, line_sum,
-        main_buf, out_acc, out_lo, out_hi, out_land, small_buf, part_k, land_k, part_q, land_q,
-        w_sem, y_s, y_r, z_s, z_r, group_s, group_r, ks_s, ks_r, qs_s, qs_r, line_s, line_r, out_s, out_r, out_y_s, out_y_r,
+        main_buf, da_all, small_buf, part_k, land_k, part_q, land_q,
+        w_sem, y_s, y_r, z_s, z_r, group_s, group_r, ks_s, ks_r, qs_s, qs_r, line_s, line_r, far_s, far_r, near_s, near_r,
     ):
         z, y, x, c = place()
         e, t = lax.axis_index("expert"), lax.axis_index("tensor")
@@ -2302,57 +2354,49 @@
             at = pl.ds(pl.multiple_of(b * depth, depth), depth)
             return dot(h1_ref[:, at], proj[s], (0, 0))
 
-        def out_copy(zz, yy, way):
-            landing = (out_lo if way == 0 else out_hi).at[zz, yy]
-            target = device(z + 1, y, x, c) if way == 0 else below
-            return remote(out_acc.at[zz, yy], landing, out_s.at[zz, yy, way], out_r.at[zz, yy, way], target)
-
-        def out_take(zz, yy, way):
-            out_copy(zz, yy, way).wait_recv()
-            total = out_acc.at[zz, yy]
-            add_to(total, total, (out_lo if way == 0 else out_hi).at[zz, yy])
-
-        def out_hop(k, way):
-            for zz in Z_ORDER:
-                for yy in range(NY):
-                    def upward(zz=zz, yy=yy):
-                        if k > 0:
-                            out_take(zz, yy, 0)
-                        out_copy(zz, yy, 0).start()
-
-                    def downward(zz=zz, yy=yy):
-                        if k > 0:
-                            out_take(zz, yy, 1)
-                        out_copy(zz, yy, 1).start()
-
-                    if k < zz and way == 0:
-                        run_if((z < zz) & (z == k), upward)
-                    if NZ - 1 - k > zz and way == 1:
-                        run_if((z > zz) & (NZ - 1 - z == k), downward)
-
-        def out_beside():
-            return remote(out_acc.at[z, 1 - y], out_land, out_y_s, out_y_r, beside)
-
-        def out_start():
-            for zz in range(NZ):
-                for yy in range(NY):
-                    at = pl.ds((zz * NY + yy) * depth, depth)
-                    out_acc[zz, yy] = dot(o_ref[...], da[:, at], (0, 0)).astype(low)
-
-        def out_home():
-            for yy in range(NY):
-                run_if(z > 0, lambda yy=yy: out_take(z, yy, 0))
-                run_if(z < NZ - 1, lambda yy=yy: out_take(z, yy, 1))
-            out_beside().start()
-
-        def out_end():
-            out_beside().wait_recv()
-            out_sum[...] = out_acc[z, y].astype(f32) + out_land[...].astype(f32)
-            out_beside().wait_send()
-            for zz in range(NZ):
-                for yy in range(NY):
-                    run_if(z < zz, lambda zz=zz, yy=yy: out_copy(zz, yy, 0).wait_send())
-                    run_if(z > zz, lambda zz=zz, yy=yy: out_copy(zz, yy, 1).wait_send())
+        peers = [(lax.rem(e + k, GROUPS), t) for k in range(1, GROUPS)]
+        share = rows // tensors
+        share_at = pl.ds(pl.multiple_of(t * share, share), share)
+
+        def columns_of(owner):
+            return pl.ds(pl.multiple_of(owner * depth, depth), depth)
+
+        def da_far(k):
+            owner = lax.rem(e + k, GROUPS)
+            return remote(
+                da.at[share_at, columns_of(owner)], da_all.at[e, share_at, :], far_s.at[k - 1], far_r.at[k - 1],
+                peers[k - 1],
+            )
+
+        def da_near(k):
+            piece = da_all.at[:, share_at, :]
+            return remote(piece, piece, near_s.at[k], near_r.at[k], mates[k])
+
+        def da_start():
+            for k in range(1, GROUPS):
+                da_far(k).start()
+            da_all[e, share_at, :] = da[share_at, columns_of(e)]
+
+        def da_spread():
+            for k in range(1, GROUPS):
+                landing = da_all.at[lax.rem(e + GROUPS - k, GROUPS), share_at, :]
+                remote(landing, landing, far_s.at[k - 1], far_r.at[k - 1], peers[k - 1]).wait_recv()
+            for k in range(tensors - 1):
+                da_near(k).start()
+
+        def da_end():
+            for k in range(tensors - 1):
+                theirs = lax.rem(t + tensors - 1 - k, tensors)
+                landing = da_all.at[:, pl.ds(pl.multiple_of(theirs * share, share), share), :]
+                remote(landing, landing, near_s.at[k], near_r.at[k], mates[k]).wait_recv()
+            result = jnp.zeros((columns, depth), f32)
+            for b in range(GROUPS):
+                result = result + dot(o_all[pl.ds(b * rows, rows), :], da_all[b], (0, 0))
+            out_sum[...] = result
+            for k in range(1, GROUPS):
+                da_far(k).wait_send()
+            for k in range(tensors - 1):
+                da_near(k).wait_send()
 
         def slot(kind):
             def view(s, zz):
@@ -2362,7 +2406,7 @@
             return view
 
         line = LineReduce([], lambda s, zz, yy: slot(3)(s, zz), slot(0), slot(1), slot(2), line_s, line_r)
-        greet(line.partners() + [(mate, None) for mate in mates])
+        greet([(target, None) for target in mates + peers])
 
         grad_probs = gates_ref[...]
         logits = dot(h2_ref[...], router_ref[...], (1, 1))
@@ -2394,8 +2438,7 @@
 
         lax.fori_loop(0, rows // 32, norm_two, 0)
 
-        out_start()
-        out_hop(0, 0)
+        da_start()
 
         do[...] = dot(da[...], out_ref[...], (1, 1)).astype(low)
         wide = lax.broadcasted_iota(jnp.int32, (rows, 128), 1)
@@ -2514,21 +2557,18 @@
         take_three(0)
         denorm(QUERY, exchanged_rows(part_q, land_q, qs_s, qs_r, mates))
         send_beside(QUERY)
-        out_hop(1, 0)
+        da_spread()
         take_one(1)
         take_one(0)
         take_four(1)
         take_four(0)
-        out_hop(0, 1)
         take_two(1)
         proj[VALUE] = dkv[0, 1].astype(low)
         send_beside(VALUE)
         take_two(0)
-        out_hop(2, 0)
         exchange_rows(unturn(KEY, lambda at: dkv[0, 0, :, at]), part_k, land_k, ks_s, ks_r, mates)
         denorm(KEY, exchanged_rows(part_k, land_k, ks_s, ks_r, mates))
         send_beside(KEY)
-        out_hop(1, 1)
         fetch.wait()
 
         def half_of(cc):
@@ -2592,10 +2632,9 @@
             return carry
 
         run_units(QUERY)
-        out_hop(2, 1)
         stages[2]()
         run_units(VALUE)
-        out_home()
+        da_end()
         stages[3]()
         stages[4]()
         lax.fori_loop(0, rows // 32, norm_one, 0)
@@ -2611,7 +2650,6 @@
         send_beside(SMALL)
         run_units(KEY)
         run_units(SMALL)
-        out_end()
         hop(*units[-1], 1)
         hop(*units[-2], 2)
         hop(*units[-1], 2)
@@ -2638,7 +2676,7 @@
             shape((columns, depth), f32),
             shape((small_rows, depth), f32),
         ),
-        in_specs=[VMEM] * 20 + [HBM, VMEM],
+        in_specs=[VMEM] * 21 + [HBM, VMEM],
         out_specs=(VMEM,) * 4,
         scratch_shapes=[
             vmem(qkv_low.shape, low),
@@ -2660,10 +2698,7 @@
             vmem((GROUPS, small_rows, depth), f32),
             vmem((8, width), f32),
             vmem((4, NZ, 3, depth, columns), low),
-            vmem((NZ, NY, columns, depth), low),
-            vmem((NZ, NY, columns, depth), low),
-            vmem((NZ, NY, columns, depth), low),
-            vmem((columns, depth), low),
+            vmem((GROUPS, rows, depth), low),
             vmem((4, NZ, small_rows, depth), f32),
             vmem((8, rows), f32),
             vmem((tensors - 1, 8, rows), f32),
@@ -2671,7 +2706,7 @@
             vmem((tensors - 1, 8, rows), f32),
             dma, dma((2, 2)), dma((2, 2)), dma((2, 2)), dma((2, 2)), dma((5,)), dma((5,)),
             dma((tensors - 1,)), dma((tensors - 1,)), dma((tensors - 1,)), dma((tensors - 1,)),
-            dma((5, NZ, 3)), dma((5, NZ, 3)), dma((NZ, NY, 2)), dma((NZ, NY, 2)), dma, dma,
+            dma((5, NZ, 3)), dma((5, NZ, 3)), dma((GROUPS - 1,)), dma((GROUPS - 1,)), dma((tensors - 1,)), dma((tensors - 1,)),
         ],
         compiler_params=comm_params(collective_id, 62),
         cost_estimate=cost(130),
@@ -2679,7 +2714,7 @@
     )(
         grad_hidden, grad_probs, router_t, hidden_two, residual, scale_two, gains, out_grad,
         query, context, segment_query, segment_keys, attended, log_sums, raw, scales,
-        cosine, sine, hidden_one, tokens, qkv_low, out_low,
+        cosine, sine, hidden_one, tokens, attended_all, qkv_low, out_low,
     )
 
 
@@ -2751,14 +2786,17 @@
         query_low, context_blocks, segment_query[:, None], segment_keys, tokens_in, out_low,
         gains, 2,
     )
-    block_out, grad_hidden_sum, grad_gate_sum, grad_gate_w, grad_up_w, grad_down = expert_layer(
-        hidden_two, grad_out_all, gate_up, down_low, router_t, chosen_all, residual, 5
+    (
+        block_out, grad_hidden_sum, grad_gate_sum, grad_gate_w, grad_up_w, grad_down, attended_all
+    ) = expert_layer(
+        hidden_two, grad_out_all, gate_up, down_low, router_t, chosen_all, residual, attended, 5
     )
     grad_probs = grad_gate_sum[:, :local_experts].reshape(experts, row_count).T * chosen
     grad_tokens, qkv_sum, out_sum, small_sum = attend_back(
         grad_hidden_sum, grad_probs, router_t, hidden_two, residual, scale_two_wide,
         gains, out_grad, query_low, context_blocks, segment_query[:, None], segment_keys,
-        attended, log_sums, raw, scales, wide_cosine, wide_sine, hidden_one, tokens_in, qkv_low, out_low, 8,
+        attended, log_sums, raw, scales, wide_cosine, wide_sine, hidden_one, tokens_in, attended_all,
+        qkv_low, out_low, 8,
     )
     return (
         block_out,

time: 517 us -> 505 us (0.977)
  local copies, waits for them, and re-layouts: 33 us -> 24.8 us
    pallas_call x1, Pallas kernels: 150 us -> 131 us  [attend_back(): pl.pallas_call(kernel, out_shape=(shape((rows, width), low), shape((3, de...]
    pallas_call x1, Pallas kernels: 162 us -> 174 us  [expert_layer(): pl.pallas_call(kernel, out_shape=(shape((rows, width), low), shape((rows,...]
    unnamed x45 -> x21, local copies, waits for them, and re-layouts: 24.7 us -> 15.3 us
where the time goes in v8:
time: 505 us; the launch traced here: 498 us
  Pallas kernels  468 us (93%)
  local copies, waits for them, and re-layouts  24.8 us (5%)
    pallas_call x1, Pallas kernels, expert_layer(): pl.pallas_call(kernel, out_shape=(shape((rows, width), low), shape((rows,...  174 us
    pallas_call x1, Pallas kernels, project(): pl.pallas_call(kernel, out_shape=(shape((parts, depth * GROUPS, columns),...  133 us
    pallas_call x1, Pallas kernels, attend_back(): pl.pallas_call(kernel, out_shape=(shape((rows, width), low), shape((3, de...  131 us
    pallas_call x1, Pallas kernels, attend(): pl.pallas_call(kernel, out_shape=(shape((rows, columns), low), shape((row...  29.8 us
    unnamed x21, local copies, waits for them, and re-layouts  15.3 us

profile of v8, /device:TPU:0, one launch (start us, length us, event | category | flops | bytes accessed | tf_op | source)
XLA Modules:
  0.0 498.5 jit_solution(9858126032795557102)
XLA Ops:
  0.7 0.5 fusion.1
  1.2 0.8 pad_maximum_fusion
  2.1 0.7 fusion
  2.8 0.7 reduce_precision.22
  3.5 0.1 reduce_precision.23
  3.6 0.7 reduce_precision.20
  4.3 0.7 reduce_precision.21
  4.9 2.5 concatenate.12.small_ref
  7.5 133.0 %project.1 = (bf16[3,2048,512]{2,1,0:T(8,128)(2,1)}, bf16[512,2048]{1,0:T(8,128)(2,1)}, bf16[2048,2048]{1,0:T(8,128)(2,1)}, bf16[256,2048]{1,0:T(8,128)(2,1)}, f...) custom-call(bf16[256,2048]{1,0:T(8,128)(2,1)} %tok_ref.5, ...), custom_call_target="tpu_custom_call" | custom-call | bytes 300000000 | tf_op jit(solution)/shard_map/project/pallas_call | solution.py:2151
  140.5 0.1 pad_dynamic-slice_fusion
  140.6 0.8 copy.43.sq_ref
  141.5 0.6 rev.3.sk_ref
  142.1 29.8 %attend.1 = (bf16[256,512]{1,0:T(8,128)(2,1)}, f32[256,128]{1,0:T(8,128)}, f32[256,2048]{1,0:T(8,128)}, bf16[256,2048]{1,0:T(8,128)(2,1)}, f32[256,128]{1,0:T(8,128)}) custom-call(bf16[256,512]{1,0:T(8,128)(2,1)} %get-tuple-element.40.q_ref, bf16[5,2,256,512]{3,2,1,0:T(8,128)(2,1)} %get-tuple-element.41.context_in.context_ref, s32[256,1]{1,0:T(8,128)} %copy.43.sq_ref, ...), custom_call_target="tpu_custom_call" | custom-call | bytes 120000000 | tf_op jit(solution)/shard_map/attend/pallas_call | solution.py:2288
  171.9 174.1 %expert_layer.1 = (bf16[256,2048]{1,0:T(8,128)(2,1)}, bf16[256,2048]{1,0:T(8,128)(2,1)}, f32[8,8,256]{2,1,0:T(8,128)}, f32[2,2048,256]{2,1,0:T(8,128)}, f32[2,20...) custom-call(bf16[256,2048]{1,0:T(8,128)(2,1)} %get-tuple-element.44.own_in.h2_ref, ...), custom_call_target="tpu_custom_call" | custom-call | bytes 240000000 | tf_op jit(solution)/shard_map/expert_layer/pallas_call | solution.py:1749
  346.0 0.8 slice.19
  346.9 0.1 copy.44
  347.0 0.1 copy.45
  347.1 0.7 bitcast_select_fusion.gates_ref
  347.8 130.7 %attend_back.1 = (bf16[256,2048]{1,0:T(8,128)(2,1)}, f32[3,256,512]{2,1,0:T(8,128)}, f32[512,256]{1,0:T(8,128)}, f32[24,256]{1,0:T(8,128)}) custom-call(bf16[256,2048]{1,0:T(8,128)(2,1)} %get-tuple-element.53.dh_ref, f32[256,16]{1,0:T(8,128)} %bitcast_select_fusion.gates_ref, bf16[16,2048]{1,0:T(8,128)(2,1)} %get-tuple-element.48.router_ref, ...), custom_call_target="tpu_custom_call" | custom-call | bytes 390000000 | tf_op jit(solution)/shard_map/attend_back/pallas_call | solution.py:2671
  478.5 0.8 slice.22
  479.4 0.7 constant_dynamic-slice_fusion
  480.1 1.3 slice_bitcast_fusion
  481.4 1.3 fusion.4
  482.7 1.0 copy.54
  483.7 3.0 copy.55
  486.7 1.1 copy.56
  487.8 0.8 copy.57
  488.6 2.1 copy.58
  490.8 1.6 copy-done.1
  492.3 2.1 copy.59
  494.5 1.6 copy-done
  496.0 2.0 copy.60
  (21 shorter events, 0.2 us)
Async XLA Ops:
  7.5 133.0 %copy-start.6 = (s32[2048]{0:T(1024)S(1)}, s32[2048]{0:T(1024)}, u32[]{:S(2)}) copy-start(s32[2048]{0:T(1024)} %param.25) | copy-start | bytes 24580
  347.8 134.9 %copy-start.4 = (bf16[256,2048]{1,0:T(8,128)(2,1)S(1)}, bf16[256,2048]{1,0:T(8,128)(2,1)}, u32[]{:S(2)}) copy-start(bf16[256,2048]{1,0:T(8,128)(2,1)} %get-tuple-element.87) | copy-start | bytes 3145732
  478.5 8.2 %copy-start.3 = (f32[3,256,512]{2,1,0:T(8,128)S(1)}, f32[3,256,512]{2,1,0:T(8,128)}, u32[]{:S(2)}) copy-start(f32[3,256,512]{2,1,0:T(8,128)} %get-tuple-element.89) | copy-start | bytes 4718596
  478.5 9.3 %copy-start.5 = (f32[512,256]{1,0:T(8,128)S(1)}, f32[512,256]{1,0:T(8,128)}, u32[]{:S(2)}) copy-start(f32[512,256]{1,0:T(8,128)} %get-tuple-element.90) | copy-start | bytes 1572868
  482.7 5.9 %copy-start.2 = (f32[2,2048,256]{2,1,0:T(8,128)S(1)}, f32[2,2048,256]{2,1,0:T(8,128)}, u32[]{:S(2)}) copy-start(f32[2,2048,256]{2,1,0:T(8,128)} %get-tuple-element.95) | copy-start | bytes 12582916
  488.6 3.7 copy-start.1
  492.3 3.7 copy-start

commit v9 on v8

--- a/solution.py
+++ b/solution.py
@@ -1832,7 +1832,8 @@
 
 
 def project(
-    tokens, w_qkv, w_out, out_grad, smalls, cosine, sine, w_gate, w_up, w_down, experts, collective_id
+    tokens, w_qkv, w_out, out_grad, gain_one, gain_two, qk_gain, w_router, routes, cosine, sine,
+    w_gate, w_up, w_down, collective_id,
 ):
     rows, width = tokens.shape
     parts, depth, columns = w_qkv.shape
@@ -1844,11 +1845,13 @@
     out_half = w_out.shape[0] // 2
     out_rows, out_columns = w_out.shape
     quarter = width // tensors
+    experts = w_router.shape[0]
+    small_shape = (8 + 2 * experts, depth)
 
     def kernel(
-        tok_ref, w_ref, out_ref, grad_in, small_ref, cos_ref, sin_ref, gate_in, up_in, down_in,
+        tok_ref, w_ref, out_ref, grad_in, gain_one_ref, gain_two_ref, qk_ref, w_router_ref, routes_ref, cos_ref, sin_ref, gate_in, up_in, down_in,
         w_all, out_all, grad_all, h1_out, raw_out, gate_up, down_out, gain_ref, router_ref, chosen_ref, scale_ref, q_ref, context,
-        small_all, h1_ref, raw_ref, wide_in, wide_low, down_f, down_low, own_w, own_out, weights, total, part_k, land_k, part_q, land_q,
+        small_ref, small_all, h1_ref, raw_ref, wide_in, wide_low, down_f, down_low, own_w, own_out, weights, total, part_k, land_k, part_q, land_q,
         send_sem, recv_sem, out_sem, small_sem, kept, ks_s, ks_r, qs_s, qs_r, c_s, c_r, hx_s, hx_r, hc_s, hc_r, wide_s,
     ):
         z, y, x, c = place()
@@ -1895,6 +1898,16 @@
             ],
             views, send_sem, recv_sem, y_first=(OUT,),
         )
+        small_ref[...] = jnp.zeros_like(small_ref)
+        small_ref[0:1, :] = gain_one_ref[...].astype(low).astype(f32)
+        small_ref[1:2, :] = gain_two_ref[...].astype(low).astype(f32)
+        small_ref[2:3, : qk_gain.shape[1]] = qk_ref[...].astype(low).astype(f32)
+        small_ref[8 : 8 + experts, :] = w_router_ref[...]
+        expert_row = lax.broadcasted_iota(jnp.int32, (experts, rows), 0)
+        named = jnp.zeros((experts, rows), f32)
+        for k in range(routes.shape[0]):
+            named = jnp.where(routes_ref[k : k + 1, :] == expert_row, 1.0, named)
+        small_ref[8 + experts : 8 + 2 * experts, :] = named
         greet(line.partners() + [(mate, None) for mate in mates])
         line.start(SMALL, 0)
         for part in (VALUE, KEY, QUERY):
@@ -2165,10 +2178,11 @@
             shape((rows, columns), low),
             shape((back + 1, 2, rows, columns), low),
         ),
-        in_specs=[VMEM, VMEM, VMEM, HBM, VMEM, VMEM, VMEM, HBM, HBM, HBM],
+        in_specs=[VMEM, VMEM, VMEM, HBM] + [VMEM] * 7 + [HBM, HBM, HBM],
         out_specs=(HBM,) * 7 + (VMEM,) * 6,
         scratch_shapes=[
-            pltpu.VMEM((GROUPS,) + smalls.shape, f32),
+            pltpu.VMEM(small_shape, f32),
+            pltpu.VMEM((GROUPS,) + small_shape, f32),
             pltpu.VMEM((rows, width), low),
             pltpu.VMEM((2, rows, columns), f32),
             pltpu.VMEM((4, width, w_down.shape[1]), f32),
@@ -2191,7 +2205,10 @@
         compiler_params=comm_params(collective_id, 62),
         cost_estimate=cost(100),
         name="project",
-    )(tokens, w_qkv, w_out, out_grad, smalls, cosine, sine, w_gate, w_up, w_down)
+    )(
+        tokens, w_qkv, w_out, out_grad, gain_one, gain_two, qk_gain, w_router, routes, cosine, sine,
+        w_gate, w_up, w_down,
+    )
 
 
 def attend(query, context, segment_query, segment_keys, tokens, out_low, gain, collective_id):
@@ -2751,20 +2768,6 @@
     ).astype(jnp.float32)
     qk_row = qk_gain.reshape(1, -1)
 
-    def rounded(v):
-        return lax.reduce_precision(v, 8, 7)
-
-    smalls = jnp.concatenate(
-        [
-            rounded(attn_gain)[None, :],
-            rounded(ffn_gain)[None, :],
-            jnp.pad(rounded(qk_row), ((0, 0), (0, row_count - qk_row.shape[1]))),
-            jnp.zeros((5, row_count), jnp.float32),
-            w_router.T,
-            chosen.T,
-        ],
-        axis=0,
-    )
     global_rows = device_index * row_count + jnp.arange(row_count, dtype=jnp.int32)
     cosine_table, sine_table = angles(global_rows % SEQ, HEAD)
     wide_cosine = jnp.concatenate([cosine_table[:, 0], cosine_table[:, 0]], axis=1)
@@ -2773,8 +2776,8 @@
         qkv_low, out_low, grad_out_all, hidden_one, raw, gate_up, down_low, gains, router_t, chosen_all,
         scales, query_low, context_blocks,
     ) = project(
-        tokens_in, w_qkv, w_attn_out, out_grad, smalls, wide_cosine, wide_sine, w_gate, w_up, w_down,
-        experts, 0,
+        tokens_in, w_qkv, w_attn_out, out_grad, attn_gain[None, :], ffn_gain[None, :], qk_row, w_router.T, routes.T,
+        wide_cosine, wide_sine, w_gate, w_up, w_down, 0,
     )
     segment_window = lax.dynamic_slice_in_dim(
         jnp.concatenate([jnp.full((WINDOW,), -1, jnp.int32), segments]),

time: 505 us -> 501 us (level)
    unnamed x21 -> x23, local copies, waits for them, and re-layouts: 15.3 us -> 15.3 us
where the time goes in v9:
time: 501 us; the launch traced here: 494 us
  Pallas kernels  468 us (93%)
  local copies, waits for them, and re-layouts  23.5 us (5%)
    pallas_call x1, Pallas kernels, expert_layer(): pl.pallas_call(kernel, out_shape=(shape((rows, width), low), shape((rows,...  174 us
    pallas_call x1, Pallas kernels, project(): pl.pallas_call(kernel, out_shape=(shape((parts, depth * GROUPS, columns),...  133 us
    pallas_call x1, Pallas kernels, attend_back(): pl.pallas_call(kernel, out_shape=(shape((rows, width), low), shape((3, de...  131 us
    pallas_call x1, Pallas kernels, attend(): pl.pallas_call(kernel, out_shape=(shape((rows, columns), low), shape((row...  29.8 us
    unnamed x23, local copies, waits for them, and re-layouts  15.3 us

profile of v9, /device:TPU:0, one launch (start us, length us, event | category | flops | bytes accessed | tf_op | source)
XLA Modules:
  0.0 494.5 jit_solution(1998532051353377296)
XLA Ops:
  0.7 0.5 fusion.1
  1.2 0.8 pad_maximum_fusion
  2.1 1.3 reshape.57.qk_ref
  3.3 133.1 %project.1 = (bf16[3,2048,512]{2,1,0:T(8,128)(2,1)}, bf16[512,2048]{1,0:T(8,128)(2,1)}, bf16[2048,2048]{1,0:T(8,128)(2,1)}, bf16[256,2048]{1,0:T(8,128)(2,1)}, f...) custom-call(bf16[256,2048]{1,0:T(8,128)(2,1)} %tok_ref.5, ...), custom_call_target="tpu_custom_call" | custom-call | bytes 300000000 | tf_op jit(solution)/shard_map/project/pallas_call | solution.py:2164
  136.4 0.1 pad_dynamic-slice_fusion
  136.5 0.8 copy.30.sq_ref
  137.3 0.1 pad_dynamic-slice_fusion.1
  137.4 0.6 rev.3.sk_ref
  138.0 29.8 %attend.1 = (bf16[256,512]{1,0:T(8,128)(2,1)}, f32[256,128]{1,0:T(8,128)}, f32[256,2048]{1,0:T(8,128)}, bf16[256,2048]{1,0:T(8,128)(2,1)}, f32[256,128]{1,0:T(8,128)}) custom-call(bf16[256,512]{1,0:T(8,128)(2,1)} %get-tuple-element.40.q_ref, bf16[5,2,256,512]{3,2,1,0:T(8,128)(2,1)} %get-tuple-element.41.context_in.context_ref, s32[256,1]{1,0:T(8,128)} %copy.30.sq_ref, ...), custom_call_target="tpu_custom_call" | custom-call | bytes 120000000 | tf_op jit(solution)/shard_map/attend/pallas_call | solution.py:2305
  167.8 0.0 copy-start.6
  167.9 174.1 %expert_layer.1 = (bf16[256,2048]{1,0:T(8,128)(2,1)}, bf16[256,2048]{1,0:T(8,128)(2,1)}, f32[8,8,256]{2,1,0:T(8,128)}, f32[2,2048,256]{2,1,0:T(8,128)}, f32[2,20...) custom-call(bf16[256,2048]{1,0:T(8,128)(2,1)} %get-tuple-element.44.own_in.h2_ref, ...), custom_call_target="tpu_custom_call" | custom-call | bytes 240000000 | tf_op jit(solution)/shard_map/expert_layer/pallas_call | solution.py:1749
  342.0 0.8 slice.19
  342.8 0.1 copy.31
  343.0 0.1 copy.32
  343.1 0.7 bitcast_select_fusion.gates_ref
  343.8 130.7 %attend_back.1 = (bf16[256,2048]{1,0:T(8,128)(2,1)}, f32[3,256,512]{2,1,0:T(8,128)}, f32[512,256]{1,0:T(8,128)}, f32[24,256]{1,0:T(8,128)}) custom-call(bf16[256,2048]{1,0:T(8,128)(2,1)} %get-tuple-element.53.dh_ref, f32[256,16]{1,0:T(8,128)} %bitcast_select_fusion.gates_ref, bf16[16,2048]{1,0:T(8,128)(2,1)} %get-tuple-element.48.router_ref, ...), custom_call_target="tpu_custom_call" | custom-call | bytes 390000000 | tf_op jit(solution)/shard_map/attend_back/pallas_call | solution.py:2688
  474.5 0.0 copy-start.3
  474.5 0.0 copy-start.5
  474.5 0.8 slice.22
  475.4 0.7 constant_dynamic-slice_fusion
  476.1 1.3 slice_bitcast_fusion
  477.4 1.3 fusion.4
  478.7 1.0 copy.41
  479.7 3.0 copy.42
  482.7 1.1 copy.43
  483.8 0.0 copy-done.5
  483.8 0.8 copy.44
  484.6 2.1 copy.45
  486.8 1.6 copy-done.1
  488.3 2.1 copy.46
  490.5 1.6 copy-done
  492.0 2.0 copy.47
  (16 shorter events, 0.1 us)
Async XLA Ops:
  3.3 133.1 %copy-start.7 = (s32[2048]{0:T(1024)S(1)}, s32[2048]{0:T(1024)}, u32[]{:S(2)}) copy-start(s32[2048]{0:T(1024)} %param.25) | copy-start | bytes 24580
  167.8 175.1 %copy-start.6 = (s32[256,8]{0,1:T(8,128)S(1)}, s32[256,8]{0,1:T(8,128)}, u32[]{:S(2)}) copy-start(s32[256,8]{0,1:T(8,128)} %param.24) | copy-start | bytes 24580
  343.8 135.0 %copy-start.4 = (bf16[256,2048]{1,0:T(8,128)(2,1)S(1)}, bf16[256,2048]{1,0:T(8,128)(2,1)}, u32[]{:S(2)}) copy-start(bf16[256,2048]{1,0:T(8,128)(2,1)} %get-tuple-element.87) | copy-start | bytes 3145732
  474.5 8.2 %copy-start.3 = (f32[3,256,512]{2,1,0:T(8,128)S(1)}, f32[3,256,512]{2,1,0:T(8,128)}, u32[]{:S(2)}) copy-start(f32[3,256,512]{2,1,0:T(8,128)} %get-tuple-element.89) | copy-start | bytes 4718596
  474.5 9.3 %copy-start.5 = (f32[512,256]{1,0:T(8,128)S(1)}, f32[512,256]{1,0:T(8,128)}, u32[]{:S(2)}) copy-start(f32[512,256]{1,0:T(8,128)} %get-tuple-element.90) | copy-start | bytes 1572868
  478.7 5.9 %copy-start.2 = (f32[2,2048,256]{2,1,0:T(8,128)S(1)}, f32[2,2048,256]{2,1,0:T(8,128)}, u32[]{:S(2)}) copy-start(f32[2,2048,256]{2,1,0:T(8,128)} %get-tuple-element.95) | copy-start | bytes 12582916
  484.6 3.7 copy-start.1
  488.3 3.7 copy-start

commit v10 on v9

--- a/solution.py
+++ b/solution.py
@@ -1135,9 +1135,9 @@
     wide = width // 4
 
     def kernel(
-        own_in, dy_in, gu_ref, down_ref, router_ref, chosen_ref, x1_in, o_in,
+        own_in, dy_in, gu_in, down_in, router_ref, chosen_ref, x1_in, o_in,
         block_out, dh_out, gates_out, gate_w, up_w, down_w, o_all,
-        h, dy, gated, dgu, dx, y_part, yc_buf, ypx_buf, ypy_buf, yqy_buf, yqx_buf, yz_sum,
+        gu_ref, down_ref, weight_sem, h, dy, gated, dgu, dx, y_part, yc_buf, ypx_buf, ypy_buf, yqy_buf, yqx_buf, yz_sum,
         ylo_buf, yhi_buf, x1, gu_stage, d_stage,
         core_buf, px_buf, py_buf, qy_buf, qx_buf, z_sum, lo_buf, hi_buf, gate_part, gate_land,
         in_sem, own_sem, o_sem, line_s, line_r, hx_s, hx_r, hc_s, hc_r, x1_sem, yc_s, yc_r, ypx_s, ypx_r, ypy_s, ypy_r,
@@ -1149,6 +1149,12 @@
         across, twin, beside = device(z, y, 1 - x, c), device(z, y, x, 1 - c), device(z, 1 - y, x, c)
         mates = [(e, lax.rem(t + k, tensors)) for k in range(1, tensors)]
         peers = [(lax.rem(e + k, GROUPS), t) for k in range(1, GROUPS)]
+        weight_loads = [
+            pltpu.make_async_copy(gu_in, gu_ref, weight_sem.at[0]),
+            pltpu.make_async_copy(down_in, down_ref, weight_sem.at[1]),
+        ]
+        for copy in weight_loads:
+            copy.start()
         greet([(target, None) for target in mates + peers])
 
         def pick(values, index):
@@ -1436,6 +1442,7 @@
             load(i).wait()
             b = block_of(i)
             pl.when(i == 0)(keep.wait)
+            pl.when(i == 0)(lambda: each(weight_loads, "wait"))
 
             def landed():
                 for stream in range(3):
@@ -1757,9 +1764,12 @@
             shape((local, hidden, width), f32),
             shape((tokens,) + attended.shape[1:], low),
         ),
-        in_specs=[HBM, HBM, VMEM, VMEM, VMEM, VMEM, HBM, HBM],
+        in_specs=[HBM, HBM, HBM, HBM, VMEM, VMEM, HBM, HBM],
         out_specs=(VMEM, VMEM, VMEM, HBM, HBM, HBM, HBM),
         scratch_shapes=[
+            pltpu.VMEM(gate_up.shape, low),
+            pltpu.VMEM(down.shape, low),
+            dma((2,)),
             pltpu.VMEM((tokens, width), low),
             pltpu.VMEM((tokens, width), low),
             pltpu.VMEM((tokens, units), low),
@@ -2350,10 +2360,10 @@
 
     def kernel(
         dh_ref, gates_ref, router_ref, h2_ref, x1_ref, s2_ref, gain_ref, dy_ref,
-        q_ref, context_ref, sq_ref, sk_ref, o_ref, lse_ref, raw_ref, scale_ref,
-        cos_ref, sin_ref, h1_ref, tok_ref, o_all, w_hbm, out_ref,
+        q_ref, context_in, sq_ref, sk_ref, o_ref, lse_ref, raw_in, scale_ref,
+        cos_ref, sin_ref, h1_in, tok_in, o_all_in, w_hbm, out_ref,
         tok_grad, qkv_sum, out_sum, small_sum,
-        weights, dx1, da, do, dot_sums, dq, dkv, scaled, proj, send_kv, land_y, land_z,
+        context_ref, raw_ref, h1_ref, tok_ref, o_all, load_sem, weights, dx1, da, do, dot_sums, dq, dkv, scaled, proj, send_kv, land_y, land_z,
         part, full, core_buf, x_buf, small, line_sum,
         main_buf, da_all, small_buf, part_k, land_k, part_q, land_q,
         w_sem, y_s, y_r, z_s, z_r, group_s, group_r, ks_s, ks_r, qs_s, qs_r, line_s, line_r, far_s, far_r, near_s, near_r,
@@ -2364,6 +2374,17 @@
         beside, below = device(z, 1 - y, x, c), device(z - 1, y, x, c)
         fetch = pltpu.make_async_copy(w_hbm, weights, w_sem)
         fetch.start()
+        loads = [
+            pltpu.make_async_copy(source, target, load_sem.at[k])
+            for k, (source, target) in enumerate(
+                (
+                    (context_in, context_ref), (raw_in, raw_ref), (h1_in, h1_ref), (tok_in, tok_ref),
+                    (o_all_in, o_all),
+                )
+            )
+        ]
+        for copy in loads:
+            copy.start()
 
         def own_part(s, b):
             if s == SMALL:
@@ -2457,6 +2478,8 @@
 
         da_start()
 
+        for copy in loads:
+            copy.wait()
         do[...] = dot(da[...], out_ref[...], (1, 1)).astype(low)
         wide = lax.broadcasted_iota(jnp.int32, (rows, 128), 1)
         sums = jnp.zeros((rows, 128), f32)
@@ -2693,9 +2716,15 @@
             shape((columns, depth), f32),
             shape((small_rows, depth), f32),
         ),
-        in_specs=[VMEM] * 21 + [HBM, VMEM],
+        in_specs=[HBM if k in (9, 14, 18, 19, 20, 21) else VMEM for k in range(23)],
         out_specs=(VMEM,) * 4,
         scratch_shapes=[
+            vmem(context.shape, low),
+            vmem(raw.shape, f32),
+            vmem(hidden_one.shape, low),
+            vmem(tokens.shape, low),
+            vmem(attended_all.shape, low),
+            dma((5,)),
             vmem(qkv_low.shape, low),
             vmem((rows, width), f32),
             vmem((rows, width), low),

time: 501 us -> 497 us (level)
  no operation moved by 1% of the time
where the time goes in v10:
time: 497 us; the launch traced here: 490 us
  Pallas kernels  464 us (93%)
  local copies, waits for them, and re-layouts  23.5 us (5%)
    pallas_call x1, Pallas kernels, expert_layer(): pl.pallas_call(kernel, out_shape=(shape((rows, width), low), shape((rows,...  172 us
    pallas_call x1, Pallas kernels, project(): pl.pallas_call(kernel, out_shape=(shape((parts, depth * GROUPS, columns),...  133 us
    pallas_call x1, Pallas kernels, attend_back(): pl.pallas_call(kernel, out_shape=(shape((rows, width), low), shape((3, de...  128 us
    pallas_call x1, Pallas kernels, attend(): pl.pallas_call(kernel, out_shape=(shape((rows, columns), low), shape((row...  29.8 us
    unnamed x23, local copies, waits for them, and re-layouts  15.3 us

profile of v10, /device:TPU:0, one launch (start us, length us, event | category | flops | bytes accessed | tf_op | source)
XLA Modules:
  0.0 490.5 jit_solution(12707625980760373600)
XLA Ops:
  0.7 0.5 fusion.1
  1.2 0.8 pad_maximum_fusion
  2.1 1.3 reshape.57.qk_ref
  3.3 133.1 %project.1 = (bf16[3,2048,512]{2,1,0:T(8,128)(2,1)}, bf16[512,2048]{1,0:T(8,128)(2,1)}, bf16[2048,2048]{1,0:T(8,128)(2,1)}, bf16[256,2048]{1,0:T(8,128)(2,1)}, f...) custom-call(bf16[256,2048]{1,0:T(8,128)(2,1)} %tok_in.1, ...), custom_call_target="tpu_custom_call" | custom-call | bytes 300000000 | tf_op jit(solution)/shard_map/project/pallas_call | solution.py:2174
  136.4 0.0 copy-done.7
  136.4 0.1 pad_dynamic-slice_fusion
  136.5 0.8 copy.30.sq_ref
  137.3 0.1 pad_dynamic-slice_fusion.1
  137.4 0.6 rev.3.sk_ref
  138.0 29.8 %attend.1 = (bf16[256,512]{1,0:T(8,128)(2,1)}, f32[256,128]{1,0:T(8,128)}, f32[256,2048]{1,0:T(8,128)}, bf16[256,2048]{1,0:T(8,128)(2,1)}, f32[256,128]{1,0:T(8,128)}) custom-call(bf16[256,512]{1,0:T(8,128)(2,1)} %get-tuple-element.40.q_ref, bf16[5,2,256,512]{3,2,1,0:T(8,128)(2,1)} %get-tuple-element.41.context_in, s32[256,1]{1,0:T(8,128)} %copy.30.sq_ref, ...), custom_call_target="tpu_custom_call" | custom-call | bytes 120000000 | tf_op jit(solution)/shard_map/attend/pallas_call | solution.py:2315
  167.8 0.0 copy-start.6
  167.9 172.3 %expert_layer.1 = (bf16[256,2048]{1,0:T(8,128)(2,1)}, bf16[256,2048]{1,0:T(8,128)(2,1)}, f32[8,8,256]{2,1,0:T(8,128)}, f32[2,2048,256]{2,1,0:T(8,128)}, f32[2,20...) custom-call(bf16[256,2048]{1,0:T(8,128)(2,1)} %get-tuple-element.44.own_in.h2_ref, ...), custom_call_target="tpu_custom_call" | custom-call | bytes 240000000 | tf_op jit(solution)/shard_map/expert_layer/pallas_call | solution.py:1756
  340.2 0.8 slice.19
  341.1 0.1 copy.31
  341.2 0.1 copy.32
  341.3 0.7 bitcast_select_fusion.gates_ref
  342.0 128.5 %attend_back.1 = (bf16[256,2048]{1,0:T(8,128)(2,1)}, f32[3,256,512]{2,1,0:T(8,128)}, f32[512,256]{1,0:T(8,128)}, f32[24,256]{1,0:T(8,128)}) custom-call(bf16[256,2048]{1,0:T(8,128)(2,1)} %get-tuple-element.53.dh_ref, f32[256,16]{1,0:T(8,128)} %bitcast_select_fusion.gates_ref, bf16[16,2048]{1,0:T(8,128)(2,1)} %get-tuple-element.48.router_ref, ...), custom_call_target="tpu_custom_call" | custom-call | bytes 390000000 | tf_op jit(solution)/shard_map/attend_back/pallas_call | solution.py:2711
  470.5 0.8 slice.22
  471.4 0.7 constant_dynamic-slice_fusion
  472.1 1.3 slice_bitcast_fusion
  473.4 1.3 fusion.4
  474.7 0.0 copy-done.4
  474.7 1.0 copy.41
  475.7 3.0 copy.42
  478.7 0.0 copy-done.3
  478.7 1.1 copy.43
  479.8 0.8 copy.44
  480.6 2.1 copy.45
  482.7 1.6 copy-done.1
  484.3 2.1 copy.46
  486.4 1.6 copy-done
  488.0 2.0 copy.47
  (16 shorter events, 0.1 us)
Async XLA Ops:
  3.3 133.1 %copy-start.7 = (s32[2048]{0:T(1024)S(1)}, s32[2048]{0:T(1024)}, u32[]{:S(2)}) copy-start(s32[2048]{0:T(1024)} %param.25) | copy-start | bytes 24580
  167.8 173.3 %copy-start.6 = (s32[256,8]{0,1:T(8,128)S(1)}, s32[256,8]{0,1:T(8,128)}, u32[]{:S(2)}) copy-start(s32[256,8]{0,1:T(8,128)} %param.24) | copy-start | bytes 24580
  342.0 132.7 %copy-start.4 = (bf16[256,2048]{1,0:T(8,128)(2,1)S(1)}, bf16[256,2048]{1,0:T(8,128)(2,1)}, u32[]{:S(2)}) copy-start(bf16[256,2048]{1,0:T(8,128)(2,1)} %get-tuple-element.87) | copy-start | bytes 3145732
  470.5 8.2 %copy-start.3 = (f32[3,256,512]{2,1,0:T(8,128)S(1)}, f32[3,256,512]{2,1,0:T(8,128)}, u32[]{:S(2)}) copy-start(f32[3,256,512]{2,1,0:T(8,128)} %get-tuple-element.89) | copy-start | bytes 4718596
  470.5 9.3 %copy-start.5 = (f32[512,256]{1,0:T(8,128)S(1)}, f32[512,256]{1,0:T(8,128)}, u32[]{:S(2)}) copy-start(f32[512,256]{1,0:T(8,128)} %get-tuple-element.90) | copy-start | bytes 1572868
  474.7 5.9 %copy-start.2 = (f32[2,2048,256]{2,1,0:T(8,128)S(1)}, f32[2,2048,256]{2,1,0:T(8,128)}, u32[]{:S(2)}) copy-start(f32[2,2048,256]{2,1,0:T(8,128)} %get-tuple-element.95) | copy-start | bytes 12582916
  480.6 3.7 copy-start.1
  484.3 3.7 copy-start

commit v11 on v10

--- a/solution.py
+++ b/solution.py
@@ -396,7 +396,7 @@
 
 
 def device(z, y, x, c):
-    return (z * NY + y, x * NC + c)
+    return (jnp.clip(z, 0, NZ - 1) * NY + y, x * NC + c)
 
 
 def run_if(condition, body):
@@ -558,135 +558,6 @@
     )
 
 
-def weight_gather(qkv_low, out_low, smalls, collective_id):
-    parts, rows, width = qkv_low.shape
-    depth, columns = out_low.shape
-
-    def kernel(qkv, out, small, qkv_all, out_all, small_all, send_sem, recv_sem, local_sem):
-        views = [
-            lambda b: qkv_all.at[:, block_rows(b, rows), :],
-            lambda b: out_all.at[:, block_rows(b, columns)],
-            lambda b: small_all.at[b],
-        ]
-        line = LineGather([2, 0, 1], [qkv, out, small], views, send_sem, recv_sem)
-        greet(line.partners())
-        own = line.block(0)
-        keep = [
-            pltpu.make_async_copy(source, view(own), local_sem.at[i])
-            for i, (source, view) in enumerate(zip([qkv, out, small], views))
-        ]
-        for copy in keep:
-            copy.start()
-        line.run()
-        line.finish()
-        for copy in keep:
-            copy.wait()
-
-    return pl.pallas_call(
-        kernel,
-        out_shape=(
-            jax.ShapeDtypeStruct((parts, rows * GROUPS, width), jnp.bfloat16),
-            jax.ShapeDtypeStruct((depth, columns * GROUPS), jnp.bfloat16),
-            jax.ShapeDtypeStruct((GROUPS,) + smalls.shape, jnp.float32),
-        ),
-        in_specs=[HBM] * 3,
-        out_specs=(HBM, HBM, HBM),
-        scratch_shapes=[
-            pltpu.SemaphoreType.DMA((3, 14, 3)),
-            pltpu.SemaphoreType.DMA((3, 14)),
-            pltpu.SemaphoreType.DMA((3,)),
-        ],
-        compiler_params=comm_params(collective_id),
-        cost_estimate=cost(100),
-        name="weight_gather",
-    )(qkv_low, out_low, smalls)
-
-
-def token_gather(block, collective_id):
-    rows, width = block.shape
-    a_cols, c_cols = width * 3 // 16, width // 8
-
-    def kernel(own_ref, all_ref, send_sem, recv_sem, x_send, x_recv, core_send, core_recv, local_sem):
-        z, y, x, c = place()
-
-        def a_at(xx, cc):
-            return pl.ds(pl.multiple_of(xx * (2 * a_cols) + cc * a_cols, 128), a_cols)
-
-        def c_at(cc):
-            return pl.ds(pl.multiple_of(4 * a_cols + cc * c_cols, 128), c_cols)
-
-        def view(b, columns):
-            return all_ref.at[block_rows(b, rows), columns]
-
-        sources = [own_ref.at[:, a_at(x, c)], own_ref.at[:, c_at(c)]]
-        views = [lambda b: view(b, a_at(x, c)), lambda b: view(b, c_at(c))]
-        line = LineGather([0, 1], sources, views, send_sem, recv_sem)
-        across, twin = device(z, y, 1 - x, c), device(z, y, x, 1 - c)
-        greet(line.partners() + [(across, None), (twin, None)])
-        keep = pltpu.make_async_copy(own_ref, all_ref.at[block_rows(line.block(0), rows), :], local_sem)
-        keep.start()
-
-        def to_twin(rel, stream, landing=False):
-            b = line.block(rel)
-            columns = [a_at(x, c), c_at(c), a_at(1 - x, c)][stream]
-            other = [a_at(x, 1 - c), c_at(1 - c), a_at(1 - x, 1 - c)][stream]
-            piece = view(b, other if landing else columns)
-            return remote(piece, piece, core_send.at[rel, stream], core_recv.at[rel, stream], twin)
-
-        def to_across(rel, landing=False):
-            b = line.block(rel)
-            piece = view(b, a_at(1 - x if landing else x, c))
-            return remote(piece, piece, x_send.at[rel], x_recv.at[rel], across)
-
-        def hook(stream, rel):
-            if stream == 0:
-                to_across(rel).start()
-            to_twin(rel, stream).start()
-
-        line.run(hook)
-        for rel in line.order():
-            def relay(rel=rel):
-                to_across(rel, True).wait_recv()
-                to_twin(rel, 2).start()
-            run_if(line.exists(rel), relay)
-        for rel in line.order():
-            def end(rel=rel):
-                to_across(rel).wait_send()
-                for stream in range(3):
-                    to_twin(rel, stream, True).wait_recv()
-                    to_twin(rel, stream).wait_send()
-            run_if(line.exists(rel), end)
-        line.finish()
-        keep.wait()
-
-    return pl.pallas_call(
-        kernel,
-        out_shape=jax.ShapeDtypeStruct((rows * GROUPS, width), block.dtype),
-        in_specs=[HBM],
-        out_specs=HBM,
-        scratch_shapes=[
-            pltpu.SemaphoreType.DMA((2, 14, 3)),
-            pltpu.SemaphoreType.DMA((2, 14)),
-            pltpu.SemaphoreType.DMA((14,)),
-            pltpu.SemaphoreType.DMA((14,)),
-            pltpu.SemaphoreType.DMA((14, 3)),
-            pltpu.SemaphoreType.DMA((14, 3)),
-            pltpu.SemaphoreType.DMA,
-        ],
-        compiler_params=comm_params(collective_id),
-        cost_estimate=cost(45),
-        name="token_gather",
-    )(block)
-
-
-def add_into(rows, step, store):
-    def body(i, carry):
-        store(pl.ds(pl.multiple_of(i * step, step), step))
-        return carry
-
-    lax.fori_loop(0, rows // step, body, 0)
-
-
 def group_stages(part_ref, out_ref, core_buf, x_buf, send_sem, recv_sem):
     rows, width = part_ref.shape
     half, quarter = width // 2, width // 4
@@ -745,31 +616,6 @@
         meanwhile()
     for stage in stages[1:]:
         stage()
-
-
-def tensor_sum(part, collective_id):
-    rows, width = part.shape
-
-    def kernel(part_ref, out_ref, core_buf, x_buf, send_sem, recv_sem):
-        z, y, x, c = place()
-        greet([(device(z, y, 1 - x, c), None), (device(z, y, x, 1 - c), None)])
-        group_sum(part_ref, out_ref, core_buf, x_buf, send_sem, recv_sem)
-
-    return pl.pallas_call(
-        kernel,
-        out_shape=jax.ShapeDtypeStruct((rows, width), jnp.bfloat16),
-        in_specs=[VMEM],
-        out_specs=VMEM,
-        scratch_shapes=[
-            pltpu.VMEM((rows, width // 2), jnp.bfloat16),
-            pltpu.VMEM((rows, width // 4), jnp.bfloat16),
-            pltpu.SemaphoreType.DMA((5,)),
-            pltpu.SemaphoreType.DMA((5,)),
-        ],
-        compiler_params=comm_params(collective_id, 16),
-        cost_estimate=cost(17),
-        name="tensor_sum",
-    )(part)
 
 
 Z_ORDER = (3, 0, 2, 1)
@@ -855,251 +701,6 @@
                 self.copy(s, zz, 0).wait_send()
                 run_if(self.z < zz, lambda s=s, zz=zz: self.copy(s, zz, 1).wait_send())
                 run_if(self.z > zz, lambda s=s, zz=zz: self.copy(s, zz, 2).wait_send())
-
-
-def weight_reduce(qkv, out, smalls, collective_id):
-    parts, depth, width = qkv.shape
-    rows = depth // GROUPS
-    out_rows, columns = out.shape[0], out.shape[1] // GROUPS
-
-    def kernel(qkv_ref, out_ref, small_ref, qkv_sum, out_sum, small_sum,
-               qkv_buf, out_buf, small_buf, send_sem, recv_sem):
-        def own(s, zz, yy):
-            b = zz * NY + yy
-            if s < parts:
-                return qkv_ref.at[s, block_rows(b, rows), :]
-            if s == parts:
-                return out_ref.at[:, block_rows(b, columns)]
-            return small_ref.at[b]
-
-        def slot(kind):
-            def view(s, zz):
-                if s < parts:
-                    return qkv_buf.at[kind, zz, s]
-                if s == parts:
-                    return out_buf.at[kind, zz]
-                return small_buf.at[kind, zz]
-            return view
-
-        streams = list(range(parts + 2))
-        line = LineReduce(streams, own, slot(0), slot(1), slot(2), send_sem, recv_sem)
-        greet(line.partners())
-        work = [(s, zz) for s in [parts + 1, parts] + list(range(parts)) for zz in Z_ORDER]
-        for s, zz in work:
-            line.to_y(s, zz)
-        for s, zz in work:
-            line.along_z(s, zz)
-
-        def done(s, total):
-            target = qkv_sum.at[s] if s < parts else (out_sum if s == parts else small_sum)
-            step = min(64, target.shape[0])
-
-            def body(i, carry):
-                r = pl.ds(pl.multiple_of(i * step, step), step)
-                target[r, :] = total[r, :].astype(jnp.float32)
-                return carry
-
-            lax.fori_loop(0, target.shape[0] // step, body, 0)
-
-        line.home(done)
-        line.finish()
-
-    return pl.pallas_call(
-        kernel,
-        out_shape=(
-            jax.ShapeDtypeStruct((parts, rows, width), jnp.float32),
-            jax.ShapeDtypeStruct((out_rows, columns), jnp.float32),
-            jax.ShapeDtypeStruct(smalls.shape[1:], jnp.float32),
-        ),
-        in_specs=[VMEM] * 3,
-        out_specs=(VMEM,) * 3,
-        scratch_shapes=[
-            pltpu.VMEM((3, NZ, parts, rows, width), jnp.bfloat16),
-            pltpu.VMEM((3, NZ, out_rows, columns), jnp.bfloat16),
-            pltpu.VMEM((3, NZ) + smalls.shape[1:], jnp.float32),
-            pltpu.SemaphoreType.DMA((parts + 2, NZ, 3)),
-            pltpu.SemaphoreType.DMA((parts + 2, NZ, 3)),
-        ],
-        compiler_params=comm_params(collective_id),
-        cost_estimate=cost(120),
-        name="weight_reduce",
-    )(qkv, out, smalls)
-
-
-def token_reduce(part, collective_id, pairs=None):
-    tokens, width = part.shape
-    rows = tokens // GROUPS
-    half, quarter = width // 2, width // 4
-
-    def kernel(part_ref, out_ref, core_buf, x_buf, y_buf, lo_buf, hi_buf,
-               core_send, core_recv, x_send, x_recv, send_sem, recv_sem):
-        z, y, x, c = place()
-        across, twin = device(z, y, 1 - x, c), device(z, y, x, 1 - c)
-
-        line = LineReduce(
-            [0], lambda s, zz, yy: x_buf.at[zz * NY + yy], lambda s, zz: y_buf.at[zz],
-            lambda s, zz: lo_buf.at[zz], lambda s, zz: hi_buf.at[zz], send_sem, recv_sem,
-        )
-        greet(line.partners() + [(across, None), (twin, None)])
-        order = [(zz, flip) for zz in Z_ORDER for flip in (1, 0)]
-
-        def number(zz, flip):
-            return zz * NY + (1 - y if flip else y)
-
-        def to_twin(zz, flip):
-            b = number(zz, flip)
-            return remote(
-                part_ref.at[block_rows(b, rows), pl.ds(pl.multiple_of((1 - c) * half, half), half)],
-                core_buf.at[b], core_send.at[zz, flip], core_recv.at[zz, flip], twin,
-            )
-
-        def to_across(zz, flip):
-            b = number(zz, flip)
-            return remote(
-                core_buf.at[b, :, pl.ds(pl.multiple_of((1 - x) * quarter, quarter), quarter)],
-                x_buf.at[b], x_send.at[zz, flip], x_recv.at[zz, flip], across,
-            )
-
-        def add_core(zz, flip):
-            b = number(zz, flip)
-
-            def store(r):
-                at = pl.ds(pl.multiple_of(b * rows + r.start, 16), r.size)
-                core_buf[b, r, :] = (
-                    core_buf[b, r, :].astype(jnp.float32)
-                    + part_ref[at, pl.ds(pl.multiple_of(c * half, half), half)].astype(jnp.float32)
-                ).astype(jnp.bfloat16)
-
-            add_into(rows, 32, store)
-
-        def add_across(zz, flip):
-            b = number(zz, flip)
-
-            def store(r):
-                x_buf[b, r, :] = (
-                    x_buf[b, r, :].astype(jnp.float32)
-                    + core_buf[b, r, pl.ds(pl.multiple_of(x * quarter, quarter), quarter)].astype(jnp.float32)
-                ).astype(jnp.bfloat16)
-
-            add_into(rows, 64, store)
-
-        def stage_twin(i):
-            to_twin(*order[i]).wait_recv()
-            add_core(*order[i])
-            to_across(*order[i]).start()
-
-        def stage_across(i):
-            zz, flip = order[i]
-            to_across(zz, flip).wait_recv()
-            add_across(zz, flip)
-            if flip:
-                line.to_y(0, zz)
-
-        def stage_y(zz):
-            line.along_z(0, zz)
-
-        for zz, flip in order:
-            to_twin(zz, flip).start()
-        count = len(order)
-        for i in range(count + 4):
-            if i < count:
-                stage_twin(i)
-            if 0 <= i - 1 < count:
-                stage_across(i - 1)
-            if i >= 3 and (i - 3) % 2 == 0 and (i - 3) // 2 < NZ:
-                stage_y(Z_ORDER[(i - 3) // 2])
-
-        def done(s, total):
-            def store(r):
-                out_ref[r, :] = total[r, :]
-
-            add_into(rows, 64, store)
-
-        line.home(done)
-        for zz, flip in order:
-            to_twin(zz, flip).wait_send()
-            to_across(zz, flip).wait_send()
-        line.finish()
-
-    return pl.pallas_call(
-        kernel,
-        out_shape=jax.ShapeDtypeStruct((rows, quarter), jnp.bfloat16),
-        in_specs=[VMEM],
-        out_specs=VMEM,
-        scratch_shapes=[
-            pltpu.VMEM((GROUPS, rows, half), jnp.bfloat16),
-            pltpu.VMEM((GROUPS, rows, quarter), jnp.bfloat16),
-            pltpu.VMEM((NZ, rows, quarter), jnp.bfloat16),
-            pltpu.VMEM((NZ, rows, quarter), jnp.bfloat16),
-            pltpu.VMEM((NZ, rows, quarter), jnp.bfloat16),
-            pltpu.SemaphoreType.DMA((NZ, 2)),
-            pltpu.SemaphoreType.DMA((NZ, 2)),
-            pltpu.SemaphoreType.DMA((NZ, 2)),
-            pltpu.SemaphoreType.DMA((NZ, 2)),
-            pltpu.SemaphoreType.DMA((1, NZ, 3)),
-            pltpu.SemaphoreType.DMA((1, NZ, 3)),
-        ],
-        compiler_params=comm_params(collective_id),
-        cost_estimate=cost(60),
-        name="token_reduce",
-    )(part)
-
-
-def gate_exchange(part, collective_id):
-    groups = part.shape[0]
-    tensors = NX * NC
-
-    def kernel(part_ref, out_ref, landing, total, send_t, recv_t, send_e, recv_e):
-        e = lax.axis_index("expert")
-        t = lax.axis_index("tensor")
-        mates = [(e, lax.rem(t + k, tensors)) for k in range(1, tensors)]
-        peers = [(lax.rem(e + k, groups), t) for k in range(1, groups)]
-        greet([(target, None) for target in mates + peers])
-        near = [
-            remote(part_ref, landing.at[k], send_t.at[k], recv_t.at[k], mates[k])
-            for k in range(tensors - 1)
-        ]
-        for copy in near:
-            copy.start()
-        for copy in near:
-            copy.wait_recv()
-        value = part_ref[...]
-        for k in range(tensors - 1):
-            value = value + landing[k]
-        total[...] = value
-        far = [
-            remote(
-                total.at[lax.rem(e + k, groups)], out_ref.at[e], send_e.at[k - 1], recv_e.at[k - 1],
-                peers[k - 1],
-            )
-            for k in range(1, groups)
-        ]
-        for copy in far:
-            copy.start()
-        out_ref[e] = total[e]
-        for k in range(1, groups):
-            source = out_ref.at[lax.rem(e + groups - k, groups)]
-            remote(source, source, send_e.at[k - 1], recv_e.at[k - 1], peers[k - 1]).wait_recv()
-        for copy in near + far:
-            copy.wait_send()
-
-    return pl.pallas_call(
-        kernel,
-        out_shape=jax.ShapeDtypeStruct(part.shape, jnp.float32),
-        in_specs=[VMEM],
-        out_specs=VMEM,
-        scratch_shapes=[
-            pltpu.VMEM((tensors - 1,) + part.shape, jnp.float32),
-            pltpu.VMEM(part.shape, jnp.float32),
-            pltpu.SemaphoreType.DMA((tensors - 1,)),
-            pltpu.SemaphoreType.DMA((tensors - 1,)),
-            pltpu.SemaphoreType.DMA((groups - 1,)),
-            pltpu.SemaphoreType.DMA((groups - 1,)),
-        ],
-        compiler_params=comm_params(collective_id, 16),
-        cost_estimate=cost(10),
-        name="gate_exchange",
-    )(part)
 
 
 def dot(a, b, dims):

time: 497 us -> 497 us (level)
  no operation moved by 1% of the time
where the time goes in v11:
time: 497 us; the launch traced here: 490 us
  Pallas kernels  464 us (93%)
  local copies, waits for them, and re-layouts  23.5 us (5%)
    pallas_call x1, Pallas kernels, expert_layer(): pl.pallas_call(kernel, out_shape=(shape((rows, width), low), shape((rows,...  172 us
    pallas_call x1, Pallas kernels, project(): pl.pallas_call(kernel, out_shape=(shape((parts, depth * GROUPS, columns),...  133 us
    pallas_call x1, Pallas kernels, attend_back(): pl.pallas_call(kernel, out_shape=(shape((rows, width), low), shape((3, de...  128 us
    pallas_call x1, Pallas kernels, attend(): pl.pallas_call(kernel, out_shape=(shape((rows, columns), low), shape((row...  29.8 us
    unnamed x23, local copies, waits for them, and re-layouts  15.3 us

profile of v11, /device:TPU:0, one launch (start us, length us, event | category | flops | bytes accessed | tf_op | source)
XLA Modules:
  0.0 490.4 jit_solution(16686036169735548588)
XLA Ops:
  0.7 0.5 fusion.1
  1.2 0.8 pad_maximum_fusion
  2.1 1.3 reshape.57.qk_ref
  3.3 133.1 %project.1 = (bf16[3,2048,512]{2,1,0:T(8,128)(2,1)}, bf16[512,2048]{1,0:T(8,128)(2,1)}, bf16[2048,2048]{1,0:T(8,128)(2,1)}, bf16[256,2048]{1,0:T(8,128)(2,1)}, f...) custom-call(bf16[256,2048]{1,0:T(8,128)(2,1)} %tok_in.1, ...), custom_call_target="tpu_custom_call" | custom-call | bytes 300000000 | tf_op jit(solution)/shard_map/project/pallas_call | solution.py:1775
  136.4 0.0 copy-done.7
  136.4 0.1 pad_dynamic-slice_fusion
  136.5 0.8 copy.30.sq_ref
  137.3 0.1 pad_dynamic-slice_fusion.1
  137.4 0.6 rev.3.sk_ref
  138.0 29.8 %attend.1 = (bf16[256,512]{1,0:T(8,128)(2,1)}, f32[256,128]{1,0:T(8,128)}, f32[256,2048]{1,0:T(8,128)}, bf16[256,2048]{1,0:T(8,128)(2,1)}, f32[256,128]{1,0:T(8,128)}) custom-call(bf16[256,512]{1,0:T(8,128)(2,1)} %get-tuple-element.40.q_ref, bf16[5,2,256,512]{3,2,1,0:T(8,128)(2,1)} %get-tuple-element.41.context_in, s32[256,1]{1,0:T(8,128)} %copy.30.sq_ref, ...), custom_call_target="tpu_custom_call" | custom-call | bytes 120000000 | tf_op jit(solution)/shard_map/attend/pallas_call | solution.py:1916
  167.8 0.0 copy-start.6
  167.9 172.3 %expert_layer.1 = (bf16[256,2048]{1,0:T(8,128)(2,1)}, bf16[256,2048]{1,0:T(8,128)(2,1)}, f32[8,8,256]{2,1,0:T(8,128)}, f32[2,2048,256]{2,1,0:T(8,128)}, f32[2,20...) custom-call(bf16[256,2048]{1,0:T(8,128)(2,1)} %get-tuple-element.44.own_in.h2_ref, ...), custom_call_target="tpu_custom_call" | custom-call | bytes 240000000 | tf_op jit(solution)/shard_map/expert_layer/pallas_call | solution.py:1357
  340.2 0.8 slice.19
  341.1 0.1 copy.31
  341.2 0.0 copy-done.6
  341.2 0.1 copy.32
  341.3 0.7 bitcast_select_fusion.gates_ref
  342.0 128.5 %attend_back.1 = (bf16[256,2048]{1,0:T(8,128)(2,1)}, f32[3,256,512]{2,1,0:T(8,128)}, f32[512,256]{1,0:T(8,128)}, f32[24,256]{1,0:T(8,128)}) custom-call(bf16[256,2048]{1,0:T(8,128)(2,1)} %get-tuple-element.53.dh_ref, f32[256,16]{1,0:T(8,128)} %bitcast_select_fusion.gates_ref, bf16[16,2048]{1,0:T(8,128)(2,1)} %get-tuple-element.48.router_ref, ...), custom_call_target="tpu_custom_call" | custom-call | bytes 390000000 | tf_op jit(solution)/shard_map/attend_back/pallas_call | solution.py:2312
  470.5 0.0 copy-start.3
  470.5 0.8 slice.22
  471.4 0.7 constant_dynamic-slice_fusion
  472.0 1.3 slice_bitcast_fusion
  473.3 1.3 fusion.4
  474.7 1.0 copy.41
  475.7 3.0 copy.42
  478.6 1.1 copy.43
  479.8 0.8 copy.44
  480.6 2.1 copy.45
  482.7 1.6 copy-done.1
  484.3 2.1 copy.46
  486.4 1.6 copy-done
  488.0 2.0 copy.47
  (16 shorter events, 0.1 us)
Async XLA Ops:
  3.3 133.1 %copy-start.7 = (s32[2048]{0:T(1024)S(1)}, s32[2048]{0:T(1024)}, u32[]{:S(2)}) copy-start(s32[2048]{0:T(1024)} %param.25) | copy-start | bytes 24580
  167.8 173.3 %copy-start.6 = (s32[256,8]{0,1:T(8,128)S(1)}, s32[256,8]{0,1:T(8,128)}, u32[]{:S(2)}) copy-start(s32[256,8]{0,1:T(8,128)} %param.24) | copy-start | bytes 24580
  342.0 132.7 %copy-start.4 = (bf16[256,2048]{1,0:T(8,128)(2,1)S(1)}, bf16[256,2048]{1,0:T(8,128)(2,1)}, u32[]{:S(2)}) copy-start(bf16[256,2048]{1,0:T(8,128)(2,1)} %get-tuple-element.87) | copy-start | bytes 3145732
  470.5 8.2 %copy-start.3 = (f32[3,256,512]{2,1,0:T(8,128)S(1)}, f32[3,256,512]{2,1,0:T(8,128)}, u32[]{:S(2)}) copy-start(f32[3,256,512]{2,1,0:T(8,128)} %get-tuple-element.89) | copy-start | bytes 4718596
  470.5 9.3 %copy-start.5 = (f32[512,256]{1,0:T(8,128)S(1)}, f32[512,256]{1,0:T(8,128)}, u32[]{:S(2)}) copy-start(f32[512,256]{1,0:T(8,128)} %get-tuple-element.90) | copy-start | bytes 1572868
  474.7 5.9 %copy-start.2 = (f32[2,2048,256]{2,1,0:T(8,128)S(1)}, f32[2,2048,256]{2,1,0:T(8,128)}, u32[]{:S(2)}) copy-start(f32[2,2048,256]{2,1,0:T(8,128)} %get-tuple-element.95) | copy-start | bytes 12582916
  480.6 3.7 copy-start.1
  484.3 3.7 copy-start

commit v12 on v11

--- a/solution.py
+++ b/solution.py
@@ -1460,13 +1460,16 @@
     small_shape = (8 + 2 * experts, depth)
 
     def kernel(
-        tok_ref, w_ref, out_ref, grad_in, gain_one_ref, gain_two_ref, qk_ref, w_router_ref, routes_ref, cos_ref, sin_ref, gate_in, up_in, down_in,
+        tok_ref, w_in, out_ref, grad_in, gain_one_ref, gain_two_ref, qk_ref, w_router_ref, routes_ref, cos_ref, sin_ref, gate_in, up_in, down_in,
         w_all, out_all, grad_all, h1_out, raw_out, gate_up, down_out, gain_ref, router_ref, chosen_ref, scale_ref, q_ref, context,
-        small_ref, small_all, h1_ref, raw_ref, wide_in, wide_low, down_f, down_low, own_w, own_out, weights, total, part_k, land_k, part_q, land_q,
+        w_ref, w_sem, small_ref, small_all, h1_ref, raw_ref, wide_in, wide_low, down_f, down_low, own_w, own_out, weights, total, part_k, land_k, part_q, land_q,
         send_sem, recv_sem, out_sem, small_sem, kept, ks_s, ks_r, qs_s, qs_r, c_s, c_r, hx_s, hx_r, hc_s, hc_r, wide_s,
     ):
         z, y, x, c = place()
         e, t = lax.axis_index("expert"), lax.axis_index("tensor")
+        w_loads = [pltpu.make_async_copy(w_in.at[k], w_ref.at[k], w_sem.at[k]) for k in range(parts)]
+        for part in (VALUE, KEY, QUERY):
+            w_loads[part].start()
         wide_loads = [
             pltpu.make_async_copy(source.at[k], wide_in.at[2 * n + k], wide_s.at[2 * n + k])
             for n, source in enumerate((gate_in, up_in))
@@ -1522,6 +1525,8 @@
         greet(line.partners() + [(mate, None) for mate in mates])
         line.start(SMALL, 0)
         for part in (VALUE, KEY, QUERY):
+            w_loads[part].wait()
+
             def cast(i, carry, part=part):
                 r = pl.ds(pl.multiple_of(i * 32, 32), 32)
                 own_w[part, r, :] = w_ref[part, r, :].astype(low)
@@ -1789,9 +1794,11 @@
             shape((rows, columns), low),
             shape((back + 1, 2, rows, columns), low),
         ),
-        in_specs=[VMEM, VMEM, VMEM, HBM] + [VMEM] * 7 + [HBM, HBM, HBM],
+        in_specs=[VMEM, HBM, VMEM, HBM] + [VMEM] * 7 + [HBM, HBM, HBM],
         out_specs=(HBM,) * 7 + (VMEM,) * 6,
         scratch_shapes=[
+            pltpu.VMEM((parts, depth, columns), f32),
+            dma((parts,)),
             pltpu.VMEM(small_shape, f32),
             pltpu.VMEM((GROUPS,) + small_shape, f32),
             pltpu.VMEM((rows, width), low),
@@ -1962,9 +1969,9 @@
     def kernel(
         dh_ref, gates_ref, router_ref, h2_ref, x1_ref, s2_ref, gain_ref, dy_ref,
         q_ref, context_in, sq_ref, sk_ref, o_ref, lse_ref, raw_in, scale_ref,
-        cos_ref, sin_ref, h1_in, tok_in, o_all_in, w_hbm, out_ref,
+        cos_ref, sin_ref, h1_in, tok_in, o_all_in, w_hbm, out_in,
         tok_grad, qkv_sum, out_sum, small_sum,
-        context_ref, raw_ref, h1_ref, tok_ref, o_all, load_sem, weights, dx1, da, do, dot_sums, dq, dkv, scaled, proj, send_kv, land_y, land_z,
+        context_ref, raw_ref, h1_ref, tok_ref, o_all, out_ref, load_sem, weights, dx1, da, do, dot_sums, dq, dkv, scaled, proj, send_kv, land_y, land_z,
         part, full, core_buf, x_buf, small, line_sum,
         main_buf, da_all, small_buf, part_k, land_k, part_q, land_q,
         w_sem, y_s, y_r, z_s, z_r, group_s, group_r, ks_s, ks_r, qs_s, qs_r, line_s, line_r, far_s, far_r, near_s, near_r,
@@ -1979,7 +1986,7 @@
             pltpu.make_async_copy(source, target, load_sem.at[k])
             for k, (source, target) in enumerate(
                 (
-                    (context_in, context_ref), (raw_in, raw_ref), (h1_in, h1_ref), (tok_in, tok_ref),
+                    (out_in, out_ref), (context_in, context_ref), (raw_in, raw_ref), (h1_in, h1_ref), (tok_in, tok_ref),
                     (o_all_in, o_all),
                 )
             )
@@ -2317,7 +2324,7 @@
             shape((columns, depth), f32),
             shape((small_rows, depth), f32),
         ),
-        in_specs=[HBM if k in (9, 14, 18, 19, 20, 21) else VMEM for k in range(23)],
+        in_specs=[HBM if k in (9, 14, 18, 19, 20, 21, 22) else VMEM for k in range(23)],
         out_specs=(VMEM,) * 4,
         scratch_shapes=[
             vmem(context.shape, low),
@@ -2325,7 +2332,8 @@
             vmem(hidden_one.shape, low),
             vmem(tokens.shape, low),
             vmem(attended_all.shape, low),
-            dma((5,)),
+            vmem(out_low.shape, low),
+            dma((6,)),
             vmem(qkv_low.shape, low),
             vmem((rows, width), f32),
             vmem((rows, width), low),

time: 497 us -> 496 us (level)
  no operation moved by 1% of the time
where the time goes in v12:
time: 496 us; the launch traced here: 489 us
  Pallas kernels  463 us (93%)
  local copies, waits for them, and re-layouts  23.5 us (5%)
    pallas_call x1, Pallas kernels, expert_layer(): pl.pallas_call(kernel, out_shape=(shape((rows, width), low), shape((rows,...  172 us
    pallas_call x1, Pallas kernels, project(): pl.pallas_call(kernel, out_shape=(shape((parts, depth * GROUPS, columns),...  133 us
    pallas_call x1, Pallas kernels, attend_back(): pl.pallas_call(kernel, out_shape=(shape((rows, width), low), shape((3, de...  128 us
    pallas_call x1, Pallas kernels, attend(): pl.pallas_call(kernel, out_shape=(shape((rows, columns), low), shape((row...  29.8 us
    unnamed x23, local copies, waits for them, and re-layouts  15.3 us

profile of v12, /device:TPU:0, one launch (start us, length us, event | category | flops | bytes accessed | tf_op | source)
XLA Modules:
  0.0 489.3 jit_solution(9294696960709194669)
XLA Ops:
  0.7 0.5 fusion.1
  1.2 0.8 pad_maximum_fusion
  2.1 1.3 reshape.57.qk_ref
  3.3 132.6 %project.1 = (bf16[3,2048,512]{2,1,0:T(8,128)(2,1)}, bf16[512,2048]{1,0:T(8,128)(2,1)}, bf16[2048,2048]{1,0:T(8,128)(2,1)}, bf16[256,2048]{1,0:T(8,128)(2,1)}, f...) custom-call(bf16[256,2048]{1,0:T(8,128)(2,1)} %tok_in.1, ...), custom_call_target="tpu_custom_call" | custom-call | bytes 300000000 | tf_op jit(solution)/shard_map/project/pallas_call | solution.py:1780
  136.0 0.0 copy-done.7
  136.0 0.1 pad_dynamic-slice_fusion
  136.1 0.8 copy.30.sq_ref
  136.9 0.1 pad_dynamic-slice_fusion.1
  137.0 0.6 rev.3.sk_ref
  137.6 29.8 %attend.1 = (bf16[256,512]{1,0:T(8,128)(2,1)}, f32[256,128]{1,0:T(8,128)}, f32[256,2048]{1,0:T(8,128)}, bf16[256,2048]{1,0:T(8,128)(2,1)}, f32[256,128]{1,0:T(8,128)}) custom-call(bf16[256,512]{1,0:T(8,128)(2,1)} %get-tuple-element.40.q_ref, bf16[5,2,256,512]{3,2,1,0:T(8,128)(2,1)} %get-tuple-element.41.context_in, s32[256,1]{1,0:T(8,128)} %copy.30.sq_ref, ...), custom_call_target="tpu_custom_call" | custom-call | bytes 120000000 | tf_op jit(solution)/shard_map/attend/pallas_call | solution.py:1923
  167.4 0.0 copy-start.6
  167.4 172.3 %expert_layer.1 = (bf16[256,2048]{1,0:T(8,128)(2,1)}, bf16[256,2048]{1,0:T(8,128)(2,1)}, f32[8,8,256]{2,1,0:T(8,128)}, f32[2,2048,256]{2,1,0:T(8,128)}, f32[2,20...) custom-call(bf16[256,2048]{1,0:T(8,128)(2,1)} %get-tuple-element.44.own_in.h2_ref, ...), custom_call_target="tpu_custom_call" | custom-call | bytes 240000000 | tf_op jit(solution)/shard_map/expert_layer/pallas_call | solution.py:1357
  339.7 0.8 slice.19
  340.6 0.1 copy.31
  340.7 0.0 copy-done.6
  340.7 0.1 copy.32
  340.9 0.7 bitcast_select_fusion.gates_ref
  341.5 127.8 %attend_back.1 = (bf16[256,2048]{1,0:T(8,128)(2,1)}, f32[3,256,512]{2,1,0:T(8,128)}, f32[512,256]{1,0:T(8,128)}, f32[24,256]{1,0:T(8,128)}) custom-call(bf16[256,2048]{1,0:T(8,128)(2,1)} %get-tuple-element.53.dh_ref, f32[256,16]{1,0:T(8,128)} %bitcast_select_fusion.gates_ref, bf16[16,2048]{1,0:T(8,128)(2,1)} %get-tuple-element.48.router_ref, ...), custom_call_target="tpu_custom_call" | custom-call | bytes 390000000 | tf_op jit(solution)/shard_map/attend_back/pallas_call | solution.py:2319
  469.3 0.8 slice.22
  470.2 0.7 constant_dynamic-slice_fusion
  470.9 1.3 slice_bitcast_fusion
  472.2 1.3 fusion.4
  473.5 1.0 copy.41
  474.5 3.0 copy.42
  477.5 0.0 copy-done.3
  477.5 1.1 copy.43
  478.6 0.8 copy.44
  479.4 2.1 copy.45
  481.6 1.6 copy-done.1
  483.1 2.1 copy.46
  485.3 1.6 copy-done
  486.8 2.0 copy.47
  (16 shorter events, 0.1 us)
Async XLA Ops:
  3.3 132.6 %copy-start.7 = (s32[2048]{0:T(1024)S(1)}, s32[2048]{0:T(1024)}, u32[]{:S(2)}) copy-start(s32[2048]{0:T(1024)} %param.25) | copy-start | bytes 24580
  167.4 173.3 %copy-start.6 = (s32[256,8]{0,1:T(8,128)S(1)}, s32[256,8]{0,1:T(8,128)}, u32[]{:S(2)}) copy-start(s32[256,8]{0,1:T(8,128)} %param.24) | copy-start | bytes 24580
  341.5 132.0 %copy-start.4 = (bf16[256,2048]{1,0:T(8,128)(2,1)S(1)}, bf16[256,2048]{1,0:T(8,128)(2,1)}, u32[]{:S(2)}) copy-start(bf16[256,2048]{1,0:T(8,128)(2,1)} %get-tuple-element.87) | copy-start | bytes 3145732
  469.3 8.2 %copy-start.3 = (f32[3,256,512]{2,1,0:T(8,128)S(1)}, f32[3,256,512]{2,1,0:T(8,128)}, u32[]{:S(2)}) copy-start(f32[3,256,512]{2,1,0:T(8,128)} %get-tuple-element.89) | copy-start | bytes 4718596
  469.3 9.3 %copy-start.5 = (f32[512,256]{1,0:T(8,128)S(1)}, f32[512,256]{1,0:T(8,128)}, u32[]{:S(2)}) copy-start(f32[512,256]{1,0:T(8,128)} %get-tuple-element.90) | copy-start | bytes 1572868
  473.5 5.9 %copy-start.2 = (f32[2,2048,256]{2,1,0:T(8,128)S(1)}, f32[2,2048,256]{2,1,0:T(8,128)}, u32[]{:S(2)}) copy-start(f32[2,2048,256]{2,1,0:T(8,128)} %get-tuple-element.95) | copy-start | bytes 12582916
  479.4 3.7 copy-start.1
  483.1 3.7 copy-start
